TPU v7x, 32 devices: a whole 2x2x4 slice. The times are simulated.
32 devices in a mesh: dp: 8 (over y, x, core), tensor: 4 (over z).
Axes of the slice: x: 2, y: 2, z: 4, core: 2. Of those that a mesh axis runs over, the one named last changes fastest.
Arguments:
- inputs: bfloat16 [16384, 512], P(('dp', 'tensor')), may hold values from -6 to 6
- memory: bfloat16 [4096, 512], P(('dp', 'tensor')), may hold values from -6 to 6
- prefix: int32 [16], P('dp'), may hold values from 102 to 512
- self_query: bfloat16 [512, 512], P('dp', 'tensor'), may hold values from -0.25 to 0.25
- self_query_bias: bfloat16 [512], P('tensor'), may hold values from -3 to 3
- self_key: bfloat16 [512, 512], P('dp', 'tensor'), may hold values from -0.25 to 0.25
- self_value: bfloat16 [512, 512], P('dp', 'tensor'), may hold values from -0.25 to 0.25
- self_value_bias: bfloat16 [512], P('tensor'), may hold values from -1.1953125 to 1.1953125
- self_out: bfloat16 [512, 512], P('tensor', 'dp'), may hold values from -1.5 to 1.5
- self_out_bias: bfloat16 [512], replicated, may hold values from -1.796875 to 1.796875
- self_norm_gain: bfloat16 [512], replicated, may hold values from 0.5 to 1.5
- self_norm_bias: bfloat16 [512], replicated, may hold values from -1.796875 to 1.796875
- cross_query: bfloat16 [512, 512], P('dp', 'tensor'), may hold values from -0.25 to 0.25
- cross_query_bias: bfloat16 [512], P('tensor'), may hold values from -3 to 3
- cross_key: bfloat16 [512, 512], P('dp', 'tensor'), may hold values from -0.25 to 0.25
- cross_value: bfloat16 [512, 512], P('dp', 'tensor'), may hold values from -0.25 to 0.25
- cross_value_bias: bfloat16 [512], P('tensor'), may hold values from -1.1953125 to 1.1953125
- cross_out: bfloat16 [512, 512], P('tensor', 'dp'), may hold values from -1.5 to 1.5
- cross_out_bias: bfloat16 [512], replicated, may hold values from -1.796875 to 1.796875
- cross_norm_gain: bfloat16 [512], replicated, may hold values from 0.5 to 1.5
- cross_norm_bias: bfloat16 [512], replicated, may hold values from -1.796875 to 1.796875
- feed_in: bfloat16 [512, 2048], P('dp', 'tensor'), may hold values from -0.25 to 0.25
- feed_in_bias: bfloat16 [2048], P('tensor'), may hold values from -3 to 3
- feed_out: bfloat16 [2048, 512], P('tensor', 'dp'), may hold values from -0.125 to 0.125
- feed_out_bias: bfloat16 [512], replicated, may hold values from -1.796875 to 1.796875
- feed_norm_gain: bfloat16 [512], replicated, may hold values from 0.5 to 1.5
- feed_norm_bias: bfloat16 [512], replicated, may hold values from -1.796875 to 1.796875
- cotangent: bfloat16 [16384, 512], P(('dp', 'tensor')), may hold values from -12 to 12
Outputs:
- outputs: bfloat16 [16384, 512], P(('dp', 'tensor'))
- grad_inputs: float32 [16384, 512], P(('dp', 'tensor'))
- grad_memory: float32 [4096, 512], P(('dp', 'tensor'))
- grad_self_query: float32 [512, 512], P('dp', 'tensor')
- grad_self_query_bias: float32 [512], P('tensor')
- grad_self_key: float32 [512, 512], P('dp', 'tensor')
- grad_self_value: float32 [512, 512], P('dp', 'tensor')
- grad_self_value_bias: float32 [512], P('tensor')
- grad_self_out: float32 [512, 512], P('tensor', 'dp')
- grad_self_out_bias: float32 [512], replicated
- grad_self_norm_gain: float32 [512], replicated
- grad_self_norm_bias: float32 [512], replicated
- grad_cross_query: float32 [512, 512], P('dp', 'tensor')
- grad_cross_query_bias: float32 [512], P('tensor')
- grad_cross_key: float32 [512, 512], P('dp', 'tensor')
- grad_cross_value: float32 [512, 512], P('dp', 'tensor')
- grad_cross_value_bias: float32 [512], P('tensor')
- grad_cross_out: float32 [512, 512], P('tensor', 'dp')
- grad_cross_out_bias: float32 [512], replicated
- grad_cross_norm_gain: float32 [512], replicated
- grad_cross_norm_bias: float32 [512], replicated
- grad_feed_in: float32 [512, 2048], P('dp', 'tensor')
- grad_feed_in_bias: float32 [2048], P('tensor')
- grad_feed_out: float32 [2048, 512], P('tensor', 'dp')
- grad_feed_out_bias: float32 [512], replicated
- grad_feed_norm_gain: float32 [512], replicated
- grad_feed_norm_bias: float32 [512], replicated
All inputs are finite; a program needn't handle non-finite values.
Results may differ from a plain program's by a relative error of at most 0.025.
Values may be sent and summed in bfloat16 or wider, within the bound.
No kernel may reach another device: no remote copies, remote signals or barrier semaphores. Data moves between devices by JAX's collectives and lax.ppermute only.
A program may use at most 128 MiB of HBM per device.

v0:
```python
import jax
import jax.numpy as jnp
from jax import lax
from jax.sharding import PartitionSpec as P

HD = 64
LEN = 1024
MEM = 256


EPSILON = 1e-05
MASKED = -1e30


def multiply(left_side, right_side, transposed):
    if transposed:
        return lax.dot_general(
            left_side, right_side, (((1,), (1,)), ((), ())), preferred_element_type=jnp.float32
        )
    return jnp.dot(left_side, right_side, preferred_element_type=jnp.float32)


def transposed_times(left_side, right_side):
    return lax.dot_general(
        left_side, right_side, (((0,), (0,)), ((), ())), preferred_element_type=jnp.float32
    )


def gather_rows(block_rows):
    return lax.all_gather(block_rows, "tensor", axis=0, tiled=True)


def reduce_rows(factor_pairs, transposed):
    local_rows = factor_pairs[0][0].shape[0] // lax.axis_size("tensor")
    partial_terms = [
        multiply(
            lax.slice_in_dim(left_side, 0, lax.axis_size("tensor") * local_rows, axis=0),
            right_side,
            transposed,
        )
        for left_side, right_side in factor_pairs
    ]
    running = partial_terms[0]
    for further in partial_terms[1:]:
        running = running + further
    return lax.psum_scatter(running, "tensor", scatter_dimension=0, tiled=True)


def project(rows_low, weight_low, bias_low):
    return (
        jnp.dot(rows_low, weight_low, preferred_element_type=jnp.float32)
        + bias_low.astype(jnp.float32)
    ).astype(jnp.bfloat16)


def norm_forward(summed, norm_gain, norm_shift):
    row_mean = jnp.mean(summed, axis=-1, keepdims=True)
    centred = summed - row_mean
    variance = jnp.mean(centred * centred, axis=-1, keepdims=True)
    inverse = lax.rsqrt(variance + EPSILON)
    normed = centred * inverse
    return (
        normed * norm_gain.astype(jnp.float32) + norm_shift.astype(jnp.float32),
        normed,
        inverse,
    )


def norm_backward(grad_out, normed, inverse, norm_gain):
    grad_normed = grad_out * norm_gain.astype(jnp.float32)
    grad_sum = inverse * (
        grad_normed
        - jnp.mean(grad_normed, axis=-1, keepdims=True)
        - normed * jnp.mean(grad_normed * normed, axis=-1, keepdims=True)
    )
    return (grad_sum, jnp.sum(grad_out * normed, axis=0), jnp.sum(grad_out, axis=0))


def split_heads(array, seq_count, length):
    return array.reshape(seq_count, length, array.shape[1] // HD, HD)


def block_scores(query_block, key_seq, row_start, prefix_len, causal):
    score_scale = float(HD) ** (-0.5)
    scores = (
        jnp.einsum("qhd,khd->hqk", query_block, key_seq, preferred_element_type=jnp.float32)
        * score_scale
    )
    if causal:
        grid_shape = (query_block.shape[0], key_seq.shape[0])
        row_pos = row_start + lax.broadcasted_iota(jnp.int32, grid_shape, 0)
        col_pos = lax.broadcasted_iota(jnp.int32, grid_shape, 1)
        allowed = (col_pos <= row_pos) | (col_pos < prefix_len)
        scores = jnp.where(allowed[None], scores, MASKED)
    return scores


def attention_forward(queries, keys, values, limits, causal, query_offset):
    length = queries.shape[1]
    block_rows = min(512, length)

    def one_sequence(seq_items):
        query_seq, key_seq, value_seq, prefix_len = seq_items
        contexts = []
        sums_log = []
        for number in range(length // block_rows):
            row_start = number * block_rows
            scores = block_scores(
                query_seq[row_start : row_start + block_rows],
                key_seq,
                query_offset + row_start,
                prefix_len,
                causal,
            )
            row_peak = jnp.max(scores, axis=-1, keepdims=True)
            exponent = jnp.exp(scores - row_peak)
            row_total = jnp.sum(exponent, axis=-1, keepdims=True)
            weights_low = (exponent / row_total).astype(jnp.bfloat16)
            context = jnp.einsum(
                "hqk,khd->qhd", weights_low, value_seq, preferred_element_type=jnp.float32
            )
            contexts.append(context.astype(jnp.bfloat16))
            sums_log.append((row_peak + jnp.log(row_total))[..., 0])
        return (jnp.concatenate(contexts, axis=0), jnp.concatenate(sums_log, axis=1))

    return lax.map(one_sequence, (queries, keys, values, limits))


def attention_backward(queries, keys, values, logsums, grad_context, limits, causal, query_offset):
    length = queries.shape[1]
    block_rows = min(512, length)
    score_scale = float(HD) ** (-0.5)

    def one_sequence(seq_items):
        query_seq, key_seq, value_seq, logsum_seq, grad_seq, prefix_len = seq_items
        grad_keys = jnp.zeros(key_seq.shape, jnp.float32)
        grad_values = jnp.zeros(value_seq.shape, jnp.float32)
        grad_queries = []
        for number in range(length // block_rows):
            row_start = number * block_rows
            query_block = query_seq[row_start : row_start + block_rows]
            grad_block = grad_seq[row_start : row_start + block_rows]
            scores = block_scores(
                query_block, key_seq, query_offset + row_start, prefix_len, causal
            )
            weights_soft = jnp.exp(scores - logsum_seq[:, row_start : row_start + block_rows, None])
            grad_weights = jnp.einsum(
                "qhd,khd->hqk", grad_block, value_seq, preferred_element_type=jnp.float32
            )
            row_delta = jnp.sum(weights_soft * grad_weights, axis=-1, keepdims=True)
            grad_scores = (weights_soft * (grad_weights - row_delta)).astype(jnp.bfloat16)
            grad_queries.append(
                jnp.einsum("hqk,khd->qhd", grad_scores, key_seq, preferred_element_type=jnp.float32)
                * score_scale
            )
            grad_keys = (
                grad_keys
                + jnp.einsum(
                    "hqk,qhd->khd", grad_scores, query_block, preferred_element_type=jnp.float32
                )
                * score_scale
            )
            grad_values = grad_values + jnp.einsum(
                "hqk,qhd->khd",
                weights_soft.astype(jnp.bfloat16),
                grad_block,
                preferred_element_type=jnp.float32,
            )
        joined_queries = jnp.concatenate(grad_queries, axis=0)
        return (
            joined_queries.astype(jnp.bfloat16),
            grad_keys.astype(jnp.bfloat16),
            grad_values.astype(jnp.bfloat16),
        )

    return lax.map(one_sequence, (queries, keys, values, logsums, grad_context, limits))


def on_device(
    inputs,
    memory,
    prefix,
    self_query,
    self_query_bias,
    self_key,
    self_value,
    self_value_bias,
    self_out,
    self_out_bias,
    self_norm_gain,
    self_norm_bias,
    cross_query,
    cross_query_bias,
    cross_key,
    cross_value,
    cross_value_bias,
    cross_out,
    cross_out_bias,
    cross_norm_gain,
    cross_norm_bias,
    feed_in,
    feed_in_bias,
    feed_out,
    feed_out_bias,
    feed_norm_gain,
    feed_norm_bias,
    cotangent,
):
    gathered_weights = (
        lax.all_gather(self_query, "dp", axis=0, tiled=True),
        lax.all_gather(self_key, "dp", axis=0, tiled=True),
        lax.all_gather(self_value, "dp", axis=0, tiled=True),
        lax.all_gather(self_out, "dp", axis=1, tiled=True),
        lax.all_gather(cross_query, "dp", axis=0, tiled=True),
        lax.all_gather(cross_key, "dp", axis=0, tiled=True),
        lax.all_gather(cross_value, "dp", axis=0, tiled=True),
        lax.all_gather(cross_out, "dp", axis=1, tiled=True),
        lax.all_gather(feed_in, "dp", axis=0, tiled=True),
        lax.all_gather(feed_out, "dp", axis=1, tiled=True),
    )
    (
        query_self,
        key_self,
        value_self,
        out_self,
        query_cross,
        key_cross,
        value_cross,
        out_cross,
        hidden_in,
        hidden_out,
    ) = gathered_weights
    memory_all = lax.all_gather(memory, "tensor", axis=0, tiled=True)
    seq_count = prefix.shape[0]
    no_prefix = jnp.zeros_like(prefix)
    tokens_all = gather_rows(inputs)
    query_one = project(tokens_all, query_self, self_query_bias)
    key_one = jnp.dot(tokens_all, key_self, preferred_element_type=jnp.float32).astype(jnp.bfloat16)
    value_one = project(tokens_all, value_self, self_value_bias)
    query_heads_one = split_heads(query_one, seq_count, LEN)
    key_heads_one = split_heads(key_one, seq_count, LEN)
    value_heads_one = split_heads(value_one, seq_count, LEN)
    context_one, logsum_one = attention_forward(
        query_heads_one, key_heads_one, value_heads_one, prefix, True, 0
    )
    context_one = context_one.reshape(query_one.shape)
    branch_one = reduce_rows(((context_one, out_self),), False) + self_out_bias.astype(jnp.float32)
    first_out, normed_one, inverse_one = norm_forward(
        inputs.astype(jnp.float32) + branch_one, self_norm_gain, self_norm_bias
    )
    first_low = first_out.astype(jnp.bfloat16)
    first_all = gather_rows(first_low)
    query_two = project(first_all, query_cross, cross_query_bias)
    key_two = jnp.dot(memory_all, key_cross, preferred_element_type=jnp.float32).astype(
        jnp.bfloat16
    )
    value_two = project(memory_all, value_cross, cross_value_bias)
    query_heads_two = split_heads(query_two, seq_count, LEN)
    key_heads_two = split_heads(key_two, seq_count, MEM)
    value_heads_two = split_heads(value_two, seq_count, MEM)
    context_two, logsum_two = attention_forward(
        query_heads_two, key_heads_two, value_heads_two, no_prefix, False, 0
    )
    context_two = context_two.reshape(query_two.shape)
    branch_two = reduce_rows(((context_two, out_cross),), False) + cross_out_bias.astype(
        jnp.float32
    )
    second_out, normed_two, inverse_two = norm_forward(
        first_out + branch_two, cross_norm_gain, cross_norm_bias
    )
    second_low = second_out.astype(jnp.bfloat16)
    second_all = gather_rows(second_low)
    hidden = jnp.dot(
        second_all, hidden_in, preferred_element_type=jnp.float32
    ) + feed_in_bias.astype(jnp.float32)
    active = jax.nn.silu(hidden).astype(jnp.bfloat16)
    branch_three = reduce_rows(((active, hidden_out),), False) + feed_out_bias.astype(jnp.float32)
    result_rows, normed_three, inverse_three = norm_forward(
        second_out + branch_three, feed_norm_gain, feed_norm_bias
    )
    tokens_back = gather_rows(inputs)
    first_back = gather_rows(first_low)
    second_back = gather_rows(second_low)
    du_three, grad_feed_norm_gain, grad_feed_norm_bias = norm_backward(
        cotangent.astype(jnp.float32), normed_three, inverse_three, feed_norm_gain
    )
    dbranch_three = du_three.astype(jnp.bfloat16)
    dbranch_three_all = gather_rows(dbranch_three)
    grad_feed_out_full = transposed_times(active, dbranch_three_all)
    dactive = multiply(dbranch_three_all, hidden_out, True)
    sigmoid_hidden = jax.nn.sigmoid(hidden)
    dhidden = (dactive * sigmoid_hidden * (1.0 + hidden * (1.0 - sigmoid_hidden))).astype(
        jnp.bfloat16
    )
    grad_feed_in_full = transposed_times(second_back, dhidden)
    dsecond = du_three + reduce_rows(((dhidden, hidden_in),), True)
    du_two, grad_cross_norm_gain, grad_cross_norm_bias = norm_backward(
        dsecond, normed_two, inverse_two, cross_norm_gain
    )
    dbranch_two = du_two.astype(jnp.bfloat16)
    dbranch_two_all = gather_rows(dbranch_two)
    dcontext_two = multiply(dbranch_two_all, out_cross, True).astype(jnp.bfloat16)
    grad_cross_out_full = transposed_times(context_two, dbranch_two_all)
    dquery_two, dkey_two, dvalue_two = attention_backward(
        query_heads_two,
        key_heads_two,
        value_heads_two,
        logsum_two,
        split_heads(dcontext_two, seq_count, LEN),
        no_prefix,
        False,
        0,
    )
    dquery_two = dquery_two.reshape(query_two.shape)
    dkey_two = dkey_two.reshape(key_two.shape)
    dvalue_two = dvalue_two.reshape(value_two.shape)
    grad_cross_query_full = transposed_times(first_back, dquery_two)
    grad_cross_key_full = transposed_times(memory_all, dkey_two)
    grad_cross_value_full = transposed_times(memory_all, dvalue_two)
    row_count = memory.shape[0] * lax.axis_size("tensor")
    key_part = multiply(lax.slice_in_dim(dkey_two, 0, row_count, axis=0), key_cross, True)
    value_part = multiply(lax.slice_in_dim(dvalue_two, 0, row_count, axis=0), value_cross, True)
    grad_memory = lax.psum_scatter(
        (key_part + value_part).astype(jnp.bfloat16), "tensor", scatter_dimension=0, tiled=True
    ).astype(jnp.float32)
    dfirst = du_two + reduce_rows(((dquery_two, query_cross),), True)
    du_one, grad_self_norm_gain, grad_self_norm_bias = norm_backward(
        dfirst, normed_one, inverse_one, self_norm_gain
    )
    dbranch_one = du_one.astype(jnp.bfloat16)
    dbranch_one_all = gather_rows(dbranch_one)
    dcontext_one = multiply(dbranch_one_all, out_self, True).astype(jnp.bfloat16)
    grad_self_out_full = transposed_times(context_one, dbranch_one_all)
    dquery_one, dkey_one, dvalue_one = attention_backward(
        query_heads_one,
        key_heads_one,
        value_heads_one,
        logsum_one,
        split_heads(dcontext_one, seq_count, LEN),
        prefix,
        True,
        0,
    )
    dquery_one = dquery_one.reshape(query_one.shape)
    dkey_one = dkey_one.reshape(key_one.shape)
    dvalue_one = dvalue_one.reshape(value_one.shape)
    grad_self_query_full = transposed_times(tokens_back, dquery_one)
    grad_self_key_full = transposed_times(tokens_back, dkey_one)
    grad_self_value_full = transposed_times(tokens_back, dvalue_one)
    grad_inputs = du_one + reduce_rows(
        ((dquery_one, query_self), (dkey_one, key_self), (dvalue_one, value_self)), True
    )
    bias_query_one = jnp.sum(dquery_one.astype(jnp.float32), axis=0)
    bias_value_one = jnp.sum(dvalue_one.astype(jnp.float32), axis=0)
    bias_query_two = jnp.sum(dquery_two.astype(jnp.float32), axis=0)
    bias_value_two = jnp.sum(dvalue_two.astype(jnp.float32), axis=0)
    bias_hidden = jnp.sum(dhidden.astype(jnp.float32), axis=0)
    weight_sums = (
        lax.psum_scatter(
            grad_self_query_full.astype(jnp.bfloat16), "dp", scatter_dimension=0, tiled=True
        ).astype(jnp.float32),
        lax.psum_scatter(
            grad_self_key_full.astype(jnp.bfloat16), "dp", scatter_dimension=0, tiled=True
        ).astype(jnp.float32),
        lax.psum_scatter(
            grad_self_value_full.astype(jnp.bfloat16), "dp", scatter_dimension=0, tiled=True
        ).astype(jnp.float32),
        lax.psum_scatter(
            grad_self_out_full.astype(jnp.bfloat16), "dp", scatter_dimension=1, tiled=True
        ).astype(jnp.float32),
        lax.psum_scatter(
            grad_cross_query_full.astype(jnp.bfloat16), "dp", scatter_dimension=0, tiled=True
        ).astype(jnp.float32),
        lax.psum_scatter(
            grad_cross_key_full.astype(jnp.bfloat16), "dp", scatter_dimension=0, tiled=True
        ).astype(jnp.float32),
        lax.psum_scatter(
            grad_cross_value_full.astype(jnp.bfloat16), "dp", scatter_dimension=0, tiled=True
        ).astype(jnp.float32),
        lax.psum_scatter(
            grad_cross_out_full.astype(jnp.bfloat16), "dp", scatter_dimension=1, tiled=True
        ).astype(jnp.float32),
        lax.psum_scatter(
            grad_feed_in_full.astype(jnp.bfloat16), "dp", scatter_dimension=0, tiled=True
        ).astype(jnp.float32),
        lax.psum_scatter(
            grad_feed_out_full.astype(jnp.bfloat16), "dp", scatter_dimension=1, tiled=True
        ).astype(jnp.float32),
    )
    (
        grad_self_query,
        grad_self_key,
        grad_self_value,
        grad_self_out,
        grad_cross_query,
        grad_cross_key,
        grad_cross_value,
        grad_cross_out,
        grad_feed_in,
        grad_feed_out,
    ) = weight_sums
    bias_out_one = jnp.sum(dbranch_one.astype(jnp.float32), axis=0)
    bias_out_two = jnp.sum(dbranch_two.astype(jnp.float32), axis=0)
    bias_out_three = jnp.sum(dbranch_three.astype(jnp.float32), axis=0)
    head_sums = lax.psum(
        (bias_query_one, bias_value_one, bias_query_two, bias_value_two, bias_hidden), "dp"
    )
    vector_sums = lax.psum(
        (
            bias_out_one,
            grad_self_norm_gain,
            grad_self_norm_bias,
            bias_out_two,
            grad_cross_norm_gain,
            grad_cross_norm_bias,
            bias_out_three,
            grad_feed_norm_gain,
            grad_feed_norm_bias,
        ),
        ("dp", "tensor"),
    )
    (
        grad_self_query_bias,
        grad_self_value_bias,
        grad_cross_query_bias,
        grad_cross_value_bias,
        grad_feed_in_bias,
    ) = head_sums
    (
        grad_self_out_bias,
        grad_self_norm_gain,
        grad_self_norm_bias,
        grad_cross_out_bias,
        grad_cross_norm_gain,
        grad_cross_norm_bias,
        grad_feed_out_bias,
        grad_feed_norm_gain,
        grad_feed_norm_bias,
    ) = vector_sums
    return (
        result_rows.astype(jnp.bfloat16),
        grad_inputs,
        grad_memory,
        grad_self_query,
        grad_self_query_bias,
        grad_self_key,
        grad_self_value,
        grad_self_value_bias,
        grad_self_out,
        grad_self_out_bias,
        grad_self_norm_gain,
        grad_self_norm_bias,
        grad_cross_query,
        grad_cross_query_bias,
        grad_cross_key,
        grad_cross_value,
        grad_cross_value_bias,
        grad_cross_out,
        grad_cross_out_bias,
        grad_cross_norm_gain,
        grad_cross_norm_bias,
        grad_feed_in,
        grad_feed_in_bias,
        grad_feed_out,
        grad_feed_out_bias,
        grad_feed_norm_gain,
        grad_feed_norm_bias,
    )


def solution(mesh):
    placed = (
        P(("dp", "tensor"), None),
        P(("dp", "tensor"), None),
        P("dp"),
        P("dp", "tensor"),
        P("tensor"),
        P("dp", "tensor"),
        P("dp", "tensor"),
        P("tensor"),
        P("tensor", "dp"),
        P(),
        P(),
        P(),
        P("dp", "tensor"),
        P("tensor"),
        P("dp", "tensor"),
        P("dp", "tensor"),
        P("tensor"),
        P("tensor", "dp"),
        P(),
        P(),
        P(),
        P("dp", "tensor"),
        P("tensor"),
        P("tensor", "dp"),
        P(),
        P(),
        P(),
        P(("dp", "tensor"), None),
    )
    return jax.shard_map(
        on_device,
        mesh=mesh,
        in_specs=placed,
        out_specs=(
            P(("dp", "tensor"), None),
            P(("dp", "tensor"), None),
            P(("dp", "tensor"), None),
            P("dp", "tensor"),
            P("tensor"),
            P("dp", "tensor"),
            P("dp", "tensor"),
            P("tensor"),
            P("tensor", "dp"),
            P(),
            P(),
            P(),
            P("dp", "tensor"),
            P("tensor"),
            P("dp", "tensor"),
            P("dp", "tensor"),
            P("tensor"),
            P("tensor", "dp"),
            P(),
            P(),
            P(),
            P("dp", "tensor"),
            P("tensor"),
            P("tensor", "dp"),
            P(),
            P(),
            P(),
        ),
        check_vma=False,
    )
```

profile of v0, /device:TPU:0, one launch (start us, length us, event | category | flops | bytes accessed | tf_op | source)
XLA Modules:
  0.0 1271.2 jit_solution(2678206188674772404)
XLA Ops:
  9.3 10.8 all_gather.56
  20.1 9.0 all_gather.57
  29.1 8.4 all_gather.55
  37.5 9.3 all_gather.58
  46.8 11.4 all-gather.7.cloned.1.call-done
  66.7 3.5 copy.136
  72.2 19.2 %while.52 = (s32[]{:T(128)}, bf16[2,1024,2,64]{1,3,2,0:T(8,128)(2,1)S(1)}, f32[2,2,1024]{2,1,0:T(2,128)S(1)}, bf16[2,1024,2,64]{1,3,2,0:T(8,128)(2,1)}, s32[2]{0...) while((s32[]{:T(128)}, ...), condition=%wide.region_5.6_spmd, body=%wide.region_0.5_spmd.sunk | while | flops 564790784 | bytes 33645236 | solution.py:126
  95.8 75.5 %reduce-scatter.28.cloned.1.call-done = f32[512,512]{1,0:T(8,128)} async-done(((f32[2048,512]{1,0:T(8,128)}), f32[512,512]{1,0:T(8,128)}) %reduce-scatter.28.cloned.1.call-update) | async-done | bytes 1048592 | tf_op jit(solution)/shard_map/reduce_scatter | solution.py:46
  174.2 9.2 all_gather.60
  183.3 23.3 %all_gather.59 = bf16[512,512]{1,0:T(8,128)(2,1)S(1)} all-gather(bf16[128,512]{1,0:T(8,128)(2,1)S(1)} %copy-done.49), channel_id=1, replica_groups=mesh['dp'=8,'tensor'=4] {'tensor'}, dimensions={0}, use_global_device_ids=true | all-gather | bytes 655360 | tf_op jit(solution)/shard_map/all_gather | solution.py:233
  207.2 9.2 all_gather.63
  217.0 8.2 all_gather.62
  225.3 10.1 all_gather.64
  239.0 3.6 while.53
  248.5 74.5 %reduce-scatter.30.cloned.1.call-done = f32[512,512]{1,0:T(8,128)} async-done(((f32[2048,512]{1,0:T(8,128)}), f32[512,512]{1,0:T(8,128)}) %reduce-scatter.30.cloned.1.call-update) | async-done | bytes 1048592 | tf_op jit(solution)/shard_map/reduce_scatter | solution.py:46
  328.2 11.7 all_gather.66
  339.9 10.8 all_gather.67
  350.7 22.8 %all-gather.11.cloned.1.call-done = bf16[2048,512]{1,0:T(8,128)(2,1)} async-done(((bf16[512,512]{1,0:T(8,128)(2,1)}), bf16[2048,512]{1,0:T(8,128)(2,1)}) %all-gather.11.cloned.1.call-update) | async-done | bytes 2097168 | tf_op jit(solution)/shard_map/all_gather | solution.py:30
  373.5 5.5 multiply_convert_fusion.5
  386.4 72.9 %reduce-scatter.32.cloned.1.call-done = f32[512,512]{1,0:T(8,128)} async-done(((f32[2048,512]{1,0:T(8,128)}), f32[512,512]{1,0:T(8,128)}) %reduce-scatter.32.cloned.1.call-update) | async-done | bytes 1048592 | tf_op jit(solution)/shard_map/reduce_scatter | solution.py:46
  464.3 46.6 %all-gather.13.cloned.1.call-done = bf16[2048,512]{1,0:T(8,128)(2,1)} async-done(((bf16[512,512]{1,0:T(8,128)(2,1)}), bf16[2048,512]{1,0:T(8,128)(2,1)}) %all-gather.13.cloned.1.call-update) | async-done | bytes 2097168 | tf_op jit(solution)/shard_map/all_gather | solution.py:30
  510.8 6.1 convert_reduce_fusion
  522.9 74.3 %reduce-scatter.34.cloned.1.call-done = f32[512,512]{1,0:T(8,128)} async-done(((f32[2048,512]{1,0:T(8,128)}), f32[512,512]{1,0:T(8,128)}) %reduce-scatter.34.cloned.1.call-update) | async-done | bytes 1048592 | tf_op jit(solution)/shard_map/reduce_scatter | solution.py:46
  597.2 3.7 multiply_reduce_fusion.4
  603.2 46.5 %all-gather.15.cloned.1.call-done = bf16[2048,512]{1,0:T(8,128)(2,1)} async-done(((bf16[512,512]{1,0:T(8,128)(2,1)}), bf16[2048,512]{1,0:T(8,128)(2,1)}) %all-gather.15.cloned.1.call-update) | async-done | bytes 2097168 | tf_op jit(solution)/shard_map/all_gather | solution.py:30
  655.8 8.4 while.54
  665.8 3.7 fusion.188
  670.0 75.2 %reduce-scatter.36.cloned.1.call-done = f32[512,512]{1,0:T(8,128)} async-done(((f32[2048,512]{1,0:T(8,128)}), f32[512,512]{1,0:T(8,128)}) %reduce-scatter.36.cloned.1.call-update) | async-done | bytes 1048592 | tf_op jit(solution)/shard_map/reduce_scatter | solution.py:46
  748.6 4.4 convolution_convert_fusion.5
  753.1 3.7 convolution_convert_fusion.6
  764.1 3.4 convolution_convert_fusion.7
  771.6 23.7 %all-gather.17.cloned.1.call-done = bf16[2048,512]{1,0:T(8,128)(2,1)} async-done(((bf16[512,512]{1,0:T(8,128)(2,1)}), bf16[2048,512]{1,0:T(8,128)(2,1)}) %all-gather.17.cloned.1.call-update) | async-done | bytes 2097168 | tf_op jit(solution)/shard_map/all_gather | solution.py:30
  800.6 32.5 %while.55 = (s32[]{:T(128)}, bf16[2,1024,2,64]{1,3,2,0:T(8,128)(2,1)}, bf16[2,1024,2,64]{1,3,2,0:T(8,128)(2,1)}, bf16[2,1024,2,64]{1,3,2,0:T(8,128)(2,1)S(1)}, b...) while((s32[]{:T(128)}, ...), condition=%wide.region_36.37_spmd, body=%wide.region_33.36_spmd.sunk | while | flops 1377172992 | bytes 73225920 | solution.py:176
  843.1 3.9 fusion.190
  847.1 3.8 fusion.189
  852.6 6.3 add_add_fusion
  860.8 8.3 reduce-scatter.48.cloned.1.call-done
  870.9 34.6 %reduce-scatter.58.cloned.1.call-done = bf16[64,128]{1,0:T(8,128)(2,1)} async-done(((bf16[512,128]{1,0:T(8,128)(2,1)}), bf16[64,128]{1,0:T(8,128)(2,1)}) %reduce-scatter.58.cloned.1.call-update) | async-done | bytes 16400
  907.1 34.7 %reduce-scatter.60.cloned.1.call-done = bf16[64,128]{1,0:T(8,128)(2,1)} async-done(((bf16[512,128]{1,0:T(8,128)(2,1)}), bf16[64,128]{1,0:T(8,128)(2,1)}) %reduce-scatter.60.cloned.1.call-update) | async-done | bytes 16400
  943.3 35.0 %reduce-scatter.46.cloned.1.call-done = bf16[128,64]{0,1:T(8,128)(2,1)} async-done(((bf16[128,512]{0,1:T(8,128)(2,1)}), bf16[128,64]{0,1:T(8,128)(2,1)}) %reduce-scatter.46.cloned.1.call-update) | async-done | bytes 16400 | tf_op jit(solution)/shard_map/reduce_scatter | solution.py:380
  979.6 34.9 %reduce-scatter.44.cloned.1.call-done = bf16[64,128]{1,0:T(8,128)(2,1)} async-done(((bf16[512,128]{1,0:T(8,128)(2,1)}), bf16[64,128]{1,0:T(8,128)(2,1)}) %reduce-scatter.44.cloned.1.call-update) | async-done | bytes 16400 | tf_op jit(solution)/shard_map/reduce_scatter | solution.py:371
  1015.9 22.6 %reduce-scatter.40.cloned.1.call-done = bf16[128,512]{1,0:T(8,128)(2,1)} async-done(((bf16[512,512]{1,0:T(8,128)(2,1)}), bf16[128,512]{1,0:T(8,128)(2,1)}) %reduce-scatter.40.cloned.1.call-update) | async-done | bytes 131088 | tf_op jit(solution)/shard_map/reduce_scatter | solution.py:323
  1040.1 39.1 %all-reduce = (f32[512]{0:T(512)}, f32[512]{0:T(512)}, f32[512]{0:T(512)}, f32[512]{0:T(512)}, f32[512]{0:T(512)}, /*index=5*/f32[512]{0:T(512)}, f32[512]{0:T(512)}, f32[512]{0:T(512)}, f32[512]{0:T(512)}) all-reduce(f32[512]{0:T(512)S(1)} %get-tuple-element.483, ...), channel_id=1, replica_groups=mesh['dp'=8,'tensor'=4] {'dp','tensor'}, use_global_device_ids=true, to_apply=%region_48.49 | all-reduce | flops 4608 | bytes 36864 | tf_op jit(solution)/shard_map/psum | solution.py:408
  1080.8 13.6 %all-reduce.1 = (f32[128]{0:T(128)}, f32[128]{0:T(128)}, f32[128]{0:T(128)}, f32[128]{0:T(128)}, f32[512]{0:T(512)}) all-reduce(f32[128]{0:T(128)S(1)} %reduce_sum.327, f32[128]{0:T(128)S(1)} %reduce_sum.329, f32[128]{0:T(128)S(1)} %reduce_sum.334, f32[128]{0:T(128)S(1)} %reduce_sum.336, ...), channel_id=1, replica_groups=mesh['dp'=8,'tensor'=4] {'dp'}, use_global_device_ids=true, to_apply=%region_41.42 | all-reduce | flops 1024 | bytes 8192 | tf_op jit(solution)/shard_map/psum | solution.py:405
  1096.0 13.8 %reduce-scatter.54.cloned.1.call-done = bf16[64,128]{1,0:T(8,128)(2,1)} async-done(((bf16[512,128]{1,0:T(8,128)(2,1)}), bf16[64,128]{1,0:T(8,128)(2,1)}) %reduce-scatter.54.cloned.1.call-update) | async-done | bytes 16400
  1111.3 35.1 %reduce-scatter.56.cloned.1.call-done = bf16[64,128]{1,0:T(8,128)(2,1)} async-done(((bf16[512,128]{1,0:T(8,128)(2,1)}), bf16[64,128]{1,0:T(8,128)(2,1)}) %reduce-scatter.56.cloned.1.call-update) | async-done | bytes 16400
  1148.0 34.8 %reduce-scatter.42.cloned.1.call-done = bf16[128,64]{0,1:T(8,128)(2,1)} async-done(((bf16[128,512]{0,1:T(8,128)(2,1)}), bf16[128,64]{0,1:T(8,128)(2,1)}) %reduce-scatter.42.cloned.1.call-update) | async-done | bytes 16400 | tf_op jit(solution)/shard_map/reduce_scatter | solution.py:368
  1184.2 77.9 %reduce-scatter.38.cloned.1.call-done = f32[512,512]{1,0:T(8,128)} async-done(((f32[2048,512]{1,0:T(8,128)}), f32[512,512]{1,0:T(8,128)}) %reduce-scatter.38.cloned.1.call-update) | async-done | bytes 1048592 | tf_op jit(solution)/shard_map/reduce_scatter | solution.py:46
  (483 shorter events, 178.9 us)
Async XLA Ops:
  7.2 51.1 %all-gather.7.cloned.1.call-start = ((), (), s32[]{:S(2)}) async-start(), calls=%async_computation.17 | async-start | bytes 2621440 | tf_op jit(solution)/shard_map/all_gather | solution.py:30
  7.9 163.3 %reduce-scatter.28.cloned.1.call-start = ((), (), s32[]{:S(2)}) async-start(), calls=%async_computation.18 | async-start | bytes 5242880 | tf_op jit(solution)/shard_map/reduce_scatter | solution.py:46
  29.1 41.1 %copy-start.38 = (bf16[512,128]{1,0:T(8,128)(2,1)}, bf16[512,128]{1,0:T(8,128)(2,1)S(1)}, u32[]{:S(2)}) copy-start(bf16[512,128]{1,0:T(8,128)(2,1)S(1)} %all_gather.57) | copy-start | bytes 393220
  46.8 45.2 %copy-start.40 = (bf16[128,512]{0,1:T(8,128)(2,1)}, bf16[128,512]{0,1:T(8,128)(2,1)S(1)}, u32[]{:S(2)}) copy-start(bf16[128,512]{0,1:T(8,128)(2,1)S(1)} %all_gather.58) | copy-start | bytes 393220
  92.9 78.3 %copy-start.26 = (bf16[512,512]{1,0:T(8,128)(2,1)S(1)}, bf16[512,512]{1,0:T(8,128)(2,1)}, u32[]{:S(2)}) copy-start(bf16[512,512]{1,0:T(8,128)(2,1)} %param.36) | copy-start | bytes 1572868
  95.6 78.5 %copy-start.88 = (bf16[128]{0:T(256)(128)(2,1)S(1)}, bf16[128]{0:T(256)(128)(2,1)}, u32[]{:S(2)}) copy-start(bf16[128]{0:T(256)(128)(2,1)} %param.49) | copy-start | bytes 772
  95.6 78.5 %copy-start.89 = (bf16[128]{0:T(256)(128)(2,1)S(1)}, bf16[128]{0:T(256)(128)(2,1)}, u32[]{:S(2)}) copy-start(bf16[128]{0:T(256)(128)(2,1)} %param.52) | copy-start | bytes 772
  95.6 78.6 %copy-start.71 = (bf16[64,128]{1,0:T(8,128)(2,1)S(1)}, bf16[64,128]{1,0:T(8,128)(2,1)}, u32[]{:S(2)}) copy-start(bf16[64,128]{1,0:T(8,128)(2,1)} %param.51) | copy-start | bytes 49156
  95.6 87.8 %copy-start.49 = (bf16[128,512]{1,0:T(8,128)(2,1)S(1)}, bf16[128,512]{1,0:T(8,128)(2,1)}, u32[]{:S(2)}) copy-start(bf16[128,512]{1,0:T(8,128)(2,1)} %param.37) | copy-start | bytes 393220
  95.6 111.6 %copy-start.72 = (bf16[64,128]{1,0:T(8,128)(2,1)S(1)}, bf16[64,128]{1,0:T(8,128)(2,1)}, u32[]{:S(2)}) copy-start(bf16[64,128]{1,0:T(8,128)(2,1)} %param.50) | copy-start | bytes 49156
  95.6 139.8 %all-gather.9.cloned.1.call-start = ((), (), s32[]{:S(2)}) async-start(), calls=%async_computation.19 | async-start | bytes 2621440 | tf_op jit(solution)/shard_map/all_gather | solution.py:30
  95.7 110.9 %copy-start.56 = (f32[512]{0:T(512)}, f32[512]{0:T(512)S(1)}, u32[]{:S(2)}) copy-start(f32[512]{0:T(512)S(1)} %convert_element_type.315) | copy-start | bytes 6148
  95.7 110.9 %copy-start.67 = (f32[512]{0:T(512)}, f32[512]{0:T(512)S(1)}, u32[]{:S(2)}) copy-start(f32[512]{0:T(512)S(1)} %convert_element_type.316) | copy-start | bytes 6148
  172.7 44.3 %copy-start.73 = (bf16[64,128]{1,0:T(8,128)(2,1)S(1)}, bf16[64,128]{1,0:T(8,128)(2,1)}, u32[]{:S(2)}) copy-start(bf16[64,128]{1,0:T(8,128)(2,1)} %param.48) | copy-start | bytes 49156
  172.7 52.6 %copy-start.74 = (bf16[128,64]{0,1:T(8,128)(2,1)S(1)}, bf16[128,64]{0,1:T(8,128)(2,1)}, u32[]{:S(2)}) copy-start(bf16[128,64]{0,1:T(8,128)(2,1)} %param.53) | copy-start | bytes 49156
  174.0 149.0 %reduce-scatter.30.cloned.1.call-start = ((), (), s32[]{:S(2)}) async-start(), calls=%async_computation.20 | async-start | bytes 5242880 | tf_op jit(solution)/shard_map/reduce_scatter | solution.py:46
  246.7 126.8 %all-gather.11.cloned.1.call-start = ((), (), s32[]{:S(2)}) async-start(), calls=%async_computation.21 | async-start | bytes 2621440 | tf_op jit(solution)/shard_map/all_gather | solution.py:30
  326.9 132.4 %reduce-scatter.32.cloned.1.call-start = ((), (), s32[]{:S(2)}) async-start(), calls=%async_computation.22 | async-start | bytes 5242880 | tf_op jit(solution)/shard_map/reduce_scatter | solution.py:46
  383.7 127.2 %all-gather.13.cloned.1.call-start = ((), (), s32[]{:S(2)}) async-start(), calls=%async_computation.23 | async-start | bytes 2621440 | tf_op jit(solution)/shard_map/all_gather | solution.py:30
  464.2 133.0 %reduce-scatter.34.cloned.1.call-start = ((), (), s32[]{:S(2)}) async-start(), calls=%async_computation.24 | async-start | bytes 5242880 | tf_op jit(solution)/shard_map/reduce_scatter | solution.py:46
  521.6 128.1 %all-gather.15.cloned.1.call-start = ((), (), s32[]{:S(2)}) async-start(), calls=%async_computation.25 | async-start | bytes 2621440 | tf_op jit(solution)/shard_map/all_gather | solution.py:30
  603.1 142.0 %reduce-scatter.36.cloned.1.call-start = ((), (), s32[]{:S(2)}) async-start(), calls=%async_computation.26 | async-start | bytes 5242880 | tf_op jit(solution)/shard_map/reduce_scatter | solution.py:46
  665.8 79.3 %copy-start.25 = (f32[512,512]{1,0:T(8,128)S(1)}, f32[512,512]{1,0:T(8,128)}, u32[]{:S(2)}) copy-start(f32[512,512]{1,0:T(8,128)} %get-tuple-element.482) | copy-start | bytes 3145732
  665.8 79.3 %copy-start.53 = (f32[512]{0:T(512)S(1)}, f32[512]{0:T(512)}, u32[]{:S(2)}) copy-start(f32[512]{0:T(512)} %copy-done.52) | copy-start | bytes 6148
  665.8 79.3 %copy-start.57 = (f32[512]{0:T(512)S(1)}, f32[512]{0:T(512)}, u32[]{:S(2)}) copy-start(f32[512]{0:T(512)} %copy-done.56) | copy-start | bytes 6148
  665.8 79.3 %copy-start.59 = (f32[512]{0:T(512)S(1)}, f32[512]{0:T(512)}, u32[]{:S(2)}) copy-start(f32[512]{0:T(512)} %copy-done.58) | copy-start | bytes 6148
  669.5 125.8 %all-gather.17.cloned.1.call-start = ((), (), s32[]{:S(2)}) async-start(), calls=%async_computation.27 | async-start | bytes 2621440 | tf_op jit(solution)/shard_map/all_gather | solution.py:30
  748.5 110.5 %reduce-scatter.50.cloned.1.call-start = ((), (), s32[]{:S(2)}) async-start(), calls=%async_computation.34 | async-start | bytes 589824 | tf_op jit(solution)/shard_map/reduce_scatter | solution.py:386
  753.0 116.0 %reduce-scatter.48.cloned.1.call-start = ((), (), s32[]{:S(2)}) async-start(), calls=%async_computation.33 | async-start | bytes 589824 | tf_op jit(solution)/shard_map/reduce_scatter | solution.py:383
  756.9 148.7 %reduce-scatter.58.cloned.1.call-start = ((), (), s32[]{:S(2)}) async-start(), calls=%async_computation.38 | async-start | bytes 147456
  761.4 180.4 %reduce-scatter.60.cloned.1.call-start = ((), (), s32[]{:S(2)}) async-start(), calls=%async_computation.39 | async-start | bytes 147456
  764.0 214.3 %reduce-scatter.46.cloned.1.call-start = ((), (), s32[]{:S(2)}) async-start(), calls=%async_computation.32 | async-start | bytes 147456 | tf_op jit(solution)/shard_map/reduce_scatter | solution.py:380
  767.5 247.1 %reduce-scatter.44.cloned.1.call-start = ((), (), s32[]{:S(2)}) async-start(), calls=%async_computation.31 | async-start | bytes 147456 | tf_op jit(solution)/shard_map/reduce_scatter | solution.py:371
  770.3 268.1 %reduce-scatter.40.cloned.1.call-start = ((), (), s32[]{:S(2)}) async-start(), calls=%async_computation.29 | async-start | bytes 655360 | tf_op jit(solution)/shard_map/reduce_scatter | solution.py:323
  771.5 322.9 %reduce-scatter.52.cloned.1.call-start = ((), (), s32[]{:S(2)}) async-start(), calls=%async_computation.35 | async-start | bytes 147456
  843.0 266.7 %reduce-scatter.54.cloned.1.call-start = ((), (), s32[]{:S(2)}) async-start(), calls=%async_computation.36 | async-start | bytes 147456
  847.0 299.5 %reduce-scatter.56.cloned.1.call-start = ((), (), s32[]{:S(2)}) async-start(), calls=%async_computation.37 | async-start | bytes 147456
  850.9 332.0 %reduce-scatter.42.cloned.1.call-start = ((), (), s32[]{:S(2)}) async-start(), calls=%async_computation.30 | async-start | bytes 147456 | tf_op jit(solution)/shard_map/reduce_scatter | solution.py:368
  852.6 409.5 %reduce-scatter.38.cloned.1.call-start = ((), (), s32[]{:S(2)}) async-start(), calls=%async_computation.28 | async-start | bytes 5242880 | tf_op jit(solution)/shard_map/reduce_scatter | solution.py:46
  858.9 181.2 %copy-start.75 = (f32[512]{0:T(512)S(1)}, f32[512]{0:T(512)}, u32[]{:S(2)}) copy-start(f32[512]{0:T(512)} %get-tuple-element.392) | copy-start | bytes 6148
  858.9 181.2 %copy-start.76 = (f32[512]{0:T(512)S(1)}, f32[512]{0:T(512)}, u32[]{:S(2)}) copy-start(f32[512]{0:T(512)} %get-tuple-element.399) | copy-start | bytes 6148
  858.9 181.2 %copy-start.77 = (f32[512]{0:T(512)S(1)}, f32[512]{0:T(512)}, u32[]{:S(2)}) copy-start(f32[512]{0:T(512)} %get-tuple-element.388) | copy-start | bytes 6148
  858.9 181.2 %copy-start.78 = (f32[512]{0:T(512)S(1)}, f32[512]{0:T(512)}, u32[]{:S(2)}) copy-start(f32[512]{0:T(512)} %get-tuple-element.396) | copy-start | bytes 6148
  859.0 181.2 %copy-start.79 = (f32[512]{0:T(512)S(1)}, f32[512]{0:T(512)}, u32[]{:S(2)}) copy-start(f32[512]{0:T(512)} %get-tuple-element.480) | copy-start | bytes 6148
  859.0 181.2 %copy-start.80 = (f32[512]{0:T(512)S(1)}, f32[512]{0:T(512)}, u32[]{:S(2)}) copy-start(f32[512]{0:T(512)} %get-tuple-element.478) | copy-start | bytes 6148
  859.0 220.3 %copy-start.21 = (bf16[2,1024,2,64]{1,3,2,0:T(8,128)(2,1)S(1)}, bf16[2,1024,2,64]{1,3,2,0:T(8,128)(2,1)}, u32[]{:S(2)}) copy-start(bf16[2,1024,2,64]{1,3,2,0:T(8,128)(2,1)} %copy-done.20) | copy-start | bytes 1572868
  859.0 221.8 %copy-start.81 = (f32[512]{0:T(512)S(1)}, f32[512]{0:T(512)}, u32[]{:S(2)}) copy-start(f32[512]{0:T(512)} %get-tuple-element.527) | copy-start | bytes 6148
  859.0 403.1 %copy-start.24 = (f32[512,512]{1,0:T(8,128)S(1)}, f32[512,512]{1,0:T(8,128)}, u32[]{:S(2)}) copy-start(f32[512,512]{1,0:T(8,128)} %get-tuple-element.485) | copy-start | bytes 3145732
  (72 other events, 483.5 us)
Sparse Core Ops, SparseCore 0:
  9.6 48.6 all-gather.6
  95.7 75.4 reduce-scatter.27
  174.2 54.7 all-gather.8
  246.8 76.1 reduce-scatter.29
  327.1 46.4 all-gather.10
  383.8 75.4 reduce-scatter.31
  464.3 46.4 all-gather.12
  521.7 75.4 reduce-scatter.33
  603.2 46.4 all-gather.14
  669.6 75.4 reduce-scatter.35
  748.6 46.6 all-gather.16
  798.6 33.1 reduce-scatter.49
  834.8 34.1 reduce-scatter.47
  872.1 33.3 reduce-scatter.57
  908.4 33.3 reduce-scatter.59
  944.9 33.3 reduce-scatter.45
  981.2 33.3 reduce-scatter.43
  1016.8 21.6 reduce-scatter.39
  1041.7 31.6 reduce-scatter.51
  1076.3 33.4 reduce-scatter.53
  1113.1 33.3 reduce-scatter.55
  1149.5 33.3 reduce-scatter.41
  1185.3 76.7 reduce-scatter.37
where the time goes:
time: 1280 us; the launch traced here: 1270 us
  waiting for transfers between devices  856 us (67%)
  blocking collectives  173 us (14%)
  matrix products  115 us (9%)
  other arithmetic  59 us (5%)
  local copies, waits for them, and re-layouts  50.4 us (4%)
  between operations  15.4 us (1%)
    reduce_scatter x6, waiting for transfers between devices, reduce_rows(): return lax.psum_scatter(running, 'tensor', scatter_dimension=0, tiled=True)  450 us
    all_gather x6, waiting for transfers between devices, gather_rows(): return lax.all_gather(block_rows, 'tensor', axis=0, tiled=True)  151 us
    unnamed x28, waiting for transfers between devices  119 us
    psum x1, blocking collectives, on_device(): lax.psum((bias_out_one, grad_self_norm_gain, grad_self_norm_bias, bias_ou...  39.1 us
    reduce_scatter x1, waiting for transfers between devices, on_device(): lax.psum_scatter(grad_cross_out_full.astype(jnp.bfloat16), 'dp', scatter_...  35 us
    reduce_scatter x1, waiting for transfers between devices, on_device(): lax.psum_scatter(grad_cross_query_full.astype(jnp.bfloat16), 'dp', scatte...  34.9 us
    reduce_scatter x1, waiting for transfers between devices, on_device(): lax.psum_scatter(grad_self_out_full.astype(jnp.bfloat16), 'dp', scatter_d...  34.8 us
    dot_general x10, matrix products, multiply(): lax.dot_general(left_side, right_side, (((1,), (1,)), ((), ())), preferre...  33.1 us
  transfers between devices with their start and end apart: 23, of which 20 were waited for; matrix products, arithmetic and copies ran while one was open for 9% of the time, Pallas kernels for 0%

commit v1 on v0

v1 whole, which is shorter than its diff:
```python
import functools

import jax
import jax.numpy as jnp
from jax import lax
from jax.experimental import pallas as pl
from jax.experimental.pallas import tpu as pltpu
from jax.sharding import PartitionSpec as P

HD = 64
LEN = 1024
MEM = 256
PAIR = 128
BLOCK = 256

EPSILON = 1e-05
MASKED = -1e30
SCALE = float(HD) ** (-0.5)

F32 = jnp.float32
BF16 = jnp.bfloat16
NN = (((1,), (0,)), ((), ()))
NT = (((1,), (1,)), ((), ()))
TN = (((0,), (0,)), ((), ()))
SMEM = pl.BlockSpec(memory_space=pltpu.SMEM)
ANY = pl.BlockSpec(memory_space=pl.ANY)
VMEM = pl.BlockSpec(memory_space=pltpu.VMEM)


def mm(left_side, right_side, dims):
    return lax.dot_general(left_side, right_side, dims, preferred_element_type=F32)


def shaped(shape, dtype):
    return jax.ShapeDtypeStruct(shape, dtype)


def cost(macs, moved):
    return pl.CostEstimate(flops=2 * macs, bytes_accessed=moved, transcendentals=0)


def limit(mebibytes):
    return pltpu.CompilerParams(vmem_limit_bytes=mebibytes << 20)


def swap(array, dp_mask, tensor_mask):
    nd, nt = lax.axis_size("dp"), lax.axis_size("tensor")
    pairs = [
        (d * nt + t, (d ^ dp_mask) * nt + (t ^ tensor_mask)) for d in range(nd) for t in range(nt)
    ]
    return lax.ppermute(array, ("dp", "tensor"), pairs)


def hand_over(array, parity, step):
    nd, nt = lax.axis_size("dp"), lax.axis_size("tensor")
    pairs = [(d * nt + t, d * nt + t + step) for d in range(nd) for t in range(parity, nt, 2)]
    return lax.ppermute(array, ("dp", "tensor"), pairs)


def tree_sum(terms):
    while len(terms) > 1:
        terms = [terms[i] + terms[i + 1] for i in range(0, len(terms), 2)]
    return terms[0]


def along_line(shard):
    return jnp.stack([shard] + [swap(shard, 0, k) for k in range(1, lax.axis_size("tensor"))])


def over_planes(line):
    planes = lax.axis_size("dp") // 2
    plane = jnp.stack([line] + [swap(line, 2 * j, 0) for j in range(1, planes)])
    return plane, swap(plane, 1, 0)


def gather_group(shard):
    return over_planes(along_line(shard))


def scatter_group(keep, send):
    nd, nt = lax.axis_size("dp"), lax.axis_size("tensor")
    chip = (keep.astype(F32) + swap(send, 1, 0).astype(F32)).astype(BF16)
    line = tree_sum(
        [chip[0].astype(F32)] + [swap(chip[j], 2 * j, 0).astype(F32) for j in range(1, nd // 2)]
    ).astype(BF16)
    return tree_sum([line[0].astype(F32)] + [swap(line[s], 0, s).astype(F32) for s in range(1, nt)])


def sum_everywhere(vector):
    nd, nt = lax.axis_size("dp"), lax.axis_size("tensor")
    vector = vector + swap(vector, 1, 0)
    vector = tree_sum([vector] + [swap(vector, 2 * j, 0) for j in range(1, nd // 2)])
    return tree_sum([vector] + [swap(vector, 0, s) for s in range(1, nt)])


def slot_blocks(info, planes, nt):
    for j in range(planes):
        for c in range(2):
            d = jnp.bitwise_xor(info[2], 2 * j + c)
            for s in range(nt):
                yield j, c, s, d, jnp.bitwise_xor(info[3], s)


def assemble_kernel(info, plane, sibling, whole):
    planes, nt, n, r, w = plane.shape
    for j, c, s, d, t in slot_blocks(info, planes, nt):
        rows = pl.ds(pl.multiple_of(d * r, r), r)
        columns = pl.ds(pl.multiple_of(t * w, w), w)
        for i in range(n):
            whole[i, rows, columns] = (plane, sibling)[c][j, s, i]


def aligned(r, w):
    return w % PAIR == 0 and r % 16 == 0


def assemble(info, plane, sibling):
    planes, nt, n, r, w = plane.shape
    nd = 2 * planes
    if aligned(r, w):
        return pl.pallas_call(
            assemble_kernel,
            out_shape=shaped((n, nd * r, nt * w), BF16),
            in_specs=[SMEM, VMEM, VMEM],
            out_specs=VMEM,
            compiler_params=limit(32),
            cost_estimate=cost(0, 4 * plane.size * 2),
        )(info, plane, sibling)
    full = jnp.stack([plane, sibling], axis=1).reshape(nd, nt, n, r, w)
    full = jnp.take(full, jnp.bitwise_xor(jnp.arange(nd), info[2]), axis=0)
    full = jnp.take(full, jnp.bitwise_xor(jnp.arange(nt), info[3]), axis=1)
    return full.transpose(2, 0, 3, 1, 4).reshape(n, nd * r, nt * w)


def disperse_kernel(info, whole, keep, send):
    planes, nt, n, r, w = keep.shape
    for j, c, s, d, t in slot_blocks(info, planes, nt):
        rows = pl.ds(pl.multiple_of(d * r, r), r)
        columns = pl.ds(pl.multiple_of(t * w, w), w)
        for i in range(n):
            (keep, send)[c][j, s, i] = whole[i, rows, columns]


def disperse(info, whole):
    nd, nt = lax.axis_size("dp"), lax.axis_size("tensor")
    n, r, w = whole.shape[0], whole.shape[1] // nd, whole.shape[2] // nt
    half = (nd // 2, nt, n, r, w)
    if aligned(r, w):
        return pl.pallas_call(
            disperse_kernel,
            out_shape=(shaped(half, BF16), shaped(half, BF16)),
            in_specs=[SMEM, VMEM],
            out_specs=(VMEM, VMEM),
            compiler_params=limit(32),
            cost_estimate=cost(0, 2 * whole.size * 2),
        )(info, whole)
    full = whole.reshape(n, nd, r, nt, w).transpose(1, 3, 0, 2, 4)
    full = jnp.take(full, jnp.bitwise_xor(jnp.arange(nd), info[2]), axis=0)
    full = jnp.take(full, jnp.bitwise_xor(jnp.arange(nt), info[3]), axis=1)
    full = full.reshape(nd // 2, 2, nt, n, r, w)
    return full[:, 0], full[:, 1]


def norm_forward(summed):
    row_mean = jnp.mean(summed, axis=-1, keepdims=True)
    centred = summed - row_mean
    variance = jnp.mean(centred * centred, axis=-1, keepdims=True)
    inverse = lax.rsqrt(variance + EPSILON)
    return centred * inverse, inverse


def norm_backward(grad_out, normed, inverse, norm_gain):
    grad_normed = grad_out * norm_gain
    return inverse * (
        grad_normed
        - jnp.mean(grad_normed, axis=-1, keepdims=True)
        - normed * jnp.mean(grad_normed * normed, axis=-1, keepdims=True)
    )


def column_sum(values):
    return jnp.sum(values.astype(F32), axis=0, keepdims=True)


def head_lanes(e):
    lane = lax.broadcasted_iota(jnp.int32, (1, PAIR), 1)
    chosen = (lane < HD) if e == 0 else (lane >= HD)
    return jnp.where(chosen, 1.0, 0.0)


def join_heads(first, second):
    lane = lax.broadcasted_iota(jnp.int32, first.shape, 1)
    return jnp.where(lane < HD, first, second)


def attend_forward(q, segments, contexts, inverses, lo):
    rows = slice(lo, lo + BLOCK)
    results = []
    for e in range(2):
        query = q[rows, :] * head_lanes(e).astype(BF16)
        scores = [edit(mm(query, k, NT)) for k, _, _, edit in segments]
        peak = functools.reduce(
            jnp.maximum, [jnp.max(piece, axis=-1, keepdims=True) for piece in scores]
        )
        total = None
        for piece, (_, v, store, _) in zip(scores, segments):
            weights = jnp.exp(piece - peak).astype(BF16)
            store(e, weights)
            wide = jnp.concatenate([v, jnp.ones(v.shape, BF16)], axis=1)
            part = mm(weights, wide, NN)
            total = part if total is None else total + part
        inverse = 1.0 / total[:, PAIR:]
        results.append((total[:, :PAIR] * inverse, inverse))
    contexts[rows, :] = join_heads(results[0][0], results[1][0]).astype(BF16)
    inverses[rows, :] = join_heads(results[0][1], results[1][1])


def attend_backward(q, grad, ctx, inv, segments, grad_query, lo):
    rows = slice(lo, lo + BLOCK)
    scaled = grad[rows, :].astype(F32) * inv[rows, :]
    product = scaled * ctx[rows, :].astype(F32)
    low = scaled.astype(BF16)
    total = None
    for e in range(2):
        lanes = head_lanes(e)
        low_lanes = lanes.astype(BF16)
        delta = jnp.sum(product * lanes, axis=-1, keepdims=True)
        grad_low = low * low_lanes
        query = q[rows, :] * low_lanes
        for k, v, load, add in segments:
            weights = load(e)
            slope = mm(grad_low, v, NT) - delta
            grad_scores = (weights.astype(F32) * slope).astype(BF16)
            part = mm(grad_scores, k * low_lanes, NN)
            total = part if total is None else total + part
            add(mm(grad_scores, query, TN), mm(weights, grad_low, TN))
    grad_query[rows, :] = (total * SCALE).astype(BF16)


def same(scores):
    return scores


def self_forward_kernel(info, q, k, v, ko, vo, ctx, inv, we, wo):
    tokens = q.shape[0]

    def masked(lo, col_lo, prefix_len):
        def edit(scores):
            row = lo + lax.broadcasted_iota(jnp.int32, scores.shape, 0)
            col = col_lo + lax.broadcasted_iota(jnp.int32, scores.shape, 1)
            allowed = col <= row
            if prefix_len is not None:
                allowed = allowed | (col < prefix_len)
            return jnp.where(allowed, scores, MASKED)

        return edit

    def keeper(target, lo, col_lo, width):
        def store(e, weights):
            target[e, lo : lo + BLOCK, col_lo : col_lo + width] = weights

        return store

    @pl.when(info[0] == 0)
    def _():
        for lo in range(0, tokens, BLOCK):
            attend_forward(
                q,
                [(k[...], v[...], keeper(we, lo, 0, tokens), masked(lo, 0, info[1]))],
                ctx,
                inv,
                lo,
            )

    @pl.when(info[0] != 0)
    def _():
        for lo in range(0, tokens, BLOCK):
            near = slice(lo, lo + BLOCK)
            segments = [(ko[...], vo[...], keeper(wo, lo, 0, tokens), same)]
            if lo:
                segments.append((k[:lo, :], v[:lo, :], keeper(we, lo, 0, lo), same))
            segments.append(
                (k[near, :], v[near, :], keeper(we, lo, lo, BLOCK), masked(lo, lo, None))
            )
            attend_forward(q, segments, ctx, inv, lo)


def self_backward_kernel(
    info, q, k, v, ko, vo, ctx, inv, we, wo, grad, dq, dk, dv, dko, dvo, ak, av, ako, avo
):
    tokens = q.shape[0]
    ak[...] = jnp.zeros_like(ak)
    av[...] = jnp.zeros_like(av)

    def loader(source, lo, col_lo, width):
        return lambda e: source[e, lo : lo + BLOCK, col_lo : col_lo + width]

    def adder(keys, values, col_lo, width):
        def add(part_keys, part_values):
            keys[col_lo : col_lo + width, :] += part_keys
            values[col_lo : col_lo + width, :] += part_values

        return add

    @pl.when(info[0] == 0)
    def _():
        for lo in range(0, tokens, BLOCK):
            attend_backward(
                q,
                grad,
                ctx,
                inv,
                [(k[...], v[...], loader(we, lo, 0, tokens), adder(ak, av, 0, tokens))],
                dq,
                lo,
            )

    @pl.when(info[0] != 0)
    def _():
        ako[...] = jnp.zeros_like(ako)
        avo[...] = jnp.zeros_like(avo)
        for lo in range(0, tokens, BLOCK):
            width = lo + BLOCK
            segments = [
                (ko[...], vo[...], loader(wo, lo, 0, tokens), adder(ako, avo, 0, tokens)),
            ]
            if lo:
                segments.append(
                    (k[:lo, :], v[:lo, :], loader(we, lo, 0, lo), adder(ak, av, 0, lo))
                )
            segments.append(
                (
                    k[lo:width, :],
                    v[lo:width, :],
                    loader(we, lo, lo, BLOCK),
                    adder(ak, av, lo, BLOCK),
                )
            )
            attend_backward(q, grad, ctx, inv, segments, dq, lo)
        dko[...] = ako[...].astype(BF16)
        dvo[...] = avo[...].astype(BF16)

    dk[...] = ak[...].astype(BF16)
    dv[...] = av[...].astype(BF16)


def cross_forward_kernel(q, k, v, ctx, inv, we):
    for lo in range(0, q.shape[0], BLOCK):

        def store(e, weights, lo=lo):
            we[e, lo : lo + BLOCK, :] = weights

        attend_forward(q, [(k[...], v[...], store, same)], ctx, inv, lo)


def cross_backward_kernel(q, k, v, ctx, inv, we, grad, dq, dk, dv, ak, av):
    ak[...] = jnp.zeros_like(ak)
    av[...] = jnp.zeros_like(av)
    for lo in range(0, q.shape[0], BLOCK):

        def load(e, lo=lo):
            return we[e, lo : lo + BLOCK, :]

        def add(part_keys, part_values):
            ak[...] += part_keys
            av[...] += part_values

        attend_backward(q, grad, ctx, inv, [(k[...], v[...], load, add)], dq, lo)
    dk[...] = ak[...].astype(BF16)
    dv[...] = av[...].astype(BF16)


def lanes_of(rows):
    return pl.BlockSpec((rows, PAIR), lambda h: (0, h))


def weights_of(rows, columns):
    return pl.BlockSpec((2, rows, columns), lambda h: (h, 0, 0))


def self_forward(info, q, k, v, ko, vo):
    tokens, width = q.shape
    heads = width // HD
    row = lanes_of(tokens)
    square = shaped((heads, tokens, tokens), BF16)
    return pl.pallas_call(
        self_forward_kernel,
        grid=(width // PAIR,),
        out_shape=(shaped((tokens, width), BF16), shaped((tokens, width), F32), square, square),
        in_specs=[SMEM] + [row] * 5,
        out_specs=(row, row) + (weights_of(tokens, tokens),) * 2,
        compiler_params=limit(48),
        cost_estimate=cost(heads * tokens * tokens * 2 * 256 * 2, 12 << 20),
    )(info, q, k, v, ko, vo)


def self_backward(info, q, k, v, ko, vo, ctx, inv, we, wo, grad):
    tokens, width = q.shape
    heads = width // HD
    row = lanes_of(tokens)
    low = shaped((tokens, width), BF16)
    return pl.pallas_call(
        self_backward_kernel,
        grid=(width // PAIR,),
        out_shape=(low,) * 5,
        in_specs=[SMEM] + [row] * 7 + [weights_of(tokens, tokens)] * 2 + [row],
        out_specs=(row,) * 5,
        scratch_shapes=[pltpu.VMEM((tokens, PAIR), F32)] * 4,
        compiler_params=limit(48),
        cost_estimate=cost(heads * tokens * tokens * 2 * 256 * 4, 14 << 20),
    )(info, q, k, v, ko, vo, ctx, inv, we, wo, grad)


def cross_forward(q, k, v):
    tokens, width = q.shape
    rows = k.shape[0]
    heads = width // HD
    return pl.pallas_call(
        cross_forward_kernel,
        grid=(width // PAIR,),
        out_shape=(
            shaped((tokens, width), BF16),
            shaped((tokens, width), F32),
            shaped((heads, tokens, rows), BF16),
        ),
        in_specs=[lanes_of(tokens), lanes_of(rows), lanes_of(rows)],
        out_specs=(lanes_of(tokens), lanes_of(tokens), weights_of(tokens, rows)),
        compiler_params=limit(48),
        cost_estimate=cost(heads * tokens * rows * 256 * 2, 5 << 20),
    )(q, k, v)


def cross_backward(q, k, v, ctx, inv, we, grad):
    tokens, width = q.shape
    rows = k.shape[0]
    heads = width // HD
    return pl.pallas_call(
        cross_backward_kernel,
        grid=(width // PAIR,),
        out_shape=(
            shaped((tokens, width), BF16),
            shaped((rows, width), BF16),
            shaped((rows, width), BF16),
        ),
        in_specs=[lanes_of(tokens), lanes_of(rows), lanes_of(rows)]
        + [lanes_of(tokens)] * 2
        + [weights_of(tokens, rows), lanes_of(tokens)],
        out_specs=(lanes_of(tokens), lanes_of(rows), lanes_of(rows)),
        scratch_shapes=[pltpu.VMEM((rows, PAIR), F32)] * 2,
        compiler_params=limit(48),
        cost_estimate=cost(heads * tokens * rows * 256 * 4, 6 << 20),
    )(q, k, v, ctx, inv, we, grad)


def project_self_kernel(info, x, xo, w, bq, bv, q, k, v, ko, vo):
    rows = x[...]
    q[...] = (mm(rows, w[0], NN) + bq[...].astype(F32)).astype(BF16) * jnp.asarray(SCALE, BF16)
    k[...] = mm(rows, w[1], NN).astype(BF16)
    v[...] = (mm(rows, w[2], NN) + bv[...].astype(F32)).astype(BF16)

    @pl.when(info[0] != 0)
    def _():
        other = xo[...]
        ko[...] = mm(other, w[1], NN).astype(BF16)
        vo[...] = (mm(other, w[2], NN) + bv[...].astype(F32)).astype(BF16)


def project_self(info, x, xo, w, bq, bv):
    low = shaped(x.shape, BF16)
    return pl.pallas_call(
        project_self_kernel,
        out_shape=(low,) * 5,
        in_specs=[SMEM] + [VMEM] * 5,
        compiler_params=limit(48),
        cost_estimate=cost(5 * x.size * x.shape[1], 5 << 20),
    )(info, x, xo, w, bq, bv)


def first_norm_kernel(
    ctx, x, mem, memo, w, ob, gain, bias, bq, bv, first, normed, inverse, q, k, v
):
    summed = x[...].astype(F32) + mm(ctx[...], w[0], NT) + ob[...].astype(F32)
    n, r = norm_forward(summed)
    out = n * gain[...].astype(F32) + bias[...].astype(F32)
    normed[...] = n
    inverse[...] = r
    first[...] = out
    q[...] = (mm(out.astype(BF16), w[1], NN) + bq[...].astype(F32)).astype(BF16) * jnp.asarray(
        SCALE, BF16
    )
    rows = mem.shape[0]
    for source, lo in ((mem, 0), (memo, rows)):
        k[lo : lo + rows, :] = mm(source[...], w[2], NN).astype(BF16)
        v[lo : lo + rows, :] = (mm(source[...], w[3], NN) + bv[...].astype(F32)).astype(BF16)


def first_norm(ctx, x, mem, memo, w, ob, gain, bias, bq, bv):
    rows = 2 * mem.shape[0]
    tokens, width = x.shape
    full = shaped(x.shape, F32)
    return pl.pallas_call(
        first_norm_kernel,
        out_shape=(
            full,
            full,
            shaped((tokens, 1), F32),
            shaped(x.shape, BF16),
            shaped((rows, width), BF16),
            shaped((rows, width), BF16),
        ),
        in_specs=[VMEM] * 10,
        compiler_params=limit(48),
        cost_estimate=cost(3 * x.size * width, 8 << 20),
    )(ctx, x, mem, memo, w, ob, gain, bias, bq, bv)


def feed_kernel(
    ctx,
    first,
    cot,
    wo,
    wf,
    ob,
    gain2,
    bias2,
    fib,
    fob,
    gain3,
    bias3,
    out,
    dw,
    du2,
    db2,
    sums,
    hsum,
    act,
    slope,
    acc,
    second,
):
    tokens, width = first.shape
    chunks = wf.shape[2] // width
    summed = first[...] + mm(ctx[...], wo[4], NT) + ob[...].astype(F32)
    n2, r2 = norm_forward(summed)
    out2 = n2 * gain2[...].astype(F32) + bias2[...].astype(F32)
    second[...] = out2.astype(BF16)
    acc[...] = out2 + fob[...].astype(F32)

    @pl.loop(0, chunks)
    def _(c):
        cols = pl.ds(pl.multiple_of(c * width, width), width)
        hidden = mm(second[...], wf[0, :, cols], NN) + fib[:, cols].astype(F32)
        gate = 1.0 / (1.0 + jnp.exp(-hidden))
        active = (hidden * gate).astype(BF16)
        act[:, cols] = active
        slope[:, cols] = (gate * (1.0 + hidden * (1.0 - gate))).astype(BF16)
        acc[...] += mm(active, wf[1, :, cols], NT)

    n3, r3 = norm_forward(acc[...])
    out[...] = (n3 * gain3[...].astype(F32) + bias3[...].astype(F32)).astype(BF16)
    dy = cot[...].astype(F32)
    du3 = norm_backward(dy, n3, r3, gain3[...].astype(F32))
    db3 = du3.astype(BF16)
    sums[6:7, :] = column_sum(db3)
    sums[7:8, :] = column_sum(dy * n3)
    sums[8:9, :] = column_sum(dy)
    acc[...] = du3
    db2[...] = db3

    @pl.loop(0, chunks)
    def _(c):
        cols = pl.ds(pl.multiple_of(c * width, width), width)
        back = db2[...]
        dact = mm(back, wf[1, :, cols], NN)
        dhid = (dact * slope[:, cols].astype(F32)).astype(BF16)
        hsum[:, cols] = column_sum(dhid)
        dw[1, :, cols] = mm(back, act[:, cols], TN).astype(BF16)
        dw[0, :, cols] = mm(second[...], dhid, TN).astype(BF16)
        acc[...] += mm(dhid, wf[0, :, cols], NT)

    dsecond = acc[...]
    grad2 = norm_backward(dsecond, n2, r2, gain2[...].astype(F32))
    low2 = grad2.astype(BF16)
    du2[...] = grad2
    db2[...] = low2
    sums[3:4, :] = column_sum(low2)
    sums[4:5, :] = column_sum(dsecond * n2)
    sums[5:6, :] = column_sum(dsecond)
    sums[0:3, :] = jnp.zeros((3, width), F32)
    sums[9:16, :] = jnp.zeros((7, width), F32)


def feed(ctx, first, cot, wo, wf, ob, gain2, bias2, fib, fob, gain3, bias3):
    tokens, width = first.shape
    wide = wf.shape[2]
    return pl.pallas_call(
        feed_kernel,
        out_shape=(
            shaped(first.shape, BF16),
            shaped(wf.shape, BF16),
            shaped(first.shape, F32),
            shaped(first.shape, BF16),
            shaped((16, width), F32),
            shaped((1, wide), F32),
        ),
        in_specs=[VMEM] * 12,
        scratch_shapes=[
            pltpu.VMEM((tokens, wide), BF16),
            pltpu.VMEM((tokens, wide), BF16),
            pltpu.VMEM((tokens, width), F32),
            pltpu.VMEM((tokens, width), BF16),
        ],
        compiler_params=limit(48),
        cost_estimate=cost(6 * tokens * width * wide, 14 << 20),
    )(ctx, first, cot, wo, wf, ob, gain2, bias2, fib, fob, gain3, bias3)


def context_grad_kernel(db, w, out):
    out[...] = mm(db[...], w[4], NN).astype(BF16)


def context_grad(db, w):
    return pl.pallas_call(
        context_grad_kernel,
        out_shape=shaped(db.shape, BF16),
        in_specs=[VMEM] * 2,
        compiler_params=limit(48),
        cost_estimate=cost(db.size * db.shape[1], 2 << 20),
    )(db, w)


def first_back_kernel(du2, dq2, normed, inverse, w, gain, du1, db1, dctx, sums):
    width = du2.shape[1]
    dfirst = du2[...] + mm(dq2[...], w[1], NT)
    n = normed[...]
    grad = norm_backward(dfirst, n, inverse[...], gain[...].astype(F32))
    low = grad.astype(BF16)
    du1[...] = grad
    db1[...] = low
    dctx[...] = mm(low, w[0], NN).astype(BF16)
    sums[0:1, :] = column_sum(low)
    sums[1:2, :] = column_sum(dfirst * n)
    sums[2:3, :] = column_sum(dfirst)
    sums[3:8, :] = jnp.zeros((5, width), F32)


def first_back(du2, dq2, normed, inverse, w, gain):
    width = du2.shape[1]
    low = shaped(du2.shape, BF16)
    return pl.pallas_call(
        first_back_kernel,
        out_shape=(shaped(du2.shape, F32), low, low, shaped((8, width), F32)),
        in_specs=[VMEM] * 6,
        compiler_params=limit(48),
        cost_estimate=cost(2 * du2.size * width, 8 << 20),
    )(du2, dq2, normed, inverse, w, gain)


def middle_grads_kernel(
    first, dq2, mem, memo, dk2, dv2, db2, ctx2, db1, ctx1, w, dw, own, other, sums
):
    rows, width = mem.shape
    dw[0] = mm(db1[...], ctx1[...], TN).astype(BF16)
    dw[1] = mm(first[...].astype(BF16), dq2[...], TN).astype(BF16)
    for slot, grad in ((2, dk2), (3, dv2)):
        dw[slot] = (
            mm(mem[...], grad[:rows, :], TN) + mm(memo[...], grad[rows:, :], TN)
        ).astype(BF16)
    dw[4] = mm(db2[...], ctx2[...], TN).astype(BF16)
    back = mm(dk2[...], w[2], NT) + mm(dv2[...], w[3], NT)
    own[...] = back[:rows, :]
    other[...] = back[rows:, :].astype(BF16)
    sums[0:1, :] = column_sum(dq2[...])
    sums[1:2, :] = column_sum(dv2[...])
    sums[2:8, :] = jnp.zeros((6, width), F32)


def middle_grads(first, dq2, mem, memo, dk2, dv2, db2, ctx2, db1, ctx1, w):
    tokens, width = first.shape
    rows = mem.shape[0]
    return pl.pallas_call(
        middle_grads_kernel,
        out_shape=(
            shaped(w.shape, BF16),
            shaped((rows, width), F32),
            shaped((rows, width), BF16),
            shaped((8, width), F32),
        ),
        in_specs=[VMEM] * 11,
        compiler_params=limit(48),
        cost_estimate=cost(5 * first.size * width, 10 << 20),
    )(first, dq2, mem, memo, dk2, dv2, db2, ctx2, db1, ctx1, w)


def self_grads_kernel(info, x, xo, dq, dk, dv, dko, dvo, w, dw, other, sums):
    width = x.shape[1]
    dw[0] = mm(x[...], dq[...], TN).astype(BF16)
    sums[0:1, :] = column_sum(dq[...])
    sums[2:8, :] = jnp.zeros((6, width), F32)

    @pl.when(info[0] == 0)
    def _():
        dw[1] = mm(x[...], dk[...], TN).astype(BF16)
        dw[2] = mm(x[...], dv[...], TN).astype(BF16)
        sums[1:2, :] = column_sum(dv[...])
        other[...] = jnp.zeros_like(other)

    @pl.when(info[0] != 0)
    def _():
        dw[1] = (mm(x[...], dk[...], TN) + mm(xo[...], dko[...], TN)).astype(BF16)
        dw[2] = (mm(x[...], dv[...], TN) + mm(xo[...], dvo[...], TN)).astype(BF16)
        sums[1:2, :] = column_sum(dv[...]) + column_sum(dvo[...])
        other[...] = (mm(dko[...], w[1], NT) + mm(dvo[...], w[2], NT)).astype(BF16)


def self_grads(info, x, xo, dq, dk, dv, dko, dvo, w):
    width = x.shape[1]
    return pl.pallas_call(
        self_grads_kernel,
        out_shape=(shaped(w.shape, BF16), shaped(x.shape, BF16), shaped((8, width), F32)),
        in_specs=[SMEM] + [VMEM] * 8,
        compiler_params=limit(48),
        cost_estimate=cost(7 * x.size * width, 8 << 20),
    )(info, x, xo, dq, dk, dv, dko, dvo, w)


def input_grads_kernel(du1, dq, dk, dv, w, back, out):
    out[...] = (
        du1[...]
        + mm(dq[...], w[0], NT)
        + mm(dk[...], w[1], NT)
        + mm(dv[...], w[2], NT)
        + back[...].astype(F32)
    )


def input_grads(du1, dq, dk, dv, w, back):
    return pl.pallas_call(
        input_grads_kernel,
        out_shape=shaped(du1.shape, F32),
        in_specs=[VMEM] * 6,
        compiler_params=limit(48),
        cost_estimate=cost(3 * du1.size * du1.shape[1], 6 << 20),
    )(du1, dq, dk, dv, w, back)


def on_device(
    inputs,
    memory,
    prefix,
    self_query,
    self_query_bias,
    self_key,
    self_value,
    self_value_bias,
    self_out,
    self_out_bias,
    self_norm_gain,
    self_norm_bias,
    cross_query,
    cross_query_bias,
    cross_key,
    cross_value,
    cross_value_bias,
    cross_out,
    cross_out_bias,
    cross_norm_gain,
    cross_norm_bias,
    feed_in,
    feed_in_bias,
    feed_out,
    feed_out_bias,
    feed_norm_gain,
    feed_norm_bias,
    cotangent,
):
    nd, nt = lax.axis_size("dp"), lax.axis_size("tensor")
    me_d, me_t = lax.axis_index("dp"), lax.axis_index("tensor")
    late = me_t % 2
    width = inputs.shape[1]
    assert LEN == 2 * inputs.shape[0] and MEM == 2 * memory.shape[0]
    assert nd & (nd - 1) == 0 and nt & (nt - 1) == 0
    prefix_here = jnp.where(late == 0, lax.dynamic_index_in_dim(prefix, me_t // 2, keepdims=False), 0)
    info = jnp.stack([late, prefix_here, me_d, me_t]).astype(jnp.int32)

    columns = self_query_bias.shape[0]
    riders = jnp.concatenate(
        [self_query_bias, self_value_bias, cross_query_bias, cross_value_bias, feed_in_bias]
    ).reshape(-1, columns)
    count = riders.shape[0]
    riders = jnp.pad(riders, ((0, -count % 16), (0, 0)))
    projections = jnp.stack([self_query, self_key, self_value])
    flat = projections.reshape(-1, columns)
    line_self = along_line(jnp.concatenate([flat, riders]))
    line_biases = line_self[:, flat.shape[0] :]
    line_self = line_self[:, : flat.shape[0]].reshape((nt,) + projections.shape)
    line_biases = jnp.take(line_biases, jnp.bitwise_xor(jnp.arange(nt), me_t), axis=0)
    biases = [line_biases[:, i].reshape(1, width) for i in range(4)]
    hidden_bias = line_biases[:, 4:count].reshape(1, -1)
    row = lambda vector: vector.reshape(1, -1)

    group_self = over_planes(line_self)
    inputs_other = hand_over(inputs, 0, 1)
    memory_other = swap(memory, 0, 1)
    group_middle = gather_group(
        jnp.stack([self_out.T, cross_query, cross_key, cross_value, cross_out.T])
    )
    group_feed = gather_group(jnp.stack([feed_in, feed_out.T]))

    w_self = assemble(info, *group_self)
    q1, k1, v1, k1o, v1o = project_self(info, inputs, inputs_other, w_self, biases[0], biases[1])
    ctx1, inv1, we1, wo1 = self_forward(info, q1, k1, v1, k1o, v1o)
    w_middle = assemble(info, *group_middle)
    first, normed1, inverse1, q2, k2, v2 = first_norm(
        ctx1,
        inputs,
        memory,
        memory_other,
        w_middle,
        row(self_out_bias),
        row(self_norm_gain),
        row(self_norm_bias),
        biases[2],
        biases[3],
    )
    ctx2, inv2, we2 = cross_forward(q2, k2, v2)
    w_feed = assemble(info, *group_feed)
    outputs, dw_feed, du2, db2, sums_feed, sums_hidden = feed(
        ctx2,
        first,
        cotangent,
        w_middle,
        w_feed,
        row(cross_out_bias),
        row(cross_norm_gain),
        row(cross_norm_bias),
        hidden_bias,
        row(feed_out_bias),
        row(feed_norm_gain),
        row(feed_norm_bias),
    )
    grad_feed = scatter_group(*disperse(info, dw_feed))
    dctx2 = context_grad(db2, w_middle)
    dq2, dk2, dv2 = cross_backward(q2, k2, v2, ctx2, inv2, we2, dctx2)
    du1, db1, dctx1, sums_first = first_back(
        du2, dq2, normed1, inverse1, w_middle, row(self_norm_gain)
    )
    dw_middle, memory_own, memory_back, sums_cross = middle_grads(
        first, dq2, memory, memory_other, dk2, dv2, db2, ctx2, db1, ctx1, w_middle
    )
    grad_middle = scatter_group(*disperse(info, dw_middle))
    grad_memory = memory_own + swap(memory_back, 0, 1).astype(F32)
    early = jnp.concatenate(
        [
            sums_feed[:9] + jnp.pad(sums_first[:3], ((0, 6), (0, 0))),
            sums_cross[:2],
            sums_hidden.reshape(-1, width),
        ]
    )
    early = jnp.pad(early, ((0, 16 - early.shape[0]), (0, 0)))
    early = sum_everywhere(early)
    dq1, dk1, dv1, dk1o, dv1o = self_backward(
        info, q1, k1, v1, k1o, v1o, ctx1, inv1, we1, wo1, dctx1
    )
    dw_self, inputs_back, sums_self = self_grads(
        info, inputs, inputs_other, dq1, dk1, dv1, dk1o, dv1o, w_self
    )
    grad_self = scatter_group(*disperse(info, dw_self))
    late_sums = sum_everywhere(sums_self)
    grad_inputs = input_grads(du1, dq1, dk1, dv1, w_self, hand_over(inputs_back, 1, -1))

    def mine(vector):
        count = vector.shape[0] // nt
        return lax.dynamic_slice_in_dim(vector, me_t * count, count)

    return (
        outputs,
        grad_inputs,
        grad_memory,
        grad_self[0],
        mine(late_sums[0]),
        grad_self[1],
        grad_self[2],
        mine(late_sums[1]),
        grad_middle[0].T,
        early[0],
        early[1],
        early[2],
        grad_middle[1],
        mine(early[9]),
        grad_middle[2],
        grad_middle[3],
        mine(early[10]),
        grad_middle[4].T,
        early[3],
        early[4],
        early[5],
        grad_feed[0],
        mine(early[11:15].reshape(-1)),
        grad_feed[1].T,
        early[6],
        early[7],
        early[8],
    )


def solution(mesh):
    placed = (
        P(("dp", "tensor"), None),
        P(("dp", "tensor"), None),
        P("dp"),
        P("dp", "tensor"),
        P("tensor"),
        P("dp", "tensor"),
        P("dp", "tensor"),
        P("tensor"),
        P("tensor", "dp"),
        P(),
        P(),
        P(),
        P("dp", "tensor"),
        P("tensor"),
        P("dp", "tensor"),
        P("dp", "tensor"),
        P("tensor"),
        P("tensor", "dp"),
        P(),
        P(),
        P(),
        P("dp", "tensor"),
        P("tensor"),
        P("tensor", "dp"),
        P(),
        P(),
        P(),
        P(("dp", "tensor"), None),
    )
    return jax.shard_map(
        on_device,
        mesh=mesh,
        in_specs=placed,
        out_specs=(
            P(("dp", "tensor"), None),
            P(("dp", "tensor"), None),
            P(("dp", "tensor"), None),
            P("dp", "tensor"),
            P("tensor"),
            P("dp", "tensor"),
            P("dp", "tensor"),
            P("tensor"),
            P("tensor", "dp"),
            P(),
            P(),
            P(),
            P("dp", "tensor"),
            P("tensor"),
            P("dp", "tensor"),
            P("dp", "tensor"),
            P("tensor"),
            P("tensor", "dp"),
            P(),
            P(),
            P(),
            P("dp", "tensor"),
            P("tensor"),
            P("tensor", "dp"),
            P(),
            P(),
            P(),
        ),
        check_vma=False,
    )
```

time: 1280 us -> 286 us (0.22)
  waiting for transfers between devices: 856 us -> 66.4 us
  blocking collectives: 173 us -> 0 us
  matrix products: 115 us -> 0 us
  starting transfers between devices: 1.54 us -> 90.4 us
  Pallas kernels: 0 us -> 74.1 us
  other arithmetic: 59 us -> 15.8 us
  local copies, waits for them, and re-layouts: 50.4 us -> 35.4 us
  between operations: 15.4 us -> 2.41 us
    reduce_scatter x12 -> x0, waiting for transfers between devices: 586 us -> none  [the longest x6 450 us: reduce_rows(): return lax.psum_scatter(running, 'tensor', scatter_dimension=0, tiled=True)]
    all_gather x6 -> x0, waiting for transfers between devices: 151 us -> none  [gather_rows(): return lax.all_gather(block_rows, 'tensor', axis=0, tiled=True)]
    all_gather x11 -> x0, blocking collectives: 120 us -> none  [the longest x1 23.3 us: on_device(): memory_all = lax.all_gather(memory, 'tensor', axis=0, tiled=True)]
    unnamed x28 -> x0, waiting for transfers between devices: 119 us -> none
    dot_general x86 -> x0, matrix products: 115 us -> none  [the longest x10 33.1 us: multiply(): lax.dot_general(left_side, right_side, (((1,), (1,)), ((), ())), preferre...]
    ppermute x0 -> x60, starting transfers between devices: none -> 90.4 us  [the longest x58 85 us: swap(): return lax.ppermute(array, ('dp', 'tensor'), pairs)]
    pallas_call x0 -> x18, Pallas kernels: none -> 74.1 us  [the longest x1 15.8 us: feed(): pl.pallas_call(feed_kernel, out_shape=(shaped(first.shape, BF16), shaped(...]
    ppermute x0 -> x60, waiting for transfers between devices: none -> 66.4 us  [the longest x58 56.6 us: swap(): return lax.ppermute(array, ('dp', 'tensor'), pairs)]
  transfers between devices with their start and end apart: 23 -> 60, of which waited for: 20 -> 23; matrix products, arithmetic and copies ran while one was open for 9% -> 12% of each run, Pallas kernels for 0% -> 19%
where the time goes in v1:
time: 286 us; the launch traced here: 285 us
  starting transfers between devices  90.4 us (32%)
  Pallas kernels  74.1 us (26%)
  waiting for transfers between devices  66.4 us (23%)
  local copies, waits for them, and re-layouts  35.4 us (12%)
  other arithmetic  15.8 us (6%)
    ppermute x58, starting transfers between devices, swap(): return lax.ppermute(array, ('dp', 'tensor'), pairs)  85 us
    ppermute x58, waiting for transfers between devices, swap(): return lax.ppermute(array, ('dp', 'tensor'), pairs)  56.6 us
    unnamed x152, local copies, waits for them, and re-layouts  20.6 us
    pallas_call x1, Pallas kernels, feed(): pl.pallas_call(feed_kernel, out_shape=(shaped(first.shape, BF16), shaped(...  15.8 us
    pallas_call x1, Pallas kernels, self_backward(): pl.pallas_call(self_backward_kernel, grid=(width // PAIR,), out_shape=(lo...  9.91 us
    ppermute x2, waiting for transfers between devices, hand_over(): return lax.ppermute(array, ('dp', 'tensor'), pairs)  9.71 us
    pallas_call x1, Pallas kernels, cross_backward(): pl.pallas_call(cross_backward_kernel, grid=(width // PAIR,), out_shape=(s...  7.01 us
    pallas_call x1, Pallas kernels, self_forward(): pl.pallas_call(self_forward_kernel, grid=(width // PAIR,), out_shape=(sha...  6.91 us
  transfers between devices with their start and end apart: 60, of which 23 were waited for; matrix products, arithmetic and copies ran while one was open for 12% of the time, Pallas kernels for 19%

profile of v1, /device:TPU:0, one launch (start us, length us, event | category | flops | bytes accessed | tf_op | source)
XLA Modules:
  0.0 284.5 jit_solution(17582798632754813185)
XLA Ops:
  1.8 3.1 %collective-permute-start.16 = (bf16[2,64,512]{2,1,0:T(8,128)(2,1)S(1)}, bf16[2,64,512]{2,1,0:T(8,128)(2,1)S(1)}, u32[]{:S(2)}, u32[]{:S(2)}) collective-permute-start(bf16[2,64,512]{2,1,0:T(8,128)(2,1)S(1)} %get-tuple-element.155), channel_id=1, source_target_pairs={{0,1},{1,0},{2,3},{3,2},{4,5},{5,4},{6,7},{7,6},{8,9},{9,8},{10,11... | collective-permute-start | bytes 393224 | tf_op jit(solution)/shard_map/ppermute | solution.py:51
  4.8 2.6 collective-permute-start.17
  13.4 3.5 %collective-permute-start.2 = (bf16[208,128]{1,0:T(8,128)(2,1)S(1)}, bf16[208,128]{1,0:T(8,128)(2,1)S(1)}, u32[]{:S(2)}, u32[]{:S(2)}) collective-permute-start(bf16[208,128]{1,0:T(8,128)(2,1)S(1)} %get-tuple-element.160), channel_id=1, source_target_pairs={{0,2},{1,3},{2,0},{3,1},{4,6},{5,7},{6,4},{7,5},{8,10},{9,11},{10,... | collective-permute-start | bytes 159752 | tf_op jit(solution)/shard_map/ppermute | solution.py:51
  29.3 2.4 collective-permute-start.9
  32.4 1.8 collective-permute-done.19
  35.8 5.8 %collective-permute-done.20 = bf16[4,2,64,512]{3,2,1,0:T(8,128)(2,1)} collective-permute-done((bf16[4,2,64,512]{3,2,1,0:T(8,128)(2,1)S(1)}, bf16[4,2,64,512]{3,2,1,0:T(8,128)(2,1)}, u32[]{:S(2)}, u32[]{:S(2)}) %collective-permute-start.20) | collective-permute-done | bytes 524320 | tf_op jit(solution)/shard_map/ppermute | solution.py:51
  41.6 4.3 %collective-permute-done.21 = bf16[4,2,64,512]{3,2,1,0:T(8,128)(2,1)} collective-permute-done((bf16[4,2,64,512]{3,2,1,0:T(8,128)(2,1)S(1)}, bf16[4,2,64,512]{3,2,1,0:T(8,128)(2,1)}, u32[]{:S(2)}, u32[]{:S(2)}) %collective-permute-start.21) | collective-permute-done | bytes 524320 | tf_op jit(solution)/shard_map/ppermute | solution.py:51
  48.1 2.5 collective-permute-start.6
  52.7 2.5 collective-permute-start.14
  55.7 4.1 %collective-permute-start = (bf16[512,512]{1,0:T(8,128)(2,1)}, bf16[512,512]{1,0:T(8,128)(2,1)}, u32[]{:S(2)}, u32[]{:S(2)}) collective-permute-start(bf16[512,512]{1,0:T(8,128)(2,1)} %x.11), channel_id=1, source_target_pairs={{0,1},{2,3},{4,5},{6,7},{8,9},{10,11},{12,13},{14,15},{16,17},{18,... | collective-permute-start | bytes 1572872 | tf_op jit(solution)/shard_map/ppermute | solution.py:57
  63.6 5.5 %collective-permute-done.13 = bf16[4,5,64,128]{3,2,1,0:T(8,128)(2,1)S(1)} collective-permute-done((bf16[4,5,64,128]{3,2,1,0:T(8,128)(2,1)S(1)}, bf16[4,5,64,128]{3,2,1,0:T(8,128)(2,1)S(1)}, u32[]{:S(2)}, u32[]{:S(2)}) %collective-permute-start.13) | collective-permute-done | bytes 327712 | tf_op jit(solution)/shard_map/ppermute | solution.py:51
  71.1 2.0 gather_fusion
  78.9 2.9 %shard_map.476 = (bf16[512,512]{1,0:T(8,128)(2,1)S(1)}, bf16[512,512]{1,0:T(8,128)(2,1)S(1)}, bf16[512,512]{1,0:T(8,128)(2,1)S(1)}, bf16[512,512]{1,0:T(8,128)(2,1)S(1)}, bf16[512,512]{1,0:T(8,128)(2,1)S(1)}) custom-call(s32[4]{0:T(128)S(1)} %pad_add_fusion.1.info, bf16[512,512]{1,0:T(8,128)(2,1)} %x.11, bf16[512,512]{1,0:T(8,128)(2,1)} %collective-permute-done.xo, ...), custom_call_target="tpu_custom_call" | custom-call | flops 1342177280 | bytes 5242880 | tf_op jit(solution)/shard_map/pallas_call | solution.py:470
  82.0 6.9 %shard_map.477 = (bf16[512,512]{1,0:T(8,128)(2,1)S(1)}, f32[512,512]{1,0:T(8,128)S(1)}, bf16[8,512,512]{2,1,0:T(8,128)(2,1)}, bf16[8,512,512]{2,1,0:T(8,128)(2,1)}) custom-call(s32[4]{0:T(128)S(1)} %pad_add_fusion.1.info, bf16[512,512]{1,0:T(8,128)(2,1)S(1)} %get-tuple-element.76.q, bf16[512,512]{1,0:T(8,128)(2,1)S(1)} %get-tuple-element.77.k, ...), custom_call_target="tpu_custom_call" | custom-call | flops 4294967296 | bytes 12582912 | tf_op jit(solution)/shard_map/pallas_call | solution.py:386
  88.9 2.2 shard_map.478.w.wo
  92.6 3.4 %shard_map.479 = (f32[512,512]{1,0:T(8,128)S(1)}, f32[512,512]{1,0:T(8,128)S(1)}, f32[512,1]{1,0:T(8,128)S(1)}, bf16[512,512]{1,0:T(8,128)(2,1)S(1)}, bf16[256,5...) custom-call(bf16[512,512]{1,0:T(8,128)(2,1)S(1)} %get-tuple-element.81.ctx.ctx1, bf16[512,512]{1,0:T(8,128)(2,1)} %x.11, ...), custom_call_target="tpu_custom_call" | custom-call | flops 805306368 | bytes 8388608 | tf_op jit(solution)/shard_map/pallas_call | solution.py:501
  96.0 3.0 %shard_map.480 = (bf16[512,512]{1,0:T(8,128)(2,1)S(1)}, f32[512,512]{1,0:T(8,128)S(1)}, bf16[8,512,256]{2,1,0:T(8,128)(2,1)S(1)}) custom-call(bf16[512,512]{1,0:T(8,128)(2,1)S(1)} %get-tuple-element.82.q, bf16[256,512]{1,0:T(8,128)(2,1)S(1)} %get-tuple-element.83.k, bf16[256,512]{1,0:T(8,128)(2,1)S(1)} %get-tuple-element.84.v), custom_call_target="tpu_custom_call" | custom-call | flops 1073741824 | bytes 5242880 | tf_op jit(solution)/shard_map/pallas_call | solution.py:418
  100.4 2.3 shard_map.481.wf
  102.8 2.0 copy-done.5
  104.8 15.8 %shard_map.482 = (bf16[512,512]{1,0:T(8,128)(2,1)}, bf16[2,512,2048]{2,1,0:T(8,128)(2,1)}, f32[512,512]{1,0:T(8,128)S(1)}, bf16[512,512]{1,0:T(8,128)(2,1)S(1)},...) custom-call(bf16[512,512]{1,0:T(8,128)(2,1)S(1)} %get-tuple-element.85.ctx.ctx2, f32[512,512]{1,0:T(8,128)S(1)} %get-tuple-element.86.first, ...), custom_call_target="tpu_custom_call" | custom-call | flops 6442450944 | bytes 14680064 | tf_op jit(solution)/shard_map/pallas_call | solution.py:596
  120.7 2.2 copy-done.4
  122.9 2.2 shard_map.492
  126.3 7.0 %shard_map.484 = (bf16[512,512]{1,0:T(8,128)(2,1)S(1)}, bf16[256,512]{1,0:T(8,128)(2,1)S(1)}, bf16[256,512]{1,0:T(8,128)(2,1)S(1)}) custom-call(bf16[512,512]{1,0:T(8,128)(2,1)S(1)} %get-tuple-element.82.q, bf16[256,512]{1,0:T(8,128)(2,1)S(1)} %get-tuple-element.83.k, bf16[256,512]{1,0:T(8,128)(2,1)S(1)} %get-tuple-element.84.v, ...), custom_call_target="tpu_custom_call" | custom-call | flops 2147483648 | bytes 6291456 | tf_op jit(solution)/shard_map/pallas_call | solution.py:437
  134.0 3.2 %shard_map.485 = (f32[512,512]{1,0:T(8,128)S(1)}, bf16[512,512]{1,0:T(8,128)(2,1)S(1)}, bf16[512,512]{1,0:T(8,128)(2,1)S(1)}, f32[8,512]{1,0:T(8,128)S(1)}) custom-call(f32[512,512]{1,0:T(8,128)S(1)} %get-tuple-element.88.du2, bf16[512,512]{1,0:T(8,128)(2,1)S(1)} %get-tuple-element.92.dq2, f32[512,512]{1,0:T(8,128)S(1)} %get-tuple-element.93.normed, ...), custom_call_target="tpu_custom_call" | custom-call | flops 536870912 | bytes 8388608 | tf_op jit(solution)/shard_map/pallas_call | solution.py:650
  138.1 9.9 %shard_map.486 = (bf16[512,512]{1,0:T(8,128)(2,1)S(1)}, bf16[512,512]{1,0:T(8,128)(2,1)S(1)}, bf16[512,512]{1,0:T(8,128)(2,1)S(1)}, bf16[512,512]{1,0:T(8,128)(2,1)S(1)}, bf16[512,512]{1,0:T(8,128)(2,1)S(1)}) custom-call(s32[4]{0:T(128)S(1)} %pad_add_fusion.1.info, bf16[512,512]{1,0:T(8,128)(2,1)S(1)} %copy-done.38, bf16[512,512]{1,0:T(8,128)(2,1)S(1)} %copy-done.40, ...), custom_call_target="tpu_custom_call" | custom-call | flops 8589934592 | bytes 14680064 | tf_op jit(solution)/shard_map/pallas_call | solution.py:402
  148.1 4.4 %shard_map.487 = (bf16[3,512,512]{2,1,0:T(8,128)(2,1)S(1)}, bf16[512,512]{1,0:T(8,128)(2,1)S(1)}, f32[8,512]{1,0:T(8,128)}) custom-call(s32[4]{0:T(128)S(1)} %pad_add_fusion.1.info, bf16[512,512]{1,0:T(8,128)(2,1)} %x.11, bf16[512,512]{1,0:T(8,128)(2,1)} %collective-permute-done.xo, bf16[512,512]{1,0:T(8,128)(2,1)S(1)} %get-tuple-element.100.dq, ...), custom_call_target="tpu_custom_call" | custom-call | flops 1879048192 | bytes 8388608 | tf_op jit(solution)/shard_map/pallas_call | solution.py:718
  154.4 5.0 %shard_map.489 = (bf16[5,512,512]{2,1,0:T(8,128)(2,1)}, f32[128,512]{1,0:T(8,128)S(1)}, bf16[128,512]{1,0:T(8,128)(2,1)S(1)}, f32[8,512]{1,0:T(8,128)S(1)}) custom-call(f32[512,512]{1,0:T(8,128)S(1)} %get-tuple-element.86.first, bf16[512,512]{1,0:T(8,128)(2,1)S(1)} %get-tuple-element.92.dq2, bf16[128,512]{1,0:T(8,128)(2,1)S(1)} %copy-done.9, ...), custom_call_target="tpu_custom_call" | custom-call | flops 1342177280 | bytes 10485760 | tf_op jit(solution)/shard_map/pallas_call | solution.py:681
  162.7 1.9 collective-permute-start.33
  171.6 13.1 %collective-permute-start.36 = (f32[8,512]{1,0:T(8,128)S(1)}, f32[8,512]{1,0:T(8,128)S(1)}, u32[]{:S(2)}, u32[]{:S(2)}) collective-permute-start(f32[8,512]{1,0:T(8,128)S(1)} %add_add_fusion.3), channel_id=1, source_target_pairs={{0,1},{1,0},{2,3},{3,2},{4,5},{5,4},{6,7},{7,6},{8,9},{9,8},{10,11... | collective-permute-start | bytes 49160 | tf_op jit(solution)/shard_map/ppermute | solution.py:51
  184.8 2.4 collective-permute-start.38
  187.2 1.8 collective-permute-start.47
  190.6 2.1 collective-permute-start.49
  193.3 2.1 collective-permute-done.49
  196.1 2.1 collective-permute-start.51
  208.2 9.7 %collective-permute-done.23.back = bf16[512,512]{1,0:T(8,128)(2,1)S(1)} collective-permute-done((bf16[512,512]{1,0:T(8,128)(2,1)S(1)}, bf16[512,512]{1,0:T(8,128)(2,1)S(1)}, u32[]{:S(2)}, u32[]{:S(2)}) %collective-permute-start.23) | collective-permute-done | bytes 524320 | tf_op jit(solution)/shard_map/ppermute | solution.py:57
  218.0 2.0 shard_map.488
  226.4 1.8 collective-permute-done.26
  229.2 2.9 %collective-permute-done.27 = bf16[4,3,64,128]{3,2,1,0:T(8,128)(2,1)S(1)} collective-permute-done((bf16[4,3,64,128]{3,2,1,0:T(8,128)(2,1)S(1)}, bf16[4,3,64,128]{3,2,1,0:T(8,128)(2,1)S(1)}, u32[]{:S(2)}, u32[]{:S(2)}) %collective-permute-start.27) | collective-permute-done | bytes 196640 | tf_op jit(solution)/shard_map/ppermute | solution.py:51
  233.1 6.3 %collective-permute-done.40 = bf16[4,5,64,128]{3,2,1,0:T(8,128)(2,1)S(1)} collective-permute-done((bf16[4,5,64,128]{3,2,1,0:T(8,128)(2,1)S(1)}, bf16[4,5,64,128]{3,2,1,0:T(8,128)(2,1)S(1)}, u32[]{:S(2)}, u32[]{:S(2)}) %collective-permute-start.40) | collective-permute-done | bytes 327712 | tf_op jit(solution)/shard_map/ppermute | solution.py:51
  241.1 3.0 %collective-permute-done.41 = bf16[4,5,64,128]{3,2,1,0:T(8,128)(2,1)S(1)} collective-permute-done((bf16[4,5,64,128]{3,2,1,0:T(8,128)(2,1)S(1)}, bf16[4,5,64,128]{3,2,1,0:T(8,128)(2,1)S(1)}, u32[]{:S(2)}, u32[]{:S(2)}) %collective-permute-start.41) | collective-permute-done | bytes 327712 | tf_op jit(solution)/shard_map/ppermute | solution.py:51
  244.1 2.9 %collective-permute-start.31 = (bf16[3,64,128]{2,1,0:T(8,128)(2,1)S(1)}, bf16[3,64,128]{2,1,0:T(8,128)(2,1)S(1)}, u32[]{:S(2)}, u32[]{:S(2)}) collective-permute-start(bf16[3,64,128]{2,1,0:T(8,128)(2,1)S(1)} %get-tuple-element.147), channel_id=1, source_target_pairs={{0,3},{1,2},{2,1},{3,0},{4,7},{5,6},{6,5},{7,4},{8,11},{9,10},{10,... | collective-permute-start | bytes 147464 | tf_op jit(solution)/shard_map/ppermute | solution.py:51
  248.9 2.3 add_convert_fusion
  252.3 2.7 collective-permute-start.56
  255.1 2.8 collective-permute-start.45
  258.5 3.5 %collective-permute-done.44 = bf16[5,64,128]{2,1,0:T(8,128)(2,1)S(1)} collective-permute-done((bf16[5,64,128]{2,1,0:T(8,128)(2,1)S(1)}, bf16[5,64,128]{2,1,0:T(8,128)(2,1)S(1)}, u32[]{:S(2)}, u32[]{:S(2)}) %collective-permute-start.44) | collective-permute-done | bytes 81952 | tf_op jit(solution)/shard_map/ppermute | solution.py:51
  264.1 5.6 %collective-permute-done.56 = bf16[4,2,64,512]{3,2,1,0:T(8,128)(2,1)S(1)} collective-permute-done((bf16[4,2,64,512]{3,2,1,0:T(8,128)(2,1)S(1)}, bf16[4,2,64,512]{3,2,1,0:T(8,128)(2,1)S(1)}, u32[]{:S(2)}, u32[]{:S(2)}) %collective-permute-start.56) | collective-permute-done | bytes 524320 | tf_op jit(solution)/shard_map/ppermute | solution.py:51
  271.0 5.9 %collective-permute-start.58 = (bf16[2,64,512]{2,1,0:T(8,128)(2,1)S(1)}, bf16[2,64,512]{2,1,0:T(8,128)(2,1)S(1)}, u32[]{:S(2)}, u32[]{:S(2)}) collective-permute-start(bf16[2,64,512]{2,1,0:T(8,128)(2,1)S(1)} %get-tuple-element.136), channel_id=1, source_target_pairs={{0,2},{1,3},{2,0},{3,1},{4,6},{5,7},{6,4},{7,5},{8,10},{9,11},{10,... | collective-permute-start | bytes 393224 | tf_op jit(solution)/shard_map/ppermute | solution.py:51
  277.5 4.7 %collective-permute-done.58 = bf16[2,64,512]{2,1,0:T(8,128)(2,1)S(1)} collective-permute-done((bf16[2,64,512]{2,1,0:T(8,128)(2,1)S(1)}, bf16[2,64,512]{2,1,0:T(8,128)(2,1)S(1)}, u32[]{:S(2)}, u32[]{:S(2)}) %collective-permute-start.58) | collective-permute-done | bytes 131104 | tf_op jit(solution)/shard_map/ppermute | solution.py:51
  (312 shorter events, 88.0 us)
Async XLA Ops:
  1.8 17.3 %collective-permute-start.16 = (bf16[2,64,512]{2,1,0:T(8,128)(2,1)S(1)}, bf16[2,64,512]{2,1,0:T(8,128)(2,1)S(1)}, u32[]{:S(2)}, u32[]{:S(2)}) collective-permute-start(bf16[2,64,512]{2,1,0:T(8,128)(2,1)S(1)} %get-tuple-element.155), channel_id=1, source_target_pairs={{0,1},{1,0},{2,3},{3,2},{4,5},{5,4},{6,7},{7,6},{8,9},{9,8},{10,11... | collective-permute-start | bytes 393224 | tf_op jit(solution)/shard_map/ppermute | solution.py:51
  4.8 14.2 %collective-permute-start.17 = (bf16[2,64,512]{2,1,0:T(8,128)(2,1)S(1)}, bf16[2,64,512]{2,1,0:T(8,128)(2,1)S(1)}, u32[]{:S(2)}, u32[]{:S(2)}) collective-permute-start(bf16[2,64,512]{2,1,0:T(8,128)(2,1)S(1)} %get-tuple-element.155), channel_id=1, source_target_pairs={{0,2},{1,3},{2,0},{3,1},{4,6},{5,7},{6,4},{7,5},{8,10},{9,11},{10,... | collective-permute-start | bytes 393224 | tf_op jit(solution)/shard_map/ppermute | solution.py:51
  7.4 11.6 %collective-permute-start.18 = (bf16[2,64,512]{2,1,0:T(8,128)(2,1)S(1)}, bf16[2,64,512]{2,1,0:T(8,128)(2,1)S(1)}, u32[]{:S(2)}, u32[]{:S(2)}) collective-permute-start(bf16[2,64,512]{2,1,0:T(8,128)(2,1)S(1)} %get-tuple-element.155), channel_id=1, source_target_pairs={{0,3},{1,2},{2,1},{3,0},{4,7},{5,6},{6,5},{7,4},{8,11},{9,10},{10,... | collective-permute-start | bytes 393224 | tf_op jit(solution)/shard_map/ppermute | solution.py:51
  12.4 10.3 %collective-permute-start.1 = (bf16[208,128]{1,0:T(8,128)(2,1)S(1)}, bf16[208,128]{1,0:T(8,128)(2,1)S(1)}, u32[]{:S(2)}, u32[]{:S(2)}) collective-permute-start(bf16[208,128]{1,0:T(8,128)(2,1)S(1)} %get-tuple-element.160), channel_id=1, source_target_pairs={{0,1},{1,0},{2,3},{3,2},{4,5},{5,4},{6,7},{7,6},{8,9},{9,8},{10,11... | collective-permute-start | bytes 159752 | tf_op jit(solution)/shard_map/ppermute | solution.py:51
  13.4 15.9 %collective-permute-start.2 = (bf16[208,128]{1,0:T(8,128)(2,1)S(1)}, bf16[208,128]{1,0:T(8,128)(2,1)S(1)}, u32[]{:S(2)}, u32[]{:S(2)}) collective-permute-start(bf16[208,128]{1,0:T(8,128)(2,1)S(1)} %get-tuple-element.160), channel_id=1, source_target_pairs={{0,2},{1,3},{2,0},{3,1},{4,6},{5,7},{6,4},{7,5},{8,10},{9,11},{10,... | collective-permute-start | bytes 159752 | tf_op jit(solution)/shard_map/ppermute | solution.py:51
  19.1 15.0 %collective-permute-start.19 = (bf16[4,2,64,512]{3,2,1,0:T(8,128)(2,1)S(1)}, bf16[4,2,64,512]{3,2,1,0:T(8,128)(2,1)}, u32[]{:S(2)}, u32[]{:S(2)}) collective-permute-start(bf16[4,2,64,512]{3,2,1,0:T(8,128)(2,1)S(1)} %get-tuple-element.138), channel_id=1, source_target_pairs={{0,8},{1,9},{2,10},{3,11},{4,12},{5,13},{6,14},{7,15},{8,0},{9,1},... | collective-permute-start | bytes 1572872 | tf_op jit(solution)/shard_map/ppermute | solution.py:51
  20.7 20.9 %collective-permute-start.20 = (bf16[4,2,64,512]{3,2,1,0:T(8,128)(2,1)S(1)}, bf16[4,2,64,512]{3,2,1,0:T(8,128)(2,1)}, u32[]{:S(2)}, u32[]{:S(2)}) collective-permute-start(bf16[4,2,64,512]{3,2,1,0:T(8,128)(2,1)S(1)} %get-tuple-element.138), channel_id=1, source_target_pairs={{0,16},{1,17},{2,18},{3,19},{4,20},{5,21},{6,22},{7,23},{8,24},{9,... | collective-permute-start | bytes 1572872 | tf_op jit(solution)/shard_map/ppermute | solution.py:51
  22.2 23.8 %collective-permute-start.21 = (bf16[4,2,64,512]{3,2,1,0:T(8,128)(2,1)S(1)}, bf16[4,2,64,512]{3,2,1,0:T(8,128)(2,1)}, u32[]{:S(2)}, u32[]{:S(2)}) collective-permute-start(bf16[4,2,64,512]{3,2,1,0:T(8,128)(2,1)S(1)} %get-tuple-element.138), channel_id=1, source_target_pairs={{0,24},{1,25},{2,26},{3,27},{4,28},{5,29},{6,30},{7,31},{8,16},{9,... | collective-permute-start | bytes 1572872 | tf_op jit(solution)/shard_map/ppermute | solution.py:51
  22.7 9.0 %collective-permute-start.3 = (bf16[208,128]{1,0:T(8,128)(2,1)S(1)}, bf16[208,128]{1,0:T(8,128)(2,1)S(1)}, u32[]{:S(2)}, u32[]{:S(2)}) collective-permute-start(bf16[208,128]{1,0:T(8,128)(2,1)S(1)} %get-tuple-element.160), channel_id=1, source_target_pairs={{0,3},{1,2},{2,1},{3,0},{4,7},{5,6},{6,5},{7,4},{8,11},{9,10},{10,... | collective-permute-start | bytes 159752 | tf_op jit(solution)/shard_map/ppermute | solution.py:51
  29.3 18.9 %collective-permute-start.9 = (bf16[5,64,128]{2,1,0:T(8,128)(2,1)S(1)}, bf16[5,64,128]{2,1,0:T(8,128)(2,1)S(1)}, u32[]{:S(2)}, u32[]{:S(2)}) collective-permute-start(bf16[5,64,128]{2,1,0:T(8,128)(2,1)S(1)} %bitcast_dynamic-update-slice_fusion), channel_id=1, source_target_pairs={{0,1},{1,0},{2,3},{3,2},{4,5},{5,4},{6,7},{7,6},{8,9},{9,8},{10,11... | collective-permute-start | bytes 245768 | tf_op jit(solution)/shard_map/ppermute | solution.py:51
  31.7 18.9 %collective-permute-start.10 = (bf16[5,64,128]{2,1,0:T(8,128)(2,1)S(1)}, bf16[5,64,128]{2,1,0:T(8,128)(2,1)S(1)}, u32[]{:S(2)}, u32[]{:S(2)}) collective-permute-start(bf16[5,64,128]{2,1,0:T(8,128)(2,1)S(1)} %bitcast_dynamic-update-slice_fusion), channel_id=1, source_target_pairs={{0,2},{1,3},{2,0},{3,1},{4,6},{5,7},{6,4},{7,5},{8,10},{9,11},{10,... | collective-permute-start | bytes 245768 | tf_op jit(solution)/shard_map/ppermute | solution.py:51
  34.2 16.5 %collective-permute-start.11 = (bf16[5,64,128]{2,1,0:T(8,128)(2,1)S(1)}, bf16[5,64,128]{2,1,0:T(8,128)(2,1)S(1)}, u32[]{:S(2)}, u32[]{:S(2)}) collective-permute-start(bf16[5,64,128]{2,1,0:T(8,128)(2,1)S(1)} %bitcast_dynamic-update-slice_fusion), channel_id=1, source_target_pairs={{0,3},{1,2},{2,1},{3,0},{4,7},{5,6},{6,5},{7,4},{8,11},{9,10},{10,... | collective-permute-start | bytes 245768 | tf_op jit(solution)/shard_map/ppermute | solution.py:51
  41.6 10.6 %collective-permute-start.4 = (bf16[4,3,64,128]{3,2,1,0:T(8,128)(2,1)S(1)}, bf16[4,3,64,128]{3,2,1,0:T(8,128)(2,1)S(1)}, u32[]{:S(2)}, u32[]{:S(2)}) collective-permute-start(bf16[4,3,64,128]{3,2,1,0:T(8,128)(2,1)S(1)} %bitcast.179), channel_id=1, source_target_pairs={{0,8},{1,9},{2,10},{3,11},{4,12},{5,13},{6,14},{7,15},{8,0},{9,1},... | collective-permute-start | bytes 589832 | tf_op jit(solution)/shard_map/ppermute | solution.py:51
  48.1 7.6 %collective-permute-start.6 = (bf16[4,3,64,128]{3,2,1,0:T(8,128)(2,1)S(1)}, bf16[4,3,64,128]{3,2,1,0:T(8,128)(2,1)S(1)}, u32[]{:S(2)}, u32[]{:S(2)}) collective-permute-start(bf16[4,3,64,128]{3,2,1,0:T(8,128)(2,1)S(1)} %bitcast.181), channel_id=1, source_target_pairs={{0,24},{1,25},{2,26},{3,27},{4,28},{5,29},{6,30},{7,31},{8,16},{9,... | collective-permute-start | bytes 589832 | tf_op jit(solution)/shard_map/ppermute | solution.py:51
  50.6 49.8 %collective-permute-start.22 = (bf16[4,4,2,64,512]{4,3,2,1,0:T(8,128)(2,1)S(1)}, bf16[4,4,2,64,512]{4,3,2,1,0:T(8,128)(2,1)}, u32[]{:S(2)}, u32[]{:S(2)}) collective-permute-start(bf16[4,4,2,64,512]{4,3,2,1,0:T(8,128)(2,1)S(1)} %pad_maximum_fusion.plane), channel_id=1, source_target_pairs={{0,4},{1,5},{2,6},{3,7},{4,0},{5,1},{6,2},{7,3},{8,12},{9,13},{10,... | collective-permute-start | bytes 6291464 | tf_op jit(solution)/shard_map/ppermute | solution.py:51
  51.6 10.6 %collective-permute-start.12 = (bf16[4,5,64,128]{3,2,1,0:T(8,128)(2,1)S(1)}, bf16[4,5,64,128]{3,2,1,0:T(8,128)(2,1)S(1)}, u32[]{:S(2)}, u32[]{:S(2)}) collective-permute-start(bf16[4,5,64,128]{3,2,1,0:T(8,128)(2,1)S(1)} %get-tuple-element.143), channel_id=1, source_target_pairs={{0,8},{1,9},{2,10},{3,11},{4,12},{5,13},{6,14},{7,15},{8,0},{9,1},... | collective-permute-start | bytes 983048 | tf_op jit(solution)/shard_map/ppermute | solution.py:51
  52.2 16.9 %collective-permute-start.13 = (bf16[4,5,64,128]{3,2,1,0:T(8,128)(2,1)S(1)}, bf16[4,5,64,128]{3,2,1,0:T(8,128)(2,1)S(1)}, u32[]{:S(2)}, u32[]{:S(2)}) collective-permute-start(bf16[4,5,64,128]{3,2,1,0:T(8,128)(2,1)S(1)} %get-tuple-element.143), channel_id=1, source_target_pairs={{0,16},{1,17},{2,18},{3,19},{4,20},{5,21},{6,22},{7,23},{8,24},{9,... | collective-permute-start | bytes 983048 | tf_op jit(solution)/shard_map/ppermute | solution.py:51
  52.7 16.4 %collective-permute-start.14 = (bf16[4,5,64,128]{3,2,1,0:T(8,128)(2,1)S(1)}, bf16[4,5,64,128]{3,2,1,0:T(8,128)(2,1)S(1)}, u32[]{:S(2)}, u32[]{:S(2)}) collective-permute-start(bf16[4,5,64,128]{3,2,1,0:T(8,128)(2,1)S(1)} %get-tuple-element.143), channel_id=1, source_target_pairs={{0,24},{1,25},{2,26},{3,27},{4,28},{5,29},{6,30},{7,31},{8,16},{9,... | collective-permute-start | bytes 983048 | tf_op jit(solution)/shard_map/ppermute | solution.py:51
  55.7 23.3 %collective-permute-start = (bf16[512,512]{1,0:T(8,128)(2,1)}, bf16[512,512]{1,0:T(8,128)(2,1)}, u32[]{:S(2)}, u32[]{:S(2)}) collective-permute-start(bf16[512,512]{1,0:T(8,128)(2,1)} %x.11), channel_id=1, source_target_pairs={{0,1},{2,3},{4,5},{6,7},{8,9},{10,11},{12,13},{14,15},{16,17},{18,... | collective-permute-start | bytes 1572872 | tf_op jit(solution)/shard_map/ppermute | solution.py:57
  62.2 30.5 %collective-permute-start.8 = (bf16[128,512]{1,0:T(8,128)(2,1)S(1)}, bf16[128,512]{1,0:T(8,128)(2,1)}, u32[]{:S(2)}, u32[]{:S(2)}) collective-permute-start(bf16[128,512]{1,0:T(8,128)(2,1)S(1)} %copy-done.9), channel_id=1, source_target_pairs={{0,1},{1,0},{2,3},{3,2},{4,5},{5,4},{6,7},{7,6},{8,9},{9,8},{10,11... | collective-permute-start | bytes 393224 | tf_op jit(solution)/shard_map/ppermute | solution.py:51
  69.1 8.2 %collective-permute-start.7 = (bf16[4,4,3,64,128]{4,3,2,1,0:T(8,128)(2,1)}, bf16[4,4,3,64,128]{4,3,2,1,0:T(8,128)(2,1)}, u32[]{:S(2)}, u32[]{:S(2)}) collective-permute-start(bf16[4,4,3,64,128]{4,3,2,1,0:T(8,128)(2,1)} %pad_maximum_fusion.2.plane), channel_id=1, source_target_pairs={{0,4},{1,5},{2,6},{3,7},{4,0},{5,1},{6,2},{7,3},{8,12},{9,13},{10,... | collective-permute-start | bytes 2359304 | tf_op jit(solution)/shard_map/ppermute | solution.py:51
  69.2 19.7 %collective-permute-start.15 = (bf16[4,4,5,64,128]{4,3,2,1,0:T(8,128)(2,1)S(1)}, bf16[4,4,5,64,128]{4,3,2,1,0:T(8,128)(2,1)}, u32[]{:S(2)}, u32[]{:S(2)}) collective-permute-start(bf16[4,4,5,64,128]{4,3,2,1,0:T(8,128)(2,1)S(1)} %pad_maximum_fusion.1.plane), channel_id=1, source_target_pairs={{0,4},{1,5},{2,6},{3,7},{4,0},{5,1},{6,2},{7,3},{8,12},{9,13},{10,... | collective-permute-start | bytes 3932168 | tf_op jit(solution)/shard_map/ppermute | solution.py:51
  125.1 123.9 %collective-permute-start.53 = (bf16[4,4,2,64,512]{4,3,2,1,0:T(8,128)(2,1)}, bf16[4,4,2,64,512]{4,3,2,1,0:T(8,128)(2,1)}, u32[]{:S(2)}, u32[]{:S(2)}) collective-permute-start(bf16[4,4,2,64,512]{4,3,2,1,0:T(8,128)(2,1)} %get-tuple-element.124), channel_id=1, source_target_pairs={{0,4},{1,5},{2,6},{3,7},{4,0},{5,1},{6,2},{7,3},{8,12},{9,13},{10,... | collective-permute-start | bytes 6291464 | tf_op jit(solution)/shard_map/ppermute | solution.py:51
  153.7 8.3 %collective-permute-start.32 = (f32[8,512]{1,0:T(8,128)}, f32[8,512]{1,0:T(8,128)}, u32[]{:S(2)}, u32[]{:S(2)}) collective-permute-start(f32[8,512]{1,0:T(8,128)} %get-tuple-element.114), channel_id=1, source_target_pairs={{0,4},{1,5},{2,6},{3,7},{4,0},{5,1},{6,2},{7,3},{8,12},{9,13},{10,... | collective-permute-start | bytes 49160 | tf_op jit(solution)/shard_map/ppermute | solution.py:51
  162.7 8.3 %collective-permute-start.33 = (f32[8,512]{1,0:T(8,128)S(1)}, f32[8,512]{1,0:T(8,128)S(1)}, u32[]{:S(2)}, u32[]{:S(2)}) collective-permute-start(f32[8,512]{1,0:T(8,128)S(1)} %add.162), channel_id=1, source_target_pairs={{0,8},{1,9},{2,10},{3,11},{4,12},{5,13},{6,14},{7,15},{8,0},{9,1},... | collective-permute-start | bytes 49160 | tf_op jit(solution)/shard_map/ppermute | solution.py:51
  164.6 7.0 %collective-permute-start.34 = (f32[8,512]{1,0:T(8,128)S(1)}, f32[8,512]{1,0:T(8,128)S(1)}, u32[]{:S(2)}, u32[]{:S(2)}) collective-permute-start(f32[8,512]{1,0:T(8,128)S(1)} %add.162), channel_id=1, source_target_pairs={{0,16},{1,17},{2,18},{3,19},{4,20},{5,21},{6,22},{7,23},{8,24},{9,... | collective-permute-start | bytes 49160 | tf_op jit(solution)/shard_map/ppermute | solution.py:51
  167.0 17.8 %collective-permute-start.46 = (f32[16,512]{1,0:T(8,128)S(1)}, f32[16,512]{1,0:T(8,128)S(1)}, u32[]{:S(2)}, u32[]{:S(2)}) collective-permute-start(f32[16,512]{1,0:T(8,128)S(1)} %select_maximum_fusion), channel_id=1, source_target_pairs={{0,4},{1,5},{2,6},{3,7},{4,0},{5,1},{6,2},{7,3},{8,12},{9,13},{10,... | collective-permute-start | bytes 98312 | tf_op jit(solution)/shard_map/ppermute | solution.py:51
  171.1 52.8 %collective-permute-start.39 = (bf16[4,4,5,64,128]{4,3,2,1,0:T(8,128)(2,1)S(1)}, bf16[4,4,5,64,128]{4,3,2,1,0:T(8,128)(2,1)S(1)}, u32[]{:S(2)}, u32[]{:S(2)}) collective-permute-start(bf16[4,4,5,64,128]{4,3,2,1,0:T(8,128)(2,1)S(1)} %get-tuple-element.117), channel_id=1, source_target_pairs={{0,4},{1,5},{2,6},{3,7},{4,0},{5,1},{6,2},{7,3},{8,12},{9,13},{10,... | collective-permute-start | bytes 3932168 | tf_op jit(solution)/shard_map/ppermute | solution.py:51
  171.6 15.6 %collective-permute-start.36 = (f32[8,512]{1,0:T(8,128)S(1)}, f32[8,512]{1,0:T(8,128)S(1)}, u32[]{:S(2)}, u32[]{:S(2)}) collective-permute-start(f32[8,512]{1,0:T(8,128)S(1)} %add_add_fusion.3), channel_id=1, source_target_pairs={{0,1},{1,0},{2,3},{3,2},{4,5},{5,4},{6,7},{7,6},{8,9},{9,8},{10,11... | collective-permute-start | bytes 49160 | tf_op jit(solution)/shard_map/ppermute | solution.py:51
  200.4 19.6 %collective-permute-start.25 = (bf16[4,4,3,64,128]{4,3,2,1,0:T(8,128)(2,1)S(1)}, bf16[4,4,3,64,128]{4,3,2,1,0:T(8,128)(2,1)S(1)}, u32[]{:S(2)}, u32[]{:S(2)}) collective-permute-start(bf16[4,4,3,64,128]{4,3,2,1,0:T(8,128)(2,1)S(1)} %get-tuple-element.113), channel_id=1, source_target_pairs={{0,4},{1,5},{2,6},{3,7},{4,0},{5,1},{6,2},{7,3},{8,12},{9,13},{10,... | collective-permute-start | bytes 2359304 | tf_op jit(solution)/shard_map/ppermute | solution.py:51
  203.9 14.0 %collective-permute-start.23 = (bf16[512,512]{1,0:T(8,128)(2,1)S(1)}, bf16[512,512]{1,0:T(8,128)(2,1)S(1)}, u32[]{:S(2)}, u32[]{:S(2)}) collective-permute-start(bf16[512,512]{1,0:T(8,128)(2,1)S(1)} %copy-done.31), channel_id=1, source_target_pairs={{1,0},{3,2},{5,4},{7,6},{9,8},{11,10},{13,12},{15,14},{17,16},{19,... | collective-permute-start | bytes 1572872 | tf_op jit(solution)/shard_map/ppermute | solution.py:57
  220.3 7.9 %collective-permute-start.26 = (bf16[4,3,64,128]{3,2,1,0:T(8,128)(2,1)S(1)}, bf16[4,3,64,128]{3,2,1,0:T(8,128)(2,1)S(1)}, u32[]{:S(2)}, u32[]{:S(2)}) collective-permute-start(bf16[4,3,64,128]{3,2,1,0:T(8,128)(2,1)S(1)} %get-tuple-element.131), channel_id=1, source_target_pairs={{0,8},{1,9},{2,10},{3,11},{4,12},{5,13},{6,14},{7,15},{8,0},{9,1},... | collective-permute-start | bytes 589832 | tf_op jit(solution)/shard_map/ppermute | solution.py:51
  222.1 10.0 %collective-permute-start.27 = (bf16[4,3,64,128]{3,2,1,0:T(8,128)(2,1)S(1)}, bf16[4,3,64,128]{3,2,1,0:T(8,128)(2,1)S(1)}, u32[]{:S(2)}, u32[]{:S(2)}) collective-permute-start(bf16[4,3,64,128]{3,2,1,0:T(8,128)(2,1)S(1)} %get-tuple-element.133), channel_id=1, source_target_pairs={{0,16},{1,17},{2,18},{3,19},{4,20},{5,21},{6,22},{7,23},{8,24},{9,... | collective-permute-start | bytes 589832 | tf_op jit(solution)/shard_map/ppermute | solution.py:51
  223.1 9.8 %collective-permute-start.28 = (bf16[4,3,64,128]{3,2,1,0:T(8,128)(2,1)S(1)}, bf16[4,3,64,128]{3,2,1,0:T(8,128)(2,1)S(1)}, u32[]{:S(2)}, u32[]{:S(2)}) collective-permute-start(bf16[4,3,64,128]{3,2,1,0:T(8,128)(2,1)S(1)} %get-tuple-element.132), channel_id=1, source_target_pairs={{0,24},{1,25},{2,26},{3,27},{4,28},{5,29},{6,30},{7,31},{8,16},{9,... | collective-permute-start | bytes 589832 | tf_op jit(solution)/shard_map/ppermute | solution.py:51
  224.6 14.8 %collective-permute-start.40 = (bf16[4,5,64,128]{3,2,1,0:T(8,128)(2,1)S(1)}, bf16[4,5,64,128]{3,2,1,0:T(8,128)(2,1)S(1)}, u32[]{:S(2)}, u32[]{:S(2)}) collective-permute-start(bf16[4,5,64,128]{3,2,1,0:T(8,128)(2,1)S(1)} %get-tuple-element.128), channel_id=1, source_target_pairs={{0,8},{1,9},{2,10},{3,11},{4,12},{5,13},{6,14},{7,15},{8,0},{9,1},... | collective-permute-start | bytes 983048 | tf_op jit(solution)/shard_map/ppermute | solution.py:51
  228.2 15.9 %collective-permute-start.41 = (bf16[4,5,64,128]{3,2,1,0:T(8,128)(2,1)S(1)}, bf16[4,5,64,128]{3,2,1,0:T(8,128)(2,1)S(1)}, u32[]{:S(2)}, u32[]{:S(2)}) collective-permute-start(bf16[4,5,64,128]{3,2,1,0:T(8,128)(2,1)S(1)} %get-tuple-element.130), channel_id=1, source_target_pairs={{0,16},{1,17},{2,18},{3,19},{4,20},{5,21},{6,22},{7,23},{8,24},{9,... | collective-permute-start | bytes 983048 | tf_op jit(solution)/shard_map/ppermute | solution.py:51
  232.1 14.9 %collective-permute-start.42 = (bf16[4,5,64,128]{3,2,1,0:T(8,128)(2,1)S(1)}, bf16[4,5,64,128]{3,2,1,0:T(8,128)(2,1)S(1)}, u32[]{:S(2)}, u32[]{:S(2)}) collective-permute-start(bf16[4,5,64,128]{3,2,1,0:T(8,128)(2,1)S(1)} %get-tuple-element.129), channel_id=1, source_target_pairs={{0,24},{1,25},{2,26},{3,27},{4,28},{5,29},{6,30},{7,31},{8,16},{9,... | collective-permute-start | bytes 983048 | tf_op jit(solution)/shard_map/ppermute | solution.py:51
  233.0 18.5 %collective-permute-start.29 = (bf16[3,64,128]{2,1,0:T(8,128)(2,1)S(1)}, bf16[3,64,128]{2,1,0:T(8,128)(2,1)S(1)}, u32[]{:S(2)}, u32[]{:S(2)}) collective-permute-start(bf16[3,64,128]{2,1,0:T(8,128)(2,1)S(1)} %get-tuple-element.146), channel_id=1, source_target_pairs={{0,1},{1,0},{2,3},{3,2},{4,5},{5,4},{6,7},{7,6},{8,9},{9,8},{10,11... | collective-permute-start | bytes 147464 | tf_op jit(solution)/shard_map/ppermute | solution.py:51
  239.4 12.9 %collective-permute-start.30 = (bf16[3,64,128]{2,1,0:T(8,128)(2,1)S(1)}, bf16[3,64,128]{2,1,0:T(8,128)(2,1)S(1)}, u32[]{:S(2)}, u32[]{:S(2)}) collective-permute-start(bf16[3,64,128]{2,1,0:T(8,128)(2,1)S(1)} %get-tuple-element.148), channel_id=1, source_target_pairs={{0,2},{1,3},{2,0},{3,1},{4,6},{5,7},{6,4},{7,5},{8,10},{9,11},{10,... | collective-permute-start | bytes 147464 | tf_op jit(solution)/shard_map/ppermute | solution.py:51
  244.1 10.9 %collective-permute-start.31 = (bf16[3,64,128]{2,1,0:T(8,128)(2,1)S(1)}, bf16[3,64,128]{2,1,0:T(8,128)(2,1)S(1)}, u32[]{:S(2)}, u32[]{:S(2)}) collective-permute-start(bf16[3,64,128]{2,1,0:T(8,128)(2,1)S(1)} %get-tuple-element.147), channel_id=1, source_target_pairs={{0,3},{1,2},{2,1},{3,0},{4,7},{5,6},{6,5},{7,4},{8,11},{9,10},{10,... | collective-permute-start | bytes 147464 | tf_op jit(solution)/shard_map/ppermute | solution.py:51
  247.3 7.8 %collective-permute-start.43 = (bf16[5,64,128]{2,1,0:T(8,128)(2,1)S(1)}, bf16[5,64,128]{2,1,0:T(8,128)(2,1)S(1)}, u32[]{:S(2)}, u32[]{:S(2)}) collective-permute-start(bf16[5,64,128]{2,1,0:T(8,128)(2,1)S(1)} %get-tuple-element.139), channel_id=1, source_target_pairs={{0,1},{1,0},{2,3},{3,2},{4,5},{5,4},{6,7},{7,6},{8,9},{9,8},{10,11... | collective-permute-start | bytes 245768 | tf_op jit(solution)/shard_map/ppermute | solution.py:51
  251.4 11.9 %collective-permute-start.54 = (bf16[4,2,64,512]{3,2,1,0:T(8,128)(2,1)S(1)}, bf16[4,2,64,512]{3,2,1,0:T(8,128)(2,1)S(1)}, u32[]{:S(2)}, u32[]{:S(2)}) collective-permute-start(bf16[4,2,64,512]{3,2,1,0:T(8,128)(2,1)S(1)} %get-tuple-element.125), channel_id=1, source_target_pairs={{0,8},{1,9},{2,10},{3,11},{4,12},{5,13},{6,14},{7,15},{8,0},{9,1},... | collective-permute-start | bytes 1572872 | tf_op jit(solution)/shard_map/ppermute | solution.py:51
  251.5 12.6 %collective-permute-start.55 = (bf16[4,2,64,512]{3,2,1,0:T(8,128)(2,1)S(1)}, bf16[4,2,64,512]{3,2,1,0:T(8,128)(2,1)S(1)}, u32[]{:S(2)}, u32[]{:S(2)}) collective-permute-start(bf16[4,2,64,512]{3,2,1,0:T(8,128)(2,1)S(1)} %get-tuple-element.127), channel_id=1, source_target_pairs={{0,16},{1,17},{2,18},{3,19},{4,20},{5,21},{6,22},{7,23},{8,24},{9,... | collective-permute-start | bytes 1572872 | tf_op jit(solution)/shard_map/ppermute | solution.py:51
  252.3 17.4 %collective-permute-start.56 = (bf16[4,2,64,512]{3,2,1,0:T(8,128)(2,1)S(1)}, bf16[4,2,64,512]{3,2,1,0:T(8,128)(2,1)S(1)}, u32[]{:S(2)}, u32[]{:S(2)}) collective-permute-start(bf16[4,2,64,512]{3,2,1,0:T(8,128)(2,1)S(1)} %get-tuple-element.126), channel_id=1, source_target_pairs={{0,24},{1,25},{2,26},{3,27},{4,28},{5,29},{6,30},{7,31},{8,16},{9,... | collective-permute-start | bytes 1572872 | tf_op jit(solution)/shard_map/ppermute | solution.py:51
  255.0 7.0 %collective-permute-start.44 = (bf16[5,64,128]{2,1,0:T(8,128)(2,1)S(1)}, bf16[5,64,128]{2,1,0:T(8,128)(2,1)S(1)}, u32[]{:S(2)}, u32[]{:S(2)}) collective-permute-start(bf16[5,64,128]{2,1,0:T(8,128)(2,1)S(1)} %get-tuple-element.141), channel_id=1, source_target_pairs={{0,2},{1,3},{2,0},{3,1},{4,6},{5,7},{6,4},{7,5},{8,10},{9,11},{10,... | collective-permute-start | bytes 245768 | tf_op jit(solution)/shard_map/ppermute | solution.py:51
  255.1 6.9 %collective-permute-start.45 = (bf16[5,64,128]{2,1,0:T(8,128)(2,1)S(1)}, bf16[5,64,128]{2,1,0:T(8,128)(2,1)S(1)}, u32[]{:S(2)}, u32[]{:S(2)}) collective-permute-start(bf16[5,64,128]{2,1,0:T(8,128)(2,1)S(1)} %get-tuple-element.140), channel_id=1, source_target_pairs={{0,3},{1,2},{2,1},{3,0},{4,7},{5,6},{6,5},{7,4},{8,11},{9,10},{10,... | collective-permute-start | bytes 245768 | tf_op jit(solution)/shard_map/ppermute | solution.py:51
  270.0 7.5 %collective-permute-start.57 = (bf16[2,64,512]{2,1,0:T(8,128)(2,1)S(1)}, bf16[2,64,512]{2,1,0:T(8,128)(2,1)S(1)}, u32[]{:S(2)}, u32[]{:S(2)}) collective-permute-start(bf16[2,64,512]{2,1,0:T(8,128)(2,1)S(1)} %get-tuple-element.134), channel_id=1, source_target_pairs={{0,1},{1,0},{2,3},{3,2},{4,5},{5,4},{6,7},{7,6},{8,9},{9,8},{10,11... | collective-permute-start | bytes 393224 | tf_op jit(solution)/shard_map/ppermute | solution.py:51
  271.0 11.2 %collective-permute-start.58 = (bf16[2,64,512]{2,1,0:T(8,128)(2,1)S(1)}, bf16[2,64,512]{2,1,0:T(8,128)(2,1)S(1)}, u32[]{:S(2)}, u32[]{:S(2)}) collective-permute-start(bf16[2,64,512]{2,1,0:T(8,128)(2,1)S(1)} %get-tuple-element.136), channel_id=1, source_target_pairs={{0,2},{1,3},{2,0},{3,1},{4,6},{5,7},{6,4},{7,5},{8,10},{9,11},{10,... | collective-permute-start | bytes 393224 | tf_op jit(solution)/shard_map/ppermute | solution.py:51
  (83 other events, 912.7 us)

commit v2 on v1

v2 whole, which is shorter than its diff:
```python
import functools

import jax
import jax.numpy as jnp
from jax import lax
from jax.experimental import pallas as pl
from jax.experimental.pallas import tpu as pltpu
from jax.sharding import PartitionSpec as P

HD = 64
LEN = 1024
MEM = 256
PAIR = 128
BLOCK = 256
BACK_BLOCK = 512

EPSILON = 1e-05
MASKED = -1e30
SCALE = float(HD) ** (-0.5)

F32 = jnp.float32
BF16 = jnp.bfloat16
NN = (((1,), (0,)), ((), ()))
NT = (((1,), (1,)), ((), ()))
TN = (((0,), (0,)), ((), ()))
SMEM = pl.BlockSpec(memory_space=pltpu.SMEM)
ANY = pl.BlockSpec(memory_space=pl.ANY)
VMEM = pl.BlockSpec(memory_space=pltpu.VMEM)


def mm(left_side, right_side, dims):
    return lax.dot_general(left_side, right_side, dims, preferred_element_type=F32)


def shaped(shape, dtype):
    return jax.ShapeDtypeStruct(shape, dtype)


def cost(macs, moved):
    return pl.CostEstimate(flops=macs // 64, bytes_accessed=moved // 64, transcendentals=0)


def limit(mebibytes):
    return pltpu.CompilerParams(vmem_limit_bytes=mebibytes << 20)


def far(*arrays):
    return [pltpu.with_memory_space_constraint(array, pltpu.HBM) for array in arrays]


def swap(array, dp_mask, tensor_mask):
    nd, nt = lax.axis_size("dp"), lax.axis_size("tensor")
    pairs = [
        (d * nt + t, (d ^ dp_mask) * nt + (t ^ tensor_mask)) for d in range(nd) for t in range(nt)
    ]
    return lax.ppermute(array, ("dp", "tensor"), pairs)


def hand_over(array, parity, step):
    nd, nt = lax.axis_size("dp"), lax.axis_size("tensor")
    pairs = [(d * nt + t, d * nt + t + step) for d in range(nd) for t in range(parity, nt, 2)]
    return lax.ppermute(array, ("dp", "tensor"), pairs)


def tree_sum(terms):
    while len(terms) > 1:
        terms = [terms[i] + terms[i + 1] for i in range(0, len(terms), 2)]
    return terms[0]


def doubled(line, bits):
    for bit in bits:
        line = jnp.concatenate([line, swap(line, 0, bit)])
    return line


def over_planes(line):
    return [line] + [swap(line, 2 * j, 0) for j in range(1, lax.axis_size("dp") // 2)]


def both_cores(planes, *others):
    plane = jnp.stack([after(planes[0], *others)] + planes[1:])
    return plane, swap(plane, 1, 0)


def rounded(values):
    return lax.optimization_barrier(values.astype(BF16))


def added(mine, other):
    return rounded(mine.astype(F32) + other.astype(F32))


def joined(arrays):
    return arrays[0] if len(arrays) == 1 else jnp.concatenate(arrays)


class Halves:
    def __init__(self, groups, r, rider):
        self.planes, self.nt = lax.axis_size("dp") // 2, lax.axis_size("tensor")
        self.groups, self.r, self.rider = groups, r, rider
        self.sizes = [self.nt * count * r for count in groups]
        self.total = self.planes * sum(self.sizes) + rider

    def parts(self, keep, got):
        pieces, lo = [], 0
        for size in self.sizes:
            cut = [slice(lo + j * size, lo + j * size + size) for j in range(self.planes)]
            pieces.append([added(keep[rows], got[rows]) for rows in cut])
            lo += self.planes * size
        return pieces, added(keep[lo:], got[lo:]) if self.rider else None

    def step(self, pieces, rider, index):
        count = self.planes.bit_length() - 1
        results = []
        for group, held in enumerate(pieces):
            bit = 1 << (index if group % 2 == 0 else count - 1 - index)
            stay = [j for j in held if not j & bit]
            carry = rider is not None and group == len(pieces) - 1
            sent = joined([held[j | bit] for j in stay] + ([rider] if carry else []))
            results.append((held, stay, carry, swap(sent, 2 * bit, 0)))
        return results

    def settle(self, moves, rider):
        pieces = []
        for group, (held, stay, carry, got) in enumerate(moves):
            size = self.sizes[group]
            pieces.append(
                {j: added(held[j], got[i * size : i * size + size]) for i, j in enumerate(stay)}
            )
            if carry:
                rider = added(rider, got[len(stay) * size :])
        return pieces, rider

    def line_parts(self, pieces, rider):
        parts = []
        for k in range(self.nt):
            rows = []
            for group, count in enumerate(self.groups):
                size = count * self.r
                rows.append(pieces[group][0][k * size : k * size + size])
            parts.append(joined(rows + ([rider] if rider is not None else [])))
        return parts


def direct_plane(pieces, rider):
    sent = [joined([piece, rider]) for piece in pieces]
    got = [sent[0]] + [swap(part, 2 * j, 0) for j, part in enumerate(sent) if j]
    total = rounded(tree_sum([part.astype(F32) for part in got]))
    return total[: pieces[0].shape[0]], total[pieces[0].shape[0] :]


def line_swaps(parts):
    return [parts[0]] + [swap(part, 0, k) for k, part in enumerate(parts) if k]


def line_sum(parts):
    return tree_sum([part.astype(F32) for part in parts])


def after(array, *others):
    return lax.optimization_barrier((array,) + others)[0]


def slot_blocks(info, planes, nt, slots=True):
    for j in range(planes):
        for c in range(2):
            d = jnp.bitwise_xor(info[2], 2 * j + c)
            for s in range(nt):
                yield j, c, s, d, jnp.bitwise_xor(info[3], s) if slots else s


def assemble_kernel(info, plane, sibling, whole, *, slots):
    planes, nt, n, r, w = plane.shape
    for j, c, s, d, t in slot_blocks(info, planes, nt, slots):
        rows = pl.ds(pl.multiple_of(d * r, r), r)
        columns = pl.ds(pl.multiple_of(t * w, w), w) if slots else slice(t * w, t * w + w)
        for i in range(n):
            whole[i, rows, columns] = (plane, sibling)[c][j, s, i]


def aligned(r, w):
    return w % PAIR == 0 and r % 16 == 0


def assemble(info, plane, sibling, slots=True):
    planes, nt, n, r, w = plane.shape
    nd = 2 * planes
    if aligned(r, w):
        return pl.pallas_call(
            functools.partial(assemble_kernel, slots=slots),
            out_shape=shaped((n, nd * r, nt * w), BF16),
            in_specs=[SMEM, VMEM, VMEM],
            out_specs=VMEM,
            compiler_params=limit(18),
            cost_estimate=cost(0, 4 * plane.size * 2),
        )(info, plane, sibling)
    full = jnp.stack([plane, sibling], axis=1).reshape(nd, nt, n, r, w)
    full = jnp.take(full, jnp.bitwise_xor(jnp.arange(nd), info[2]), axis=0)
    if slots:
        full = jnp.take(full, jnp.bitwise_xor(jnp.arange(nt), info[3]), axis=1)
    return full.transpose(2, 0, 3, 1, 4).reshape(n, nd * r, nt * w)


def disperse_kernel(info, whole, rider, keep, send, *, halves):
    n, r, w = whole.shape[0], halves.r, whole.shape[2] // halves.nt
    for j, c, s, d, t in slot_blocks(info, halves.planes, halves.nt):
        rows = pl.ds(pl.multiple_of(d * r, r), r)
        columns = pl.ds(pl.multiple_of(t * w, w), w)
        base, first = 0, 0
        for count, size in zip(halves.groups, halves.sizes):
            for i in range(count):
                lo = base + j * size + (s * count + i) * r
                (keep, send)[c][lo : lo + r, :] = whole[first + i, rows, columns]
            base += halves.planes * size
            first += count
    if halves.rider:
        for target in (keep, send):
            target[halves.total - halves.rider :, :] = rider[...]


def disperse(info, whole, groups, rider):
    nd, nt = lax.axis_size("dp"), lax.axis_size("tensor")
    n, r, w = whole.shape[0], whole.shape[1] // nd, whole.shape[2] // nt
    rider = rider.astype(BF16).reshape(-1, w)
    halves = Halves(groups, r, rider.shape[0])
    if aligned(r, w):
        flat = shaped((halves.total, w), BF16)
        if rider.shape[0] == 0:
            rider = jnp.zeros((16, w), BF16)
        keep, send = pl.pallas_call(
            functools.partial(disperse_kernel, halves=halves),
            out_shape=(flat, flat),
            in_specs=[SMEM, VMEM, VMEM],
            out_specs=(VMEM, VMEM),
            compiler_params=limit(18),
            cost_estimate=cost(0, 2 * whole.size * 2),
        )(info, whole, rider)
        return keep, send, halves
    full = whole.reshape(n, nd, r, nt, w).transpose(1, 3, 0, 2, 4)
    full = jnp.take(full, jnp.bitwise_xor(jnp.arange(nd), info[2]), axis=0)
    full = jnp.take(full, jnp.bitwise_xor(jnp.arange(nt), info[3]), axis=1)
    full = full.reshape(nd // 2, 2, nt, n, r, w)
    flats = []
    for c in range(2):
        rows, first = [], 0
        for count in groups:
            rows.append(full[:, c, :, first : first + count].reshape(-1, w))
            first += count
        flats.append(jnp.concatenate(rows + [rider]))
    return flats[0], flats[1], halves


def pack_kernel(wq, wk, wv, *rest):
    vectors, out = rest[:-1], rest[-1]
    r, w = wq.shape
    for i, block in enumerate((wq, wk, wv)):
        out[i * r : (i + 1) * r, :] = block[...]
    row = lax.broadcasted_iota(jnp.int32, (16, w), 0)
    filled = jnp.zeros((16, w), F32)
    count = 0
    for vector in vectors:
        for lo in range(0, vector.shape[1], w):
            filled = jnp.where(row == count, vector[:, lo : lo + w].astype(F32), filled)
            count += 1
    out[3 * r :, :] = filled.astype(BF16)


def pack(blocks, vectors):
    r, w = blocks[0].shape
    if aligned(r, w):
        return pl.pallas_call(
            pack_kernel,
            out_shape=shaped((3 * r + 16, w), BF16),
            in_specs=[VMEM] * (3 + len(vectors)),
            out_specs=VMEM,
            cost_estimate=cost(0, 8 * r * w * 2),
        )(*blocks, *[vector.reshape(1, -1) for vector in vectors])
    rows = jnp.concatenate(vectors).reshape(-1, w)
    return jnp.concatenate(list(blocks) + [jnp.pad(rows, ((0, 16 - rows.shape[0]), (0, 0)))])


def pack_rest_kernel(wo, wq, wk, wv, co, fi, fo, middle, feed):
    for i, block in enumerate((wo, wq, wk, wv, co)):
        middle[i] = block[...]
    feed[0] = fi[...]
    feed[1] = fo[...]


def pack_rest(middle, feed):
    if aligned(*middle[0].shape):
        return pl.pallas_call(
            pack_rest_kernel,
            out_shape=(
                shaped((len(middle),) + middle[0].shape, BF16),
                shaped((len(feed),) + feed[0].shape, BF16),
            ),
            in_specs=[VMEM] * (len(middle) + len(feed)),
            out_specs=(VMEM, VMEM),
            cost_estimate=cost(0, 8 * feed[0].size * 2),
        )(*middle, *feed)
    return jnp.stack(middle), jnp.stack(feed)


def spread_kernel(info, riders, small, hidden):
    nt, _, w = riders.shape
    for s in range(nt):
        t = jnp.bitwise_xor(info[3], s)
        block = riders[s].astype(F32)
        small[:, pl.ds(pl.multiple_of(t * w, w), w)] = block
        for i in range(4):
            hidden[:, pl.ds(pl.multiple_of((4 * t + i) * w, w), w)] = block[4 + i : 5 + i]


def spread(info, riders):
    nt, _, w = riders.shape
    if aligned(16, w):
        return pl.pallas_call(
            spread_kernel,
            out_shape=(shaped((16, nt * w), F32), shaped((1, 4 * nt * w), F32)),
            in_specs=[SMEM, VMEM],
            out_specs=(VMEM, VMEM),
            cost_estimate=cost(0, 64 * nt * w),
        )(info, riders)
    full = jnp.take(riders, jnp.bitwise_xor(jnp.arange(nt), info[3]), axis=0).astype(F32)
    return full.transpose(1, 0, 2).reshape(16, nt * w), full[:, 4:8].reshape(1, -1)


def norm_forward(summed):
    row_mean = jnp.mean(summed, axis=-1, keepdims=True)
    centred = summed - row_mean
    variance = jnp.mean(centred * centred, axis=-1, keepdims=True)
    inverse = lax.rsqrt(variance + EPSILON)
    return centred * inverse, inverse


def norm_backward(grad_out, normed, inverse, norm_gain):
    grad_normed = grad_out * norm_gain
    return inverse * (
        grad_normed
        - jnp.mean(grad_normed, axis=-1, keepdims=True)
        - normed * jnp.mean(grad_normed * normed, axis=-1, keepdims=True)
    )


def column_sum(values):
    return jnp.sum(values.astype(F32), axis=0, keepdims=True)


def head_lanes(e):
    lane = lax.broadcasted_iota(jnp.int32, (1, PAIR), 1)
    chosen = (lane < HD) if e == 0 else (lane >= HD)
    return jnp.where(chosen, 1.0, 0.0)


def join_heads(first, second):
    lane = lax.broadcasted_iota(jnp.int32, first.shape, 1)
    return jnp.where(lane < HD, first, second)


def attend_forward(q, segments, contexts, logs, lo):
    rows = slice(lo, lo + BLOCK)
    results = []
    for e in range(2):
        query = q[rows, :] * head_lanes(e).astype(BF16)
        scores = [edit(mm(query, k, NT)) for k, _, edit in segments]
        peak = functools.reduce(
            jnp.maximum, [jnp.max(piece, axis=-1, keepdims=True) for piece in scores]
        )
        total = None
        for piece, (_, v, _) in zip(scores, segments):
            weights = jnp.exp(piece - peak).astype(BF16)
            wide = jnp.concatenate([v, jnp.ones(v.shape, BF16)], axis=1)
            part = mm(weights, wide, NN)
            total = part if total is None else total + part
        row_total = total[:, PAIR:]
        results.append((total[:, :PAIR] / row_total, peak + jnp.log(row_total)))
    contexts[rows, :] = join_heads(results[0][0], results[1][0]).astype(BF16)
    logs[rows, :] = join_heads(results[0][1], results[1][1])


def attend_backward(q, grad, ctx, logs, segments, grad_query, lo):
    rows = slice(lo, lo + BACK_BLOCK)
    grad_rows = grad[rows, :]
    product = grad_rows.astype(F32) * ctx[rows, :].astype(F32)
    query_rows = q[rows, :]
    query_turned = jnp.transpose(query_rows)
    grad_turned = jnp.transpose(grad_rows)
    total = None
    for e in range(2):
        lanes = head_lanes(e)
        low_lanes = lanes.astype(BF16)
        delta = jnp.sum(product * lanes, axis=-1, keepdims=True)
        row_log = logs[rows, e * HD : e * HD + 1]
        grad_low = grad_rows * low_lanes
        query = query_rows * low_lanes
        for k, v, edit, add in segments:
            weights = jnp.exp(edit(mm(query, k, NT)) - row_log)
            slope = mm(grad_low, v, NT) - delta
            grad_scores = (weights * slope).astype(BF16)
            part = mm(grad_scores, k * low_lanes, NN)
            total = part if total is None else total + part
            head = slice(e * HD, e * HD + HD)
            add(
                head,
                mm(query_turned[head], grad_scores, NN),
                mm(grad_turned[head], weights.astype(BF16), NN),
            )
    grad_query[rows, :] = (total * SCALE).astype(BF16)


def same(scores):
    return scores


def masked(lo, col_lo, prefix_len):
    def edit(scores):
        row = lo + lax.broadcasted_iota(jnp.int32, scores.shape, 0)
        col = col_lo + lax.broadcasted_iota(jnp.int32, scores.shape, 1)
        allowed = col <= row
        if prefix_len is not None:
            allowed = allowed | (col < prefix_len)
        return jnp.where(allowed, scores, MASKED)

    return edit


def adder(keys, values, col_lo, width):
    def add(head, part_keys, part_values):
        keys[head, col_lo : col_lo + width] += part_keys
        values[head, col_lo : col_lo + width] += part_values

    return add


def self_forward_kernel(info, q, k, v, ko, vo, ctx, logs):
    tokens = q.shape[0]

    @pl.when(info[0] == 0)
    def _():
        for lo in range(0, tokens, BLOCK):
            attend_forward(q, [(k[...], v[...], masked(lo, 0, info[1]))], ctx, logs, lo)

    @pl.when(info[0] != 0)
    def _():
        for lo in range(0, tokens, BLOCK):
            near = slice(lo, lo + BLOCK)
            segments = [(ko[...], vo[...], same)]
            if lo:
                segments.append((k[:lo, :], v[:lo, :], same))
            segments.append((k[near, :], v[near, :], masked(lo, lo, None)))
            attend_forward(q, segments, ctx, logs, lo)


def self_backward_kernel(
    info, q, k, v, ko, vo, ctx, logs, low, w, dq, dk, dv, dko, dvo, ak, av, ako, avo, grad
):
    tokens = q.shape[0]
    ak[...] = jnp.zeros_like(ak)
    av[...] = jnp.zeros_like(av)
    grad[...] = mm(low[...], w[0], NN).astype(BF16)

    @pl.when(info[0] == 0)
    def _():
        for lo in range(0, tokens, BACK_BLOCK):
            segments = [(k[...], v[...], masked(lo, 0, info[1]), adder(ak, av, 0, tokens))]
            attend_backward(q, grad, ctx, logs, segments, dq, lo)

    @pl.when(info[0] != 0)
    def _():
        ako[...] = jnp.zeros_like(ako)
        avo[...] = jnp.zeros_like(avo)
        for lo in range(0, tokens, BACK_BLOCK):
            near = slice(lo, lo + BACK_BLOCK)
            segments = [(ko[...], vo[...], same, adder(ako, avo, 0, tokens))]
            if lo:
                segments.append((k[:lo, :], v[:lo, :], same, adder(ak, av, 0, lo)))
            segments.append(
                (k[near, :], v[near, :], masked(lo, lo, None), adder(ak, av, lo, BACK_BLOCK))
            )
            attend_backward(q, grad, ctx, logs, segments, dq, lo)
        dko[...] = jnp.transpose(ako[...]).astype(BF16)
        dvo[...] = jnp.transpose(avo[...]).astype(BF16)

    dk[...] = jnp.transpose(ak[...]).astype(BF16)
    dv[...] = jnp.transpose(av[...]).astype(BF16)


def cross_forward_kernel(q, k, v, ctx, logs):
    for lo in range(0, q.shape[0], BLOCK):
        attend_forward(q, [(k[...], v[...], same)], ctx, logs, lo)


def cross_backward_kernel(q, k, v, ctx, logs, low, w, dq, dk, dv, ak, av, grad):
    ak[...] = jnp.zeros_like(ak)
    av[...] = jnp.zeros_like(av)
    grad[...] = mm(low[...], w[0], NN).astype(BF16)
    for lo in range(0, q.shape[0], BACK_BLOCK):
        segments = [(k[...], v[...], same, adder(ak, av, 0, k.shape[0]))]
        attend_backward(q, grad, ctx, logs, segments, dq, lo)
    dk[...] = jnp.transpose(ak[...]).astype(BF16)
    dv[...] = jnp.transpose(av[...]).astype(BF16)


def lanes_of(rows, first=0):
    return pl.BlockSpec((rows, PAIR), lambda h: (0, first + h))


def output_columns(slot, width, first=0):
    return pl.BlockSpec((1, width, PAIR), lambda h: (slot, 0, first + h))


def self_forward(info, q, k, v, ko, vo):
    tokens, width = q.shape
    row = lanes_of(tokens)
    return pl.pallas_call(
        self_forward_kernel,
        grid=(width // PAIR,),
        out_shape=(shaped((tokens, width), BF16), shaped((tokens, width), F32)),
        in_specs=[SMEM] + [row] * 5,
        out_specs=(row, row),
        compiler_params=limit(16),
        cost_estimate=cost(width // HD * tokens * tokens * 2 * 256 * 2, 5 << 20),
    )(info, q, k, v, ko, vo)


def self_backward(info, q, k, v, ko, vo, ctx, logs, low, w, first, pairs):
    tokens, width = q.shape
    row = lanes_of(tokens, first)
    out = shaped((tokens, pairs * PAIR), BF16)
    return pl.pallas_call(
        self_backward_kernel,
        grid=(pairs,),
        out_shape=(out,) * 5,
        in_specs=[SMEM] + [row] * 7 + [VMEM, output_columns(0, width, first)],
        out_specs=(lanes_of(tokens),) * 5,
        scratch_shapes=[pltpu.VMEM((PAIR, tokens), F32)] * 4 + [pltpu.VMEM((tokens, PAIR), BF16)],
        compiler_params=limit(16),
        cost_estimate=cost(width // HD * tokens * tokens * 256 * 5, 8 << 20),
    )(info, *far(q, k, v, ko, vo, ctx, logs), low, *far(w))


def cross_forward(q, k, v):
    tokens, width = q.shape
    rows = k.shape[0]
    return pl.pallas_call(
        cross_forward_kernel,
        grid=(width // PAIR,),
        out_shape=(shaped((tokens, width), BF16), shaped((tokens, width), F32)),
        in_specs=[lanes_of(tokens), lanes_of(rows), lanes_of(rows)],
        out_specs=(lanes_of(tokens), lanes_of(tokens)),
        compiler_params=limit(16),
        cost_estimate=cost(width // HD * tokens * rows * 256 * 2, 3 << 20),
    )(q, k, v)


def cross_backward(q, k, v, ctx, logs, low, w):
    tokens, width = q.shape
    rows = k.shape[0]
    small = shaped((rows, width), BF16)
    return pl.pallas_call(
        cross_backward_kernel,
        grid=(width // PAIR,),
        out_shape=(shaped((tokens, width), BF16), small, small),
        in_specs=[lanes_of(tokens), lanes_of(rows), lanes_of(rows)]
        + [lanes_of(tokens)] * 2
        + [VMEM, output_columns(4, width)],
        out_specs=(lanes_of(tokens), lanes_of(rows), lanes_of(rows)),
        scratch_shapes=[pltpu.VMEM((PAIR, rows), F32)] * 2 + [pltpu.VMEM((tokens, PAIR), BF16)],
        compiler_params=limit(16),
        cost_estimate=cost(width // HD * tokens * rows * 256 * 5, 4 << 20),
    )(*far(q, k, v, ctx, logs), low, *far(w))


def project_self_kernel(info, x, xo, w, b, q, k, v, ko, vo):
    rows = x[...]
    q[...] = (mm(rows, w[0], NN) + b[0:1, :]).astype(BF16) * jnp.asarray(SCALE, BF16)
    k[...] = mm(rows, w[1], NN).astype(BF16)
    v[...] = (mm(rows, w[2], NN) + b[1:2, :]).astype(BF16)

    @pl.when(info[0] != 0)
    def _():
        other = xo[...]
        ko[...] = mm(other, w[1], NN).astype(BF16)
        vo[...] = (mm(other, w[2], NN) + b[1:2, :]).astype(BF16)


def project_self(info, x, xo, w, b):
    low = shaped(x.shape, BF16)
    return pl.pallas_call(
        project_self_kernel,
        out_shape=(low,) * 5,
        in_specs=[SMEM] + [VMEM] * 4,
        compiler_params=limit(16),
        cost_estimate=cost(5 * x.size * x.shape[1], 5 << 20),
    )(info, x, xo, w, b)


def first_norm_kernel(
    ctx, x, mem, memo, w, ob, gain, bias, b, first, normed, inverse, q, k, v
):
    summed = x[...].astype(F32) + mm(ctx[...], w[0], NT) + ob[...].astype(F32)
    n, r = norm_forward(summed)
    out = n * gain[...].astype(F32) + bias[...].astype(F32)
    normed[...] = n
    inverse[...] = r
    first[...] = out
    q[...] = (mm(out.astype(BF16), w[1], NN) + b[2:3, :]).astype(BF16) * jnp.asarray(SCALE, BF16)
    rows = mem.shape[0]
    for source, lo in ((mem, 0), (memo, rows)):
        k[lo : lo + rows, :] = mm(source[...], w[2], NN).astype(BF16)
        v[lo : lo + rows, :] = (mm(source[...], w[3], NN) + b[3:4, :]).astype(BF16)


def first_norm(ctx, x, mem, memo, w, ob, gain, bias, b):
    rows = 2 * mem.shape[0]
    tokens, width = x.shape
    full = shaped(x.shape, F32)
    return pl.pallas_call(
        first_norm_kernel,
        out_shape=(
            full,
            full,
            shaped((tokens, 1), F32),
            shaped(x.shape, BF16),
            shaped((rows, width), BF16),
            shaped((rows, width), BF16),
        ),
        in_specs=[VMEM] * 9,
        compiler_params=limit(16),
        cost_estimate=cost(3 * x.size * width, 8 << 20),
    )(ctx, x, mem, memo, w, ob, gain, bias, b)


def feed_kernel(
    ctx,
    first,
    cot,
    wo,
    wf,
    ob,
    gain2,
    bias2,
    fib,
    fob,
    gain3,
    bias3,
    out,
    dw,
    du2,
    db2,
    sums,
    hsum,
    act,
    slope,
    acc,
    second,
):
    tokens, width = first.shape
    chunks = wf.shape[2] // width
    summed = first[...] + mm(ctx[...], wo[4], NT) + ob[...].astype(F32)
    n2, r2 = norm_forward(summed)
    out2 = n2 * gain2[...].astype(F32) + bias2[...].astype(F32)
    second[...] = out2.astype(BF16)
    acc[...] = out2 + fob[...].astype(F32)

    @pl.loop(0, chunks)
    def _(c):
        cols = pl.ds(pl.multiple_of(c * width, width), width)
        hidden = mm(second[...], wf[0, :, cols], NN) + fib[:, cols]
        gate = 1.0 / (1.0 + jnp.exp(-hidden))
        active = (hidden * gate).astype(BF16)
        act[:, cols] = active
        slope[:, cols] = (gate * (1.0 + hidden * (1.0 - gate))).astype(BF16)
        acc[...] += mm(active, wf[1, :, cols], NT)

    n3, r3 = norm_forward(acc[...])
    out[...] = (n3 * gain3[...].astype(F32) + bias3[...].astype(F32)).astype(BF16)
    dy = cot[...].astype(F32)
    du3 = norm_backward(dy, n3, r3, gain3[...].astype(F32))
    db3 = du3.astype(BF16)
    sums[6:7, :] = column_sum(db3)
    sums[7:8, :] = column_sum(dy * n3)
    sums[8:9, :] = column_sum(dy)
    acc[...] = du3
    db2[...] = db3

    @pl.loop(0, chunks)
    def _(c):
        cols = pl.ds(pl.multiple_of(c * width, width), width)
        back = db2[...]
        dact = mm(back, wf[1, :, cols], NN)
        dhid = (dact * slope[:, cols].astype(F32)).astype(BF16)
        hsum[:, cols] = column_sum(dhid)
        dw[1, :, cols] = mm(back, act[:, cols], TN).astype(BF16)
        dw[0, :, cols] = mm(second[...], dhid, TN).astype(BF16)
        acc[...] += mm(dhid, wf[0, :, cols], NT)

    dsecond = acc[...]
    grad2 = norm_backward(dsecond, n2, r2, gain2[...].astype(F32))
    low2 = grad2.astype(BF16)
    du2[...] = grad2
    db2[...] = low2
    sums[3:4, :] = column_sum(low2)
    sums[4:5, :] = column_sum(dsecond * n2)
    sums[5:6, :] = column_sum(dsecond)
    sums[0:3, :] = jnp.zeros((3, width), F32)
    sums[9:16, :] = jnp.zeros((7, width), F32)


def feed(ctx, first, cot, wo, wf, ob, gain2, bias2, fib, fob, gain3, bias3):
    tokens, width = first.shape
    wide = wf.shape[2]
    return pl.pallas_call(
        feed_kernel,
        out_shape=(
            shaped(first.shape, BF16),
            shaped(wf.shape, BF16),
            shaped(first.shape, F32),
            shaped(first.shape, BF16),
            shaped((16, width), F32),
            shaped((1, wide), F32),
        ),
        in_specs=[VMEM] * 12,
        scratch_shapes=[
            pltpu.VMEM((tokens, wide), BF16),
            pltpu.VMEM((tokens, wide), BF16),
            pltpu.VMEM((tokens, width), F32),
            pltpu.VMEM((tokens, width), BF16),
        ],
        compiler_params=limit(28),
        cost_estimate=cost(6 * tokens * width * wide, 14 << 20),
    )(ctx, first, cot, wo, wf, ob, gain2, bias2, fib, fob, gain3, bias3)


def first_back_kernel(du2, dq2, normed, inverse, w, gain, du1, db1, sums):
    width = du2.shape[1]
    dfirst = du2[...] + mm(dq2[...], w[1], NT)
    n = normed[...]
    grad = norm_backward(dfirst, n, inverse[...], gain[...].astype(F32))
    low = grad.astype(BF16)
    du1[...] = grad
    db1[...] = low
    sums[0:1, :] = column_sum(low)
    sums[1:2, :] = column_sum(dfirst * n)
    sums[2:3, :] = column_sum(dfirst)
    sums[3:8, :] = jnp.zeros((5, width), F32)


def first_back(du2, dq2, normed, inverse, w, gain):
    width = du2.shape[1]
    low = shaped(du2.shape, BF16)
    return pl.pallas_call(
        first_back_kernel,
        out_shape=(shaped(du2.shape, F32), low, shaped((8, width), F32)),
        in_specs=[VMEM] * 6,
        compiler_params=limit(16),
        cost_estimate=cost(2 * du2.size * width, 8 << 20),
    )(du2, dq2, *far(normed, inverse, w), gain)


def middle_grads_kernel(
    first, dq2, mem, memo, dk2, dv2, db2, ctx2, db1, ctx1, w, dw, own, other, sums
):
    rows, width = mem.shape
    dw[0] = mm(db1[...], ctx1[...], TN).astype(BF16)
    dw[1] = mm(first[...].astype(BF16), dq2[...], TN).astype(BF16)
    for slot, grad in ((2, dk2), (3, dv2)):
        dw[slot] = (
            mm(mem[...], grad[:rows, :], TN) + mm(memo[...], grad[rows:, :], TN)
        ).astype(BF16)
    dw[4] = mm(db2[...], ctx2[...], TN).astype(BF16)
    back = mm(dk2[...], w[2], NT) + mm(dv2[...], w[3], NT)
    own[...] = back[:rows, :]
    other[...] = back[rows:, :].astype(BF16)
    sums[0:1, :] = column_sum(dq2[...])
    sums[1:2, :] = column_sum(dv2[...])
    sums[2:8, :] = jnp.zeros((6, width), F32)


def middle_grads(first, dq2, mem, memo, dk2, dv2, db2, ctx2, db1, ctx1, w):
    tokens, width = first.shape
    rows = mem.shape[0]
    return pl.pallas_call(
        middle_grads_kernel,
        out_shape=(
            shaped(w.shape, BF16),
            shaped((rows, width), F32),
            shaped((rows, width), BF16),
            shaped((8, width), F32),
        ),
        in_specs=[VMEM] * 11,
        compiler_params=limit(16),
        cost_estimate=cost(5 * first.size * width, 10 << 20),
    )(*far(first), dq2, *far(mem, memo), dk2, dv2, db2, *far(ctx2), db1, *far(ctx1, w))


def self_grads_kernel(
    info, x, xo, dqa, dka, dva, dkoa, dvoa, dqb, dkb, dvb, dkob, dvob, w, dw, other, sums
):
    width = x.shape[1]
    both = lambda left, right: jnp.concatenate([left[...], right[...]], axis=1)
    dq, dk, dv = both(dqa, dqb), both(dka, dkb), both(dva, dvb)
    dw[0] = mm(x[...], dq, TN).astype(BF16)
    sums[0:1, :] = column_sum(dq)
    sums[2:8, :] = jnp.zeros((6, width), F32)

    @pl.when(info[0] == 0)
    def _():
        dw[1] = mm(x[...], dk, TN).astype(BF16)
        dw[2] = mm(x[...], dv, TN).astype(BF16)
        sums[1:2, :] = column_sum(dv)
        other[...] = jnp.zeros_like(other)

    @pl.when(info[0] != 0)
    def _():
        dko, dvo = both(dkoa, dkob), both(dvoa, dvob)
        dw[1] = (mm(x[...], dk, TN) + mm(xo[...], dko, TN)).astype(BF16)
        dw[2] = (mm(x[...], dv, TN) + mm(xo[...], dvo, TN)).astype(BF16)
        sums[1:2, :] = column_sum(dv) + column_sum(dvo)
        other[...] = (mm(dko, w[1], NT) + mm(dvo, w[2], NT)).astype(BF16)


def self_grads(info, x, xo, early, late, w):
    width = x.shape[1]
    return pl.pallas_call(
        self_grads_kernel,
        out_shape=(shaped(w.shape, BF16), shaped(x.shape, BF16), shaped((8, width), F32)),
        in_specs=[SMEM] + [VMEM] * 13,
        compiler_params=limit(16),
        cost_estimate=cost(7 * x.size * width, 8 << 20),
    )(info, *far(x, xo), *early, *late, *far(w))


def input_grads_kernel(du1, dqa, dka, dva, dqb, dkb, dvb, w, back, out):
    both = lambda left, right: jnp.concatenate([left[...], right[...]], axis=1)
    out[...] = (
        du1[...]
        + mm(both(dqa, dqb), w[0], NT)
        + mm(both(dka, dkb), w[1], NT)
        + mm(both(dva, dvb), w[2], NT)
        + back[...].astype(F32)
    )


def input_grads(du1, early, late, w, back):
    return pl.pallas_call(
        input_grads_kernel,
        out_shape=shaped(du1.shape, F32),
        in_specs=[VMEM] * 9,
        compiler_params=limit(16),
        cost_estimate=cost(3 * du1.size * du1.shape[1], 6 << 20),
    )(*far(du1), *early, *late, *far(w), back)


def on_device(
    inputs,
    memory,
    prefix,
    self_query,
    self_query_bias,
    self_key,
    self_value,
    self_value_bias,
    self_out,
    self_out_bias,
    self_norm_gain,
    self_norm_bias,
    cross_query,
    cross_query_bias,
    cross_key,
    cross_value,
    cross_value_bias,
    cross_out,
    cross_out_bias,
    cross_norm_gain,
    cross_norm_bias,
    feed_in,
    feed_in_bias,
    feed_out,
    feed_out_bias,
    feed_norm_gain,
    feed_norm_bias,
    cotangent,
):
    nd, nt = lax.axis_size("dp"), lax.axis_size("tensor")
    me_d, me_t = lax.axis_index("dp"), lax.axis_index("tensor")
    late = me_t % 2
    width = inputs.shape[1]
    assert LEN == 2 * inputs.shape[0] and MEM == 2 * memory.shape[0]
    assert nd & (nd - 1) == 0 and nt & (nt - 1) == 0
    prefix_here = jnp.where(late == 0, lax.dynamic_index_in_dim(prefix, me_t // 2, keepdims=False), 0)
    info = jnp.stack([late, prefix_here, me_d, me_t]).astype(jnp.int32)

    columns = self_query_bias.shape[0]
    row = lambda vector: vector.reshape(1, -1)
    packed = pack(
        (self_query, self_key, self_value),
        (self_query_bias, self_value_bias, cross_query_bias, cross_value_bias, feed_in_bias),
    )
    middle_shard, feed_shard = pack_rest(
        (self_out.T, after(cross_query, packed), cross_key, cross_value, cross_out.T),
        (feed_in, feed_out.T),
    )

    bits = [1 << i for i in range(nt.bit_length() - 1)]
    swapped = [swap(packed, 0, k) for k in range(1, nt)]
    line_middle = doubled(middle_shard[None], bits[:1])
    inputs_other = hand_over(after(inputs, middle_shard), 0, 1)
    line_self = jnp.stack([after(packed, line_middle)] + swapped)
    count = 3 * self_query.shape[0]
    riders = line_self[:, count:]
    line_self = line_self[:, :count].reshape((nt, 3) + self_query.shape)
    line_middle = doubled(after(line_middle, line_self), bits[1:])
    line_feed = doubled(after(feed_shard, line_self)[None], bits[:1])
    group_self = both_cores(over_planes(line_self), line_middle, line_feed)
    planes_middle = over_planes(after(line_middle, group_self[0]))
    line_feed = doubled(after(line_feed, group_self[0]), bits[1:])
    head_biases, hidden_bias = spread(info, riders)

    w_self = assemble(info, *group_self)
    q1, k1, v1, k1o, v1o = project_self(info, inputs, inputs_other, w_self, head_biases)
    group_middle = both_cores(planes_middle, q1, line_feed)
    line_feed = after(line_feed, group_middle[0])
    planes_feed = over_planes(line_feed)
    memory_other = swap(after(memory, line_feed), 0, 1)
    q1 = after(q1, group_middle[0])
    ctx1, log1 = self_forward(info, q1, k1, v1, k1o, v1o)
    w_middle = assemble(info, *group_middle)
    first, normed1, inverse1, q2, k2, v2 = first_norm(
        ctx1,
        inputs,
        memory,
        memory_other,
        w_middle,
        row(self_out_bias),
        row(self_norm_gain),
        row(self_norm_bias),
        head_biases,
    )
    ctx2, log2 = cross_forward(q2, k2, v2)
    w_feed = assemble(info, *both_cores(planes_feed, ctx2))
    outputs, dw_feed, du2, db2, sums_feed, sums_hidden = feed(
        ctx2,
        first,
        cotangent,
        w_middle,
        w_feed,
        row(cross_out_bias),
        row(cross_norm_gain),
        row(cross_norm_bias),
        hidden_bias,
        row(feed_out_bias),
        row(feed_norm_gain),
        row(feed_norm_bias),
    )
    rounds = (nd // 2).bit_length() - 1
    keep, send, feed_halves = disperse(info, dw_feed, (1, 1), jnp.zeros((0, PAIR), BF16))
    got = swap(send, 1, 0)
    dq2, dk2, dv2 = cross_backward(q2, k2, v2, ctx2, log2, db2, w_middle)
    held, _ = feed_halves.parts(after(keep, dq2), got)
    held = [dict(enumerate(pieces)) for pieces in held]
    moves = feed_halves.step(held, None, 0)
    du2, _ = lax.optimization_barrier((du2, held))
    du1, db1, sums_first = first_back(
        du2, dq2, normed1, inverse1, w_middle, row(self_norm_gain)
    )
    dw_middle, memory_own, memory_back, sums_cross = middle_grads(
        first, dq2, memory, memory_other, dk2, dv2, db2, ctx2, db1, ctx1, w_middle
    )
    early = jnp.concatenate(
        [
            sums_first[:3],
            sums_feed[3:9],
            sums_cross[:2],
            sums_hidden.reshape(-1, width),
            jnp.zeros((1, width), F32),
        ]
    )
    early_rows = early.size // columns
    keep, send, middle_halves = disperse(info, dw_middle, (3, 2), early)
    held[0][0] = after(held[0][0], send)
    held, _ = feed_halves.settle(moves, None)
    got = swap(send, 1, 0)
    memory_got = swap(memory_back, 0, 1)
    for index in range(1, rounds):
        moves = feed_halves.step(held, None, index)
        if index < rounds - 1:
            held, _ = feed_halves.settle(moves, None)
    db1, _ = lax.optimization_barrier((db1, held))
    pairs = width // PAIR // 2
    operands = (info, q1, k1, v1, k1o, v1o, ctx1, log1)
    grads_early = self_backward(*operands, db1, w_middle, 0, pairs)
    moves[0][0][0] = after(moves[0][0][0], grads_early[0])
    held, _ = feed_halves.settle(moves, None)
    lines_feed = line_swaps(feed_halves.line_parts(held, None))
    held, rider = middle_halves.parts(after(keep, grads_early[0]), got)
    held = [dict(enumerate(pieces)) for pieces in held]
    moves = middle_halves.step(held, rider, 0)
    db1, _, _ = lax.optimization_barrier((db1, held, lines_feed[0]))
    grads_late = self_backward(*operands, db1, w_middle, pairs, pairs)
    moves[0][0][0] = after(moves[0][0][0], grads_late[0])
    held, rider = middle_halves.settle(moves, rider)
    for index in range(1, rounds):
        moves = middle_halves.step(held, rider, index)
        if index < rounds - 1:
            held, rider = middle_halves.settle(moves, rider)
    grad_feed = line_sum([after(lines_feed[0], grads_late[0])] + lines_feed[1:])
    grad_feed = grad_feed.reshape(2, -1, feed_in.shape[1])
    grads_late = list(grads_late)
    grads_late[0], _ = lax.optimization_barrier((grads_late[0], held))
    dw_self, inputs_back, sums_self = self_grads(
        info, inputs, inputs_other, grads_early, grads_late, w_self
    )
    sums_self = sums_self[:4]
    late_rows = sums_self.size // columns
    keep, send, self_halves = disperse(info, dw_self, (3,), sums_self)
    got = swap(send, 1, 0)
    inputs_got = hand_over(inputs_back, 1, -1)
    moves[0][0][0] = after(moves[0][0][0], send)
    held, rider = middle_halves.settle(moves, rider)
    lines_middle = line_swaps(middle_halves.line_parts(held, rider))
    grad_memory = memory_own + memory_got.astype(F32)
    held, rider = self_halves.parts(keep, got)
    grad_self, rider = direct_plane(held[0], rider)
    grad_middle = line_sum([after(lines_middle[0], grad_self)] + lines_middle[1:])
    lines_self = line_swaps(self_halves.line_parts([{0: grad_self}], rider))
    grad_inputs = input_grads(du1, grads_early[:3], grads_late[:3], w_self, inputs_got)
    grad_self = line_sum(lines_self)
    early = grad_middle[-early_rows:].reshape(-1, width)
    late_sums = grad_self[-late_rows:].reshape(-1, width)
    grad_middle = grad_middle[:-early_rows].reshape(5, -1, columns)
    grad_self = grad_self[:-late_rows].reshape(3, -1, columns)

    def mine(vector):
        count = vector.shape[0] // nt
        return lax.dynamic_slice_in_dim(vector, me_t * count, count)

    return (
        outputs,
        grad_inputs,
        grad_memory,
        grad_self[0],
        mine(late_sums[0]),
        grad_self[1],
        grad_self[2],
        mine(late_sums[1]),
        grad_middle[0].T,
        early[0],
        early[1],
        early[2],
        grad_middle[1],
        mine(early[9]),
        grad_middle[2],
        grad_middle[3],
        mine(early[10]),
        grad_middle[4].T,
        early[3],
        early[4],
        early[5],
        grad_feed[0],
        mine(early[11:15].reshape(-1)),
        grad_feed[1].T,
        early[6],
        early[7],
        early[8],
    )


def solution(mesh):
    placed = (
        P(("dp", "tensor"), None),
        P(("dp", "tensor"), None),
        P("dp"),
        P("dp", "tensor"),
        P("tensor"),
        P("dp", "tensor"),
        P("dp", "tensor"),
        P("tensor"),
        P("tensor", "dp"),
        P(),
        P(),
        P(),
        P("dp", "tensor"),
        P("tensor"),
        P("dp", "tensor"),
        P("dp", "tensor"),
        P("tensor"),
        P("tensor", "dp"),
        P(),
        P(),
        P(),
        P("dp", "tensor"),
        P("tensor"),
        P("tensor", "dp"),
        P(),
        P(),
        P(),
        P(("dp", "tensor"), None),
    )
    return jax.shard_map(
        on_device,
        mesh=mesh,
        in_specs=placed,
        out_specs=(
            P(("dp", "tensor"), None),
            P(("dp", "tensor"), None),
            P(("dp", "tensor"), None),
            P("dp", "tensor"),
            P("tensor"),
            P("dp", "tensor"),
            P("dp", "tensor"),
            P("tensor"),
            P("tensor", "dp"),
            P(),
            P(),
            P(),
            P("dp", "tensor"),
            P("tensor"),
            P("dp", "tensor"),
            P("dp", "tensor"),
            P("tensor"),
            P("tensor", "dp"),
            P(),
            P(),
            P(),
            P("dp", "tensor"),
            P("tensor"),
            P("tensor", "dp"),
            P(),
            P(),
            P(),
        ),
        check_vma=False,
    )
```

time: 286 us -> 218 us (0.76)
  starting transfers between devices: 90.4 us -> 57 us
  local copies, waits for them, and re-layouts: 35.4 us -> 18.6 us
  waiting for transfers between devices: 66.4 us -> 55.7 us
  Pallas kernels: 74.1 us -> 65.6 us
    ppermute x58 -> x44, starting transfers between devices: 85 us -> 52.3 us  [swap(): return lax.ppermute(array, ('dp', 'tensor'), pairs)]
    unnamed x152 -> x118, local copies, waits for them, and re-layouts: 20.6 us -> 10.1 us
    ppermute x2, waiting for transfers between devices: 9.71 us -> 0.01 us  [hand_over(): return lax.ppermute(array, ('dp', 'tensor'), pairs)]
    convert_element_type x6 -> x17, other arithmetic: 3.9 us -> 8.38 us  [rounded(): return lax.optimization_barrier(values.astype(BF16))]
    pallas_call x1, Pallas kernels: 15.8 us -> 11.6 us  [feed(): pl.pallas_call(feed_kernel, out_shape=(shaped(first.shape, BF16), shaped(...]
    reshape x9, local copies, waits for them, and re-layouts: 3.5 us -> 0.04 us  [on_device(): row = lambda vector: vector.reshape(1, -1)]
    another operation x9 -> x5, other arithmetic: 5.55 us -> 2.67 us  [the longest x3 1.8 us: both_cores(): plane = jnp.stack([after(planes[0], *others)] + planes[1:])]
    pallas_call x8 -> x11, Pallas kernels: 20.5 us -> 21.7 us  [the longest x2 12 us: self_backward(): pl.pallas_call(self_backward_kernel, grid=(pairs,), out_shape=(out,) * 5,...]
  transfers between devices with their start and end apart: 60 -> 46, of which waited for: 23 -> 16; matrix products, arithmetic and copies ran while one was open for 12% -> 8% of each run, Pallas kernels for 19% -> 23%
where the time goes in v2:
time: 218 us; the launch traced here: 217 us
  Pallas kernels  65.6 us (30%)
  starting transfers between devices  57 us (26%)
  waiting for transfers between devices  55.7 us (26%)
  local copies, waits for them, and re-layouts  18.6 us (9%)
  other arithmetic  17.3 us (8%)
  between operations  2.58 us (1%)
    ppermute x44, waiting for transfers between devices, swap(): return lax.ppermute(array, ('dp', 'tensor'), pairs)  55.7 us
    ppermute x44, starting transfers between devices, swap(): return lax.ppermute(array, ('dp', 'tensor'), pairs)  52.3 us
    pallas_call x2, Pallas kernels, self_backward(): pl.pallas_call(self_backward_kernel, grid=(pairs,), out_shape=(out,) * 5,...  12 us
    pallas_call x1, Pallas kernels, feed(): pl.pallas_call(feed_kernel, out_shape=(shaped(first.shape, BF16), shaped(...  11.6 us
    unnamed x118, local copies, waits for them, and re-layouts  10.1 us
    convert_element_type x17, other arithmetic, rounded(): return lax.optimization_barrier(values.astype(BF16))  8.38 us
    pallas_call x1, Pallas kernels, cross_backward(): pl.pallas_call(cross_backward_kernel, grid=(width // PAIR,), out_shape=(s...  6.7 us
    pallas_call x1, Pallas kernels, self_forward(): pl.pallas_call(self_forward_kernel, grid=(width // PAIR,), out_shape=(sha...  5.29 us
  transfers between devices with their start and end apart: 46, of which 16 were waited for; matrix products, arithmetic and copies ran while one was open for 8% of the time, Pallas kernels for 23%

profile of v2, /device:TPU:0, one launch (start us, length us, event | category | flops | bytes accessed | tf_op | source)
XLA Modules:
  0.0 216.7 jit_solution(10207517367103245330)
XLA Ops:
  1.9 1.4 shard_map.475
  3.4 1.6 shard_map.476
  5.0 3.0 %collective-permute-start.1 = (bf16[1,5,64,128]{3,2,1,0:T(8,128)(2,1)}, bf16[1,5,64,128]{3,2,1,0:T(8,128)(2,1)S(1)}, u32[]{:S(2)}, u32[]{:S(2)}) collective-permute-start(bf16[1,5,64,128]{3,2,1,0:T(8,128)(2,1)} %bitcast.86), channel_id=1, source_target_pairs={{0,1},{1,0},{2,3},{3,2},{4,5},{5,4},{6,7},{7,6},{8,9},{9,8},{10,11... | collective-permute-start | bytes 245768 | tf_op jit(solution)/shard_map/ppermute | solution.py:56
  8.1 3.0 %collective-permute-start.3 = (bf16[208,128]{1,0:T(8,128)(2,1)}, bf16[208,128]{1,0:T(8,128)(2,1)S(1)}, u32[]{:S(2)}, u32[]{:S(2)}) collective-permute-start(bf16[208,128]{1,0:T(8,128)(2,1)} %shard_map.475), channel_id=1, source_target_pairs={{0,2},{1,3},{2,0},{3,1},{4,6},{5,7},{6,4},{7,5},{8,10},{9,11},{10,... | collective-permute-start | bytes 159752 | tf_op jit(solution)/shard_map/ppermute | solution.py:56
  11.1 1.3 collective-permute-start.4
  13.4 3.8 %collective-permute-done.4 = bf16[208,128]{1,0:T(8,128)(2,1)S(1)} collective-permute-done((bf16[208,128]{1,0:T(8,128)(2,1)}, bf16[208,128]{1,0:T(8,128)(2,1)S(1)}, u32[]{:S(2)}, u32[]{:S(2)}) %collective-permute-start.4) | collective-permute-done | bytes 53280 | tf_op jit(solution)/shard_map/ppermute | solution.py:56
  18.2 2.3 %collective-permute-start.5 = (bf16[2,5,64,128]{3,2,1,0:T(8,128)(2,1)S(1)}, bf16[2,5,64,128]{3,2,1,0:T(8,128)(2,1)S(1)}, u32[]{:S(2)}, u32[]{:S(2)}) collective-permute-start(bf16[2,5,64,128]{3,2,1,0:T(8,128)(2,1)S(1)} %pad_maximum_fusion.17), channel_id=1, source_target_pairs={{0,2},{1,3},{2,0},{3,1},{4,6},{5,7},{6,4},{7,5},{8,10},{9,11},{10,... | collective-permute-start | bytes 491528 | tf_op jit(solution)/shard_map/ppermute | solution.py:56
  21.2 1.5 collective-permute-start.7
  22.7 1.5 collective-permute-start.8
  25.4 2.6 %collective-permute-done.5 = bf16[2,5,64,128]{3,2,1,0:T(8,128)(2,1)S(1)} collective-permute-done((bf16[2,5,64,128]{3,2,1,0:T(8,128)(2,1)S(1)}, bf16[2,5,64,128]{3,2,1,0:T(8,128)(2,1)S(1)}, u32[]{:S(2)}, u32[]{:S(2)}) %collective-permute-start.5) | collective-permute-done | bytes 163872 | tf_op jit(solution)/shard_map/ppermute | solution.py:56
  28.9 3.3 %collective-permute-done.8 = bf16[4,3,64,128]{3,2,1,0:T(8,128)(2,1)S(1)} collective-permute-done((bf16[4,3,64,128]{3,2,1,0:T(8,128)(2,1)S(1)}, bf16[4,3,64,128]{3,2,1,0:T(8,128)(2,1)S(1)}, u32[]{:S(2)}, u32[]{:S(2)}) %collective-permute-start.8) | collective-permute-done | bytes 196640 | tf_op jit(solution)/shard_map/ppermute | solution.py:56
  33.1 3.3 %collective-permute-start = (bf16[512,512]{1,0:T(8,128)(2,1)S(1)}, bf16[512,512]{1,0:T(8,128)(2,1)S(1)}, u32[]{:S(2)}, u32[]{:S(2)}) collective-permute-start(bf16[512,512]{1,0:T(8,128)(2,1)S(1)} %copy-done.4), channel_id=1, source_target_pairs={{0,1},{2,3},{4,5},{6,7},{8,9},{10,11},{12,13},{14,15},{16,17},{18,... | collective-permute-start | bytes 1572872 | tf_op jit(solution)/shard_map/ppermute | solution.py:62
  40.1 7.6 %collective-permute-done.11 = bf16[2,2,64,512]{3,2,1,0:T(8,128)(2,1)S(1)} collective-permute-done((bf16[2,2,64,512]{3,2,1,0:T(8,128)(2,1)S(1)}, bf16[2,2,64,512]{3,2,1,0:T(8,128)(2,1)S(1)}, u32[]{:S(2)}, u32[]{:S(2)}) %collective-permute-start.11) | collective-permute-done | bytes 262176 | tf_op jit(solution)/shard_map/ppermute | solution.py:56
  49.5 1.4 shard_map.478
  52.4 1.7 shard_map.479
  54.3 3.9 %collective-permute-done.14 = bf16[4,5,64,128]{3,2,1,0:T(8,128)(2,1)} collective-permute-done((bf16[4,5,64,128]{3,2,1,0:T(8,128)(2,1)}, bf16[4,5,64,128]{3,2,1,0:T(8,128)(2,1)}, u32[]{:S(2)}, u32[]{:S(2)}) %collective-permute-start.14) | collective-permute-done | bytes 327712 | tf_op jit(solution)/shard_map/ppermute | solution.py:56
  58.2 1.4 pad_maximum_fusion.1.plane
  61.5 1.7 collective-permute-start.19
  63.3 5.3 %shard_map.480 = (bf16[512,512]{1,0:T(8,128)(2,1)S(1)}, f32[512,512]{1,0:T(8,128)S(1)}) custom-call(s32[4]{0:T(128)S(1)} %copy-done.36, bf16[512,512]{1,0:T(8,128)(2,1)S(1)} %get-tuple-element.118.q, bf16[512,512]{1,0:T(8,128)(2,1)S(1)} %get-tuple-element.119.k, bf16[512,512]{1,0:T(8,128)(2,1)S(1)} %get-tuple-element.120.v, ...), custom_call_target="tpu_custom_call" | custom-call | flops 33554432 | bytes 81920 | tf_op jit(solution)/shard_map/pallas_call | solution.py:516
  70.9 1.4 shard_map.482
  74.0 3.0 %shard_map.483 = (bf16[512,512]{1,0:T(8,128)(2,1)S(1)}, f32[512,512]{1,0:T(8,128)S(1)}) custom-call(bf16[512,512]{1,0:T(8,128)(2,1)S(1)} %get-tuple-element.126.q, bf16[256,512]{1,0:T(8,128)(2,1)S(1)} %get-tuple-element.127.k, bf16[256,512]{1,0:T(8,128)(2,1)S(1)} %get-tuple-element.128.v), custom_call_target="tpu_custom_call" | custom-call | flops 8388608 | bytes 49152 | tf_op jit(solution)/shard_map/pallas_call | solution.py:546
  78.0 7.9 %collective-permute-done.19 = bf16[4,2,64,512]{3,2,1,0:T(8,128)(2,1)S(1)} collective-permute-done((bf16[4,2,64,512]{3,2,1,0:T(8,128)(2,1)S(1)}, bf16[4,2,64,512]{3,2,1,0:T(8,128)(2,1)S(1)}, u32[]{:S(2)}, u32[]{:S(2)}) %collective-permute-start.19) | collective-permute-done | bytes 524320 | tf_op jit(solution)/shard_map/ppermute | solution.py:56
  86.7 3.8 %collective-permute-done.20.sibling = bf16[4,4,2,64,512]{4,3,2,1,0:T(8,128)(2,1)S(1)} collective-permute-done((bf16[4,4,2,64,512]{4,3,2,1,0:T(8,128)(2,1)S(1)}, bf16[4,4,2,64,512]{4,3,2,1,0:T(8,128)(2,1)S(1)}, u32[]{:S(2)}, u32[]{:S(2)}) %collective-permute-start.20) | collective-permute-done | bytes 2097184 | tf_op jit(solution)/shard_map/ppermute | solution.py:56
  91.4 11.6 %shard_map.485 = (bf16[512,512]{1,0:T(8,128)(2,1)}, bf16[2,512,2048]{2,1,0:T(8,128)(2,1)S(1)}, f32[512,512]{1,0:T(8,128)S(1)}, bf16[512,512]{1,0:T(8,128)(2,1)S(...) custom-call(bf16[512,512]{1,0:T(8,128)(2,1)S(1)} %get-tuple-element.129.ctx.ctx2, ...), custom_call_target="tpu_custom_call" | custom-call | flops 50331648 | bytes 229376 | tf_op jit(solution)/shard_map/pallas_call | solution.py:714
  104.1 6.7 %shard_map.487 = (bf16[512,512]{1,0:T(8,128)(2,1)S(1)}, bf16[256,512]{1,0:T(8,128)(2,1)S(1)}, bf16[256,512]{1,0:T(8,128)(2,1)S(1)}) custom-call(bf16[512,512]{1,0:T(8,128)(2,1)} %copy-done.17, bf16[256,512]{1,0:T(8,128)(2,1)} %copy-done.22, bf16[256,512]{1,0:T(8,128)(2,1)} %copy-done.23, bf16[512,512]{1,0:T(8,128)(2,1)} %copy-done.3, f32[512,512]{1,0:T(8,128)} %copy-done.25, ...), custom_call_target="tpu_custom_call" | custom-call | flops 20971520 | bytes 65536 | tf_op jit(solution)/shard_map/pallas_call | solution.py:561
  111.5 1.6 add_convert_fusion.6
  115.5 1.5 collective-permute-start.22
  117.1 3.1 %shard_map.488 = (f32[512,512]{1,0:T(8,128)S(1)}, bf16[512,512]{1,0:T(8,128)(2,1)S(1)}, f32[8,512]{1,0:T(8,128)S(1)}) custom-call(f32[512,512]{1,0:T(8,128)S(1)} %copy-done.21, bf16[512,512]{1,0:T(8,128)(2,1)S(1)} %get-tuple-element.139.dq2, f32[512,512]{1,0:T(8,128)} %copy-done.19, f32[512,1]{1,0:T(8,128)} %copy-done.31, bf16[5,512,512]{2,1,0:T(8,128)(2,1)} %copy-done, ...), custom_call_target="tpu_custom_call" | custom-call | flops 4194304 | bytes 131072 | tf_op jit(solution)/shard_map/pallas_call | solution.py:753
  122.3 4.4 %shard_map.489 = (bf16[5,512,512]{2,1,0:T(8,128)(2,1)S(1)}, f32[128,512]{1,0:T(8,128)S(1)}, bf16[128,512]{1,0:T(8,128)(2,1)S(1)}, f32[8,512]{1,0:T(8,128)S(1)}) custom-call(f32[512,512]{1,0:T(8,128)} %copy-done.11, bf16[512,512]{1,0:T(8,128)(2,1)S(1)} %copy-done.14, bf16[128,512]{1,0:T(8,128)(2,1)} %mem.3, bf16[128,512]{1,0:T(8,128)(2,1)} %copy-done.27, ...), custom_call_target="tpu_custom_call" | custom-call | flops 10485760 | bytes 163840 | tf_op jit(solution)/shard_map/pallas_call | solution.py:784
  133.2 1.5 collective-permute-done.30
  135.4 5.8 %shard_map.491 = (bf16[512,256]{1,0:T(8,128)(2,1)S(1)}, bf16[512,256]{1,0:T(8,128)(2,1)S(1)}, bf16[512,256]{1,0:T(8,128)(2,1)S(1)}, bf16[512,256]{1,0:T(8,128)(2,1)S(1)}, bf16[512,256]{1,0:T(8,128)(2,1)S(1)}) custom-call(s32[4]{0:T(128)S(1)} %copy-done.36, bf16[512,512]{1,0:T(8,128)(2,1)} %copy-done.6, bf16[512,512]{1,0:T(8,128)(2,1)} %copy-done.7, ...), custom_call_target="tpu_custom_call" | custom-call | flops 41943040 | bytes 131072 | tf_op jit(solution)/shard_map/pallas_call | solution.py:531
  141.5 3.0 %collective-permute-start.43 = (bf16[128,512]{1,0:T(8,128)(2,1)S(1)}, bf16[128,512]{1,0:T(8,128)(2,1)S(1)}, u32[]{:S(2)}, u32[]{:S(2)}) collective-permute-start(bf16[128,512]{1,0:T(8,128)(2,1)S(1)} %pad_maximum_fusion.20), channel_id=1, source_target_pairs={{0,1},{1,0},{2,3},{3,2},{4,5},{5,4},{6,7},{7,6},{8,9},{9,8},{10,11... | collective-permute-start | bytes 393224 | tf_op jit(solution)/shard_map/ppermute | solution.py:56
  144.5 3.4 %collective-permute-start.44 = (bf16[128,512]{1,0:T(8,128)(2,1)S(1)}, bf16[128,512]{1,0:T(8,128)(2,1)S(1)}, u32[]{:S(2)}, u32[]{:S(2)}) collective-permute-start(bf16[128,512]{1,0:T(8,128)(2,1)S(1)} %pad_maximum_fusion.21), channel_id=1, source_target_pairs={{0,2},{1,3},{2,0},{3,1},{4,6},{5,7},{6,4},{7,5},{8,10},{9,11},{10,... | collective-permute-start | bytes 393224 | tf_op jit(solution)/shard_map/ppermute | solution.py:56
  149.1 6.1 %shard_map.492 = (bf16[512,256]{1,0:T(8,128)(2,1)S(1)}, bf16[512,256]{1,0:T(8,128)(2,1)S(1)}, bf16[512,256]{1,0:T(8,128)(2,1)S(1)}, bf16[512,256]{1,0:T(8,128)(2,1)S(1)}, bf16[512,256]{1,0:T(8,128)(2,1)S(1)}) custom-call(s32[4]{0:T(128)S(1)} %copy-done.36, bf16[512,512]{1,0:T(8,128)(2,1)} %copy-done.6, bf16[512,512]{1,0:T(8,128)(2,1)} %copy-done.7, ...), custom_call_target="tpu_custom_call" | custom-call | flops 41943040 | bytes 131072 | tf_op jit(solution)/shard_map/pallas_call | solution.py:531
  156.4 1.5 collective-permute-done.44
  160.1 6.7 %collective-permute-done.27 = bf16[1536,128]{1,0:T(8,128)(2,1)S(1)} collective-permute-done((bf16[1536,128]{1,0:T(8,128)(2,1)S(1)}, bf16[1536,128]{1,0:T(8,128)(2,1)S(1)}, u32[]{:S(2)}, u32[]{:S(2)}) %collective-permute-start.27) | collective-permute-done | bytes 393248 | tf_op jit(solution)/shard_map/ppermute | solution.py:56
  167.6 1.4 collective-permute-start.38
  169.1 3.0 %shard_map.493 = (bf16[3,512,512]{2,1,0:T(8,128)(2,1)S(1)}, bf16[512,512]{1,0:T(8,128)(2,1)S(1)}, f32[8,512]{1,0:T(8,128)S(1)}) custom-call(s32[4]{0:T(128)S(1)} %copy-done.36, bf16[512,512]{1,0:T(8,128)(2,1)} %x.5, bf16[512,512]{1,0:T(8,128)(2,1)} %copy-done.18, bf16[512,256]{1,0:T(8,128)(2,1)S(1)} %get-tuple-element.158.dqa, ...), custom_call_target="tpu_custom_call" | custom-call | flops 14680064 | bytes 131072 | tf_op jit(solution)/shard_map/pallas_call | solution.py:826
  176.6 4.2 %collective-permute-start.40 = (bf16[384,128]{1,0:T(8,128)(2,1)S(1)}, bf16[384,128]{1,0:T(8,128)(2,1)S(1)}, u32[]{:S(2)}, u32[]{:S(2)}) collective-permute-start(bf16[384,128]{1,0:T(8,128)(2,1)S(1)} %get-tuple-element.254), channel_id=1, source_target_pairs={{0,1},{1,0},{2,3},{3,2},{4,5},{5,4},{6,7},{7,6},{8,9},{9,8},{10,11... | collective-permute-start | bytes 294920 | tf_op jit(solution)/shard_map/ppermute | solution.py:56
  180.8 3.5 %collective-permute-start.41 = (bf16[384,128]{1,0:T(8,128)(2,1)S(1)}, bf16[384,128]{1,0:T(8,128)(2,1)S(1)}, u32[]{:S(2)}, u32[]{:S(2)}) collective-permute-start(bf16[384,128]{1,0:T(8,128)(2,1)S(1)} %get-tuple-element.255), channel_id=1, source_target_pairs={{0,2},{1,3},{2,0},{3,1},{4,6},{5,7},{6,4},{7,5},{8,10},{9,11},{10,... | collective-permute-start | bytes 294920 | tf_op jit(solution)/shard_map/ppermute | solution.py:56
  185.1 1.3 collective-permute-start.29
  186.4 5.8 %collective-permute-done.41 = bf16[384,128]{1,0:T(8,128)(2,1)S(1)} collective-permute-done((bf16[384,128]{1,0:T(8,128)(2,1)S(1)}, bf16[384,128]{1,0:T(8,128)(2,1)S(1)}, u32[]{:S(2)}, u32[]{:S(2)}) %collective-permute-start.41) | collective-permute-done | bytes 98336 | tf_op jit(solution)/shard_map/ppermute | solution.py:56
  195.0 1.8 collective-permute-start.34
  197.4 3.8 %collective-permute-done.32 = bf16[784,128]{1,0:T(8,128)(2,1)S(1)} collective-permute-done((bf16[784,128]{1,0:T(8,128)(2,1)S(1)}, bf16[784,128]{1,0:T(8,128)(2,1)S(1)}, u32[]{:S(2)}, u32[]{:S(2)}) %collective-permute-start.32) | collective-permute-done | bytes 200736 | tf_op jit(solution)/shard_map/ppermute | solution.py:56
  201.2 2.4 %collective-permute-done.33 = bf16[784,128]{1,0:T(8,128)(2,1)S(1)} collective-permute-done((bf16[784,128]{1,0:T(8,128)(2,1)S(1)}, bf16[784,128]{1,0:T(8,128)(2,1)S(1)}, u32[]{:S(2)}, u32[]{:S(2)}) %collective-permute-start.33) | collective-permute-done | bytes 200736 | tf_op jit(solution)/shard_map/ppermute | solution.py:56
  203.8 3.0 %collective-permute-start.35 = (bf16[208,128]{1,0:T(8,128)(2,1)S(1)}, bf16[208,128]{1,0:T(8,128)(2,1)S(1)}, u32[]{:S(2)}, u32[]{:S(2)}) collective-permute-start(bf16[208,128]{1,0:T(8,128)(2,1)S(1)} %get-tuple-element.257), channel_id=1, source_target_pairs={{0,1},{1,0},{2,3},{3,2},{4,5},{5,4},{6,7},{7,6},{8,9},{9,8},{10,11... | collective-permute-start | bytes 159752 | tf_op jit(solution)/shard_map/ppermute | solution.py:56
  207.9 1.4 collective-permute-start.37
  211.1 3.7 %shard_map.494 = f32[512,512]{1,0:T(8,128)} custom-call(f32[512,512]{1,0:T(8,128)} %copy-done.24, bf16[512,256]{1,0:T(8,128)(2,1)S(1)} %get-tuple-element.158.dqa, bf16[512,256]{1,0:T(8,128)(2,1)S(1)} %get-tuple-element.159.dka, bf16[512,256]{1,0:T(8,128)(2,1)S(1)} %get-tuple-element.160.dva, bf16[512,256]{1,0:T(8,128)(2,1)S(1)} %get-tuple-element.167.dqb, ...), custom_call_target="tpu_custom_call" | custom-call | flops 6291456 | bytes 98304 | tf_op jit(solution)/shard_map/pallas_call | solution.py:847
  (266 shorter events, 54.0 us)
Async XLA Ops:
  5.0 7.4 %collective-permute-start.1 = (bf16[1,5,64,128]{3,2,1,0:T(8,128)(2,1)}, bf16[1,5,64,128]{3,2,1,0:T(8,128)(2,1)S(1)}, u32[]{:S(2)}, u32[]{:S(2)}) collective-permute-start(bf16[1,5,64,128]{3,2,1,0:T(8,128)(2,1)} %bitcast.86), channel_id=1, source_target_pairs={{0,1},{1,0},{2,3},{3,2},{4,5},{5,4},{6,7},{7,6},{8,9},{9,8},{10,11... | collective-permute-start | bytes 245768 | tf_op jit(solution)/shard_map/ppermute | solution.py:56
  8.0 5.3 %collective-permute-start.2 = (bf16[208,128]{1,0:T(8,128)(2,1)}, bf16[208,128]{1,0:T(8,128)(2,1)S(1)}, u32[]{:S(2)}, u32[]{:S(2)}) collective-permute-start(bf16[208,128]{1,0:T(8,128)(2,1)} %shard_map.475), channel_id=1, source_target_pairs={{0,1},{1,0},{2,3},{3,2},{4,5},{5,4},{6,7},{7,6},{8,9},{9,8},{10,11... | collective-permute-start | bytes 159752 | tf_op jit(solution)/shard_map/ppermute | solution.py:56
  8.1 5.3 %collective-permute-start.3 = (bf16[208,128]{1,0:T(8,128)(2,1)}, bf16[208,128]{1,0:T(8,128)(2,1)S(1)}, u32[]{:S(2)}, u32[]{:S(2)}) collective-permute-start(bf16[208,128]{1,0:T(8,128)(2,1)} %shard_map.475), channel_id=1, source_target_pairs={{0,2},{1,3},{2,0},{3,1},{4,6},{5,7},{6,4},{7,5},{8,10},{9,11},{10,... | collective-permute-start | bytes 159752 | tf_op jit(solution)/shard_map/ppermute | solution.py:56
  11.1 6.1 %collective-permute-start.4 = (bf16[208,128]{1,0:T(8,128)(2,1)}, bf16[208,128]{1,0:T(8,128)(2,1)S(1)}, u32[]{:S(2)}, u32[]{:S(2)}) collective-permute-start(bf16[208,128]{1,0:T(8,128)(2,1)} %shard_map.475), channel_id=1, source_target_pairs={{0,3},{1,2},{2,1},{3,0},{4,7},{5,6},{6,5},{7,4},{8,11},{9,10},{10,... | collective-permute-start | bytes 159752 | tf_op jit(solution)/shard_map/ppermute | solution.py:56
  18.1 30.8 %copy-start.46 = (bf16[208,128]{1,0:T(8,128)(2,1)S(1)}, bf16[208,128]{1,0:T(8,128)(2,1)}, u32[]{:S(2)}) copy-start(bf16[208,128]{1,0:T(8,128)(2,1)} %shard_map.475) | copy-start | bytes 159748
  18.1 7.3 %collective-permute-start.6 = (bf16[1,2,64,512]{3,2,1,0:T(8,128)(2,1)}, bf16[1,2,64,512]{3,2,1,0:T(8,128)(2,1)S(1)}, u32[]{:S(2)}, u32[]{:S(2)}) collective-permute-start(bf16[1,2,64,512]{3,2,1,0:T(8,128)(2,1)} %bitcast.84), channel_id=1, source_target_pairs={{0,1},{1,0},{2,3},{3,2},{4,5},{5,4},{6,7},{7,6},{8,9},{9,8},{10,11... | collective-permute-start | bytes 393224 | tf_op jit(solution)/shard_map/ppermute | solution.py:56
  18.2 9.8 %collective-permute-start.5 = (bf16[2,5,64,128]{3,2,1,0:T(8,128)(2,1)S(1)}, bf16[2,5,64,128]{3,2,1,0:T(8,128)(2,1)S(1)}, u32[]{:S(2)}, u32[]{:S(2)}) collective-permute-start(bf16[2,5,64,128]{3,2,1,0:T(8,128)(2,1)S(1)} %pad_maximum_fusion.17), channel_id=1, source_target_pairs={{0,2},{1,3},{2,0},{3,1},{4,6},{5,7},{6,4},{7,5},{8,10},{9,11},{10,... | collective-permute-start | bytes 491528 | tf_op jit(solution)/shard_map/ppermute | solution.py:56
  21.2 7.7 %collective-permute-start.7 = (bf16[4,3,64,128]{3,2,1,0:T(8,128)(2,1)S(1)}, bf16[4,3,64,128]{3,2,1,0:T(8,128)(2,1)S(1)}, u32[]{:S(2)}, u32[]{:S(2)}) collective-permute-start(bf16[4,3,64,128]{3,2,1,0:T(8,128)(2,1)S(1)} %bitcast.66), channel_id=1, source_target_pairs={{0,8},{1,9},{2,10},{3,11},{4,12},{5,13},{6,14},{7,15},{8,0},{9,1},... | collective-permute-start | bytes 589832 | tf_op jit(solution)/shard_map/ppermute | solution.py:56
  22.7 9.5 %collective-permute-start.8 = (bf16[4,3,64,128]{3,2,1,0:T(8,128)(2,1)S(1)}, bf16[4,3,64,128]{3,2,1,0:T(8,128)(2,1)S(1)}, u32[]{:S(2)}, u32[]{:S(2)}) collective-permute-start(bf16[4,3,64,128]{3,2,1,0:T(8,128)(2,1)S(1)} %bitcast.67), channel_id=1, source_target_pairs={{0,16},{1,17},{2,18},{3,19},{4,20},{5,21},{6,22},{7,23},{8,24},{9,... | collective-permute-start | bytes 589832 | tf_op jit(solution)/shard_map/ppermute | solution.py:56
  24.2 8.0 %collective-permute-start.9 = (bf16[4,3,64,128]{3,2,1,0:T(8,128)(2,1)S(1)}, bf16[4,3,64,128]{3,2,1,0:T(8,128)(2,1)S(1)}, u32[]{:S(2)}, u32[]{:S(2)}) collective-permute-start(bf16[4,3,64,128]{3,2,1,0:T(8,128)(2,1)S(1)} %bitcast.68), channel_id=1, source_target_pairs={{0,24},{1,25},{2,26},{3,27},{4,28},{5,29},{6,30},{7,31},{8,16},{9,... | collective-permute-start | bytes 589832 | tf_op jit(solution)/shard_map/ppermute | solution.py:56
  32.3 18.6 %collective-permute-start.10 = (bf16[4,4,3,64,128]{4,3,2,1,0:T(8,128)(2,1)S(1)}, bf16[4,4,3,64,128]{4,3,2,1,0:T(8,128)(2,1)S(1)}, u32[]{:S(2)}, u32[]{:S(2)}) collective-permute-start(bf16[4,4,3,64,128]{4,3,2,1,0:T(8,128)(2,1)S(1)} %pad_maximum_fusion.2.plane), channel_id=1, source_target_pairs={{0,4},{1,5},{2,6},{3,7},{4,0},{5,1},{6,2},{7,3},{8,12},{9,13},{10,... | collective-permute-start | bytes 2359304 | tf_op jit(solution)/shard_map/ppermute | solution.py:56
  32.4 15.2 %collective-permute-start.11 = (bf16[2,2,64,512]{3,2,1,0:T(8,128)(2,1)S(1)}, bf16[2,2,64,512]{3,2,1,0:T(8,128)(2,1)S(1)}, u32[]{:S(2)}, u32[]{:S(2)}) collective-permute-start(bf16[2,2,64,512]{3,2,1,0:T(8,128)(2,1)S(1)} %pad_maximum_fusion.11), channel_id=1, source_target_pairs={{0,2},{1,3},{2,0},{3,1},{4,6},{5,7},{6,4},{7,5},{8,10},{9,11},{10,... | collective-permute-start | bytes 786440 | tf_op jit(solution)/shard_map/ppermute | solution.py:56
  33.1 19.3 %collective-permute-start = (bf16[512,512]{1,0:T(8,128)(2,1)S(1)}, bf16[512,512]{1,0:T(8,128)(2,1)S(1)}, u32[]{:S(2)}, u32[]{:S(2)}) collective-permute-start(bf16[512,512]{1,0:T(8,128)(2,1)S(1)} %copy-done.4), channel_id=1, source_target_pairs={{0,1},{2,3},{4,5},{6,7},{8,9},{10,11},{12,13},{14,15},{16,17},{18,... | collective-permute-start | bytes 1572872 | tf_op jit(solution)/shard_map/ppermute | solution.py:62
  38.3 15.9 %collective-permute-start.12 = (bf16[4,5,64,128]{3,2,1,0:T(8,128)(2,1)}, bf16[4,5,64,128]{3,2,1,0:T(8,128)(2,1)}, u32[]{:S(2)}, u32[]{:S(2)}) collective-permute-start(bf16[4,5,64,128]{3,2,1,0:T(8,128)(2,1)} %constant_dynamic-update-slice_fusion), channel_id=1, source_target_pairs={{0,8},{1,9},{2,10},{3,11},{4,12},{5,13},{6,14},{7,15},{8,0},{9,1},... | collective-permute-start | bytes 983048 | tf_op jit(solution)/shard_map/ppermute | solution.py:56
  39.2 15.0 %collective-permute-start.13 = (bf16[4,5,64,128]{3,2,1,0:T(8,128)(2,1)}, bf16[4,5,64,128]{3,2,1,0:T(8,128)(2,1)}, u32[]{:S(2)}, u32[]{:S(2)}) collective-permute-start(bf16[4,5,64,128]{3,2,1,0:T(8,128)(2,1)} %constant_dynamic-update-slice_fusion), channel_id=1, source_target_pairs={{0,16},{1,17},{2,18},{3,19},{4,20},{5,21},{6,22},{7,23},{8,24},{9,... | collective-permute-start | bytes 983048 | tf_op jit(solution)/shard_map/ppermute | solution.py:56
  47.7 10.5 %collective-permute-start.14 = (bf16[4,5,64,128]{3,2,1,0:T(8,128)(2,1)}, bf16[4,5,64,128]{3,2,1,0:T(8,128)(2,1)}, u32[]{:S(2)}, u32[]{:S(2)}) collective-permute-start(bf16[4,5,64,128]{3,2,1,0:T(8,128)(2,1)} %constant_dynamic-update-slice_fusion), channel_id=1, source_target_pairs={{0,24},{1,25},{2,26},{3,27},{4,28},{5,29},{6,30},{7,31},{8,16},{9,... | collective-permute-start | bytes 983048 | tf_op jit(solution)/shard_map/ppermute | solution.py:56
  59.6 10.0 %collective-permute-start.16 = (bf16[4,4,5,64,128]{4,3,2,1,0:T(8,128)(2,1)S(1)}, bf16[4,4,5,64,128]{4,3,2,1,0:T(8,128)(2,1)S(1)}, u32[]{:S(2)}, u32[]{:S(2)}) collective-permute-start(bf16[4,4,5,64,128]{4,3,2,1,0:T(8,128)(2,1)S(1)} %pad_maximum_fusion.1.plane), channel_id=1, source_target_pairs={{0,4},{1,5},{2,6},{3,7},{4,0},{5,1},{6,2},{7,3},{8,12},{9,13},{10,... | collective-permute-start | bytes 3932168 | tf_op jit(solution)/shard_map/ppermute | solution.py:56
  59.7 18.3 %collective-permute-start.17 = (bf16[4,2,64,512]{3,2,1,0:T(8,128)(2,1)S(1)}, bf16[4,2,64,512]{3,2,1,0:T(8,128)(2,1)S(1)}, u32[]{:S(2)}, u32[]{:S(2)}) collective-permute-start(bf16[4,2,64,512]{3,2,1,0:T(8,128)(2,1)S(1)} %constant_dynamic-update-slice_fusion.2), channel_id=1, source_target_pairs={{0,8},{1,9},{2,10},{3,11},{4,12},{5,13},{6,14},{7,15},{8,0},{9,1},... | collective-permute-start | bytes 1572872 | tf_op jit(solution)/shard_map/ppermute | solution.py:56
  60.7 17.3 %collective-permute-start.18 = (bf16[4,2,64,512]{3,2,1,0:T(8,128)(2,1)S(1)}, bf16[4,2,64,512]{3,2,1,0:T(8,128)(2,1)S(1)}, u32[]{:S(2)}, u32[]{:S(2)}) collective-permute-start(bf16[4,2,64,512]{3,2,1,0:T(8,128)(2,1)S(1)} %constant_dynamic-update-slice_fusion.2), channel_id=1, source_target_pairs={{0,16},{1,17},{2,18},{3,19},{4,20},{5,21},{6,22},{7,23},{8,24},{9,... | collective-permute-start | bytes 1572872 | tf_op jit(solution)/shard_map/ppermute | solution.py:56
  61.5 24.4 %collective-permute-start.19 = (bf16[4,2,64,512]{3,2,1,0:T(8,128)(2,1)S(1)}, bf16[4,2,64,512]{3,2,1,0:T(8,128)(2,1)S(1)}, u32[]{:S(2)}, u32[]{:S(2)}) collective-permute-start(bf16[4,2,64,512]{3,2,1,0:T(8,128)(2,1)S(1)} %constant_dynamic-update-slice_fusion.2), channel_id=1, source_target_pairs={{0,24},{1,25},{2,26},{3,27},{4,28},{5,29},{6,30},{7,31},{8,16},{9,... | collective-permute-start | bytes 1572872 | tf_op jit(solution)/shard_map/ppermute | solution.py:56
  63.2 7.4 %collective-permute-start.15 = (bf16[128,512]{1,0:T(8,128)(2,1)S(1)}, bf16[128,512]{1,0:T(8,128)(2,1)S(1)}, u32[]{:S(2)}, u32[]{:S(2)}) collective-permute-start(bf16[128,512]{1,0:T(8,128)(2,1)S(1)} %copy-done.26), channel_id=1, source_target_pairs={{0,1},{1,0},{2,3},{3,2},{4,5},{5,4},{6,7},{7,6},{8,9},{9,8},{10,11... | collective-permute-start | bytes 393224 | tf_op jit(solution)/shard_map/ppermute | solution.py:56
  70.7 20.6 %copy-start = (bf16[5,512,512]{2,1,0:T(8,128)(2,1)}, bf16[5,512,512]{2,1,0:T(8,128)(2,1)S(1)}, u32[]{:S(2)}) copy-start(bf16[5,512,512]{2,1,0:T(8,128)(2,1)S(1)} %shard_map.481.w.wo) | copy-start | bytes 7864324
  86.3 4.2 %collective-permute-start.20 = (bf16[4,4,2,64,512]{4,3,2,1,0:T(8,128)(2,1)S(1)}, bf16[4,4,2,64,512]{4,3,2,1,0:T(8,128)(2,1)S(1)}, u32[]{:S(2)}, u32[]{:S(2)}) collective-permute-start(bf16[4,4,2,64,512]{4,3,2,1,0:T(8,128)(2,1)S(1)} %pad_maximum_fusion.plane), channel_id=1, source_target_pairs={{0,4},{1,5},{2,6},{3,7},{4,0},{5,1},{6,2},{7,3},{8,12},{9,13},{10,... | collective-permute-start | bytes 6291464 | tf_op jit(solution)/shard_map/ppermute | solution.py:56
  103.9 7.6 %collective-permute-start.21 = (bf16[2048,512]{1,0:T(8,128)(2,1)S(1)}, bf16[2048,512]{1,0:T(8,128)(2,1)S(1)}, u32[]{:S(2)}, u32[]{:S(2)}) collective-permute-start(bf16[2048,512]{1,0:T(8,128)(2,1)S(1)} %get-tuple-element.141), channel_id=1, source_target_pairs={{0,4},{1,5},{2,6},{3,7},{4,0},{5,1},{6,2},{7,3},{8,12},{9,13},{10,... | collective-permute-start | bytes 6291464 | tf_op jit(solution)/shard_map/ppermute | solution.py:56
  113.9 14.9 %collective-permute-start.23 = (bf16[512,512]{1,0:T(8,128)(2,1)}, bf16[512,512]{1,0:T(8,128)(2,1)}, u32[]{:S(2)}, u32[]{:S(2)}) collective-permute-start(bf16[512,512]{1,0:T(8,128)(2,1)} %pad_maximum_fusion.4), channel_id=1, source_target_pairs={{0,16},{1,17},{2,18},{3,19},{4,20},{5,21},{6,22},{7,23},{8,24},{9,... | collective-permute-start | bytes 1572872 | tf_op jit(solution)/shard_map/ppermute | solution.py:56
  115.5 15.2 %collective-permute-start.22 = (bf16[512,512]{1,0:T(8,128)(2,1)}, bf16[512,512]{1,0:T(8,128)(2,1)}, u32[]{:S(2)}, u32[]{:S(2)}) collective-permute-start(bf16[512,512]{1,0:T(8,128)(2,1)} %pad_maximum_fusion.3), channel_id=1, source_target_pairs={{0,8},{1,9},{2,10},{3,11},{4,12},{5,13},{6,14},{7,15},{8,0},{9,1},... | collective-permute-start | bytes 1572872 | tf_op jit(solution)/shard_map/ppermute | solution.py:56
  128.7 19.3 %collective-permute-start.24 = (bf16[5184,128]{1,0:T(8,128)(2,1)S(1)}, bf16[5184,128]{1,0:T(8,128)(2,1)S(1)}, u32[]{:S(2)}, u32[]{:S(2)}) collective-permute-start(bf16[5184,128]{1,0:T(8,128)(2,1)S(1)} %get-tuple-element.155), channel_id=1, source_target_pairs={{0,4},{1,5},{2,6},{3,7},{4,0},{5,1},{6,2},{7,3},{8,12},{9,13},{10,... | collective-permute-start | bytes 3981320 | tf_op jit(solution)/shard_map/ppermute | solution.py:56
  128.8 5.9 %collective-permute-start.30 = (bf16[128,512]{1,0:T(8,128)(2,1)S(1)}, bf16[128,512]{1,0:T(8,128)(2,1)S(1)}, u32[]{:S(2)}, u32[]{:S(2)}) collective-permute-start(bf16[128,512]{1,0:T(8,128)(2,1)S(1)} %get-tuple-element.176), channel_id=1, source_target_pairs={{0,1},{1,0},{2,3},{3,2},{4,5},{5,4},{6,7},{7,6},{8,9},{9,8},{10,11... | collective-permute-start | bytes 393224 | tf_op jit(solution)/shard_map/ppermute | solution.py:56
  130.1 11.2 %collective-permute-start.26 = (bf16[256,512]{1,0:T(8,128)(2,1)S(1)}, bf16[256,512]{1,0:T(8,128)(2,1)S(1)}, u32[]{:S(2)}, u32[]{:S(2)}) collective-permute-start(bf16[256,512]{1,0:T(8,128)(2,1)S(1)} %get-tuple-element.203), channel_id=1, source_target_pairs={{0,8},{1,9},{2,10},{3,11},{4,12},{5,13},{6,14},{7,15},{8,0},{9,1},... | collective-permute-start | bytes 786440 | tf_op jit(solution)/shard_map/ppermute | solution.py:56
  131.9 9.4 %collective-permute-start.25 = (bf16[256,512]{1,0:T(8,128)(2,1)S(1)}, bf16[256,512]{1,0:T(8,128)(2,1)S(1)}, u32[]{:S(2)}, u32[]{:S(2)}) collective-permute-start(bf16[256,512]{1,0:T(8,128)(2,1)S(1)} %get-tuple-element.205), channel_id=1, source_target_pairs={{0,16},{1,17},{2,18},{3,19},{4,20},{5,21},{6,22},{7,23},{8,24},{9,... | collective-permute-start | bytes 786440 | tf_op jit(solution)/shard_map/ppermute | solution.py:56
  141.5 14.9 %collective-permute-start.43 = (bf16[128,512]{1,0:T(8,128)(2,1)S(1)}, bf16[128,512]{1,0:T(8,128)(2,1)S(1)}, u32[]{:S(2)}, u32[]{:S(2)}) collective-permute-start(bf16[128,512]{1,0:T(8,128)(2,1)S(1)} %pad_maximum_fusion.20), channel_id=1, source_target_pairs={{0,1},{1,0},{2,3},{3,2},{4,5},{5,4},{6,7},{7,6},{8,9},{9,8},{10,11... | collective-permute-start | bytes 393224 | tf_op jit(solution)/shard_map/ppermute | solution.py:56
  144.5 13.4 %collective-permute-start.44 = (bf16[128,512]{1,0:T(8,128)(2,1)S(1)}, bf16[128,512]{1,0:T(8,128)(2,1)S(1)}, u32[]{:S(2)}, u32[]{:S(2)}) collective-permute-start(bf16[128,512]{1,0:T(8,128)(2,1)S(1)} %pad_maximum_fusion.21), channel_id=1, source_target_pairs={{0,2},{1,3},{2,0},{3,1},{4,6},{5,7},{6,4},{7,5},{8,10},{9,11},{10,... | collective-permute-start | bytes 393224 | tf_op jit(solution)/shard_map/ppermute | solution.py:56
  147.9 10.0 %collective-permute-start.45 = (bf16[128,512]{1,0:T(8,128)(2,1)S(1)}, bf16[128,512]{1,0:T(8,128)(2,1)S(1)}, u32[]{:S(2)}, u32[]{:S(2)}) collective-permute-start(bf16[128,512]{1,0:T(8,128)(2,1)S(1)} %pad_maximum_fusion.22), channel_id=1, source_target_pairs={{0,3},{1,2},{2,1},{3,0},{4,7},{5,6},{6,5},{7,4},{8,11},{9,10},{10,... | collective-permute-start | bytes 393224 | tf_op jit(solution)/shard_map/ppermute | solution.py:56
  148.4 10.2 %collective-permute-start.28 = (bf16[1088,128]{1,0:T(8,128)(2,1)S(1)}, bf16[1088,128]{1,0:T(8,128)(2,1)S(1)}, u32[]{:S(2)}, u32[]{:S(2)}) collective-permute-start(bf16[1088,128]{1,0:T(8,128)(2,1)S(1)} %pad_maximum_fusion.10), channel_id=1, source_target_pairs={{0,16},{1,17},{2,18},{3,19},{4,20},{5,21},{6,22},{7,23},{8,24},{9,... | collective-permute-start | bytes 835592 | tf_op jit(solution)/shard_map/ppermute | solution.py:56
  155.3 11.5 %collective-permute-start.27 = (bf16[1536,128]{1,0:T(8,128)(2,1)S(1)}, bf16[1536,128]{1,0:T(8,128)(2,1)S(1)}, u32[]{:S(2)}, u32[]{:S(2)}) collective-permute-start(bf16[1536,128]{1,0:T(8,128)(2,1)S(1)} %pad_maximum_fusion.9), channel_id=1, source_target_pairs={{0,8},{1,9},{2,10},{3,11},{4,12},{5,13},{6,14},{7,15},{8,0},{9,1},... | collective-permute-start | bytes 1179656 | tf_op jit(solution)/shard_map/ppermute | solution.py:56
  159.4 14.4 %collective-permute-start.39 = (bf16[576,128]{1,0:T(8,128)(2,1)}, bf16[576,128]{1,0:T(8,128)(2,1)}, u32[]{:S(2)}, u32[]{:S(2)}) collective-permute-start(bf16[576,128]{1,0:T(8,128)(2,1)} %pad_maximum_fusion.18), channel_id=1, source_target_pairs={{0,8},{1,9},{2,10},{3,11},{4,12},{5,13},{6,14},{7,15},{8,0},{9,1},... | collective-permute-start | bytes 442376 | tf_op jit(solution)/shard_map/ppermute | solution.py:56
  167.6 8.0 %collective-permute-start.38 = (bf16[768,128]{1,0:T(8,128)(2,1)}, bf16[768,128]{1,0:T(8,128)(2,1)}, u32[]{:S(2)}, u32[]{:S(2)}) collective-permute-start(bf16[768,128]{1,0:T(8,128)(2,1)} %get-tuple-element.207), channel_id=1, source_target_pairs={{0,16},{1,17},{2,18},{3,19},{4,20},{5,21},{6,22},{7,23},{8,24},{9,... | collective-permute-start | bytes 589832 | tf_op jit(solution)/shard_map/ppermute | solution.py:56
  173.7 19.2 %collective-permute-start.31 = (bf16[3088,128]{1,0:T(8,128)(2,1)S(1)}, bf16[3088,128]{1,0:T(8,128)(2,1)S(1)}, u32[]{:S(2)}, u32[]{:S(2)}) collective-permute-start(bf16[3088,128]{1,0:T(8,128)(2,1)S(1)} %get-tuple-element.180), channel_id=1, source_target_pairs={{0,4},{1,5},{2,6},{3,7},{4,0},{5,1},{6,2},{7,3},{8,12},{9,13},{10,... | collective-permute-start | bytes 2371592 | tf_op jit(solution)/shard_map/ppermute | solution.py:56
  176.6 9.7 %collective-permute-start.40 = (bf16[384,128]{1,0:T(8,128)(2,1)S(1)}, bf16[384,128]{1,0:T(8,128)(2,1)S(1)}, u32[]{:S(2)}, u32[]{:S(2)}) collective-permute-start(bf16[384,128]{1,0:T(8,128)(2,1)S(1)} %get-tuple-element.254), channel_id=1, source_target_pairs={{0,1},{1,0},{2,3},{3,2},{4,5},{5,4},{6,7},{7,6},{8,9},{9,8},{10,11... | collective-permute-start | bytes 294920 | tf_op jit(solution)/shard_map/ppermute | solution.py:56
  180.8 11.4 %collective-permute-start.41 = (bf16[384,128]{1,0:T(8,128)(2,1)S(1)}, bf16[384,128]{1,0:T(8,128)(2,1)S(1)}, u32[]{:S(2)}, u32[]{:S(2)}) collective-permute-start(bf16[384,128]{1,0:T(8,128)(2,1)S(1)} %get-tuple-element.255), channel_id=1, source_target_pairs={{0,2},{1,3},{2,0},{3,1},{4,6},{5,7},{6,4},{7,5},{8,10},{9,11},{10,... | collective-permute-start | bytes 294920 | tf_op jit(solution)/shard_map/ppermute | solution.py:56
  184.4 7.8 %collective-permute-start.42 = (bf16[384,128]{1,0:T(8,128)(2,1)S(1)}, bf16[384,128]{1,0:T(8,128)(2,1)S(1)}, u32[]{:S(2)}, u32[]{:S(2)}) collective-permute-start(bf16[384,128]{1,0:T(8,128)(2,1)S(1)} %get-tuple-element.256), channel_id=1, source_target_pairs={{0,3},{1,2},{2,1},{3,0},{4,7},{5,6},{6,5},{7,4},{8,11},{9,10},{10,... | collective-permute-start | bytes 294920 | tf_op jit(solution)/shard_map/ppermute | solution.py:56
  185.1 26.0 %collective-permute-start.29 = (bf16[512,512]{1,0:T(8,128)(2,1)S(1)}, bf16[512,512]{1,0:T(8,128)(2,1)S(1)}, u32[]{:S(2)}, u32[]{:S(2)}) collective-permute-start(bf16[512,512]{1,0:T(8,128)(2,1)S(1)} %copy-done.39), channel_id=1, source_target_pairs={{1,0},{3,2},{5,4},{7,6},{9,8},{11,10},{13,12},{15,14},{17,16},{19,... | collective-permute-start | bytes 1572872 | tf_op jit(solution)/shard_map/ppermute | solution.py:62
  193.2 8.0 %collective-permute-start.32 = (bf16[784,128]{1,0:T(8,128)(2,1)S(1)}, bf16[784,128]{1,0:T(8,128)(2,1)S(1)}, u32[]{:S(2)}, u32[]{:S(2)}) collective-permute-start(bf16[784,128]{1,0:T(8,128)(2,1)S(1)} %get-tuple-element.259), channel_id=1, source_target_pairs={{0,8},{1,9},{2,10},{3,11},{4,12},{5,13},{6,14},{7,15},{8,0},{9,1},... | collective-permute-start | bytes 602120 | tf_op jit(solution)/shard_map/ppermute | solution.py:56
  193.8 9.8 %collective-permute-start.33 = (bf16[784,128]{1,0:T(8,128)(2,1)S(1)}, bf16[784,128]{1,0:T(8,128)(2,1)S(1)}, u32[]{:S(2)}, u32[]{:S(2)}) collective-permute-start(bf16[784,128]{1,0:T(8,128)(2,1)S(1)} %get-tuple-element.260), channel_id=1, source_target_pairs={{0,16},{1,17},{2,18},{3,19},{4,20},{5,21},{6,22},{7,23},{8,24},{9,... | collective-permute-start | bytes 602120 | tf_op jit(solution)/shard_map/ppermute | solution.py:56
  195.0 8.7 %collective-permute-start.34 = (bf16[784,128]{1,0:T(8,128)(2,1)S(1)}, bf16[784,128]{1,0:T(8,128)(2,1)S(1)}, u32[]{:S(2)}, u32[]{:S(2)}) collective-permute-start(bf16[784,128]{1,0:T(8,128)(2,1)S(1)} %get-tuple-element.261), channel_id=1, source_target_pairs={{0,24},{1,25},{2,26},{3,27},{4,28},{5,29},{6,30},{7,31},{8,16},{9,... | collective-permute-start | bytes 602120 | tf_op jit(solution)/shard_map/ppermute | solution.py:56
  203.8 11.0 %collective-permute-start.35 = (bf16[208,128]{1,0:T(8,128)(2,1)S(1)}, bf16[208,128]{1,0:T(8,128)(2,1)S(1)}, u32[]{:S(2)}, u32[]{:S(2)}) collective-permute-start(bf16[208,128]{1,0:T(8,128)(2,1)S(1)} %get-tuple-element.257), channel_id=1, source_target_pairs={{0,1},{1,0},{2,3},{3,2},{4,5},{5,4},{6,7},{7,6},{8,9},{9,8},{10,11... | collective-permute-start | bytes 159752 | tf_op jit(solution)/shard_map/ppermute | solution.py:56
  206.8 8.0 %collective-permute-start.36 = (bf16[208,128]{1,0:T(8,128)(2,1)S(1)}, bf16[208,128]{1,0:T(8,128)(2,1)S(1)}, u32[]{:S(2)}, u32[]{:S(2)}) collective-permute-start(bf16[208,128]{1,0:T(8,128)(2,1)S(1)} %get-tuple-element.258), channel_id=1, source_target_pairs={{0,2},{1,3},{2,0},{3,1},{4,6},{5,7},{6,4},{7,5},{8,10},{9,11},{10,... | collective-permute-start | bytes 159752 | tf_op jit(solution)/shard_map/ppermute | solution.py:56
  207.9 6.9 %collective-permute-start.37 = (bf16[208,128]{1,0:T(8,128)(2,1)S(1)}, bf16[208,128]{1,0:T(8,128)(2,1)S(1)}, u32[]{:S(2)}, u32[]{:S(2)}) collective-permute-start(bf16[208,128]{1,0:T(8,128)(2,1)S(1)} %concatenate.105), channel_id=1, source_target_pairs={{0,3},{1,2},{2,1},{3,0},{4,7},{5,6},{6,5},{7,4},{8,11},{9,10},{10,... | collective-permute-start | bytes 159752 | tf_op jit(solution)/shard_map/ppermute | solution.py:56
  (56 other events, 326.7 us)

commit v3 on v2

v3 whole, which is shorter than its diff:
```python
import functools

import jax
import jax.numpy as jnp
from jax import lax
from jax.experimental import pallas as pl
from jax.experimental.pallas import tpu as pltpu
from jax.sharding import PartitionSpec as P

HD = 64
LEN = 1024
MEM = 256
PAIR = 128
BLOCK = 256
BACK_BLOCK = 512

EPSILON = 1e-05
MASKED = -1e30
SCALE = float(HD) ** (-0.5)

F32 = jnp.float32
BF16 = jnp.bfloat16
NN = (((1,), (0,)), ((), ()))
NT = (((1,), (1,)), ((), ()))
TN = (((0,), (0,)), ((), ()))
SMEM = pl.BlockSpec(memory_space=pltpu.SMEM)
ANY = pl.BlockSpec(memory_space=pl.ANY)
VMEM = pl.BlockSpec(memory_space=pltpu.VMEM)


def mm(left_side, right_side, dims):
    return lax.dot_general(left_side, right_side, dims, preferred_element_type=F32)


def shaped(shape, dtype):
    return jax.ShapeDtypeStruct(shape, dtype)


def cost(macs, moved):
    return pl.CostEstimate(flops=macs // 64, bytes_accessed=moved // 64, transcendentals=0)


def limit(mebibytes):
    return pltpu.CompilerParams(vmem_limit_bytes=mebibytes << 20)


def far(*arrays):
    return [pltpu.with_memory_space_constraint(array, pltpu.HBM) for array in arrays]


def swap(array, dp_mask, tensor_mask):
    nd, nt = lax.axis_size("dp"), lax.axis_size("tensor")
    pairs = [
        (d * nt + t, (d ^ dp_mask) * nt + (t ^ tensor_mask)) for d in range(nd) for t in range(nt)
    ]
    return lax.ppermute(array, ("dp", "tensor"), pairs)


def hand_over(array, parity, step):
    nd, nt = lax.axis_size("dp"), lax.axis_size("tensor")
    pairs = [(d * nt + t, d * nt + t + step) for d in range(nd) for t in range(parity, nt, 2)]
    return lax.ppermute(array, ("dp", "tensor"), pairs)


def tree_sum(terms):
    while len(terms) > 1:
        terms = [terms[i] + terms[i + 1] for i in range(0, len(terms), 2)]
    return terms[0]


def doubled(line, bits):
    for bit in bits:
        line = jnp.concatenate([line, swap(line, 0, bit)])
    return line


def over_planes(line):
    return [line] + [swap(line, 2 * j, 0) for j in range(1, lax.axis_size("dp") // 2)]


def both_cores(planes, *others):
    plane = jnp.stack([after(planes[0], *others)] + planes[1:])
    return plane, swap(plane, 1, 0)


class Halves:
    def __init__(self, groups, r, rider):
        self.planes, self.nt = lax.axis_size("dp") // 2, lax.axis_size("tensor")
        self.groups, self.r, self.rider = groups, r, rider
        self.rounds = self.planes.bit_length() - 1
        self.sizes = [self.nt * count * r for count in groups]
        self.bases = [self.planes * sum(self.sizes[:g]) for g in range(len(groups))]
        self.main = self.planes * sum(self.sizes)
        self.total = self.main + rider

    def bit(self, group, index):
        return 1 << (index if group % 2 == 0 else self.rounds - 1 - index)

    def place(self, i, j):
        group = 0
        while i >= self.groups[group]:
            i -= self.groups[group]
            group += 1
        bits = [self.bit(group, index) for index in range(self.rounds)]
        position = sum((j & b > 0) << (self.rounds - 1 - n) for n, b in enumerate(bits))
        count = self.groups[group]
        return self.bases[group] + position * self.sizes[group] + i * self.r, count * self.r

    def split(self, arrays, held, rider, index):
        stay, sent = [], []
        for group, terms in enumerate(held):
            rows = (self.planes >> (index + 1)) * self.sizes[group]
            stay.append([(rows, terms)])
            sent.append([(rows, [(array, lo + rows) for array, lo in terms])])
        if self.rider:
            sent[-1].append((self.rider, rider))
        return stay + sent

    def line(self, held, rider):
        plans = []
        for k in range(self.nt):
            plan = []
            for group, terms in enumerate(held):
                rows = self.groups[group] * self.r
                plan.append((rows, [(array, lo + k * rows) for array, lo in terms]))
            if self.rider:
                plan.append((self.rider, rider))
            plans.append(plan)
        return plans


def add_rows_kernel(*refs, plans, count):
    for out, plan in zip(refs[count:], plans):
        at = 0
        for rows, terms in plan:
            total = tree_sum([refs[i][lo : lo + rows, :].astype(F32) for i, lo in terms])
            out[at : at + rows, :] = total.astype(out.dtype)
            at += rows


def add_rows(arrays, plans, dtype=BF16):
    width = arrays[0].shape[1]
    moved = sum(array.size * array.dtype.itemsize for array in arrays)
    return pl.pallas_call(
        functools.partial(add_rows_kernel, plans=plans, count=len(arrays)),
        out_shape=tuple(shaped((sum(n for n, _ in plan), width), dtype) for plan in plans),
        in_specs=[VMEM] * len(arrays),
        out_specs=(VMEM,) * len(plans),
        compiler_params=limit(20),
        cost_estimate=cost(0, 2 * moved),
    )(*arrays)


def halve(halves, arrays, held, rider, index):
    groups = len(halves.groups)
    outs = list(add_rows(arrays, halves.split(arrays, held, rider, index)))
    stay, sent = outs[:groups], outs[groups:]
    got = [swap(part, 2 * halves.bit(group, index), 0) for group, part in enumerate(sent)]
    held = [[(group, 0), (groups + group, 0)] for group in range(groups)]
    end = sent[-1].shape[0] - halves.rider
    rider = [(2 * groups, end), (2 * groups - 1, end)]
    return stay + got + sent[-1:], held, rider


def line_swaps(parts):
    return [parts[0]] + [swap(part, 0, k) for k, part in enumerate(parts) if k]


def after(array, *others):
    return lax.optimization_barrier((array,) + others)[0]


def slot_blocks(info, planes, nt):
    for j in range(planes):
        for c in range(2):
            d = jnp.bitwise_xor(info[2], 2 * j + c)
            for s in range(nt):
                yield j, c, s, d, jnp.bitwise_xor(info[3], s)


def aligned(r, w):
    return w % PAIR == 0 and r % 16 == 0


def assemble_kernel(info, *refs, planes):
    whole = refs[-1]
    nt, n, r, w = refs[0].shape[-4:]
    for j, c, s, d, t in slot_blocks(info, planes, nt):
        rows = pl.ds(pl.multiple_of(d * r, r), r)
        columns = pl.ds(pl.multiple_of(t * w, w), w)
        piece = refs[c].at[j] if len(refs) == 3 else refs[c * planes + j]
        for i in range(n):
            whole[i, rows, columns] = piece[s, i]


def assemble(info, halves):
    nt, n, r, w = halves[0].shape[-4:]
    planes = lax.axis_size("dp") // 2
    nd = 2 * planes
    if aligned(r, w):
        return pl.pallas_call(
            functools.partial(assemble_kernel, planes=planes),
            out_shape=shaped((n, nd * r, nt * w), BF16),
            in_specs=[SMEM] + [VMEM] * len(halves),
            out_specs=VMEM,
            compiler_params=limit(18),
            cost_estimate=cost(0, 8 * nd * nt * n * r * w),
        )(info, *halves)
    full = jnp.stack(halves).reshape(2, planes, nt, n, r, w).swapaxes(0, 1)
    full = full.reshape(nd, nt, n, r, w)
    full = jnp.take(full, jnp.bitwise_xor(jnp.arange(nd), info[2]), axis=0)
    full = jnp.take(full, jnp.bitwise_xor(jnp.arange(nt), info[3]), axis=1)
    return full.transpose(2, 0, 3, 1, 4).reshape(n, nd * r, nt * w)


def disperse(info, halves, scratch, i, t, s, keep, send):
    for j in range(halves.planes):
        base, stride = halves.place(i, j)
        lo = base + s * stride
        if not isinstance(s, int):
            lo = pl.multiple_of(lo, 16)
        for c in range(2):
            d = jnp.bitwise_xor(info[2], 2 * j + c)
            rows = pl.ds(pl.multiple_of(d * halves.r, halves.r), halves.r)
            (keep, send)[c][pl.ds(lo, halves.r), :] = scratch[rows, t]


def disperse_whole(info, halves, scratch, i, keep, send):
    w = keep.shape[1]
    for s in range(halves.nt):
        t = jnp.bitwise_xor(info[3], s)
        disperse(info, halves, scratch, i, pl.ds(pl.multiple_of(t * w, w), w), s, keep, send)


def disperse_plain(info, halves, whole, rider):
    nd, nt = 2 * halves.planes, halves.nt
    n, r, w = whole.shape[0], halves.r, whole.shape[2] // nt
    full = whole.reshape(n, nd, r, nt, w).transpose(1, 3, 0, 2, 4)
    full = jnp.take(full, jnp.bitwise_xor(jnp.arange(nd), info[2]), axis=0)
    full = jnp.take(full, jnp.bitwise_xor(jnp.arange(nt), info[3]), axis=1)
    full = full.reshape(nd // 2, 2, nt, n, r, w)
    flats = []
    for c in range(2):
        rows, first = [], 0
        for count in halves.groups:
            order = sorted(range(halves.planes), key=lambda j: halves.place(first, j)[0])
            group = jnp.stack([full[j, c, :, first : first + count] for j in order])
            rows.append(group.reshape(-1, w))
            first += count
        flats.append(jnp.concatenate(rows + [rider]))
    return flats


def pack_kernel(*refs, blocks):
    out = refs[-1]
    r, w = refs[0].shape
    for i, block in enumerate(refs[:blocks]):
        out[i * r : (i + 1) * r, :] = block[...]
    row = lax.broadcasted_iota(jnp.int32, (16, w), 0)
    filled = jnp.zeros((16, w), F32)
    count = 0
    for vector in refs[blocks:-1]:
        for i in range(vector.shape[0]):
            filled = jnp.where(row == count, vector[i : i + 1, :].astype(F32), filled)
            count += 1
    out[blocks * r :, :] = filled.astype(BF16)


def pack(blocks, vectors):
    r, w = blocks[0].shape
    if aligned(r, w):
        return pl.pallas_call(
            functools.partial(pack_kernel, blocks=len(blocks)),
            out_shape=shaped((len(blocks) * r + 16, w), BF16),
            in_specs=[VMEM] * (len(blocks) + len(vectors)),
            out_specs=VMEM,
            cost_estimate=cost(0, 32 * r * w),
        )(*blocks, *[vector.reshape(-1, w) for vector in vectors])
    rows = jnp.concatenate(vectors).reshape(-1, w)
    return jnp.concatenate(list(blocks) + [jnp.pad(rows, ((0, 16 - rows.shape[0]), (0, 0)))])


def spread_kernel(info, riders, small, hidden):
    nt, _, w = riders.shape
    for s in range(nt):
        t = jnp.bitwise_xor(info[3], s)
        block = riders[s].astype(F32)
        small[:, pl.ds(pl.multiple_of(t * w, w), w)] = block
        for i in range(4):
            hidden[:, pl.ds(pl.multiple_of((4 * t + i) * w, w), w)] = block[4 + i : 5 + i]


def spread(info, riders):
    nt, _, w = riders.shape
    if aligned(16, w):
        return pl.pallas_call(
            spread_kernel,
            out_shape=(shaped((16, nt * w), F32), shaped((1, 4 * nt * w), F32)),
            in_specs=[SMEM, VMEM],
            out_specs=(VMEM, VMEM),
            cost_estimate=cost(0, 64 * nt * w),
        )(info, riders)
    full = jnp.take(riders, jnp.bitwise_xor(jnp.arange(nt), info[3]), axis=0).astype(F32)
    return full.transpose(1, 0, 2).reshape(16, nt * w), full[:, 4:8].reshape(1, -1)


def norm_forward(summed):
    row_mean = jnp.mean(summed, axis=-1, keepdims=True)
    centred = summed - row_mean
    variance = jnp.mean(centred * centred, axis=-1, keepdims=True)
    inverse = lax.rsqrt(variance + EPSILON)
    return centred * inverse, inverse


def norm_backward(grad_out, normed, inverse, norm_gain):
    grad_normed = grad_out * norm_gain
    return inverse * (
        grad_normed
        - jnp.mean(grad_normed, axis=-1, keepdims=True)
        - normed * jnp.mean(grad_normed * normed, axis=-1, keepdims=True)
    )


def column_sum(values):
    return jnp.sum(values.astype(F32), axis=0, keepdims=True)


def head_lanes(e):
    lane = lax.broadcasted_iota(jnp.int32, (1, PAIR), 1)
    chosen = (lane < HD) if e == 0 else (lane >= HD)
    return jnp.where(chosen, 1.0, 0.0)


def join_heads(first, second):
    lane = lax.broadcasted_iota(jnp.int32, first.shape, 1)
    return jnp.where(lane < HD, first, second)


def attend_forward(q, segments, contexts, logs, lo):
    rows = slice(lo, lo + BLOCK)
    results = []
    for e in range(2):
        query = q[rows, :] * head_lanes(e).astype(BF16)
        scores = [edit(mm(query, k, NT)) for k, _, edit in segments]
        peak = functools.reduce(
            jnp.maximum, [jnp.max(piece, axis=-1, keepdims=True) for piece in scores]
        )
        total = None
        for piece, (_, v, _) in zip(scores, segments):
            weights = jnp.exp(piece - peak).astype(BF16)
            wide = jnp.concatenate([v, jnp.ones(v.shape, BF16)], axis=1)
            part = mm(weights, wide, NN)
            total = part if total is None else total + part
        row_total = total[:, PAIR:]
        results.append((total[:, :PAIR] / row_total, peak + jnp.log(row_total)))
    contexts[rows, :] = join_heads(results[0][0], results[1][0]).astype(BF16)
    logs[rows, :] = join_heads(results[0][1], results[1][1])


def attend_backward(q, grad, ctx, logs, segments, grad_query, lo):
    rows = slice(lo, lo + BACK_BLOCK)
    grad_rows = grad[rows, :]
    product = grad_rows.astype(F32) * ctx[rows, :].astype(F32)
    query_rows = q[rows, :]
    query_turned = jnp.transpose(query_rows)
    grad_turned = jnp.transpose(grad_rows)
    total = None
    for e in range(2):
        lanes = head_lanes(e)
        low_lanes = lanes.astype(BF16)
        delta = jnp.sum(product * lanes, axis=-1, keepdims=True)
        row_log = logs[rows, e * HD : e * HD + 1]
        grad_low = grad_rows * low_lanes
        query = query_rows * low_lanes
        for k, v, edit, add in segments:
            weights = jnp.exp(edit(mm(query, k, NT)) - row_log)
            slope = mm(grad_low, v, NT) - delta
            grad_scores = (weights * slope).astype(BF16)
            part = mm(grad_scores, k * low_lanes, NN)
            total = part if total is None else total + part
            head = slice(e * HD, e * HD + HD)
            add(
                head,
                mm(query_turned[head], grad_scores, NN),
                mm(grad_turned[head], weights.astype(BF16), NN),
            )
    grad_query[rows, :] = (total * SCALE).astype(BF16)


def same(scores):
    return scores


def masked(lo, col_lo, prefix_len):
    def edit(scores):
        row = lo + lax.broadcasted_iota(jnp.int32, scores.shape, 0)
        col = col_lo + lax.broadcasted_iota(jnp.int32, scores.shape, 1)
        allowed = col <= row
        if prefix_len is not None:
            allowed = allowed | (col < prefix_len)
        return jnp.where(allowed, scores, MASKED)

    return edit


def adder(keys, values, col_lo, width):
    def add(head, part_keys, part_values):
        keys[head, col_lo : col_lo + width] += part_keys
        values[head, col_lo : col_lo + width] += part_values

    return add


def self_forward_kernel(info, q, k, v, ko, vo, ctx, logs):
    tokens = q.shape[0]

    @pl.when(info[0] == 0)
    def _():
        for lo in range(0, tokens, BLOCK):
            attend_forward(q, [(k[...], v[...], masked(lo, 0, info[1]))], ctx, logs, lo)

    @pl.when(info[0] != 0)
    def _():
        for lo in range(0, tokens, BLOCK):
            near = slice(lo, lo + BLOCK)
            segments = [(ko[...], vo[...], same)]
            if lo:
                segments.append((k[:lo, :], v[:lo, :], same))
            segments.append((k[near, :], v[near, :], masked(lo, lo, None)))
            attend_forward(q, segments, ctx, logs, lo)


def self_backward_kernel(
    info, q, k, v, ko, vo, ctx, logs, low, w, dq, dk, dv, dko, dvo, ak, av, ako, avo, grad
):
    tokens = q.shape[0]
    ak[...] = jnp.zeros_like(ak)
    av[...] = jnp.zeros_like(av)
    grad[...] = mm(low[...], w[0], NN).astype(BF16)

    @pl.when(info[0] == 0)
    def _():
        for lo in range(0, tokens, BACK_BLOCK):
            segments = [(k[...], v[...], masked(lo, 0, info[1]), adder(ak, av, 0, tokens))]
            attend_backward(q, grad, ctx, logs, segments, dq, lo)

    @pl.when(info[0] != 0)
    def _():
        ako[...] = jnp.zeros_like(ako)
        avo[...] = jnp.zeros_like(avo)
        for lo in range(0, tokens, BACK_BLOCK):
            near = slice(lo, lo + BACK_BLOCK)
            segments = [(ko[...], vo[...], same, adder(ako, avo, 0, tokens))]
            if lo:
                segments.append((k[:lo, :], v[:lo, :], same, adder(ak, av, 0, lo)))
            segments.append(
                (k[near, :], v[near, :], masked(lo, lo, None), adder(ak, av, lo, BACK_BLOCK))
            )
            attend_backward(q, grad, ctx, logs, segments, dq, lo)
        dko[...] = jnp.transpose(ako[...]).astype(BF16)
        dvo[...] = jnp.transpose(avo[...]).astype(BF16)

    dk[...] = jnp.transpose(ak[...]).astype(BF16)
    dv[...] = jnp.transpose(av[...]).astype(BF16)


def cross_forward_kernel(q, k, v, ctx, logs):
    for lo in range(0, q.shape[0], BLOCK):
        attend_forward(q, [(k[...], v[...], same)], ctx, logs, lo)


def cross_backward_kernel(q, k, v, ctx, logs, low, w, dq, dk, dv, ak, av, grad):
    ak[...] = jnp.zeros_like(ak)
    av[...] = jnp.zeros_like(av)
    grad[...] = mm(low[...], w[0], NN).astype(BF16)
    for lo in range(0, q.shape[0], BACK_BLOCK):
        segments = [(k[...], v[...], same, adder(ak, av, 0, k.shape[0]))]
        attend_backward(q, grad, ctx, logs, segments, dq, lo)
    dk[...] = jnp.transpose(ak[...]).astype(BF16)
    dv[...] = jnp.transpose(av[...]).astype(BF16)


def lanes_of(rows, first=0):
    return pl.BlockSpec((rows, PAIR), lambda h: (0, first + h))


def output_columns(slot, width, first=0):
    return pl.BlockSpec((1, width, PAIR), lambda h: (slot, 0, first + h))


def self_forward(info, q, k, v, ko, vo):
    tokens, width = q.shape
    row = lanes_of(tokens)
    return pl.pallas_call(
        self_forward_kernel,
        grid=(width // PAIR,),
        out_shape=(shaped((tokens, width), BF16), shaped((tokens, width), F32)),
        in_specs=[SMEM] + [row] * 5,
        out_specs=(row, row),
        compiler_params=limit(16),
        cost_estimate=cost(width // HD * tokens * tokens * 2 * 256 * 2, 5 << 20),
    )(info, q, k, v, ko, vo)


def self_backward(info, q, k, v, ko, vo, ctx, logs, low, w, first, pairs):
    tokens, width = q.shape
    row = lanes_of(tokens, first)
    out = shaped((tokens, pairs * PAIR), BF16)
    return pl.pallas_call(
        self_backward_kernel,
        grid=(pairs,),
        out_shape=(out,) * 5,
        in_specs=[SMEM] + [row] * 7 + [VMEM, output_columns(3, width, first)],
        out_specs=(lanes_of(tokens),) * 5,
        scratch_shapes=[pltpu.VMEM((PAIR, tokens), F32)] * 4 + [pltpu.VMEM((tokens, PAIR), BF16)],
        compiler_params=limit(16),
        cost_estimate=cost(width // HD * tokens * tokens * 256 * 5, 8 << 20),
    )(info, *far(q, k, v, ko, vo, ctx, logs), low, *far(w))


def cross_forward(q, k, v):
    tokens, width = q.shape
    rows = k.shape[0]
    return pl.pallas_call(
        cross_forward_kernel,
        grid=(width // PAIR,),
        out_shape=(shaped((tokens, width), BF16), shaped((tokens, width), F32)),
        in_specs=[lanes_of(tokens), lanes_of(rows), lanes_of(rows)],
        out_specs=(lanes_of(tokens), lanes_of(tokens)),
        compiler_params=limit(16),
        cost_estimate=cost(width // HD * tokens * rows * 256 * 2, 3 << 20),
    )(q, k, v)


def cross_backward(q, k, v, ctx, logs, low, w):
    tokens, width = q.shape
    rows = k.shape[0]
    small = shaped((rows, width), BF16)
    return pl.pallas_call(
        cross_backward_kernel,
        grid=(width // PAIR,),
        out_shape=(shaped((tokens, width), BF16), small, small),
        in_specs=[lanes_of(tokens), lanes_of(rows), lanes_of(rows)]
        + [lanes_of(tokens)] * 2
        + [VMEM, output_columns(7, width)],
        out_specs=(lanes_of(tokens), lanes_of(rows), lanes_of(rows)),
        scratch_shapes=[pltpu.VMEM((PAIR, rows), F32)] * 2 + [pltpu.VMEM((tokens, PAIR), BF16)],
        compiler_params=limit(16),
        cost_estimate=cost(width // HD * tokens * rows * 256 * 5, 4 << 20),
    )(*far(q, k, v, ctx, logs), low, *far(w))


def project_self_kernel(info, x, xo, wq, wk, wv, b, q, k, v, ko, vo):
    rows = x[...]
    q[...] = (mm(rows, wq[0], NN) + b[0:1, :]).astype(BF16) * jnp.asarray(SCALE, BF16)
    k[...] = mm(rows, wk[0], NN).astype(BF16)
    v[...] = (mm(rows, wv[0], NN) + b[1:2, :]).astype(BF16)

    @pl.when(info[0] != 0)
    def _():
        other = xo[...]
        ko[...] = mm(other, wk[0], NN).astype(BF16)
        vo[...] = (mm(other, wv[0], NN) + b[1:2, :]).astype(BF16)


def project_self(info, x, xo, w, b):
    low = shaped(x.shape, BF16)
    return pl.pallas_call(
        project_self_kernel,
        grid=(1,),
        out_shape=(low,) * 5,
        in_specs=[SMEM] + [VMEM] * 2 + [matrix(i, x.shape[1]) for i in range(3)] + [VMEM],
        compiler_params=limit(16),
        cost_estimate=cost(5 * x.size * x.shape[1], 5 << 20),
    )(info, x, xo, w, w, w, b)


def first_norm_kernel(
    ctx, x, mem, memo, wo, wq, wk, wv, ob, gain, bias, b, first, normed, inverse, q, k, v
):
    summed = x[...].astype(F32) + mm(ctx[...], wo[0], NT) + ob[...].astype(F32)
    n, r = norm_forward(summed)
    out = n * gain[...].astype(F32) + bias[...].astype(F32)
    normed[...] = n
    inverse[...] = r
    first[...] = out
    q[...] = (mm(out.astype(BF16), wq[0], NN) + b[2:3, :]).astype(BF16) * jnp.asarray(SCALE, BF16)
    rows = mem.shape[0]
    for source, lo in ((mem, 0), (memo, rows)):
        k[lo : lo + rows, :] = mm(source[...], wk[0], NN).astype(BF16)
        v[lo : lo + rows, :] = (mm(source[...], wv[0], NN) + b[3:4, :]).astype(BF16)


def first_norm(ctx, x, mem, memo, w, ob, gain, bias, b):
    rows = 2 * mem.shape[0]
    tokens, width = x.shape
    full = shaped(x.shape, F32)
    return pl.pallas_call(
        first_norm_kernel,
        grid=(1,),
        out_shape=(
            full,
            full,
            shaped((tokens, 1), F32),
            shaped(x.shape, BF16),
            shaped((rows, width), BF16),
            shaped((rows, width), BF16),
        ),
        in_specs=[VMEM] * 4 + [matrix(i, width) for i in range(3, 7)] + [VMEM] * 4,
        compiler_params=limit(16),
        cost_estimate=cost(3 * x.size * width, 8 << 20),
    )(ctx, x, mem, memo, w, w, w, w, ob, gain, bias, b)


def feed_kernel(
    info,
    ctx,
    first,
    cot,
    wo,
    wf,
    ob,
    gain2,
    bias2,
    fib,
    fob,
    gain3,
    bias3,
    out,
    keep,
    send,
    du2,
    db2,
    sums,
    hsum,
    act,
    slope,
    acc,
    second,
    turn,
    *,
    halves,
):
    tokens, width = first.shape
    w = keep.shape[1]
    summed = first[...] + mm(ctx[...], wo[0], NT) + ob[...].astype(F32)
    n2, r2 = norm_forward(summed)
    out2 = n2 * gain2[...].astype(F32) + bias2[...].astype(F32)
    second[...] = out2.astype(BF16)
    acc[...] = out2 + fob[...].astype(F32)

    @pl.loop(0, halves.nt, unroll=2)
    def _(t):
        cols = pl.ds(pl.multiple_of(t * w, w), w)
        hidden = mm(second[...], wf[0, :, cols], NN) + fib[:, cols]
        gate = 1.0 / (1.0 + jnp.exp(-hidden))
        active = (hidden * gate).astype(BF16)
        act[:, cols] = active
        slope[:, cols] = (gate * (1.0 + hidden * (1.0 - gate))).astype(BF16)
        acc[...] += mm(active, wf[1, :, cols], NT)

    n3, r3 = norm_forward(acc[...])
    out[...] = (n3 * gain3[...].astype(F32) + bias3[...].astype(F32)).astype(BF16)
    dy = cot[...].astype(F32)
    du3 = norm_backward(dy, n3, r3, gain3[...].astype(F32))
    db3 = du3.astype(BF16)
    sums[3:4, :] = column_sum(db3)
    sums[4:5, :] = column_sum(dy * n3)
    sums[5:6, :] = column_sum(dy)
    acc[...] = du3
    db2[...] = db3

    @pl.loop(0, halves.nt, unroll=2)
    def _(t):
        cols = pl.ds(pl.multiple_of(t * w, w), w)
        s = jnp.bitwise_xor(info[3], t)
        everything = slice(None)
        back = db2[...]
        dact = mm(back, wf[1, :, cols], NN)
        dhid = (dact * slope[:, cols].astype(F32)).astype(BF16)
        hsum[:, cols] = column_sum(dhid)
        turn[0] = mm(second[...], dhid, TN).astype(BF16)
        disperse(info, halves, turn.at[0], 0, everything, s, keep, send)
        turn[1] = mm(back, act[:, cols], TN).astype(BF16)
        disperse(info, halves, turn.at[1], 1, everything, s, keep, send)
        acc[...] += mm(dhid, wf[0, :, cols], NT)

    dsecond = acc[...]
    grad2 = norm_backward(dsecond, n2, r2, gain2[...].astype(F32))
    low2 = grad2.astype(BF16)
    du2[...] = grad2
    db2[...] = low2
    sums[0:1, :] = column_sum(low2)
    sums[1:2, :] = column_sum(dsecond * n2)
    sums[2:3, :] = column_sum(dsecond)
    sums[6:8, :] = jnp.zeros((2, width), F32)


def matrix(slot, width):
    return pl.BlockSpec((1, width, width), lambda h: (slot, 0, 0))


def feed(info, halves, ctx, first, cot, wo, wf, ob, gain2, bias2, fib, fob, gain3, bias3):
    tokens, width = first.shape
    wide = wf.shape[2]
    w = wide // halves.nt
    flat = shaped((halves.total, w), BF16)
    return pl.pallas_call(
        functools.partial(feed_kernel, halves=halves),
        grid=(1,),
        out_shape=(
            shaped(first.shape, BF16),
            flat,
            flat,
            shaped(first.shape, F32),
            shaped(first.shape, BF16),
            shaped((8, width), F32),
            shaped((1, wide), F32),
        ),
        in_specs=[SMEM] + [VMEM] * 3 + [matrix(7, width)] + [VMEM] * 8,
        scratch_shapes=[
            pltpu.VMEM((tokens, wide), BF16),
            pltpu.VMEM((tokens, wide), BF16),
            pltpu.VMEM((tokens, width), F32),
            pltpu.VMEM((tokens, width), BF16),
            pltpu.VMEM((2, width, w), BF16),
        ],
        compiler_params=limit(28),
        cost_estimate=cost(6 * tokens * width * wide, 14 << 20),
    )(info, ctx, first, cot, wo, wf, ob, gain2, bias2, fib, fob, gain3, bias3)


def middle_kernel(
    info,
    du2,
    dq2,
    dk2,
    dv2,
    db2,
    sums2,
    hsum,
    normed,
    inverse,
    first,
    mem,
    memo,
    ctx2,
    ctx1,
    wq,
    wk,
    wv,
    gain,
    *outs,
    halves,
):
    du1, db1, own, other = outs[:4]
    turn, riders = outs[-2:]
    rows, width = mem.shape
    dfirst = du2[...] + mm(dq2[...], wq[0], NT)
    n = normed[...]
    grad = norm_backward(dfirst, n, inverse[...], gain[...].astype(F32))
    low = grad.astype(BF16)
    du1[...] = grad
    db1[...] = low
    riders[0:1, :] = column_sum(low)
    riders[1:2, :] = column_sum(dfirst * n)
    riders[2:3, :] = column_sum(dfirst)
    riders[3:9, :] = sums2[0:6, :]
    riders[9:10, :] = column_sum(dq2[...])
    riders[10:11, :] = column_sum(dv2[...])
    for i in range(4):
        riders[11 + i : 12 + i, :] = hsum[:, i * width : (i + 1) * width]
    riders[15:16, :] = jnp.zeros((1, width), F32)
    turn[0] = mm(low, ctx1[...], TN).astype(BF16)
    turn[1] = mm(first[...].astype(BF16), dq2[...], TN).astype(BF16)
    for slot, part in ((2, dk2), (3, dv2)):
        turn[slot] = (
            mm(mem[...], part[:rows, :], TN) + mm(memo[...], part[rows:, :], TN)
        ).astype(BF16)
    turn[4] = mm(db2[...], ctx2[...], TN).astype(BF16)
    back = mm(dk2[...], wk[0], NT) + mm(dv2[...], wv[0], NT)
    own[...] = back[:rows, :]
    other[...] = back[rows:, :].astype(BF16)
    if halves is None:
        outs[4][...] = turn[...]
        outs[5][...] = riders[...]
        return
    for i in range(5):
        disperse_whole(info, halves, turn.at[i], i, outs[4], outs[5])
    w = outs[4].shape[1]
    for target in outs[4:6]:
        for q in range(width // w):
            lo = halves.main + 16 * q
            target[lo : lo + 16, :] = riders[:, q * w : q * w + w].astype(BF16)


def middle(info, du2, dq2, dk2, dv2, db2, sums2, hsum, normed, inverse, first, mem, memo, ctx2, ctx1, w, gain):
    tokens, width = first.shape
    rows = mem.shape[0]
    nd, nt = lax.axis_size("dp"), lax.axis_size("tensor")
    r, columns = width // nd, width // nt
    halves = Halves((3, 2), r, 16 * nt)
    direct = aligned(r, columns)
    if direct:
        last = (shaped((halves.total, columns), BF16),) * 2
    else:
        last = (shaped((5, width, width), BF16), shaped((16, width), F32))
    outs = pl.pallas_call(
        functools.partial(middle_kernel, halves=halves if direct else None),
        grid=(1,),
        out_shape=(
            shaped(first.shape, F32),
            shaped(first.shape, BF16),
            shaped((rows, width), F32),
            shaped((rows, width), BF16),
        )
        + last,
        in_specs=[SMEM] + [VMEM] * 14 + [matrix(i, width) for i in (4, 5, 6)] + [VMEM],
        scratch_shapes=[pltpu.VMEM((5, width, width), BF16), pltpu.VMEM((16, width), F32)],
        compiler_params=limit(20),
        cost_estimate=cost(6 * first.size * width, 12 << 20),
    )(
        info,
        *(du2, dq2, dk2, dv2, db2, sums2, hsum),
        *far(normed, inverse, first, mem, memo, ctx2, ctx1, w, w, w),
        gain,
    )
    if not direct:
        rider = outs[5].astype(BF16).reshape(16, nt, columns).transpose(1, 0, 2)
        outs = outs[:4] + tuple(disperse_plain(info, halves, outs[4], rider.reshape(-1, columns)))
    return halves, outs


def self_grads_kernel(
    info, x, xo, dqa, dka, dva, dkoa, dvoa, dqb, dkb, dvb, dkob, dvob, wk, wv, *outs, halves
):
    other = outs[0]
    turn, sums = outs[-2:]
    width = x.shape[1]
    both = lambda left, right: jnp.concatenate([left[...], right[...]], axis=1)
    dq, dk, dv = both(dqa, dqb), both(dka, dkb), both(dva, dvb)
    turn[0] = mm(x[...], dq, TN).astype(BF16)
    sums[0:1, :] = column_sum(dq)

    @pl.when(info[0] == 0)
    def _():
        turn[1] = mm(x[...], dk, TN).astype(BF16)
        turn[2] = mm(x[...], dv, TN).astype(BF16)
        sums[1:2, :] = column_sum(dv)
        other[...] = jnp.zeros_like(other)

    @pl.when(info[0] != 0)
    def _():
        dko, dvo = both(dkoa, dkob), both(dvoa, dvob)
        turn[1] = (mm(x[...], dk, TN) + mm(xo[...], dko, TN)).astype(BF16)
        turn[2] = (mm(x[...], dv, TN) + mm(xo[...], dvo, TN)).astype(BF16)
        sums[1:2, :] = column_sum(dv) + column_sum(dvo)
        other[...] = (mm(dko, wk[0], NT) + mm(dvo, wv[0], NT)).astype(BF16)

    if halves is None:
        outs[1][...] = turn[...]
        outs[2][...] = sums[...]
        return
    for i in range(3):
        disperse_whole(info, halves, turn.at[i], i, outs[1], outs[2])
    w = outs[1].shape[1]
    row = lax.broadcasted_iota(jnp.int32, (16, w), 0)
    filled = jnp.zeros((16, w), F32)
    for i in range(2):
        for t in range(width // w):
            piece = sums[i : i + 1, t * w : t * w + w]
            filled = jnp.where(row == i * (width // w) + t, piece, filled)
    for target in outs[1:3]:
        target[halves.main :, :] = filled.astype(BF16)


def self_grads(info, x, xo, early, late, w):
    width = x.shape[1]
    nd, nt = lax.axis_size("dp"), lax.axis_size("tensor")
    r, columns = width // nd, width // nt
    halves = Halves((3,), r, 16)
    direct = aligned(r, columns)
    if direct:
        last = (shaped((halves.total, columns), BF16),) * 2
    else:
        last = (shaped((3, width, width), BF16), shaped((8, width), F32))
    outs = pl.pallas_call(
        functools.partial(self_grads_kernel, halves=halves if direct else None),
        grid=(1,),
        out_shape=(shaped(x.shape, BF16),) + last,
        in_specs=[SMEM] + [VMEM] * 12 + [matrix(i, width) for i in (1, 2)],
        scratch_shapes=[pltpu.VMEM((3, width, width), BF16), pltpu.VMEM((8, width), F32)],
        compiler_params=limit(16),
        cost_estimate=cost(7 * x.size * width, 8 << 20),
    )(info, *far(x, xo), *early, *late, *far(w, w))
    if not direct:
        rider = outs[2][:2].astype(BF16).reshape(-1, columns)
        rider = jnp.pad(rider, ((0, 16 - rider.shape[0]), (0, 0)))
        outs = outs[:1] + tuple(disperse_plain(info, halves, outs[1], rider))
    return halves, outs


def input_grads_kernel(du1, dqa, dka, dva, dqb, dkb, dvb, wq, wk, wv, back, out):
    both = lambda left, right: jnp.concatenate([left[...], right[...]], axis=1)
    out[...] = (
        du1[...]
        + mm(both(dqa, dqb), wq[0], NT)
        + mm(both(dka, dkb), wk[0], NT)
        + mm(both(dva, dvb), wv[0], NT)
        + back[...].astype(F32)
    )


def input_grads(du1, early, late, w, back):
    return pl.pallas_call(
        input_grads_kernel,
        grid=(1,),
        out_shape=shaped(du1.shape, F32),
        in_specs=[VMEM] * 7 + [matrix(i, du1.shape[1]) for i in range(3)] + [VMEM],
        compiler_params=limit(16),
        cost_estimate=cost(3 * du1.size * du1.shape[1], 6 << 20),
    )(*far(du1), *early, *late, *far(w, w, w), back)


def on_device(
    inputs,
    memory,
    prefix,
    self_query,
    self_query_bias,
    self_key,
    self_value,
    self_value_bias,
    self_out,
    self_out_bias,
    self_norm_gain,
    self_norm_bias,
    cross_query,
    cross_query_bias,
    cross_key,
    cross_value,
    cross_value_bias,
    cross_out,
    cross_out_bias,
    cross_norm_gain,
    cross_norm_bias,
    feed_in,
    feed_in_bias,
    feed_out,
    feed_out_bias,
    feed_norm_gain,
    feed_norm_bias,
    cotangent,
):
    nd, nt = lax.axis_size("dp"), lax.axis_size("tensor")
    me_d, me_t = lax.axis_index("dp"), lax.axis_index("tensor")
    late = me_t % 2
    width = inputs.shape[1]
    assert LEN == 2 * inputs.shape[0] and MEM == 2 * memory.shape[0]
    assert nd & (nd - 1) == 0 and nt & (nt - 1) == 0
    prefix_here = jnp.where(late == 0, lax.dynamic_index_in_dim(prefix, me_t // 2, keepdims=False), 0)
    info = jnp.stack([late, prefix_here, me_d, me_t]).astype(jnp.int32)

    columns = self_query_bias.shape[0]
    row = lambda vector: vector.reshape(1, -1)
    packed = pack(
        (
            self_query,
            self_key,
            self_value,
            self_out.T,
            cross_query,
            cross_key,
            cross_value,
            cross_out.T,
        ),
        (self_query_bias, self_value_bias, cross_query_bias, cross_value_bias, feed_in_bias),
    )
    feed_shard = jnp.stack([feed_in, feed_out.T])

    bits = [1 << i for i in range(nt.bit_length() - 1)]
    swapped = [swap(packed, 0, k) for k in range(1, nt)]
    line_feed = doubled(after(feed_shard, packed)[None], bits[:1])
    line = jnp.stack([after(packed, line_feed)] + swapped)
    count = 8 * self_query.shape[0]
    riders = line[:, count:]
    line = line[:, :count].reshape((nt, 8) + self_query.shape)
    line_feed = doubled(after(line_feed, line), bits[1:])
    inputs_other = hand_over(after(inputs, line), 0, 1)
    memory_other = swap(after(memory, line_feed), 0, 1)
    head_biases, hidden_bias = spread(info, riders)
    group = both_cores(over_planes(line), inputs_other, memory_other, head_biases)
    line_feed = after(line_feed, group[0])
    planes_feed = over_planes(line_feed)

    weights = assemble(info, group)
    q1, k1, v1, k1o, v1o = project_self(info, inputs, inputs_other, weights, head_biases)
    ctx1, log1 = self_forward(info, q1, k1, v1, k1o, v1o)
    first, normed1, inverse1, q2, k2, v2 = first_norm(
        ctx1,
        inputs,
        memory,
        memory_other,
        weights,
        row(self_out_bias),
        row(self_norm_gain),
        row(self_norm_bias),
        head_biases,
    )
    ctx2, log2 = cross_forward(q2, k2, v2)
    own = [planes_feed[0]] + [after(piece, ctx2) for piece in planes_feed[1:]]
    w_feed = assemble(info, planes_feed + [swap(piece, 1, 0) for piece in own])
    feed_halves = Halves((1, 1), width // nd, 0)
    outputs, keep, send, du2, db2, sums_feed, sums_hidden = feed(
        info,
        feed_halves,
        ctx2,
        first,
        cotangent,
        weights,
        w_feed,
        row(cross_out_bias),
        row(cross_norm_gain),
        row(cross_norm_bias),
        hidden_bias,
        row(feed_out_bias),
        row(feed_norm_gain),
        row(feed_norm_bias),
    )
    rounds = feed_halves.rounds
    got = swap(send, 1, 0)
    dq2, dk2, dv2 = cross_backward(q2, k2, v2, ctx2, log2, db2, weights)
    whole = [[(0, base), (1, base)] for base in feed_halves.bases]
    arrays, held, _ = halve(feed_halves, [after(keep, dq2), got], whole, None, 0)
    du2 = after(du2, arrays[0])
    middle_halves, (du1, db1, memory_own, memory_back, keep, send) = middle(
        info,
        du2,
        dq2,
        dk2,
        dv2,
        db2,
        sums_feed,
        sums_hidden,
        normed1,
        inverse1,
        first,
        memory,
        memory_other,
        ctx2,
        ctx1,
        weights,
        row(self_norm_gain),
    )
    arrays[0] = after(arrays[0], db1)
    for index in range(1, rounds):
        arrays, held, _ = halve(feed_halves, arrays, held, None, index)
    got = swap(after(send, arrays[0]), 1, 0)
    db1 = after(db1, arrays[0])
    pairs = width // PAIR // 2
    operands = (info, q1, k1, v1, k1o, v1o, ctx1, log1)
    grads_early = self_backward(*operands, db1, weights, 0, pairs)
    arrays[0] = after(arrays[0], grads_early[0])
    plans = feed_halves.line(held, None)
    riding = memory_back.shape[1] == arrays[0].shape[1]
    if riding:
        plans[1].append((memory_back.shape[0], [(len(arrays), 0)]))
        arrays.append(memory_back)
    lines_feed = line_swaps(add_rows(arrays, plans))
    whole = [[(0, base), (1, base)] for base in middle_halves.bases]
    rider = [(0, middle_halves.main), (1, middle_halves.main)]
    keep = after(keep, lines_feed[0])
    arrays, held, rider = halve(middle_halves, [keep, got], whole, rider, 0)
    db1, _, _ = lax.optimization_barrier((db1, arrays[0], lines_feed[0]))
    grads_late = list(self_backward(*operands, db1, weights, pairs, pairs))
    lines_feed[0] = after(lines_feed[0], grads_late[0])
    block = feed_in.shape[0]
    each = range(nt)
    grad_feed_in, grad_feed_out = add_rows(
        lines_feed,
        [[(block, [(k, i * block) for k in each])] for i in range(2)],
        F32,
    )
    arrays[0] = after(arrays[0], grad_feed_in)
    for index in range(1, rounds):
        arrays, held, rider = halve(middle_halves, arrays, held, rider, index)
    grads_late[0] = after(grads_late[0], arrays[0])
    self_halves, (inputs_back, keep, send) = self_grads(
        info, inputs, inputs_other, grads_early, grads_late, weights
    )
    got = swap(after(send, *arrays), 1, 0)
    if riding:
        memory_got = lines_feed[1][2 * block :]
    else:
        memory_got = swap(after(memory_back, lines_feed[0]), 0, 1)
    grad_memory = memory_own + memory_got.astype(F32)

    rider_self = self_halves.rider
    size = self_halves.sizes[0]
    parts = add_rows(
        [keep, got],
        [
            [(size, [(0, j * size), (1, j * size)]), (rider_self, [(0, self_halves.main), (1, self_halves.main)])]
            for j in map(lambda j: self_halves.place(0, j)[0] // size, range(nd // 2))
        ],
    )
    planes = [parts[0]] + [swap(part, 2 * j, 0) for j, part in enumerate(parts) if j]
    inputs_got = hand_over(after(inputs_back, parts[0]), 1, -1)
    count = len(arrays)
    planes_at = range(count, count + len(planes))
    plans = middle_halves.line(held, rider)
    for k, plan in enumerate(plans):
        rows = 3 * block
        plan.append((rows, [(p, k * rows) for p in planes_at]))
        plan.append((rider_self, [(p, size) for p in planes_at]))
    lines = line_swaps(add_rows(arrays + planes, plans))
    grad_inputs = input_grads(du1, grads_early[:3], grads_late[:3], weights, inputs_got)
    lines[0] = after(lines[0], grad_inputs)
    middle_rider = 5 * block
    self_at = middle_rider + middle_halves.rider
    cuts = [(i * block, block) for i in range(5)] + [(middle_rider, middle_halves.rider)]
    cuts += [(self_at + i * block, block) for i in range(3)] + [(self_at + 3 * block, rider_self)]
    sums = add_rows(lines, [[(n, [(k, lo) for k in each])] for lo, n in cuts], F32)
    grad_middle, early = sums[:5], sums[5]
    grad_self, late_sums = sums[6:9], sums[9]
    early = early.reshape(nt, 16, columns).transpose(1, 0, 2).reshape(16, width)
    late_sums = late_sums[: 2 * nt].reshape(2, width)

    def mine(vector):
        count = vector.shape[0] // nt
        return lax.dynamic_slice_in_dim(vector, me_t * count, count)

    return (
        outputs,
        grad_inputs,
        grad_memory,
        grad_self[0],
        mine(late_sums[0]),
        grad_self[1],
        grad_self[2],
        mine(late_sums[1]),
        grad_middle[0].T,
        early[0],
        early[1],
        early[2],
        grad_middle[1],
        mine(early[9]),
        grad_middle[2],
        grad_middle[3],
        mine(early[10]),
        grad_middle[4].T,
        early[3],
        early[4],
        early[5],
        grad_feed_in,
        mine(early[11:15].reshape(-1)),
        grad_feed_out.T,
        early[6],
        early[7],
        early[8],
    )


def solution(mesh):
    placed = (
        P(("dp", "tensor"), None),
        P(("dp", "tensor"), None),
        P("dp"),
        P("dp", "tensor"),
        P("tensor"),
        P("dp", "tensor"),
        P("dp", "tensor"),
        P("tensor"),
        P("tensor", "dp"),
        P(),
        P(),
        P(),
        P("dp", "tensor"),
        P("tensor"),
        P("dp", "tensor"),
        P("dp", "tensor"),
        P("tensor"),
        P("tensor", "dp"),
        P(),
        P(),
        P(),
        P("dp", "tensor"),
        P("tensor"),
        P("tensor", "dp"),
        P(),
        P(),
        P(),
        P(("dp", "tensor"), None),
    )
    return jax.shard_map(
        on_device,
        mesh=mesh,
        in_specs=placed,
        out_specs=(
            P(("dp", "tensor"), None),
            P(("dp", "tensor"), None),
            P(("dp", "tensor"), None),
            P("dp", "tensor"),
            P("tensor"),
            P("dp", "tensor"),
            P("dp", "tensor"),
            P("tensor"),
            P("tensor", "dp"),
            P(),
            P(),
            P(),
            P("dp", "tensor"),
            P("tensor"),
            P("dp", "tensor"),
            P("dp", "tensor"),
            P("tensor"),
            P("tensor", "dp"),
            P(),
            P(),
            P(),
            P("dp", "tensor"),
            P("tensor"),
            P("tensor", "dp"),
            P(),
            P(),
            P(),
        ),
        check_vma=False,
    )
```

time: 218 us -> 192 us (0.88)
  starting transfers between devices: 57 us -> 43.6 us
  other arithmetic: 17.3 us -> 5.54 us
  waiting for transfers between devices: 55.7 us -> 64.6 us
  local copies, waits for them, and re-layouts: 18.6 us -> 11.5 us
    ppermute x44 -> x37, starting transfers between devices: 52.3 us -> 40.4 us  [swap(): return lax.ppermute(array, ('dp', 'tensor'), pairs)]
    ppermute x44 -> x37, waiting for transfers between devices: 55.7 us -> 64.6 us  [swap(): return lax.ppermute(array, ('dp', 'tensor'), pairs)]
    convert_element_type x17 -> x0, other arithmetic: 8.38 us -> none  [rounded(): return lax.optimization_barrier(values.astype(BF16))]
    unnamed x118 -> x89, local copies, waits for them, and re-layouts: 10.1 us -> 7.24 us
    concatenate x12 -> x0, other arithmetic: 2.55 us -> none  [joined(): return arrays[0] if len(arrays) == 1 else jnp.concatenate(arrays)]
    pallas_call x15 -> x18, Pallas kernels: 37.3 us -> 35.7 us  [the longest x1 11.7 us: feed(): pl.pallas_call(functools.partial(feed_kernel, halves=halves), grid=(1,),...]
  transfers between devices with their start and end apart: 46 -> 39, of which waited for: 16 -> 22; matrix products, arithmetic and copies ran while one was open for 8% -> 1% of each run, Pallas kernels for 23% -> 25%
where the time goes in v3:
time: 192 us; the launch traced here: 191 us
  waiting for transfers between devices  64.6 us (34%)
  Pallas kernels  63.8 us (33%)
  starting transfers between devices  43.6 us (23%)
  local copies, waits for them, and re-layouts  11.5 us (6%)
  other arithmetic  5.54 us (3%)
  between operations  2.09 us (1%)
    ppermute x37, waiting for transfers between devices, swap(): return lax.ppermute(array, ('dp', 'tensor'), pairs)  64.6 us
    ppermute x37, starting transfers between devices, swap(): return lax.ppermute(array, ('dp', 'tensor'), pairs)  40.4 us
    pallas_call x2, Pallas kernels, self_backward(): pl.pallas_call(self_backward_kernel, grid=(pairs,), out_shape=(out,) * 5,...  11.7 us
    pallas_call x1, Pallas kernels, feed(): pl.pallas_call(functools.partial(feed_kernel, halves=halves), grid=(1,),...  11.7 us
    unnamed x89, local copies, waits for them, and re-layouts  7.24 us
    pallas_call x1, Pallas kernels, cross_backward(): pl.pallas_call(cross_backward_kernel, grid=(width // PAIR,), out_shape=(s...  6.73 us
    pallas_call x1, Pallas kernels, middle(): pl.pallas_call(functools.partial(middle_kernel, halves=halves if direct e...  5.81 us
    pallas_call x1, Pallas kernels, self_forward(): pl.pallas_call(self_forward_kernel, grid=(width // PAIR,), out_shape=(sha...  5.29 us
  transfers between devices with their start and end apart: 39, of which 22 were waited for; matrix products, arithmetic and copies ran while one was open for 1% of the time, Pallas kernels for 25%

profile of v3, /device:TPU:0, one launch (start us, length us, event | category | flops | bytes accessed | tf_op | source)
XLA Modules:
  0.0 191.2 jit_solution(1669994050308282866)
XLA Ops:
  1.7 1.5 shard_map.475
  3.2 3.0 %collective-permute-start = (bf16[1,2,64,512]{3,2,1,0:T(8,128)(2,1)S(1)}, bf16[1,2,64,512]{3,2,1,0:T(8,128)(2,1)S(1)}, u32[]{:S(2)}, u32[]{:S(2)}) collective-permute-start(bf16[1,2,64,512]{3,2,1,0:T(8,128)(2,1)S(1)} %bitcast.73), channel_id=1, source_target_pairs={{0,1},{1,0},{2,3},{3,2},{4,5},{5,4},{6,7},{7,6},{8,9},{9,8},{10,11... | collective-permute-start | bytes 393224 | tf_op jit(solution)/shard_map/ppermute | solution.py:56
  6.3 3.0 %collective-permute-start.2 = (bf16[528,128]{1,0:T(8,128)(2,1)}, bf16[528,128]{1,0:T(8,128)(2,1)S(1)}, u32[]{:S(2)}, u32[]{:S(2)}) collective-permute-start(bf16[528,128]{1,0:T(8,128)(2,1)} %shard_map.475), channel_id=1, source_target_pairs={{0,2},{1,3},{2,0},{3,1},{4,6},{5,7},{6,4},{7,5},{8,10},{9,11},{10,... | collective-permute-start | bytes 405512 | tf_op jit(solution)/shard_map/ppermute | solution.py:56
  9.3 1.3 collective-permute-start.3
  10.6 2.8 %collective-permute-done = bf16[1,2,64,512]{3,2,1,0:T(8,128)(2,1)S(1)} collective-permute-done((bf16[1,2,64,512]{3,2,1,0:T(8,128)(2,1)S(1)}, bf16[1,2,64,512]{3,2,1,0:T(8,128)(2,1)S(1)}, u32[]{:S(2)}, u32[]{:S(2)}) %collective-permute-start) | collective-permute-done | bytes 131104 | tf_op jit(solution)/shard_map/ppermute | solution.py:56
  13.5 2.0 %collective-permute-done.1 = bf16[528,128]{1,0:T(8,128)(2,1)S(1)} collective-permute-done((bf16[528,128]{1,0:T(8,128)(2,1)}, bf16[528,128]{1,0:T(8,128)(2,1)S(1)}, u32[]{:S(2)}, u32[]{:S(2)}) %collective-permute-start.1) | collective-permute-done | bytes 135200 | tf_op jit(solution)/shard_map/ppermute | solution.py:56
  16.1 4.6 %collective-permute-done.3 = bf16[528,128]{1,0:T(8,128)(2,1)S(1)} collective-permute-done((bf16[528,128]{1,0:T(8,128)(2,1)}, bf16[528,128]{1,0:T(8,128)(2,1)S(1)}, u32[]{:S(2)}, u32[]{:S(2)}) %collective-permute-start.3) | collective-permute-done | bytes 135200 | tf_op jit(solution)/shard_map/ppermute | solution.py:56
  21.7 3.3 %collective-permute-start.5 = (bf16[2,2,64,512]{3,2,1,0:T(8,128)(2,1)S(1)}, bf16[2,2,64,512]{3,2,1,0:T(8,128)(2,1)S(1)}, u32[]{:S(2)}, u32[]{:S(2)}) collective-permute-start(bf16[2,2,64,512]{3,2,1,0:T(8,128)(2,1)S(1)} %pad_maximum_fusion.2), channel_id=1, source_target_pairs={{0,2},{1,3},{2,0},{3,1},{4,6},{5,7},{6,4},{7,5},{8,10},{9,11},{10,... | collective-permute-start | bytes 786440 | tf_op jit(solution)/shard_map/ppermute | solution.py:56
  25.1 1.9 %collective-permute-start.4 = (bf16[512,512]{1,0:T(8,128)(2,1)S(1)}, bf16[512,512]{1,0:T(8,128)(2,1)S(1)}, u32[]{:S(2)}, u32[]{:S(2)}) collective-permute-start(bf16[512,512]{1,0:T(8,128)(2,1)S(1)} %copy-done.8), channel_id=1, source_target_pairs={{0,1},{2,3},{4,5},{6,7},{8,9},{10,11},{12,13},{14,15},{16,17},{18,... | collective-permute-start | bytes 1572872 | tf_op jit(solution)/shard_map/ppermute | solution.py:62
  27.0 1.6 collective-permute-start.7
  28.6 1.5 collective-permute-start.8
  31.8 3.6 %collective-permute-done.5 = bf16[2,2,64,512]{3,2,1,0:T(8,128)(2,1)S(1)} collective-permute-done((bf16[2,2,64,512]{3,2,1,0:T(8,128)(2,1)S(1)}, bf16[2,2,64,512]{3,2,1,0:T(8,128)(2,1)S(1)}, u32[]{:S(2)}, u32[]{:S(2)}) %collective-permute-start.5) | collective-permute-done | bytes 262176 | tf_op jit(solution)/shard_map/ppermute | solution.py:56
  36.7 1.4 shard_map.476
  38.1 4.9 %collective-permute-done.6.memo = bf16[128,512]{1,0:T(8,128)(2,1)S(1)} collective-permute-done((bf16[128,512]{1,0:T(8,128)(2,1)S(1)}, bf16[128,512]{1,0:T(8,128)(2,1)S(1)}, u32[]{:S(2)}, u32[]{:S(2)}) %collective-permute-start.6) | collective-permute-done | bytes 131104 | tf_op jit(solution)/shard_map/ppermute | solution.py:56
  43.0 7.7 %collective-permute-done.8 = bf16[4,8,64,128]{3,2,1,0:T(8,128)(2,1)} collective-permute-done((bf16[4,8,64,128]{3,2,1,0:T(8,128)(2,1)S(1)}, bf16[4,8,64,128]{3,2,1,0:T(8,128)(2,1)}, u32[]{:S(2)}, u32[]{:S(2)}) %collective-permute-start.8) | collective-permute-done | bytes 524320 | tf_op jit(solution)/shard_map/ppermute | solution.py:56
  50.7 1.7 pad_maximum_fusion.refs_0_
  52.4 1.6 collective-permute-start.13
  54.0 1.2 collective-permute-start.12
  56.6 1.3 shard_map.477.wq.wk.wv.wo.w
  57.9 1.7 shard_map.478
  59.7 5.3 %shard_map.479 = (bf16[512,512]{1,0:T(8,128)(2,1)S(1)}, f32[512,512]{1,0:T(8,128)S(1)}) custom-call(s32[4]{0:T(128)S(1)} %copy-done.31, bf16[512,512]{1,0:T(8,128)(2,1)S(1)} %get-tuple-element.144.q, bf16[512,512]{1,0:T(8,128)(2,1)S(1)} %get-tuple-element.145.k, bf16[512,512]{1,0:T(8,128)(2,1)S(1)} %get-tuple-element.146.v, ...), custom_call_target="tpu_custom_call" | custom-call | flops 33554432 | bytes 81920 | tf_op jit(solution)/shard_map/pallas_call | solution.py:494
  65.1 1.4 shard_map.480
  68.3 3.0 %shard_map.481 = (bf16[512,512]{1,0:T(8,128)(2,1)S(1)}, f32[512,512]{1,0:T(8,128)S(1)}) custom-call(bf16[512,512]{1,0:T(8,128)(2,1)S(1)} %get-tuple-element.150.q, bf16[256,512]{1,0:T(8,128)(2,1)S(1)} %get-tuple-element.151.k, bf16[256,512]{1,0:T(8,128)(2,1)S(1)} %get-tuple-element.152.v), custom_call_target="tpu_custom_call" | custom-call | flops 8388608 | bytes 49152 | tf_op jit(solution)/shard_map/pallas_call | solution.py:524
  71.5 7.4 %collective-permute-done.12.refs_2_ = bf16[4,2,64,512]{3,2,1,0:T(8,128)(2,1)S(1)} collective-permute-done((bf16[4,2,64,512]{3,2,1,0:T(8,128)(2,1)S(1)}, bf16[4,2,64,512]{3,2,1,0:T(8,128)(2,1)S(1)}, u32[]{:S(2)}, u32[]{:S(2)}) %collective-permute-start.12) | collective-permute-done | bytes 524320 | tf_op jit(solution)/shard_map/ppermute | solution.py:56
  79.6 1.2 collective-permute-done.16.refs_6_
  82.5 11.7 %shard_map.483 = (bf16[512,512]{1,0:T(8,128)(2,1)}, bf16[2048,512]{1,0:T(8,128)(2,1)S(1)}, bf16[2048,512]{1,0:T(8,128)(2,1)S(1)}, f32[512,512]{1,0:T(8,128)S(1)}...) custom-call(s32[4]{0:T(128)S(1)} %copy-done.31, ...), custom_call_target="tpu_custom_call" | custom-call | flops 50331648 | bytes 229376 | tf_op jit(solution)/shard_map/pallas_call | solution.py:708
  94.3 6.7 %shard_map.484 = (bf16[512,512]{1,0:T(8,128)(2,1)S(1)}, bf16[256,512]{1,0:T(8,128)(2,1)S(1)}, bf16[256,512]{1,0:T(8,128)(2,1)S(1)}) custom-call(bf16[512,512]{1,0:T(8,128)(2,1)} %copy-done.11, bf16[256,512]{1,0:T(8,128)(2,1)} %copy-done.16, bf16[256,512]{1,0:T(8,128)(2,1)} %copy-done.17, bf16[512,512]{1,0:T(8,128)(2,1)} %copy-done.2, f32[512,512]{1,0:T(8,128)} %copy-done.15, ...), custom_call_target="tpu_custom_call" | custom-call | flops 20971520 | bytes 65536 | tf_op jit(solution)/shard_map/pallas_call | solution.py:539
  101.6 1.3 collective-permute-start.19
  103.7 5.8 %shard_map.486 = (f32[512,512]{1,0:T(8,128)S(1)}, bf16[512,512]{1,0:T(8,128)(2,1)S(1)}, f32[128,512]{1,0:T(8,128)S(1)}, bf16[128,512]{1,0:T(8,128)(2,1)S(1)}, bf...) custom-call(s32[4]{0:T(128)S(1)} %copy-done.31, f32[512,512]{1,0:T(8,128)S(1)} %get-tuple-element.169.du2, ...), custom_call_target="tpu_custom_call" | custom-call | flops 12582912 | bytes 196608 | tf_op jit(solution)/shard_map/pallas_call | solution.py:808
  110.5 5.3 %collective-permute-done.19.refs_2_ = bf16[512,512]{1,0:T(8,128)(2,1)S(1)} collective-permute-done((bf16[512,512]{1,0:T(8,128)(2,1)S(1)}, bf16[512,512]{1,0:T(8,128)(2,1)S(1)}, u32[]{:S(2)}, u32[]{:S(2)}) %collective-permute-start.19) | collective-permute-done | bytes 524320 | tf_op jit(solution)/shard_map/ppermute | solution.py:56
  118.1 1.5 collective-permute-start.22
  119.5 5.8 %shard_map.488 = (bf16[512,256]{1,0:T(8,128)(2,1)S(1)}, bf16[512,256]{1,0:T(8,128)(2,1)S(1)}, bf16[512,256]{1,0:T(8,128)(2,1)S(1)}, bf16[512,256]{1,0:T(8,128)(2,1)S(1)}, bf16[512,256]{1,0:T(8,128)(2,1)S(1)}) custom-call(s32[4]{0:T(128)S(1)} %copy-done.31, bf16[512,512]{1,0:T(8,128)(2,1)} %copy-done.3, bf16[512,512]{1,0:T(8,128)(2,1)} %copy-done.4, ...), custom_call_target="tpu_custom_call" | custom-call | flops 41943040 | bytes 131072 | tf_op jit(solution)/shard_map/pallas_call | solution.py:509
  126.9 1.5 collective-permute-start.27
  129.5 2.0 %collective-permute-start.25 = (bf16[128,512]{1,0:T(8,128)(2,1)S(1)}, bf16[128,512]{1,0:T(8,128)(2,1)S(1)}, u32[]{:S(2)}, u32[]{:S(2)}) collective-permute-start(bf16[128,512]{1,0:T(8,128)(2,1)S(1)} %get-tuple-element.203), channel_id=1, source_target_pairs={{0,2},{1,3},{2,0},{3,1},{4,6},{5,7},{6,4},{7,5},{8,10},{9,11},{10,... | collective-permute-start | bytes 393224 | tf_op jit(solution)/shard_map/ppermute | solution.py:56
  131.5 1.8 collective-permute-start.26
  133.3 5.9 %shard_map.491 = (bf16[512,256]{1,0:T(8,128)(2,1)S(1)}, bf16[512,256]{1,0:T(8,128)(2,1)S(1)}, bf16[512,256]{1,0:T(8,128)(2,1)S(1)}, bf16[512,256]{1,0:T(8,128)(2,1)S(1)}, bf16[512,256]{1,0:T(8,128)(2,1)S(1)}) custom-call(s32[4]{0:T(128)S(1)} %copy-done.31, bf16[512,512]{1,0:T(8,128)(2,1)} %copy-done.3, bf16[512,512]{1,0:T(8,128)(2,1)} %copy-done.4, ...), custom_call_target="tpu_custom_call" | custom-call | flops 41943040 | bytes 131072 | tf_op jit(solution)/shard_map/pallas_call | solution.py:509
  139.2 3.7 %collective-permute-done.26.refs_3_ = bf16[128,512]{1,0:T(8,128)(2,1)S(1)} collective-permute-done((bf16[128,512]{1,0:T(8,128)(2,1)S(1)}, bf16[128,512]{1,0:T(8,128)(2,1)S(1)}, u32[]{:S(2)}, u32[]{:S(2)}) %collective-permute-start.26) | collective-permute-done | bytes 131104 | tf_op jit(solution)/shard_map/ppermute | solution.py:56
  144.5 1.4 collective-permute-start.29
  146.5 3.9 %shard_map.494 = (bf16[512,512]{1,0:T(8,128)(2,1)}, bf16[3088,128]{1,0:T(8,128)(2,1)S(1)}, bf16[3088,128]{1,0:T(8,128)(2,1)S(1)}) custom-call(s32[4]{0:T(128)S(1)} %copy-done.31, bf16[512,512]{1,0:T(8,128)(2,1)} %x.5, bf16[512,512]{1,0:T(8,128)(2,1)} %copy-done.12, bf16[512,256]{1,0:T(8,128)(2,1)S(1)} %get-tuple-element.185.dqa, ...), custom_call_target="tpu_custom_call" | custom-call | flops 14680064 | bytes 131072 | tf_op jit(solution)/shard_map/pallas_call | solution.py:887
  151.1 2.3 %collective-permute-done.31.refs_1_ = bf16[3088,128]{1,0:T(8,128)(2,1)S(1)} collective-permute-done((bf16[3088,128]{1,0:T(8,128)(2,1)S(1)}, bf16[3088,128]{1,0:T(8,128)(2,1)S(1)}, u32[]{:S(2)}, u32[]{:S(2)}) %collective-permute-start.31) | collective-permute-done | bytes 790560 | tf_op jit(solution)/shard_map/ppermute | solution.py:56
  154.3 1.3 collective-permute-start.32
  157.4 1.7 collective-permute-start.35
  159.1 4.6 %collective-permute-done.33.refs_6_ = bf16[784,128]{1,0:T(8,128)(2,1)S(1)} collective-permute-done((bf16[784,128]{1,0:T(8,128)(2,1)}, bf16[784,128]{1,0:T(8,128)(2,1)S(1)}, u32[]{:S(2)}, u32[]{:S(2)}) %collective-permute-start.33) | collective-permute-done | bytes 200736 | tf_op jit(solution)/shard_map/ppermute | solution.py:56
  163.7 4.0 %collective-permute-done.34.refs_7_ = bf16[784,128]{1,0:T(8,128)(2,1)S(1)} collective-permute-done((bf16[784,128]{1,0:T(8,128)(2,1)}, bf16[784,128]{1,0:T(8,128)(2,1)S(1)}, u32[]{:S(2)}, u32[]{:S(2)}) %collective-permute-start.34) | collective-permute-done | bytes 200736 | tf_op jit(solution)/shard_map/ppermute | solution.py:56
  171.6 2.5 %collective-permute-start.36 = (bf16[592,128]{1,0:T(8,128)(2,1)S(1)}, bf16[592,128]{1,0:T(8,128)(2,1)S(1)}, u32[]{:S(2)}, u32[]{:S(2)}) collective-permute-start(bf16[592,128]{1,0:T(8,128)(2,1)S(1)} %get-tuple-element.233), channel_id=1, source_target_pairs={{0,1},{1,0},{2,3},{3,2},{4,5},{5,4},{6,7},{7,6},{8,9},{9,8},{10,11... | collective-permute-start | bytes 454664 | tf_op jit(solution)/shard_map/ppermute | solution.py:56
  174.1 1.7 collective-permute-start.37
  177.2 3.7 %shard_map.496 = f32[512,512]{1,0:T(8,128)} custom-call(f32[512,512]{1,0:T(8,128)} %copy-done.13, bf16[512,256]{1,0:T(8,128)(2,1)S(1)} %get-tuple-element.185.dqa, bf16[512,256]{1,0:T(8,128)(2,1)S(1)} %get-tuple-element.186.dka, bf16[512,256]{1,0:T(8,128)(2,1)S(1)} %get-tuple-element.187.dva, bf16[512,256]{1,0:T(8,128)(2,1)S(1)} %get-tuple-element.211.dqb, ...), custom_call_target="tpu_custom_call" | custom-call | flops 6291456 | bytes 98304 | tf_op jit(solution)/shard_map/pallas_call | solution.py:915
  180.9 6.0 %collective-permute-done.37.refs_2_ = bf16[592,128]{1,0:T(8,128)(2,1)S(1)} collective-permute-done((bf16[592,128]{1,0:T(8,128)(2,1)S(1)}, bf16[592,128]{1,0:T(8,128)(2,1)S(1)}, u32[]{:S(2)}, u32[]{:S(2)}) %collective-permute-start.37) | collective-permute-done | bytes 151584 | tf_op jit(solution)/shard_map/ppermute | solution.py:56
  (171 shorter events, 33.1 us)
Async XLA Ops:
  0.7 24.4 %copy-start.8 = (bf16[512,512]{1,0:T(8,128)(2,1)S(1)}, bf16[512,512]{1,0:T(8,128)(2,1)}, u32[]{:S(2)}) copy-start(bf16[512,512]{1,0:T(8,128)(2,1)} %x.5) | copy-start | bytes 1572868
  0.7 29.9 %copy-start.43 = (s32[2]{0:T(128)S(1)}, s32[2]{0:T(128)}, u32[]{:S(2)}) copy-start(s32[2]{0:T(128)} %param.30) | copy-start | bytes 28
  0.7 34.8 %copy-start.18 = (bf16[128,512]{1,0:T(8,128)(2,1)S(1)}, bf16[128,512]{1,0:T(8,128)(2,1)}, u32[]{:S(2)}) copy-start(bf16[128,512]{1,0:T(8,128)(2,1)} %mem.3) | copy-start | bytes 393220
  3.2 32.9 %copy-start.33 = (bf16[528,128]{1,0:T(8,128)(2,1)S(1)}, bf16[528,128]{1,0:T(8,128)(2,1)}, u32[]{:S(2)}) copy-start(bf16[528,128]{1,0:T(8,128)(2,1)} %shard_map.475) | copy-start | bytes 405508
  3.2 10.2 %collective-permute-start = (bf16[1,2,64,512]{3,2,1,0:T(8,128)(2,1)S(1)}, bf16[1,2,64,512]{3,2,1,0:T(8,128)(2,1)S(1)}, u32[]{:S(2)}, u32[]{:S(2)}) collective-permute-start(bf16[1,2,64,512]{3,2,1,0:T(8,128)(2,1)S(1)} %bitcast.73), channel_id=1, source_target_pairs={{0,1},{1,0},{2,3},{3,2},{4,5},{5,4},{6,7},{7,6},{8,9},{9,8},{10,11... | collective-permute-start | bytes 393224 | tf_op jit(solution)/shard_map/ppermute | solution.py:56
  6.2 9.3 %collective-permute-start.1 = (bf16[528,128]{1,0:T(8,128)(2,1)}, bf16[528,128]{1,0:T(8,128)(2,1)S(1)}, u32[]{:S(2)}, u32[]{:S(2)}) collective-permute-start(bf16[528,128]{1,0:T(8,128)(2,1)} %shard_map.475), channel_id=1, source_target_pairs={{0,1},{1,0},{2,3},{3,2},{4,5},{5,4},{6,7},{7,6},{8,9},{9,8},{10,11... | collective-permute-start | bytes 405512 | tf_op jit(solution)/shard_map/ppermute | solution.py:56
  6.3 9.8 %collective-permute-start.2 = (bf16[528,128]{1,0:T(8,128)(2,1)}, bf16[528,128]{1,0:T(8,128)(2,1)S(1)}, u32[]{:S(2)}, u32[]{:S(2)}) collective-permute-start(bf16[528,128]{1,0:T(8,128)(2,1)} %shard_map.475), channel_id=1, source_target_pairs={{0,2},{1,3},{2,0},{3,1},{4,6},{5,7},{6,4},{7,5},{8,10},{9,11},{10,... | collective-permute-start | bytes 405512 | tf_op jit(solution)/shard_map/ppermute | solution.py:56
  9.3 11.4 %collective-permute-start.3 = (bf16[528,128]{1,0:T(8,128)(2,1)}, bf16[528,128]{1,0:T(8,128)(2,1)S(1)}, u32[]{:S(2)}, u32[]{:S(2)}) collective-permute-start(bf16[528,128]{1,0:T(8,128)(2,1)} %shard_map.475), channel_id=1, source_target_pairs={{0,3},{1,2},{2,1},{3,0},{4,7},{5,6},{6,5},{7,4},{8,11},{9,10},{10,... | collective-permute-start | bytes 405512 | tf_op jit(solution)/shard_map/ppermute | solution.py:56
  21.7 13.7 %collective-permute-start.5 = (bf16[2,2,64,512]{3,2,1,0:T(8,128)(2,1)S(1)}, bf16[2,2,64,512]{3,2,1,0:T(8,128)(2,1)S(1)}, u32[]{:S(2)}, u32[]{:S(2)}) collective-permute-start(bf16[2,2,64,512]{3,2,1,0:T(8,128)(2,1)S(1)} %pad_maximum_fusion.2), channel_id=1, source_target_pairs={{0,2},{1,3},{2,0},{3,1},{4,6},{5,7},{6,4},{7,5},{8,10},{9,11},{10,... | collective-permute-start | bytes 786440 | tf_op jit(solution)/shard_map/ppermute | solution.py:56
  25.1 17.9 %collective-permute-start.4 = (bf16[512,512]{1,0:T(8,128)(2,1)S(1)}, bf16[512,512]{1,0:T(8,128)(2,1)S(1)}, u32[]{:S(2)}, u32[]{:S(2)}) collective-permute-start(bf16[512,512]{1,0:T(8,128)(2,1)S(1)} %copy-done.8), channel_id=1, source_target_pairs={{0,1},{2,3},{4,5},{6,7},{8,9},{10,11},{12,13},{14,15},{16,17},{18,... | collective-permute-start | bytes 1572872 | tf_op jit(solution)/shard_map/ppermute | solution.py:62
  27.0 16.0 %collective-permute-start.7 = (bf16[4,8,64,128]{3,2,1,0:T(8,128)(2,1)S(1)}, bf16[4,8,64,128]{3,2,1,0:T(8,128)(2,1)}, u32[]{:S(2)}, u32[]{:S(2)}) collective-permute-start(bf16[4,8,64,128]{3,2,1,0:T(8,128)(2,1)S(1)} %bitcast.61), channel_id=1, source_target_pairs={{0,8},{1,9},{2,10},{3,11},{4,12},{5,13},{6,14},{7,15},{8,0},{9,1},... | collective-permute-start | bytes 1572872 | tf_op jit(solution)/shard_map/ppermute | solution.py:56
  28.6 22.1 %collective-permute-start.8 = (bf16[4,8,64,128]{3,2,1,0:T(8,128)(2,1)S(1)}, bf16[4,8,64,128]{3,2,1,0:T(8,128)(2,1)}, u32[]{:S(2)}, u32[]{:S(2)}) collective-permute-start(bf16[4,8,64,128]{3,2,1,0:T(8,128)(2,1)S(1)} %bitcast.62), channel_id=1, source_target_pairs={{0,16},{1,17},{2,18},{3,19},{4,20},{5,21},{6,22},{7,23},{8,24},{9,... | collective-permute-start | bytes 1572872 | tf_op jit(solution)/shard_map/ppermute | solution.py:56
  30.1 20.6 %collective-permute-start.9 = (bf16[4,8,64,128]{3,2,1,0:T(8,128)(2,1)S(1)}, bf16[4,8,64,128]{3,2,1,0:T(8,128)(2,1)}, u32[]{:S(2)}, u32[]{:S(2)}) collective-permute-start(bf16[4,8,64,128]{3,2,1,0:T(8,128)(2,1)S(1)} %bitcast.63), channel_id=1, source_target_pairs={{0,24},{1,25},{2,26},{3,27},{4,28},{5,29},{6,30},{7,31},{8,16},{9,... | collective-permute-start | bytes 1572872 | tf_op jit(solution)/shard_map/ppermute | solution.py:56
  35.5 7.5 %collective-permute-start.6 = (bf16[128,512]{1,0:T(8,128)(2,1)S(1)}, bf16[128,512]{1,0:T(8,128)(2,1)S(1)}, u32[]{:S(2)}, u32[]{:S(2)}) collective-permute-start(bf16[128,512]{1,0:T(8,128)(2,1)S(1)} %copy-done.18), channel_id=1, source_target_pairs={{0,1},{1,0},{2,3},{3,2},{4,5},{5,4},{6,7},{7,6},{8,9},{9,8},{10,11... | collective-permute-start | bytes 393224 | tf_op jit(solution)/shard_map/ppermute | solution.py:56
  43.0 22.0 %copy-start.19 = (bf16[128,512]{1,0:T(8,128)(2,1)}, bf16[128,512]{1,0:T(8,128)(2,1)S(1)}, u32[]{:S(2)}) copy-start(bf16[128,512]{1,0:T(8,128)(2,1)S(1)} %collective-permute-done.6.memo) | copy-start | bytes 393220
  43.0 14.9 %copy-start.12 = (bf16[512,512]{1,0:T(8,128)(2,1)}, bf16[512,512]{1,0:T(8,128)(2,1)S(1)}, u32[]{:S(2)}) copy-start(bf16[512,512]{1,0:T(8,128)(2,1)S(1)} %collective-permute-done.4.xo) | copy-start | bytes 1572868
  52.4 4.2 %collective-permute-start.10 = (bf16[4,4,8,64,128]{4,3,2,1,0:T(8,128)(2,1)S(1)}, bf16[4,4,8,64,128]{4,3,2,1,0:T(8,128)(2,1)S(1)}, u32[]{:S(2)}, u32[]{:S(2)}) collective-permute-start(bf16[4,4,8,64,128]{4,3,2,1,0:T(8,128)(2,1)S(1)} %pad_maximum_fusion.refs_0_), channel_id=1, source_target_pairs={{0,4},{1,5},{2,6},{3,7},{4,0},{5,1},{6,2},{7,3},{8,12},{9,13},{10,... | collective-permute-start | bytes 6291464 | tf_op jit(solution)/shard_map/ppermute | solution.py:56
  52.4 18.9 %collective-permute-start.13 = (bf16[4,2,64,512]{3,2,1,0:T(8,128)(2,1)S(1)}, bf16[4,2,64,512]{3,2,1,0:T(8,128)(2,1)S(1)}, u32[]{:S(2)}, u32[]{:S(2)}) collective-permute-start(bf16[4,2,64,512]{3,2,1,0:T(8,128)(2,1)S(1)} %constant_dynamic-update-slice_fusion.refs_0_), channel_id=1, source_target_pairs={{0,24},{1,25},{2,26},{3,27},{4,28},{5,29},{6,30},{7,31},{8,16},{9,... | collective-permute-start | bytes 1572872 | tf_op jit(solution)/shard_map/ppermute | solution.py:56
  54.0 24.9 %collective-permute-start.12 = (bf16[4,2,64,512]{3,2,1,0:T(8,128)(2,1)S(1)}, bf16[4,2,64,512]{3,2,1,0:T(8,128)(2,1)S(1)}, u32[]{:S(2)}, u32[]{:S(2)}) collective-permute-start(bf16[4,2,64,512]{3,2,1,0:T(8,128)(2,1)S(1)} %constant_dynamic-update-slice_fusion.refs_0_), channel_id=1, source_target_pairs={{0,16},{1,17},{2,18},{3,19},{4,20},{5,21},{6,22},{7,23},{8,24},{9,... | collective-permute-start | bytes 1572872 | tf_op jit(solution)/shard_map/ppermute | solution.py:56
  55.2 23.8 %collective-permute-start.11 = (bf16[4,2,64,512]{3,2,1,0:T(8,128)(2,1)S(1)}, bf16[4,2,64,512]{3,2,1,0:T(8,128)(2,1)S(1)}, u32[]{:S(2)}, u32[]{:S(2)}) collective-permute-start(bf16[4,2,64,512]{3,2,1,0:T(8,128)(2,1)S(1)} %constant_dynamic-update-slice_fusion.refs_0_), channel_id=1, source_target_pairs={{0,8},{1,9},{2,10},{3,11},{4,12},{5,13},{6,14},{7,15},{8,0},{9,1},... | collective-permute-start | bytes 1572872 | tf_op jit(solution)/shard_map/ppermute | solution.py:56
  56.0 23.5 %collective-permute-start.14 = (bf16[4,2,64,512]{3,2,1,0:T(8,128)(2,1)S(1)}, bf16[4,2,64,512]{3,2,1,0:T(8,128)(2,1)S(1)}, u32[]{:S(2)}, u32[]{:S(2)}) collective-permute-start(bf16[4,2,64,512]{3,2,1,0:T(8,128)(2,1)S(1)} %constant_dynamic-update-slice_fusion.refs_0_), channel_id=1, source_target_pairs={{0,4},{1,5},{2,6},{3,7},{4,0},{5,1},{6,2},{7,3},{8,12},{9,13},{10,... | collective-permute-start | bytes 1572872 | tf_op jit(solution)/shard_map/ppermute | solution.py:56
  57.9 24.6 %copy-start = (bf16[8,512,512]{2,1,0:T(8,128)(2,1)}, bf16[8,512,512]{2,1,0:T(8,128)(2,1)S(1)}, u32[]{:S(2)}) copy-start(bf16[8,512,512]{2,1,0:T(8,128)(2,1)S(1)} %shard_map.477.wq.wk.wv.wo.w) | copy-start | bytes 12582916
  65.0 14.5 %copy-start.41 = (bf16[512]{0:T(512)(128)(2,1)S(1)}, bf16[512]{0:T(512)(128)(2,1)}, u32[]{:S(2)}) copy-start(bf16[512]{0:T(512)(128)(2,1)} %param.53) | copy-start | bytes 3076
  65.1 14.5 %copy-start.42 = (bf16[512]{0:T(512)(128)(2,1)S(1)}, bf16[512]{0:T(512)(128)(2,1)}, u32[]{:S(2)}) copy-start(bf16[512]{0:T(512)(128)(2,1)} %param.54) | copy-start | bytes 3076
  71.3 8.2 %collective-permute-start.17 = (bf16[4,2,64,512]{3,2,1,0:T(8,128)(2,1)S(1)}, bf16[4,2,64,512]{3,2,1,0:T(8,128)(2,1)S(1)}, u32[]{:S(2)}, u32[]{:S(2)}) collective-permute-start(bf16[4,2,64,512]{3,2,1,0:T(8,128)(2,1)S(1)} %collective-permute-done.13.refs_3_), channel_id=1, source_target_pairs={{0,4},{1,5},{2,6},{3,7},{4,0},{5,1},{6,2},{7,3},{8,12},{9,13},{10,... | collective-permute-start | bytes 1572872 | tf_op jit(solution)/shard_map/ppermute | solution.py:56
  78.9 1.9 collective-permute-start.16
  79.0 2.6 %collective-permute-start.15 = (bf16[4,2,64,512]{3,2,1,0:T(8,128)(2,1)S(1)}, bf16[4,2,64,512]{3,2,1,0:T(8,128)(2,1)S(1)}, u32[]{:S(2)}, u32[]{:S(2)}) collective-permute-start(bf16[4,2,64,512]{3,2,1,0:T(8,128)(2,1)S(1)} %collective-permute-done.11.refs_1_), channel_id=1, source_target_pairs={{0,4},{1,5},{2,6},{3,7},{4,0},{5,1},{6,2},{7,3},{8,12},{9,13},{10,... | collective-permute-start | bytes 1572872 | tf_op jit(solution)/shard_map/ppermute | solution.py:56
  94.2 6.9 %collective-permute-start.18 = (bf16[2048,512]{1,0:T(8,128)(2,1)S(1)}, bf16[2048,512]{1,0:T(8,128)(2,1)S(1)}, u32[]{:S(2)}, u32[]{:S(2)}) collective-permute-start(bf16[2048,512]{1,0:T(8,128)(2,1)S(1)} %get-tuple-element.167), channel_id=1, source_target_pairs={{0,4},{1,5},{2,6},{3,7},{4,0},{5,1},{6,2},{7,3},{8,12},{9,13},{10,... | collective-permute-start | bytes 6291464 | tf_op jit(solution)/shard_map/ppermute | solution.py:56
  101.6 14.3 %collective-permute-start.19 = (bf16[512,512]{1,0:T(8,128)(2,1)S(1)}, bf16[512,512]{1,0:T(8,128)(2,1)S(1)}, u32[]{:S(2)}, u32[]{:S(2)}) collective-permute-start(bf16[512,512]{1,0:T(8,128)(2,1)S(1)} %get-tuple-element.181), channel_id=1, source_target_pairs={{0,8},{1,9},{2,10},{3,11},{4,12},{5,13},{6,14},{7,15},{8,0},{9,1},... | collective-permute-start | bytes 1572872 | tf_op jit(solution)/shard_map/ppermute | solution.py:56
  102.9 13.9 %collective-permute-start.20 = (bf16[512,512]{1,0:T(8,128)(2,1)S(1)}, bf16[512,512]{1,0:T(8,128)(2,1)S(1)}, u32[]{:S(2)}, u32[]{:S(2)}) collective-permute-start(bf16[512,512]{1,0:T(8,128)(2,1)S(1)} %get-tuple-element.182.refs_4_), channel_id=1, source_target_pairs={{0,16},{1,17},{2,18},{3,19},{4,20},{5,21},{6,22},{7,23},{8,24},{9,... | collective-permute-start | bytes 1572872 | tf_op jit(solution)/shard_map/ppermute | solution.py:56
  117.1 9.5 %collective-permute-start.23 = (bf16[5184,128]{1,0:T(8,128)(2,1)S(1)}, bf16[5184,128]{1,0:T(8,128)(2,1)S(1)}, u32[]{:S(2)}, u32[]{:S(2)}) collective-permute-start(bf16[5184,128]{1,0:T(8,128)(2,1)S(1)} %get-tuple-element.197), channel_id=1, source_target_pairs={{0,4},{1,5},{2,6},{3,7},{4,0},{5,1},{6,2},{7,3},{8,12},{9,13},{10,... | collective-permute-start | bytes 3981320 | tf_op jit(solution)/shard_map/ppermute | solution.py:56
  117.2 8.7 %collective-permute-start.21 = (bf16[256,512]{1,0:T(8,128)(2,1)S(1)}, bf16[256,512]{1,0:T(8,128)(2,1)S(1)}, u32[]{:S(2)}, u32[]{:S(2)}) collective-permute-start(bf16[256,512]{1,0:T(8,128)(2,1)S(1)} %get-tuple-element.191), channel_id=1, source_target_pairs={{0,16},{1,17},{2,18},{3,19},{4,20},{5,21},{6,22},{7,23},{8,24},{9,... | collective-permute-start | bytes 786440 | tf_op jit(solution)/shard_map/ppermute | solution.py:56
  118.1 8.4 %collective-permute-start.22 = (bf16[256,512]{1,0:T(8,128)(2,1)S(1)}, bf16[256,512]{1,0:T(8,128)(2,1)S(1)}, u32[]{:S(2)}, u32[]{:S(2)}) collective-permute-start(bf16[256,512]{1,0:T(8,128)(2,1)S(1)} %get-tuple-element.192.refs_4_), channel_id=1, source_target_pairs={{0,8},{1,9},{2,10},{3,11},{4,12},{5,13},{6,14},{7,15},{8,0},{9,1},... | collective-permute-start | bytes 786440 | tf_op jit(solution)/shard_map/ppermute | solution.py:56
  126.9 16.8 %collective-permute-start.27 = (bf16[1536,128]{1,0:T(8,128)(2,1)S(1)}, bf16[1536,128]{1,0:T(8,128)(2,1)S(1)}, u32[]{:S(2)}, u32[]{:S(2)}) collective-permute-start(bf16[1536,128]{1,0:T(8,128)(2,1)S(1)} %get-tuple-element.208), channel_id=1, source_target_pairs={{0,8},{1,9},{2,10},{3,11},{4,12},{5,13},{6,14},{7,15},{8,0},{9,1},... | collective-permute-start | bytes 1179656 | tf_op jit(solution)/shard_map/ppermute | solution.py:56
  128.4 15.3 %collective-permute-start.28 = (bf16[1088,128]{1,0:T(8,128)(2,1)S(1)}, bf16[1088,128]{1,0:T(8,128)(2,1)S(1)}, u32[]{:S(2)}, u32[]{:S(2)}) collective-permute-start(bf16[1088,128]{1,0:T(8,128)(2,1)S(1)} %get-tuple-element.209.refs_4_), channel_id=1, source_target_pairs={{0,16},{1,17},{2,18},{3,19},{4,20},{5,21},{6,22},{7,23},{8,24},{9,... | collective-permute-start | bytes 835592 | tf_op jit(solution)/shard_map/ppermute | solution.py:56
  128.9 14.0 %collective-permute-start.24 = (bf16[256,512]{1,0:T(8,128)(2,1)S(1)}, bf16[256,512]{1,0:T(8,128)(2,1)S(1)}, u32[]{:S(2)}, u32[]{:S(2)}) collective-permute-start(bf16[256,512]{1,0:T(8,128)(2,1)S(1)} %get-tuple-element.202), channel_id=1, source_target_pairs={{0,1},{1,0},{2,3},{3,2},{4,5},{5,4},{6,7},{7,6},{8,9},{9,8},{10,11... | collective-permute-start | bytes 786440 | tf_op jit(solution)/shard_map/ppermute | solution.py:56
  129.5 9.7 %collective-permute-start.25 = (bf16[128,512]{1,0:T(8,128)(2,1)S(1)}, bf16[128,512]{1,0:T(8,128)(2,1)S(1)}, u32[]{:S(2)}, u32[]{:S(2)}) collective-permute-start(bf16[128,512]{1,0:T(8,128)(2,1)S(1)} %get-tuple-element.203), channel_id=1, source_target_pairs={{0,2},{1,3},{2,0},{3,1},{4,6},{5,7},{6,4},{7,5},{8,10},{9,11},{10,... | collective-permute-start | bytes 393224 | tf_op jit(solution)/shard_map/ppermute | solution.py:56
  131.5 11.4 %collective-permute-start.26 = (bf16[128,512]{1,0:T(8,128)(2,1)S(1)}, bf16[128,512]{1,0:T(8,128)(2,1)S(1)}, u32[]{:S(2)}, u32[]{:S(2)}) collective-permute-start(bf16[128,512]{1,0:T(8,128)(2,1)S(1)} %get-tuple-element.204), channel_id=1, source_target_pairs={{0,3},{1,2},{2,1},{3,0},{4,7},{5,6},{6,5},{7,4},{8,11},{9,10},{10,... | collective-permute-start | bytes 393224 | tf_op jit(solution)/shard_map/ppermute | solution.py:56
  144.5 6.5 %collective-permute-start.29 = (bf16[768,128]{1,0:T(8,128)(2,1)S(1)}, bf16[768,128]{1,0:T(8,128)(2,1)S(1)}, u32[]{:S(2)}, u32[]{:S(2)}) collective-permute-start(bf16[768,128]{1,0:T(8,128)(2,1)S(1)} %get-tuple-element.222), channel_id=1, source_target_pairs={{0,16},{1,17},{2,18},{3,19},{4,20},{5,21},{6,22},{7,23},{8,24},{9,... | collective-permute-start | bytes 589832 | tf_op jit(solution)/shard_map/ppermute | solution.py:56
  145.9 5.1 %collective-permute-start.30 = (bf16[576,128]{1,0:T(8,128)(2,1)S(1)}, bf16[576,128]{1,0:T(8,128)(2,1)S(1)}, u32[]{:S(2)}, u32[]{:S(2)}) collective-permute-start(bf16[576,128]{1,0:T(8,128)(2,1)S(1)} %get-tuple-element.223.refs_4_), channel_id=1, source_target_pairs={{0,8},{1,9},{2,10},{3,11},{4,12},{5,13},{6,14},{7,15},{8,0},{9,1},... | collective-permute-start | bytes 442376 | tf_op jit(solution)/shard_map/ppermute | solution.py:56
  151.1 2.4 %collective-permute-start.31 = (bf16[3088,128]{1,0:T(8,128)(2,1)S(1)}, bf16[3088,128]{1,0:T(8,128)(2,1)S(1)}, u32[]{:S(2)}, u32[]{:S(2)}) collective-permute-start(bf16[3088,128]{1,0:T(8,128)(2,1)S(1)} %get-tuple-element.224), channel_id=1, source_target_pairs={{0,4},{1,5},{2,6},{3,7},{4,0},{5,1},{6,2},{7,3},{8,12},{9,13},{10,... | collective-permute-start | bytes 2371592 | tf_op jit(solution)/shard_map/ppermute | solution.py:56
  154.3 22.9 %collective-permute-start.32 = (bf16[512,512]{1,0:T(8,128)(2,1)}, bf16[512,512]{1,0:T(8,128)(2,1)S(1)}, u32[]{:S(2)}, u32[]{:S(2)}) collective-permute-start(bf16[512,512]{1,0:T(8,128)(2,1)} %get-tuple-element.226), channel_id=1, source_target_pairs={{1,0},{3,2},{5,4},{7,6},{9,8},{11,10},{13,12},{15,14},{17,16},{19,... | collective-permute-start | bytes 1572872 | tf_op jit(solution)/shard_map/ppermute | solution.py:62
  155.6 8.1 %collective-permute-start.33 = (bf16[784,128]{1,0:T(8,128)(2,1)}, bf16[784,128]{1,0:T(8,128)(2,1)S(1)}, u32[]{:S(2)}, u32[]{:S(2)}) collective-permute-start(bf16[784,128]{1,0:T(8,128)(2,1)} %get-tuple-element.228), channel_id=1, source_target_pairs={{0,8},{1,9},{2,10},{3,11},{4,12},{5,13},{6,14},{7,15},{8,0},{9,1},... | collective-permute-start | bytes 602120 | tf_op jit(solution)/shard_map/ppermute | solution.py:56
  156.5 11.3 %collective-permute-start.34 = (bf16[784,128]{1,0:T(8,128)(2,1)}, bf16[784,128]{1,0:T(8,128)(2,1)S(1)}, u32[]{:S(2)}, u32[]{:S(2)}) collective-permute-start(bf16[784,128]{1,0:T(8,128)(2,1)} %get-tuple-element.229), channel_id=1, source_target_pairs={{0,16},{1,17},{2,18},{3,19},{4,20},{5,21},{6,22},{7,23},{8,24},{9,... | collective-permute-start | bytes 602120 | tf_op jit(solution)/shard_map/ppermute | solution.py:56
  157.4 10.3 %collective-permute-start.35 = (bf16[784,128]{1,0:T(8,128)(2,1)}, bf16[784,128]{1,0:T(8,128)(2,1)S(1)}, u32[]{:S(2)}, u32[]{:S(2)}) collective-permute-start(bf16[784,128]{1,0:T(8,128)(2,1)} %get-tuple-element.230), channel_id=1, source_target_pairs={{0,24},{1,25},{2,26},{3,27},{4,28},{5,29},{6,30},{7,31},{8,16},{9,... | collective-permute-start | bytes 602120 | tf_op jit(solution)/shard_map/ppermute | solution.py:56
  171.6 9.3 %collective-permute-start.36 = (bf16[592,128]{1,0:T(8,128)(2,1)S(1)}, bf16[592,128]{1,0:T(8,128)(2,1)S(1)}, u32[]{:S(2)}, u32[]{:S(2)}) collective-permute-start(bf16[592,128]{1,0:T(8,128)(2,1)S(1)} %get-tuple-element.233), channel_id=1, source_target_pairs={{0,1},{1,0},{2,3},{3,2},{4,5},{5,4},{6,7},{7,6},{8,9},{9,8},{10,11... | collective-permute-start | bytes 454664 | tf_op jit(solution)/shard_map/ppermute | solution.py:56
  174.1 12.8 %collective-permute-start.37 = (bf16[592,128]{1,0:T(8,128)(2,1)S(1)}, bf16[592,128]{1,0:T(8,128)(2,1)S(1)}, u32[]{:S(2)}, u32[]{:S(2)}) collective-permute-start(bf16[592,128]{1,0:T(8,128)(2,1)S(1)} %get-tuple-element.234), channel_id=1, source_target_pairs={{0,2},{1,3},{2,0},{3,1},{4,6},{5,7},{6,4},{7,5},{8,10},{9,11},{10,... | collective-permute-start | bytes 454664 | tf_op jit(solution)/shard_map/ppermute | solution.py:56
  175.8 11.1 %collective-permute-start.38 = (bf16[592,128]{1,0:T(8,128)(2,1)S(1)}, bf16[592,128]{1,0:T(8,128)(2,1)S(1)}, u32[]{:S(2)}, u32[]{:S(2)}) collective-permute-start(bf16[592,128]{1,0:T(8,128)(2,1)S(1)} %get-tuple-element.235), channel_id=1, source_target_pairs={{0,3},{1,2},{2,1},{3,0},{4,7},{5,6},{6,5},{7,4},{8,11},{9,10},{10,... | collective-permute-start | bytes 454664 | tf_op jit(solution)/shard_map/ppermute | solution.py:56
  (35 other events, 223.2 us)

commit v4 on v3

--- a/solution.py
+++ b/solution.py
@@ -115,18 +115,6 @@
         if self.rider:
             sent[-1].append((self.rider, rider))
         return stay + sent
-
-    def line(self, held, rider):
-        plans = []
-        for k in range(self.nt):
-            plan = []
-            for group, terms in enumerate(held):
-                rows = self.groups[group] * self.r
-                plan.append((rows, [(array, lo + k * rows) for array, lo in terms]))
-            if self.rider:
-                plan.append((self.rider, rider))
-            plans.append(plan)
-        return plans
 
 
 def add_rows_kernel(*refs, plans, count):
@@ -160,6 +148,24 @@
     end = sent[-1].shape[0] - halves.rider
     rider = [(2 * groups, end), (2 * groups - 1, end)]
     return stay + got + sent[-1:], held, rider
+
+
+def line_round(arrays, segments, rider, bit, extra=None):
+    stay, sent, after_round, lo = [], [], [], 0
+    for rows, terms in segments:
+        half = rows // 2
+        stay.append((half, terms))
+        sent.append((half, [(array, first + half) for array, first in terms]))
+        after_round.append((half, [(0, lo), (1, lo)]))
+        lo += half
+    if rider:
+        sent.append(rider)
+        rider = (rider[0], [(1, lo), (2, lo)])
+    if extra is not None:
+        sent.append((extra.shape[0], [(len(arrays), 0)]))
+        arrays = arrays + [extra]
+    stay, sent = add_rows(arrays, [stay, sent])
+    return [stay, swap(sent, 0, bit), sent], after_round, rider
 
 
 def line_swaps(parts):
@@ -629,14 +635,17 @@
     out,
     keep,
     send,
-    du2,
-    db2,
+    du3,
+    dhid,
+    normed,
+    inverse,
     sums,
     hsum,
     act,
     slope,
     acc,
     second,
+    db3,
     turn,
     *,
     halves,
@@ -645,6 +654,8 @@
     w = keep.shape[1]
     summed = first[...] + mm(ctx[...], wo[0], NT) + ob[...].astype(F32)
     n2, r2 = norm_forward(summed)
+    normed[...] = n2
+    inverse[...] = r2
     out2 = n2 * gain2[...].astype(F32) + bias2[...].astype(F32)
     second[...] = out2.astype(BF16)
     acc[...] = out2 + fob[...].astype(F32)
@@ -662,38 +673,55 @@
     n3, r3 = norm_forward(acc[...])
     out[...] = (n3 * gain3[...].astype(F32) + bias3[...].astype(F32)).astype(BF16)
     dy = cot[...].astype(F32)
-    du3 = norm_backward(dy, n3, r3, gain3[...].astype(F32))
-    db3 = du3.astype(BF16)
-    sums[3:4, :] = column_sum(db3)
-    sums[4:5, :] = column_sum(dy * n3)
-    sums[5:6, :] = column_sum(dy)
-    acc[...] = du3
-    db2[...] = db3
+    grad3 = norm_backward(dy, n3, r3, gain3[...].astype(F32))
+    low3 = grad3.astype(BF16)
+    sums[0:1, :] = column_sum(low3)
+    sums[1:2, :] = column_sum(dy * n3)
+    sums[2:3, :] = column_sum(dy)
+    sums[3:8, :] = jnp.zeros((5, width), F32)
+    du3[...] = grad3
+    db3[...] = low3
 
     @pl.loop(0, halves.nt, unroll=2)
     def _(t):
         cols = pl.ds(pl.multiple_of(t * w, w), w)
         s = jnp.bitwise_xor(info[3], t)
         everything = slice(None)
-        back = db2[...]
+        back = db3[...]
         dact = mm(back, wf[1, :, cols], NN)
-        dhid = (dact * slope[:, cols].astype(F32)).astype(BF16)
-        hsum[:, cols] = column_sum(dhid)
-        turn[0] = mm(second[...], dhid, TN).astype(BF16)
+        part = (dact * slope[:, cols].astype(F32)).astype(BF16)
+        dhid[:, cols] = part
+        hsum[:, cols] = column_sum(part)
+        turn[0] = mm(second[...], part, TN).astype(BF16)
         disperse(info, halves, turn.at[0], 0, everything, s, keep, send)
         turn[1] = mm(back, act[:, cols], TN).astype(BF16)
         disperse(info, halves, turn.at[1], 1, everything, s, keep, send)
-        acc[...] += mm(dhid, wf[0, :, cols], NT)
-
-    dsecond = acc[...]
-    grad2 = norm_backward(dsecond, n2, r2, gain2[...].astype(F32))
-    low2 = grad2.astype(BF16)
-    du2[...] = grad2
-    db2[...] = low2
-    sums[0:1, :] = column_sum(low2)
-    sums[1:2, :] = column_sum(dsecond * n2)
+
+
+def feed_back_kernel(du3, dhid, normed, inverse, wf, gain, du2, db2, sums):
+    dsecond = du3[...] + mm(dhid[...], wf[0], NT)
+    n = normed[...]
+    grad = norm_backward(dsecond, n, inverse[...], gain[...].astype(F32))
+    low = grad.astype(BF16)
+    du2[...] = grad
+    db2[...] = low
+    sums[0:1, :] = column_sum(low)
+    sums[1:2, :] = column_sum(dsecond * n)
     sums[2:3, :] = column_sum(dsecond)
-    sums[6:8, :] = jnp.zeros((2, width), F32)
+    sums[3:8, :] = jnp.zeros((5, du2.shape[1]), F32)
+
+
+def feed_back(du3, dhid, normed, inverse, wf, gain):
+    tokens, width = du3.shape
+    wide = wf.shape[2]
+    return pl.pallas_call(
+        feed_back_kernel,
+        grid=(1,),
+        out_shape=(shaped(du3.shape, F32), shaped(du3.shape, BF16), shaped((8, width), F32)),
+        in_specs=[VMEM] * 4 + [pl.BlockSpec((1, width, wide), lambda h: (0, 0, 0)), VMEM],
+        compiler_params=limit(16),
+        cost_estimate=cost(tokens * width * wide, 8 << 20),
+    )(du3, dhid, normed, inverse, wf, gain)
 
 
 def matrix(slot, width):
@@ -713,7 +741,9 @@
             flat,
             flat,
             shaped(first.shape, F32),
-            shaped(first.shape, BF16),
+            shaped((tokens, wide), BF16),
+            shaped(first.shape, F32),
+            shaped((tokens, 1), F32),
             shaped((8, width), F32),
             shaped((1, wide), F32),
         ),
@@ -723,6 +753,7 @@
             pltpu.VMEM((tokens, wide), BF16),
             pltpu.VMEM((tokens, width), F32),
             pltpu.VMEM((tokens, width), BF16),
+            pltpu.VMEM((tokens, width), BF16),
             pltpu.VMEM((2, width, w), BF16),
         ],
         compiler_params=limit(28),
@@ -738,6 +769,7 @@
     dv2,
     db2,
     sums2,
+    sums3,
     hsum,
     normed,
     inverse,
@@ -765,7 +797,8 @@
     riders[0:1, :] = column_sum(low)
     riders[1:2, :] = column_sum(dfirst * n)
     riders[2:3, :] = column_sum(dfirst)
-    riders[3:9, :] = sums2[0:6, :]
+    riders[3:6, :] = sums2[0:3, :]
+    riders[6:9, :] = sums3[0:3, :]
     riders[9:10, :] = column_sum(dq2[...])
     riders[10:11, :] = column_sum(dv2[...])
     for i in range(4):
@@ -794,7 +827,7 @@
             target[lo : lo + 16, :] = riders[:, q * w : q * w + w].astype(BF16)
 
 
-def middle(info, du2, dq2, dk2, dv2, db2, sums2, hsum, normed, inverse, first, mem, memo, ctx2, ctx1, w, gain):
+def middle(info, near, normed, inverse, first, mem, memo, ctx2, ctx1, w, gain):
     tokens, width = first.shape
     rows = mem.shape[0]
     nd, nt = lax.axis_size("dp"), lax.axis_size("tensor")
@@ -815,13 +848,13 @@
             shaped((rows, width), BF16),
         )
         + last,
-        in_specs=[SMEM] + [VMEM] * 14 + [matrix(i, width) for i in (4, 5, 6)] + [VMEM],
+        in_specs=[SMEM] + [VMEM] * 15 + [matrix(i, width) for i in (4, 5, 6)] + [VMEM],
         scratch_shapes=[pltpu.VMEM((5, width, width), BF16), pltpu.VMEM((16, width), F32)],
         compiler_params=limit(20),
         cost_estimate=cost(6 * first.size * width, 12 << 20),
     )(
         info,
-        *(du2, dq2, dk2, dv2, db2, sums2, hsum),
+        *near,
         *far(normed, inverse, first, mem, memo, ctx2, ctx1, w, w, w),
         gain,
     )
@@ -980,17 +1013,16 @@
 
     bits = [1 << i for i in range(nt.bit_length() - 1)]
     swapped = [swap(packed, 0, k) for k in range(1, nt)]
-    line_feed = doubled(after(feed_shard, packed)[None], bits[:1])
-    line = jnp.stack([after(packed, line_feed)] + swapped)
+    line = jnp.stack([packed] + swapped)
     count = 8 * self_query.shape[0]
     riders = line[:, count:]
     line = line[:, :count].reshape((nt, 8) + self_query.shape)
-    line_feed = doubled(after(line_feed, line), bits[1:])
+    line_feed = doubled(after(feed_shard, line)[None], bits)
     inputs_other = hand_over(after(inputs, line), 0, 1)
-    memory_other = swap(after(memory, line_feed), 0, 1)
     head_biases, hidden_bias = spread(info, riders)
-    group = both_cores(over_planes(line), inputs_other, memory_other, head_biases)
+    group = both_cores(over_planes(line), inputs_other, line_feed, head_biases)
     line_feed = after(line_feed, group[0])
+    memory_other = swap(after(memory, group[0]), 0, 1)
     planes_feed = over_planes(line_feed)
 
     weights = assemble(info, group)
@@ -1011,7 +1043,7 @@
     own = [planes_feed[0]] + [after(piece, ctx2) for piece in planes_feed[1:]]
     w_feed = assemble(info, planes_feed + [swap(piece, 1, 0) for piece in own])
     feed_halves = Halves((1, 1), width // nd, 0)
-    outputs, keep, send, du2, db2, sums_feed, sums_hidden = feed(
+    outputs, keep, send, du3, dhidden, normed2, inverse2, sums_feed, sums_hidden = feed(
         info,
         feed_halves,
         ctx2,
@@ -1029,19 +1061,16 @@
     )
     rounds = feed_halves.rounds
     got = swap(send, 1, 0)
+    du2, db2, sums_second = feed_back(
+        du3, dhidden, normed2, inverse2, w_feed, row(cross_norm_gain)
+    )
+    whole = [[(0, base), (1, base)] for base in feed_halves.bases]
+    arrays, held, _ = halve(feed_halves, [after(keep, db2), got], whole, None, 0)
+    db2 = after(db2, arrays[0])
     dq2, dk2, dv2 = cross_backward(q2, k2, v2, ctx2, log2, db2, weights)
-    whole = [[(0, base), (1, base)] for base in feed_halves.bases]
-    arrays, held, _ = halve(feed_halves, [after(keep, dq2), got], whole, None, 0)
-    du2 = after(du2, arrays[0])
     middle_halves, (du1, db1, memory_own, memory_back, keep, send) = middle(
         info,
-        du2,
-        dq2,
-        dk2,
-        dv2,
-        db2,
-        sums_feed,
-        sums_hidden,
+        (du2, dq2, dk2, dv2, db2, sums_second, sums_feed, sums_hidden),
         normed1,
         inverse1,
         first,
@@ -1061,66 +1090,72 @@
     operands = (info, q1, k1, v1, k1o, v1o, ctx1, log1)
     grads_early = self_backward(*operands, db1, weights, 0, pairs)
     arrays[0] = after(arrays[0], grads_early[0])
-    plans = feed_halves.line(held, None)
-    riding = memory_back.shape[1] == arrays[0].shape[1]
-    if riding:
-        plans[1].append((memory_back.shape[0], [(len(arrays), 0)]))
-        arrays.append(memory_back)
-    lines_feed = line_swaps(add_rows(arrays, plans))
+    block = feed_in.shape[0]
+    feed_segments = list(zip(feed_halves.sizes, held))
+    feed_arrays = arrays
+    for bit in reversed(bits[1:]):
+        feed_arrays, feed_segments, _ = line_round(feed_arrays, feed_segments, None, bit)
     whole = [[(0, base), (1, base)] for base in middle_halves.bases]
     rider = [(0, middle_halves.main), (1, middle_halves.main)]
-    keep = after(keep, lines_feed[0])
+    keep = after(keep, feed_arrays[0])
     arrays, held, rider = halve(middle_halves, [keep, got], whole, rider, 0)
-    db1, _, _ = lax.optimization_barrier((db1, arrays[0], lines_feed[0]))
+    db1 = after(db1, arrays[0])
     grads_late = list(self_backward(*operands, db1, weights, pairs, pairs))
-    lines_feed[0] = after(lines_feed[0], grads_late[0])
-    block = feed_in.shape[0]
-    each = range(nt)
-    grad_feed_in, grad_feed_out = add_rows(
-        lines_feed,
-        [[(block, [(k, i * block) for k in each])] for i in range(2)],
-        F32,
-    )
-    arrays[0] = after(arrays[0], grad_feed_in)
+    arrays[0] = after(arrays[0], grads_late[0])
     for index in range(1, rounds):
         arrays, held, rider = halve(middle_halves, arrays, held, rider, index)
     grads_late[0] = after(grads_late[0], arrays[0])
     self_halves, (inputs_back, keep, send) = self_grads(
         info, inputs, inputs_other, grads_early, grads_late, weights
     )
-    got = swap(after(send, *arrays), 1, 0)
+    send = after(send, *arrays, *feed_arrays)
+    got = swap(send, 1, 0)
+    inputs_got = hand_over(after(inputs_back, send), 1, -1)
+    arrays[0] = after(arrays[0], send)
+    segments = list(zip(middle_halves.sizes, held))
+    rider = (middle_halves.rider, rider)
+    for bit in reversed(bits[1:]):
+        arrays, segments, rider = line_round(arrays, segments, rider, bit)
+    keep = after(keep, arrays[0])
+
+    size = self_halves.sizes[0]
+    end = (self_halves.rider, [(0, self_halves.main), (1, self_halves.main)])
+    places = [self_halves.place(0, j)[0] for j in range(nd // 2)]
+    parts = add_rows([keep, got], [[(size, [(0, lo), (1, lo)]), end] for lo in places])
+    planes = [parts[0]] + [swap(part, 2 * j, 0) for j, part in enumerate(parts) if j]
+    planes[0] = after(planes[0], *arrays, inputs_got)
+    at = range(len(planes))
+    rows = 3 * block
+    end = (self_halves.rider, [(p, size) for p in at])
+    lines = add_rows(planes, [[(rows, [(p, k * rows) for p in at]), end] for k in range(nt)])
+    lines = line_swaps(lines)
+    arrays[0] = after(arrays[0], lines[0])
+    arrays, segments, rider = line_round(arrays, segments, rider, 1)
+    riding = memory_back.shape[1] == feed_arrays[0].shape[1]
+    feed_arrays[0] = after(feed_arrays[0], lines[0])
+    feed_arrays, feed_segments, _ = line_round(
+        feed_arrays, feed_segments, None, 1, memory_back if riding else None
+    )
+
+    grad_feed_in, grad_feed_out = add_rows(
+        feed_arrays[:2], [[(block, terms)] for _, terms in feed_segments], F32
+    )
     if riding:
-        memory_got = lines_feed[1][2 * block :]
+        memory_got = feed_arrays[1][2 * block :]
     else:
-        memory_got = swap(after(memory_back, lines_feed[0]), 0, 1)
+        memory_got = swap(after(memory_back, lines[0]), 0, 1)
     grad_memory = memory_own + memory_got.astype(F32)
-
-    rider_self = self_halves.rider
-    size = self_halves.sizes[0]
-    parts = add_rows(
-        [keep, got],
-        [
-            [(size, [(0, j * size), (1, j * size)]), (rider_self, [(0, self_halves.main), (1, self_halves.main)])]
-            for j in map(lambda j: self_halves.place(0, j)[0] // size, range(nd // 2))
-        ],
-    )
-    planes = [parts[0]] + [swap(part, 2 * j, 0) for j, part in enumerate(parts) if j]
-    inputs_got = hand_over(after(inputs_back, parts[0]), 1, -1)
-    count = len(arrays)
-    planes_at = range(count, count + len(planes))
-    plans = middle_halves.line(held, rider)
-    for k, plan in enumerate(plans):
-        rows = 3 * block
-        plan.append((rows, [(p, k * rows) for p in planes_at]))
-        plan.append((rider_self, [(p, size) for p in planes_at]))
-    lines = line_swaps(add_rows(arrays + planes, plans))
     grad_inputs = input_grads(du1, grads_early[:3], grads_late[:3], weights, inputs_got)
-    lines[0] = after(lines[0], grad_inputs)
-    middle_rider = 5 * block
-    self_at = middle_rider + middle_halves.rider
-    cuts = [(i * block, block) for i in range(5)] + [(middle_rider, middle_halves.rider)]
-    cuts += [(self_at + i * block, block) for i in range(3)] + [(self_at + 3 * block, rider_self)]
-    sums = add_rows(lines, [[(n, [(k, lo) for k in each])] for lo, n in cuts], F32)
+    lines[0] = after(lines[0], grad_inputs, grad_feed_in)
+    plans = [
+        [(block, [(array, lo + i * block) for array, lo in terms])]
+        for count, (_, terms) in zip(middle_halves.groups, segments)
+        for i in range(count)
+    ]
+    plans.append([rider])
+    cuts = [(i * block, block) for i in range(3)] + [(rows, self_halves.rider)]
+    plans += [[(n, [(3 + k, lo) for k in range(nt)])] for lo, n in cuts]
+    sums = add_rows(arrays + lines, plans, F32)
     grad_middle, early = sums[:5], sums[5]
     grad_self, late_sums = sums[6:9], sums[9]
     early = early.reshape(nt, 16, columns).transpose(1, 0, 2).reshape(16, width)

time: 192 us -> 179 us (0.932)
  waiting for transfers between devices: 64.6 us -> 57.2 us
  local copies, waits for them, and re-layouts: 11.5 us -> 6.34 us
    ppermute x37 -> x38, waiting for transfers between devices: 64.6 us -> 49.9 us  [swap(): return lax.ppermute(array, ('dp', 'tensor'), pairs)]
    ppermute x2, waiting for transfers between devices: 0.01 us -> 7.29 us  [hand_over(): return lax.ppermute(array, ('dp', 'tensor'), pairs)]
    unnamed x89 -> x72, local copies, waits for them, and re-layouts: 7.24 us -> 2.06 us
    ppermute x37 -> x38, starting transfers between devices: 40.4 us -> 36.5 us  [swap(): return lax.ppermute(array, ('dp', 'tensor'), pairs)]
    ppermute x2, starting transfers between devices: 3.22 us -> 5.21 us  [hand_over(): return lax.ppermute(array, ('dp', 'tensor'), pairs)]
    pallas_call x9 -> x12, Pallas kernels: 3.85 us -> 3.81 us  [add_rows(): pl.pallas_call(functools.partial(add_rows_kernel, plans=plans, count=len(...]
  transfers between devices with their start and end apart: 39 -> 40, of which waited for: 22 -> 19; matrix products, arithmetic and copies ran while one was open for 1% -> 2% of each run, Pallas kernels for 25% -> 27%
where the time goes in v4:
time: 179 us; the launch traced here: 178 us
  Pallas kernels  63.8 us (36%)
  waiting for transfers between devices  57.2 us (32%)
  starting transfers between devices  41.7 us (23%)
  other arithmetic  6.86 us (4%)
  local copies, waits for them, and re-layouts  6.34 us (4%)
  between operations  2.14 us (1%)
    ppermute x38, waiting for transfers between devices, swap(): return lax.ppermute(array, ('dp', 'tensor'), pairs)  49.9 us
    ppermute x38, starting transfers between devices, swap(): return lax.ppermute(array, ('dp', 'tensor'), pairs)  36.5 us
    pallas_call x2, Pallas kernels, self_backward(): pl.pallas_call(self_backward_kernel, grid=(pairs,), out_shape=(out,) * 5,...  11.7 us
    pallas_call x1, Pallas kernels, feed(): pl.pallas_call(functools.partial(feed_kernel, halves=halves), grid=(1,),...  11.1 us
    ppermute x2, waiting for transfers between devices, hand_over(): return lax.ppermute(array, ('dp', 'tensor'), pairs)  7.29 us
    pallas_call x1, Pallas kernels, cross_backward(): pl.pallas_call(cross_backward_kernel, grid=(width // PAIR,), out_shape=(s...  6.48 us
    pallas_call x1, Pallas kernels, middle(): pl.pallas_call(functools.partial(middle_kernel, halves=halves if direct e...  5.77 us
    pallas_call x1, Pallas kernels, self_forward(): pl.pallas_call(self_forward_kernel, grid=(width // PAIR,), out_shape=(sha...  5.3 us
  transfers between devices with their start and end apart: 40, of which 19 were waited for; matrix products, arithmetic and copies ran while one was open for 2% of the time, Pallas kernels for 27%

profile of v4, /device:TPU:0, one launch (start us, length us, event | category | flops | bytes accessed | tf_op | source)
XLA Modules:
  0.0 178.1 jit_solution(8700854650450052770)
XLA Ops:
  0.7 1.6 shard_map.475
  2.3 5.0 %collective-permute-start.2 = (bf16[528,128]{1,0:T(8,128)(2,1)}, bf16[528,128]{1,0:T(8,128)(2,1)S(1)}, u32[]{:S(2)}, u32[]{:S(2)}) collective-permute-start(bf16[528,128]{1,0:T(8,128)(2,1)} %shard_map.475), channel_id=1, source_target_pairs={{0,3},{1,2},{2,1},{3,0},{4,7},{5,6},{6,5},{7,4},{8,11},{9,10},{10,... | collective-permute-start | bytes 405512 | tf_op jit(solution)/shard_map/ppermute | solution.py:56
  8.8 3.3 %collective-permute-done.2 = bf16[528,128]{1,0:T(8,128)(2,1)S(1)} collective-permute-done((bf16[528,128]{1,0:T(8,128)(2,1)}, bf16[528,128]{1,0:T(8,128)(2,1)S(1)}, u32[]{:S(2)}, u32[]{:S(2)}) %collective-permute-start.2) | collective-permute-done | bytes 135200 | tf_op jit(solution)/shard_map/ppermute | solution.py:56
  12.1 6.8 %collective-permute-done.1 = bf16[528,128]{1,0:T(8,128)(2,1)S(1)} collective-permute-done((bf16[528,128]{1,0:T(8,128)(2,1)}, bf16[528,128]{1,0:T(8,128)(2,1)S(1)}, u32[]{:S(2)}, u32[]{:S(2)}) %collective-permute-start.1) | collective-permute-done | bytes 135200 | tf_op jit(solution)/shard_map/ppermute | solution.py:56
  19.0 1.0 pad_maximum_fusion.1
  20.1 3.9 %collective-permute-start.3 = (bf16[512,512]{1,0:T(8,128)(2,1)S(1)}, bf16[512,512]{1,0:T(8,128)(2,1)S(1)}, u32[]{:S(2)}, u32[]{:S(2)}) collective-permute-start(bf16[512,512]{1,0:T(8,128)(2,1)S(1)} %copy-done.8), channel_id=1, source_target_pairs={{0,1},{2,3},{4,5},{6,7},{8,9},{10,11},{12,13},{14,15},{16,17},{18,... | collective-permute-start | bytes 1572872 | tf_op jit(solution)/shard_map/ppermute | solution.py:62
  24.0 2.5 %collective-permute-start.8 = (bf16[4,8,64,128]{3,2,1,0:T(8,128)(2,1)S(1)}, bf16[4,8,64,128]{3,2,1,0:T(8,128)(2,1)S(1)}, u32[]{:S(2)}, u32[]{:S(2)}) collective-permute-start(bf16[4,8,64,128]{3,2,1,0:T(8,128)(2,1)S(1)} %bitcast.61), channel_id=1, source_target_pairs={{0,24},{1,25},{2,26},{3,27},{4,28},{5,29},{6,30},{7,31},{8,16},{9,... | collective-permute-start | bytes 1572872 | tf_op jit(solution)/shard_map/ppermute | solution.py:56
  28.3 1.1 collective-permute-start.5
  31.8 1.4 shard_map.476
  33.2 6.9 %collective-permute-done.5 = bf16[2,2,64,512]{3,2,1,0:T(8,128)(2,1)} collective-permute-done((bf16[2,2,64,512]{3,2,1,0:T(8,128)(2,1)}, bf16[2,2,64,512]{3,2,1,0:T(8,128)(2,1)}, u32[]{:S(2)}, u32[]{:S(2)}) %collective-permute-start.5) | collective-permute-done | bytes 262176 | tf_op jit(solution)/shard_map/ppermute | solution.py:56
  40.1 1.0 pad_maximum_fusion.2.refs_0_
  41.1 7.4 %collective-permute-done.7 = bf16[4,8,64,128]{3,2,1,0:T(8,128)(2,1)S(1)} collective-permute-done((bf16[4,8,64,128]{3,2,1,0:T(8,128)(2,1)S(1)}, bf16[4,8,64,128]{3,2,1,0:T(8,128)(2,1)S(1)}, u32[]{:S(2)}, u32[]{:S(2)}) %collective-permute-start.7) | collective-permute-done | bytes 524320 | tf_op jit(solution)/shard_map/ppermute | solution.py:56
  48.8 1.3 pad_maximum_fusion.refs_0_
  50.2 1.6 collective-permute-start.11
  52.4 1.3 collective-permute-start.13
  54.5 1.3 shard_map.477.wq.wk.wv.wo.w
  55.8 1.7 shard_map.478
  57.6 5.3 %shard_map.479 = (bf16[512,512]{1,0:T(8,128)(2,1)S(1)}, f32[512,512]{1,0:T(8,128)S(1)}) custom-call(s32[4]{0:T(128)S(1)} %copy-done.23, bf16[512,512]{1,0:T(8,128)(2,1)S(1)} %get-tuple-element.152.q, bf16[512,512]{1,0:T(8,128)(2,1)S(1)} %get-tuple-element.153.k, bf16[512,512]{1,0:T(8,128)(2,1)S(1)} %get-tuple-element.154.v, ...), custom_call_target="tpu_custom_call" | custom-call | flops 33554432 | bytes 81920 | tf_op jit(solution)/shard_map/pallas_call | solution.py:500
  63.0 1.4 shard_map.480
  65.4 3.0 %shard_map.481 = (bf16[512,512]{1,0:T(8,128)(2,1)S(1)}, f32[512,512]{1,0:T(8,128)S(1)}) custom-call(bf16[512,512]{1,0:T(8,128)(2,1)S(1)} %get-tuple-element.159.q, bf16[256,512]{1,0:T(8,128)(2,1)S(1)} %get-tuple-element.160.k, bf16[256,512]{1,0:T(8,128)(2,1)S(1)} %get-tuple-element.161.v), custom_call_target="tpu_custom_call" | custom-call | flops 8388608 | bytes 49152 | tf_op jit(solution)/shard_map/pallas_call | solution.py:530
  68.9 8.1 %collective-permute-done.12.refs_2_ = bf16[4,2,64,512]{3,2,1,0:T(8,128)(2,1)S(1)} collective-permute-done((bf16[4,2,64,512]{3,2,1,0:T(8,128)(2,1)S(1)}, bf16[4,2,64,512]{3,2,1,0:T(8,128)(2,1)S(1)}, u32[]{:S(2)}, u32[]{:S(2)}) %collective-permute-start.12) | collective-permute-done | bytes 524320 | tf_op jit(solution)/shard_map/ppermute | solution.py:56
  77.7 1.2 collective-permute-done.16.refs_6_
  80.6 11.1 %shard_map.483 = (bf16[512,512]{1,0:T(8,128)(2,1)}, bf16[2048,512]{1,0:T(8,128)(2,1)S(1)}, bf16[2048,512]{1,0:T(8,128)(2,1)S(1)}, f32[512,512]{1,0:T(8,128)S(1)}...) custom-call(s32[4]{0:T(128)S(1)} %copy-done.23, ...), custom_call_target="tpu_custom_call" | custom-call | flops 50331648 | bytes 229376 | tf_op jit(solution)/shard_map/pallas_call | solution.py:736
  91.8 1.8 shard_map.484
  93.6 2.3 %collective-permute-done.18.refs_1_ = bf16[2048,512]{1,0:T(8,128)(2,1)S(1)} collective-permute-done((bf16[2048,512]{1,0:T(8,128)(2,1)S(1)}, bf16[2048,512]{1,0:T(8,128)(2,1)S(1)}, u32[]{:S(2)}, u32[]{:S(2)}) %collective-permute-start.18) | collective-permute-done | bytes 2097184 | tf_op jit(solution)/shard_map/ppermute | solution.py:56
  96.9 1.4 collective-permute-start.20
  98.3 6.5 %shard_map.486 = (bf16[512,512]{1,0:T(8,128)(2,1)S(1)}, bf16[256,512]{1,0:T(8,128)(2,1)S(1)}, bf16[256,512]{1,0:T(8,128)(2,1)S(1)}) custom-call(bf16[512,512]{1,0:T(8,128)(2,1)} %copy-done.11, bf16[256,512]{1,0:T(8,128)(2,1)} %copy-done.15, bf16[256,512]{1,0:T(8,128)(2,1)} %copy-done.16, bf16[512,512]{1,0:T(8,128)(2,1)} %copy-done.2, f32[512,512]{1,0:T(8,128)} %copy-done.14, ...), custom_call_target="tpu_custom_call" | custom-call | flops 20971520 | bytes 65536 | tf_op jit(solution)/shard_map/pallas_call | solution.py:545
  104.8 5.8 %shard_map.487 = (f32[512,512]{1,0:T(8,128)S(1)}, bf16[512,512]{1,0:T(8,128)(2,1)S(1)}, f32[128,512]{1,0:T(8,128)S(1)}, bf16[128,512]{1,0:T(8,128)(2,1)S(1)}, bf...) custom-call(s32[4]{0:T(128)S(1)} %copy-done.23, f32[512,512]{1,0:T(8,128)S(1)} %get-tuple-element.174.du2, ...), custom_call_target="tpu_custom_call" | custom-call | flops 12582912 | bytes 196608 | tf_op jit(solution)/shard_map/pallas_call | solution.py:841
  112.6 1.5 collective-permute-start.22
  114.1 5.8 %shard_map.489 = (bf16[512,256]{1,0:T(8,128)(2,1)S(1)}, bf16[512,256]{1,0:T(8,128)(2,1)S(1)}, bf16[512,256]{1,0:T(8,128)(2,1)S(1)}, bf16[512,256]{1,0:T(8,128)(2,1)S(1)}, bf16[512,256]{1,0:T(8,128)(2,1)S(1)}) custom-call(s32[4]{0:T(128)S(1)} %copy-done.23, bf16[512,512]{1,0:T(8,128)(2,1)} %copy-done.3, bf16[512,512]{1,0:T(8,128)(2,1)} %copy-done.4, ...), custom_call_target="tpu_custom_call" | custom-call | flops 41943040 | bytes 131072 | tf_op jit(solution)/shard_map/pallas_call | solution.py:515
  121.4 1.6 collective-permute-start.24
  123.6 1.2 collective-permute-start.28
  124.9 5.9 %shard_map.492 = (bf16[512,256]{1,0:T(8,128)(2,1)S(1)}, bf16[512,256]{1,0:T(8,128)(2,1)S(1)}, bf16[512,256]{1,0:T(8,128)(2,1)S(1)}, bf16[512,256]{1,0:T(8,128)(2,1)S(1)}, bf16[512,256]{1,0:T(8,128)(2,1)S(1)}) custom-call(s32[4]{0:T(128)S(1)} %copy-done.23, bf16[512,512]{1,0:T(8,128)(2,1)} %copy-done.3, bf16[512,512]{1,0:T(8,128)(2,1)} %copy-done.4, ...), custom_call_target="tpu_custom_call" | custom-call | flops 41943040 | bytes 131072 | tf_op jit(solution)/shard_map/pallas_call | solution.py:515
  130.7 1.1 collective-permute-done.24.refs_2_
  132.0 1.5 collective-permute-start.26
  134.2 3.1 %shard_map.494 = (bf16[512,512]{1,0:T(8,128)(2,1)S(1)}, bf16[3088,128]{1,0:T(8,128)(2,1)S(1)}, bf16[3088,128]{1,0:T(8,128)(2,1)S(1)}) custom-call(s32[4]{0:T(128)S(1)} %copy-done.23, bf16[512,512]{1,0:T(8,128)(2,1)} %x.5, bf16[512,512]{1,0:T(8,128)(2,1)} %copy-done.12, bf16[512,256]{1,0:T(8,128)(2,1)S(1)} %get-tuple-element.199.dqa, ...), custom_call_target="tpu_custom_call" | custom-call | flops 14680064 | bytes 131072 | tf_op jit(solution)/shard_map/pallas_call | solution.py:920
  137.3 1.2 collective-permute-done.27.refs_3_
  138.6 1.3 collective-permute-start.29
  141.9 1.3 collective-permute-start.33
  143.2 1.4 collective-permute-start.34
  144.6 1.2 collective-permute-start.31
  145.8 5.5 %collective-permute-done.31.refs_1_ = bf16[704,128]{1,0:T(8,128)(2,1)S(1)} collective-permute-done((bf16[704,128]{1,0:T(8,128)(2,1)S(1)}, bf16[704,128]{1,0:T(8,128)(2,1)S(1)}, u32[]{:S(2)}, u32[]{:S(2)}) %collective-permute-start.31) | collective-permute-done | bytes 180256 | tf_op jit(solution)/shard_map/ppermute | solution.py:56
  151.4 7.3 %collective-permute-done.29.back = bf16[512,512]{1,0:T(8,128)(2,1)S(1)} collective-permute-done((bf16[512,512]{1,0:T(8,128)(2,1)S(1)}, bf16[512,512]{1,0:T(8,128)(2,1)S(1)}, u32[]{:S(2)}, u32[]{:S(2)}) %collective-permute-start.29) | collective-permute-done | bytes 524320 | tf_op jit(solution)/shard_map/ppermute | solution.py:62
  159.4 1.6 collective-permute-start.35
  161.6 1.5 collective-permute-start.37
  163.2 2.9 %collective-permute-start.39 = (bf16[208,128]{1,0:T(8,128)(2,1)}, bf16[208,128]{1,0:T(8,128)(2,1)S(1)}, u32[]{:S(2)}, u32[]{:S(2)}) collective-permute-start(bf16[208,128]{1,0:T(8,128)(2,1)} %get-tuple-element.257), channel_id=1, source_target_pairs={{0,3},{1,2},{2,1},{3,0},{4,7},{5,6},{6,5},{7,4},{8,11},{9,10},{10,... | collective-permute-start | bytes 159752 | tf_op jit(solution)/shard_map/ppermute | solution.py:56
  166.0 3.7 %shard_map.495 = f32[512,512]{1,0:T(8,128)} custom-call(f32[512,512]{1,0:T(8,128)} %copy-done.13, bf16[512,256]{1,0:T(8,128)(2,1)S(1)} %get-tuple-element.199.dqa, bf16[512,256]{1,0:T(8,128)(2,1)S(1)} %get-tuple-element.200.dka, bf16[512,256]{1,0:T(8,128)(2,1)S(1)} %get-tuple-element.201.dva, bf16[512,256]{1,0:T(8,128)(2,1)S(1)} %get-tuple-element.219.dqb, ...), custom_call_target="tpu_custom_call" | custom-call | flops 6291456 | bytes 98304 | tf_op jit(solution)/shard_map/pallas_call | solution.py:948
  170.6 2.4 %collective-permute-done.37.refs_4_ = bf16[208,128]{1,0:T(8,128)(2,1)S(1)} collective-permute-done((bf16[208,128]{1,0:T(8,128)(2,1)}, bf16[208,128]{1,0:T(8,128)(2,1)S(1)}, u32[]{:S(2)}, u32[]{:S(2)}) %collective-permute-start.37) | collective-permute-done | bytes 53280 | tf_op jit(solution)/shard_map/ppermute | solution.py:56
  (160 shorter events, 26.2 us)
Async XLA Ops:
  0.7 19.4 %copy-start.8 = (bf16[512,512]{1,0:T(8,128)(2,1)S(1)}, bf16[512,512]{1,0:T(8,128)(2,1)}, u32[]{:S(2)}) copy-start(bf16[512,512]{1,0:T(8,128)(2,1)} %x.5) | copy-start | bytes 1572868
  0.7 28.7 %copy-start.35 = (s32[2]{0:T(128)S(1)}, s32[2]{0:T(128)}, u32[]{:S(2)}) copy-start(s32[2]{0:T(128)} %param.30) | copy-start | bytes 28
  2.3 28.9 %copy-start.25 = (bf16[528,128]{1,0:T(8,128)(2,1)S(1)}, bf16[528,128]{1,0:T(8,128)(2,1)}, u32[]{:S(2)}) copy-start(bf16[528,128]{1,0:T(8,128)(2,1)} %shard_map.475) | copy-start | bytes 405508
  2.3 9.8 %collective-permute-start.2 = (bf16[528,128]{1,0:T(8,128)(2,1)}, bf16[528,128]{1,0:T(8,128)(2,1)S(1)}, u32[]{:S(2)}, u32[]{:S(2)}) collective-permute-start(bf16[528,128]{1,0:T(8,128)(2,1)} %shard_map.475), channel_id=1, source_target_pairs={{0,3},{1,2},{2,1},{3,0},{4,7},{5,6},{6,5},{7,4},{8,11},{9,10},{10,... | collective-permute-start | bytes 405512 | tf_op jit(solution)/shard_map/ppermute | solution.py:56
  7.3 11.6 %collective-permute-start.1 = (bf16[528,128]{1,0:T(8,128)(2,1)}, bf16[528,128]{1,0:T(8,128)(2,1)S(1)}, u32[]{:S(2)}, u32[]{:S(2)}) collective-permute-start(bf16[528,128]{1,0:T(8,128)(2,1)} %shard_map.475), channel_id=1, source_target_pairs={{0,2},{1,3},{2,0},{3,1},{4,6},{5,7},{6,4},{7,5},{8,10},{9,11},{10,... | collective-permute-start | bytes 405512 | tf_op jit(solution)/shard_map/ppermute | solution.py:56
  7.3 11.6 %collective-permute-start = (bf16[528,128]{1,0:T(8,128)(2,1)}, bf16[528,128]{1,0:T(8,128)(2,1)S(1)}, u32[]{:S(2)}, u32[]{:S(2)}) collective-permute-start(bf16[528,128]{1,0:T(8,128)(2,1)} %shard_map.475), channel_id=1, source_target_pairs={{0,1},{1,0},{2,3},{3,2},{4,5},{5,4},{6,7},{7,6},{8,9},{9,8},{10,11... | collective-permute-start | bytes 405512 | tf_op jit(solution)/shard_map/ppermute | solution.py:56
  20.0 7.6 %collective-permute-start.4 = (bf16[1,2,64,512]{3,2,1,0:T(8,128)(2,1)S(1)}, bf16[1,2,64,512]{3,2,1,0:T(8,128)(2,1)S(1)}, u32[]{:S(2)}, u32[]{:S(2)}) collective-permute-start(bf16[1,2,64,512]{3,2,1,0:T(8,128)(2,1)S(1)} %bitcast.67), channel_id=1, source_target_pairs={{0,1},{1,0},{2,3},{3,2},{4,5},{5,4},{6,7},{7,6},{8,9},{9,8},{10,11... | collective-permute-start | bytes 393224 | tf_op jit(solution)/shard_map/ppermute | solution.py:56
  20.1 21.0 %collective-permute-start.3 = (bf16[512,512]{1,0:T(8,128)(2,1)S(1)}, bf16[512,512]{1,0:T(8,128)(2,1)S(1)}, u32[]{:S(2)}, u32[]{:S(2)}) collective-permute-start(bf16[512,512]{1,0:T(8,128)(2,1)S(1)} %copy-done.8), channel_id=1, source_target_pairs={{0,1},{2,3},{4,5},{6,7},{8,9},{10,11},{12,13},{14,15},{16,17},{18,... | collective-permute-start | bytes 1572872 | tf_op jit(solution)/shard_map/ppermute | solution.py:62
  24.0 17.1 %collective-permute-start.8 = (bf16[4,8,64,128]{3,2,1,0:T(8,128)(2,1)S(1)}, bf16[4,8,64,128]{3,2,1,0:T(8,128)(2,1)S(1)}, u32[]{:S(2)}, u32[]{:S(2)}) collective-permute-start(bf16[4,8,64,128]{3,2,1,0:T(8,128)(2,1)S(1)} %bitcast.61), channel_id=1, source_target_pairs={{0,24},{1,25},{2,26},{3,27},{4,28},{5,29},{6,30},{7,31},{8,16},{9,... | collective-permute-start | bytes 1572872 | tf_op jit(solution)/shard_map/ppermute | solution.py:56
  26.5 22.0 %collective-permute-start.7 = (bf16[4,8,64,128]{3,2,1,0:T(8,128)(2,1)S(1)}, bf16[4,8,64,128]{3,2,1,0:T(8,128)(2,1)S(1)}, u32[]{:S(2)}, u32[]{:S(2)}) collective-permute-start(bf16[4,8,64,128]{3,2,1,0:T(8,128)(2,1)S(1)} %bitcast.62), channel_id=1, source_target_pairs={{0,16},{1,17},{2,18},{3,19},{4,20},{5,21},{6,22},{7,23},{8,24},{9,... | collective-permute-start | bytes 1572872 | tf_op jit(solution)/shard_map/ppermute | solution.py:56
  27.0 21.7 %collective-permute-start.6 = (bf16[4,8,64,128]{3,2,1,0:T(8,128)(2,1)S(1)}, bf16[4,8,64,128]{3,2,1,0:T(8,128)(2,1)}, u32[]{:S(2)}, u32[]{:S(2)}) collective-permute-start(bf16[4,8,64,128]{3,2,1,0:T(8,128)(2,1)S(1)} %bitcast.63), channel_id=1, source_target_pairs={{0,8},{1,9},{2,10},{3,11},{4,12},{5,13},{6,14},{7,15},{8,0},{9,1},... | collective-permute-start | bytes 1572872 | tf_op jit(solution)/shard_map/ppermute | solution.py:56
  28.3 11.8 %collective-permute-start.5 = (bf16[2,2,64,512]{3,2,1,0:T(8,128)(2,1)}, bf16[2,2,64,512]{3,2,1,0:T(8,128)(2,1)}, u32[]{:S(2)}, u32[]{:S(2)}) collective-permute-start(bf16[2,2,64,512]{3,2,1,0:T(8,128)(2,1)} %pad_maximum_fusion.3), channel_id=1, source_target_pairs={{0,2},{1,3},{2,0},{3,1},{4,6},{5,7},{6,4},{7,5},{8,10},{9,11},{10,... | collective-permute-start | bytes 786440 | tf_op jit(solution)/shard_map/ppermute | solution.py:56
  50.1 4.2 %collective-permute-start.9 = (bf16[4,4,8,64,128]{4,3,2,1,0:T(8,128)(2,1)S(1)}, bf16[4,4,8,64,128]{4,3,2,1,0:T(8,128)(2,1)S(1)}, u32[]{:S(2)}, u32[]{:S(2)}) collective-permute-start(bf16[4,4,8,64,128]{4,3,2,1,0:T(8,128)(2,1)S(1)} %pad_maximum_fusion.refs_0_), channel_id=1, source_target_pairs={{0,4},{1,5},{2,6},{3,7},{4,0},{5,1},{6,2},{7,3},{8,12},{9,13},{10,... | collective-permute-start | bytes 6291464 | tf_op jit(solution)/shard_map/ppermute | solution.py:56
  50.2 18.3 %collective-permute-start.11 = (bf16[4,2,64,512]{3,2,1,0:T(8,128)(2,1)S(1)}, bf16[4,2,64,512]{3,2,1,0:T(8,128)(2,1)S(1)}, u32[]{:S(2)}, u32[]{:S(2)}) collective-permute-start(bf16[4,2,64,512]{3,2,1,0:T(8,128)(2,1)S(1)} %pad_maximum_fusion.2.refs_0_), channel_id=1, source_target_pairs={{0,8},{1,9},{2,10},{3,11},{4,12},{5,13},{6,14},{7,15},{8,0},{9,1},... | collective-permute-start | bytes 1572872 | tf_op jit(solution)/shard_map/ppermute | solution.py:56
  51.8 25.2 %collective-permute-start.12 = (bf16[4,2,64,512]{3,2,1,0:T(8,128)(2,1)S(1)}, bf16[4,2,64,512]{3,2,1,0:T(8,128)(2,1)S(1)}, u32[]{:S(2)}, u32[]{:S(2)}) collective-permute-start(bf16[4,2,64,512]{3,2,1,0:T(8,128)(2,1)S(1)} %pad_maximum_fusion.2.refs_0_), channel_id=1, source_target_pairs={{0,16},{1,17},{2,18},{3,19},{4,20},{5,21},{6,22},{7,23},{8,24},{9,... | collective-permute-start | bytes 1572872 | tf_op jit(solution)/shard_map/ppermute | solution.py:56
  52.4 24.6 %collective-permute-start.13 = (bf16[4,2,64,512]{3,2,1,0:T(8,128)(2,1)S(1)}, bf16[4,2,64,512]{3,2,1,0:T(8,128)(2,1)S(1)}, u32[]{:S(2)}, u32[]{:S(2)}) collective-permute-start(bf16[4,2,64,512]{3,2,1,0:T(8,128)(2,1)S(1)} %pad_maximum_fusion.2.refs_0_), channel_id=1, source_target_pairs={{0,24},{1,25},{2,26},{3,27},{4,28},{5,29},{6,30},{7,31},{8,16},{9,... | collective-permute-start | bytes 1572872 | tf_op jit(solution)/shard_map/ppermute | solution.py:56
  53.8 9.1 %collective-permute-start.10 = (bf16[128,512]{1,0:T(8,128)(2,1)S(1)}, bf16[128,512]{1,0:T(8,128)(2,1)S(1)}, u32[]{:S(2)}, u32[]{:S(2)}) collective-permute-start(bf16[128,512]{1,0:T(8,128)(2,1)S(1)} %copy-done.18), channel_id=1, source_target_pairs={{0,1},{1,0},{2,3},{3,2},{4,5},{5,4},{6,7},{7,6},{8,9},{9,8},{10,11... | collective-permute-start | bytes 393224 | tf_op jit(solution)/shard_map/ppermute | solution.py:56
  54.4 23.3 %collective-permute-start.14 = (bf16[4,2,64,512]{3,2,1,0:T(8,128)(2,1)S(1)}, bf16[4,2,64,512]{3,2,1,0:T(8,128)(2,1)S(1)}, u32[]{:S(2)}, u32[]{:S(2)}) collective-permute-start(bf16[4,2,64,512]{3,2,1,0:T(8,128)(2,1)S(1)} %pad_maximum_fusion.2.refs_0_), channel_id=1, source_target_pairs={{0,4},{1,5},{2,6},{3,7},{4,0},{5,1},{6,2},{7,3},{8,12},{9,13},{10,... | collective-permute-start | bytes 1572872 | tf_op jit(solution)/shard_map/ppermute | solution.py:56
  55.8 24.7 %copy-start = (bf16[8,512,512]{2,1,0:T(8,128)(2,1)}, bf16[8,512,512]{2,1,0:T(8,128)(2,1)S(1)}, u32[]{:S(2)}) copy-start(bf16[8,512,512]{2,1,0:T(8,128)(2,1)S(1)} %shard_map.477.wq.wk.wv.wo.w) | copy-start | bytes 12582916
  65.4 15.1 %copy-start.15 = (bf16[256,512]{1,0:T(8,128)(2,1)}, bf16[256,512]{1,0:T(8,128)(2,1)S(1)}, u32[]{:S(2)}) copy-start(bf16[256,512]{1,0:T(8,128)(2,1)S(1)} %get-tuple-element.160.k) | copy-start | bytes 786436
  65.4 15.1 %copy-start.16 = (bf16[256,512]{1,0:T(8,128)(2,1)}, bf16[256,512]{1,0:T(8,128)(2,1)S(1)}, u32[]{:S(2)}) copy-start(bf16[256,512]{1,0:T(8,128)(2,1)S(1)} %get-tuple-element.161.v) | copy-start | bytes 786436
  65.4 15.1 %copy-start.21 = (f32[512,1]{1,0:T(8,128)}, f32[512,1]{1,0:T(8,128)S(1)}, u32[]{:S(2)}) copy-start(f32[512,1]{1,0:T(8,128)S(1)} %get-tuple-element.189.inverse) | copy-start | bytes 6148
  65.4 15.1 %copy-start.10 = (f32[512,512]{1,0:T(8,128)}, f32[512,512]{1,0:T(8,128)S(1)}, u32[]{:S(2)}) copy-start(f32[512,512]{1,0:T(8,128)S(1)} %get-tuple-element.163.first) | copy-start | bytes 3145732
  68.5 9.2 %collective-permute-start.15 = (bf16[4,2,64,512]{3,2,1,0:T(8,128)(2,1)S(1)}, bf16[4,2,64,512]{3,2,1,0:T(8,128)(2,1)S(1)}, u32[]{:S(2)}, u32[]{:S(2)}) collective-permute-start(bf16[4,2,64,512]{3,2,1,0:T(8,128)(2,1)S(1)} %collective-permute-done.11.refs_1_), channel_id=1, source_target_pairs={{0,4},{1,5},{2,6},{3,7},{4,0},{5,1},{6,2},{7,3},{8,12},{9,13},{10,... | collective-permute-start | bytes 1572872 | tf_op jit(solution)/shard_map/ppermute | solution.py:56
  77.0 1.9 %collective-permute-start.16 = (bf16[4,2,64,512]{3,2,1,0:T(8,128)(2,1)S(1)}, bf16[4,2,64,512]{3,2,1,0:T(8,128)(2,1)S(1)}, u32[]{:S(2)}, u32[]{:S(2)}) collective-permute-start(bf16[4,2,64,512]{3,2,1,0:T(8,128)(2,1)S(1)} %collective-permute-done.12.refs_2_), channel_id=1, source_target_pairs={{0,4},{1,5},{2,6},{3,7},{4,0},{5,1},{6,2},{7,3},{8,12},{9,13},{10,... | collective-permute-start | bytes 1572872 | tf_op jit(solution)/shard_map/ppermute | solution.py:56
  77.0 2.7 %collective-permute-start.17 = (bf16[4,2,64,512]{3,2,1,0:T(8,128)(2,1)S(1)}, bf16[4,2,64,512]{3,2,1,0:T(8,128)(2,1)S(1)}, u32[]{:S(2)}, u32[]{:S(2)}) collective-permute-start(bf16[4,2,64,512]{3,2,1,0:T(8,128)(2,1)S(1)} %collective-permute-done.13.refs_3_), channel_id=1, source_target_pairs={{0,4},{1,5},{2,6},{3,7},{4,0},{5,1},{6,2},{7,3},{8,12},{9,13},{10,... | collective-permute-start | bytes 1572872 | tf_op jit(solution)/shard_map/ppermute | solution.py:56
  91.7 4.2 %collective-permute-start.18 = (bf16[2048,512]{1,0:T(8,128)(2,1)S(1)}, bf16[2048,512]{1,0:T(8,128)(2,1)S(1)}, u32[]{:S(2)}, u32[]{:S(2)}) collective-permute-start(bf16[2048,512]{1,0:T(8,128)(2,1)S(1)} %get-tuple-element.179), channel_id=1, source_target_pairs={{0,4},{1,5},{2,6},{3,7},{4,0},{5,1},{6,2},{7,3},{8,12},{9,13},{10,... | collective-permute-start | bytes 6291464 | tf_op jit(solution)/shard_map/ppermute | solution.py:56
  96.3 15.2 %collective-permute-start.19 = (bf16[512,512]{1,0:T(8,128)(2,1)S(1)}, bf16[512,512]{1,0:T(8,128)(2,1)S(1)}, u32[]{:S(2)}, u32[]{:S(2)}) collective-permute-start(bf16[512,512]{1,0:T(8,128)(2,1)S(1)} %get-tuple-element.195), channel_id=1, source_target_pairs={{0,8},{1,9},{2,10},{3,11},{4,12},{5,13},{6,14},{7,15},{8,0},{9,1},... | collective-permute-start | bytes 1572872 | tf_op jit(solution)/shard_map/ppermute | solution.py:56
  96.9 14.6 %collective-permute-start.20 = (bf16[512,512]{1,0:T(8,128)(2,1)S(1)}, bf16[512,512]{1,0:T(8,128)(2,1)S(1)}, u32[]{:S(2)}, u32[]{:S(2)}) collective-permute-start(bf16[512,512]{1,0:T(8,128)(2,1)S(1)} %get-tuple-element.196.refs_4_), channel_id=1, source_target_pairs={{0,16},{1,17},{2,18},{3,19},{4,20},{5,21},{6,22},{7,23},{8,24},{9,... | collective-permute-start | bytes 1572872 | tf_op jit(solution)/shard_map/ppermute | solution.py:56
  111.8 9.3 %collective-permute-start.23 = (bf16[5184,128]{1,0:T(8,128)(2,1)S(1)}, bf16[5184,128]{1,0:T(8,128)(2,1)S(1)}, u32[]{:S(2)}, u32[]{:S(2)}) collective-permute-start(bf16[5184,128]{1,0:T(8,128)(2,1)S(1)} %get-tuple-element.210), channel_id=1, source_target_pairs={{0,4},{1,5},{2,6},{3,7},{4,0},{5,1},{6,2},{7,3},{8,12},{9,13},{10,... | collective-permute-start | bytes 3981320 | tf_op jit(solution)/shard_map/ppermute | solution.py:56
  111.9 8.7 %collective-permute-start.21 = (bf16[256,512]{1,0:T(8,128)(2,1)S(1)}, bf16[256,512]{1,0:T(8,128)(2,1)S(1)}, u32[]{:S(2)}, u32[]{:S(2)}) collective-permute-start(bf16[256,512]{1,0:T(8,128)(2,1)S(1)} %get-tuple-element.205), channel_id=1, source_target_pairs={{0,16},{1,17},{2,18},{3,19},{4,20},{5,21},{6,22},{7,23},{8,24},{9,... | collective-permute-start | bytes 786440 | tf_op jit(solution)/shard_map/ppermute | solution.py:56
  112.6 8.4 %collective-permute-start.22 = (bf16[256,512]{1,0:T(8,128)(2,1)S(1)}, bf16[256,512]{1,0:T(8,128)(2,1)S(1)}, u32[]{:S(2)}, u32[]{:S(2)}) collective-permute-start(bf16[256,512]{1,0:T(8,128)(2,1)S(1)} %get-tuple-element.206.refs_4_), channel_id=1, source_target_pairs={{0,8},{1,9},{2,10},{3,11},{4,12},{5,13},{6,14},{7,15},{8,0},{9,1},... | collective-permute-start | bytes 786440 | tf_op jit(solution)/shard_map/ppermute | solution.py:56
  121.4 10.4 %collective-permute-start.24 = (bf16[1536,128]{1,0:T(8,128)(2,1)S(1)}, bf16[1536,128]{1,0:T(8,128)(2,1)S(1)}, u32[]{:S(2)}, u32[]{:S(2)}) collective-permute-start(bf16[1536,128]{1,0:T(8,128)(2,1)S(1)} %get-tuple-element.216), channel_id=1, source_target_pairs={{0,8},{1,9},{2,10},{3,11},{4,12},{5,13},{6,14},{7,15},{8,0},{9,1},... | collective-permute-start | bytes 1179656 | tf_op jit(solution)/shard_map/ppermute | solution.py:56
  122.9 7.8 %collective-permute-start.25 = (bf16[1088,128]{1,0:T(8,128)(2,1)S(1)}, bf16[1088,128]{1,0:T(8,128)(2,1)S(1)}, u32[]{:S(2)}, u32[]{:S(2)}) collective-permute-start(bf16[1088,128]{1,0:T(8,128)(2,1)S(1)} %get-tuple-element.217.refs_4_), channel_id=1, source_target_pairs={{0,16},{1,17},{2,18},{3,19},{4,20},{5,21},{6,22},{7,23},{8,24},{9,... | collective-permute-start | bytes 835592 | tf_op jit(solution)/shard_map/ppermute | solution.py:56
  123.6 13.7 %collective-permute-start.28 = (bf16[256,512]{1,0:T(8,128)(2,1)S(1)}, bf16[256,512]{1,0:T(8,128)(2,1)S(1)}, u32[]{:S(2)}, u32[]{:S(2)}) collective-permute-start(bf16[256,512]{1,0:T(8,128)(2,1)S(1)} %get-tuple-element.231.refs_2_), channel_id=1, source_target_pairs={{0,2},{1,3},{2,0},{3,1},{4,6},{5,7},{6,4},{7,5},{8,10},{9,11},{10,... | collective-permute-start | bytes 786440 | tf_op jit(solution)/shard_map/ppermute | solution.py:56
  132.0 6.6 %collective-permute-start.26 = (bf16[768,128]{1,0:T(8,128)(2,1)S(1)}, bf16[768,128]{1,0:T(8,128)(2,1)S(1)}, u32[]{:S(2)}, u32[]{:S(2)}) collective-permute-start(bf16[768,128]{1,0:T(8,128)(2,1)S(1)} %get-tuple-element.229), channel_id=1, source_target_pairs={{0,16},{1,17},{2,18},{3,19},{4,20},{5,21},{6,22},{7,23},{8,24},{9,... | collective-permute-start | bytes 589832 | tf_op jit(solution)/shard_map/ppermute | solution.py:56
  133.4 5.1 %collective-permute-start.27 = (bf16[576,128]{1,0:T(8,128)(2,1)S(1)}, bf16[576,128]{1,0:T(8,128)(2,1)S(1)}, u32[]{:S(2)}, u32[]{:S(2)}) collective-permute-start(bf16[576,128]{1,0:T(8,128)(2,1)S(1)} %get-tuple-element.230.refs_4_), channel_id=1, source_target_pairs={{0,8},{1,9},{2,10},{3,11},{4,12},{5,13},{6,14},{7,15},{8,0},{9,1},... | collective-permute-start | bytes 442376 | tf_op jit(solution)/shard_map/ppermute | solution.py:56
  138.6 2.3 %collective-permute-start.30 = (bf16[3088,128]{1,0:T(8,128)(2,1)S(1)}, bf16[3088,128]{1,0:T(8,128)(2,1)S(1)}, u32[]{:S(2)}, u32[]{:S(2)}) collective-permute-start(bf16[3088,128]{1,0:T(8,128)(2,1)S(1)} %get-tuple-element.232), channel_id=1, source_target_pairs={{0,4},{1,5},{2,6},{3,7},{4,0},{5,1},{6,2},{7,3},{8,12},{9,13},{10,... | collective-permute-start | bytes 2371592 | tf_op jit(solution)/shard_map/ppermute | solution.py:56
  138.6 20.1 %collective-permute-start.29 = (bf16[512,512]{1,0:T(8,128)(2,1)S(1)}, bf16[512,512]{1,0:T(8,128)(2,1)S(1)}, u32[]{:S(2)}, u32[]{:S(2)}) collective-permute-start(bf16[512,512]{1,0:T(8,128)(2,1)S(1)} %get-tuple-element.233), channel_id=1, source_target_pairs={{1,0},{3,2},{5,4},{7,6},{9,8},{11,10},{13,12},{15,14},{17,16},{19,... | collective-permute-start | bytes 1572872 | tf_op jit(solution)/shard_map/ppermute | solution.py:62
  141.0 17.6 %collective-permute-start.32 = (bf16[784,128]{1,0:T(8,128)(2,1)S(1)}, bf16[784,128]{1,0:T(8,128)(2,1)S(1)}, u32[]{:S(2)}, u32[]{:S(2)}) collective-permute-start(bf16[784,128]{1,0:T(8,128)(2,1)S(1)} %get-tuple-element.242), channel_id=1, source_target_pairs={{0,8},{1,9},{2,10},{3,11},{4,12},{5,13},{6,14},{7,15},{8,0},{9,1},... | collective-permute-start | bytes 602120 | tf_op jit(solution)/shard_map/ppermute | solution.py:56
  141.9 16.8 %collective-permute-start.33 = (bf16[784,128]{1,0:T(8,128)(2,1)S(1)}, bf16[784,128]{1,0:T(8,128)(2,1)S(1)}, u32[]{:S(2)}, u32[]{:S(2)}) collective-permute-start(bf16[784,128]{1,0:T(8,128)(2,1)S(1)} %get-tuple-element.243), channel_id=1, source_target_pairs={{0,16},{1,17},{2,18},{3,19},{4,20},{5,21},{6,22},{7,23},{8,24},{9,... | collective-permute-start | bytes 602120 | tf_op jit(solution)/shard_map/ppermute | solution.py:56
  143.2 15.4 %collective-permute-start.34 = (bf16[784,128]{1,0:T(8,128)(2,1)S(1)}, bf16[784,128]{1,0:T(8,128)(2,1)S(1)}, u32[]{:S(2)}, u32[]{:S(2)}) collective-permute-start(bf16[784,128]{1,0:T(8,128)(2,1)S(1)} %get-tuple-element.244), channel_id=1, source_target_pairs={{0,24},{1,25},{2,26},{3,27},{4,28},{5,29},{6,30},{7,31},{8,16},{9,... | collective-permute-start | bytes 602120 | tf_op jit(solution)/shard_map/ppermute | solution.py:56
  144.6 6.8 %collective-permute-start.31 = (bf16[704,128]{1,0:T(8,128)(2,1)S(1)}, bf16[704,128]{1,0:T(8,128)(2,1)S(1)}, u32[]{:S(2)}, u32[]{:S(2)}) collective-permute-start(bf16[704,128]{1,0:T(8,128)(2,1)S(1)} %get-tuple-element.240.refs_2_), channel_id=1, source_target_pairs={{0,2},{1,3},{2,0},{3,1},{4,6},{5,7},{6,4},{7,5},{8,10},{9,11},{10,... | collective-permute-start | bytes 540680 | tf_op jit(solution)/shard_map/ppermute | solution.py:56
  159.4 10.4 %collective-permute-start.35 = (bf16[256,512]{1,0:T(8,128)(2,1)S(1)}, bf16[256,512]{1,0:T(8,128)(2,1)S(1)}, u32[]{:S(2)}, u32[]{:S(2)}) collective-permute-start(bf16[256,512]{1,0:T(8,128)(2,1)S(1)} %get-tuple-element.248), channel_id=1, source_target_pairs={{0,1},{1,0},{2,3},{3,2},{4,5},{5,4},{6,7},{7,6},{8,9},{9,8},{10,11... | collective-permute-start | bytes 786440 | tf_op jit(solution)/shard_map/ppermute | solution.py:56
  161.1 11.9 %collective-permute-start.36 = (bf16[384,128]{1,0:T(8,128)(2,1)S(1)}, bf16[384,128]{1,0:T(8,128)(2,1)S(1)}, u32[]{:S(2)}, u32[]{:S(2)}) collective-permute-start(bf16[384,128]{1,0:T(8,128)(2,1)S(1)} %get-tuple-element.251.refs_2_), channel_id=1, source_target_pairs={{0,1},{1,0},{2,3},{3,2},{4,5},{5,4},{6,7},{7,6},{8,9},{9,8},{10,11... | collective-permute-start | bytes 294920 | tf_op jit(solution)/shard_map/ppermute | solution.py:56
  161.6 11.3 %collective-permute-start.37 = (bf16[208,128]{1,0:T(8,128)(2,1)}, bf16[208,128]{1,0:T(8,128)(2,1)S(1)}, u32[]{:S(2)}, u32[]{:S(2)}) collective-permute-start(bf16[208,128]{1,0:T(8,128)(2,1)} %get-tuple-element.255), channel_id=1, source_target_pairs={{0,1},{1,0},{2,3},{3,2},{4,5},{5,4},{6,7},{7,6},{8,9},{9,8},{10,11... | collective-permute-start | bytes 159752 | tf_op jit(solution)/shard_map/ppermute | solution.py:56
  163.2 9.8 %collective-permute-start.38 = (bf16[208,128]{1,0:T(8,128)(2,1)}, bf16[208,128]{1,0:T(8,128)(2,1)S(1)}, u32[]{:S(2)}, u32[]{:S(2)}) collective-permute-start(bf16[208,128]{1,0:T(8,128)(2,1)} %get-tuple-element.256), channel_id=1, source_target_pairs={{0,2},{1,3},{2,0},{3,1},{4,6},{5,7},{6,4},{7,5},{8,10},{9,11},{10,... | collective-permute-start | bytes 159752 | tf_op jit(solution)/shard_map/ppermute | solution.py:56
  163.2 9.8 %collective-permute-start.39 = (bf16[208,128]{1,0:T(8,128)(2,1)}, bf16[208,128]{1,0:T(8,128)(2,1)S(1)}, u32[]{:S(2)}, u32[]{:S(2)}) collective-permute-start(bf16[208,128]{1,0:T(8,128)(2,1)} %get-tuple-element.257), channel_id=1, source_target_pairs={{0,3},{1,2},{2,1},{3,0},{4,7},{5,6},{6,5},{7,4},{8,11},{9,10},{10,... | collective-permute-start | bytes 159752 | tf_op jit(solution)/shard_map/ppermute | solution.py:56
  (28 other events, 216.0 us)

commit v5 on v4

--- a/solution.py
+++ b/solution.py
@@ -36,6 +36,10 @@
     return jax.ShapeDtypeStruct(shape, dtype)
 
 
+def shaped_far(shape, dtype):
+    return pltpu.HBM(shape, dtype)
+
+
 def cost(macs, moved):
     return pl.CostEstimate(flops=macs // 64, bytes_accessed=moved // 64, transcendentals=0)
 
@@ -74,13 +78,18 @@
     return line
 
 
-def over_planes(line):
-    return [line] + [swap(line, 2 * j, 0) for j in range(1, lax.axis_size("dp") // 2)]
-
-
-def both_cores(planes, *others):
-    plane = jnp.stack([after(planes[0], *others)] + planes[1:])
-    return plane, swap(plane, 1, 0)
+def plane_bits(group):
+    bits = [1 << i for i in range((lax.axis_size("dp") // 2).bit_length() - 1)]
+    return bits if group % 2 == 0 else bits[::-1]
+
+
+def grown(slots, pieces, bit):
+    return [j | bit for j in slots], swap(pieces, 2 * bit, 0)
+
+
+def merged(held):
+    (slots, pieces), (more_slots, more) = held
+    return slots + more_slots, jnp.concatenate([pieces, more])
 
 
 class Halves:
@@ -137,6 +146,40 @@
         compiler_params=limit(20),
         cost_estimate=cost(0, 2 * moved),
     )(*arrays)
+
+
+def finish_kernel(info, *refs, plans, count, nt):
+    outs = refs[count:-2]
+    early, late = refs[-2:]
+    w = early.shape[1]
+    add_rows_kernel(*refs[:count], *outs[:-3], early, late, plans=plans, count=count)
+    rows, mine, hidden = outs[-3:]
+    for q in range(nt):
+        lanes = slice(q * w, q * w + w)
+        rows[:, lanes] = early[16 * q : 16 * q + 16, :]
+    for k in range(4):
+        block = 4 * info[3] + k
+        at = 16 * lax.rem(block, nt) + 11 + lax.div(block, nt)
+        hidden[:, k * w : k * w + w] = early[pl.ds(at, 1), :]
+    for i, (source, at) in enumerate(
+        ((early, 16 * info[3] + 9), (early, 16 * info[3] + 10), (late, info[3]), (late, nt + info[3]))
+    ):
+        mine[i : i + 1, :] = source[pl.ds(at, 1), :]
+
+
+def finish(info, arrays, plans, nt, width):
+    w = arrays[0].shape[1]
+    sizes = [sum(n for n, _ in plan) for plan in plans]
+    shapes = [(n, w) for n in sizes[:-2]] + [(16, width), (4, w), (1, 4 * w)]
+    return pl.pallas_call(
+        functools.partial(finish_kernel, plans=plans, count=len(arrays), nt=nt),
+        out_shape=tuple(shaped(shape, F32) for shape in shapes),
+        in_specs=[SMEM] + [VMEM] * len(arrays),
+        out_specs=(VMEM,) * len(shapes),
+        scratch_shapes=[pltpu.VMEM((n, w), F32) for n in sizes[-2:]],
+        compiler_params=limit(20),
+        cost_estimate=cost(0, 16 * w * sum(sizes)),
+    )(info, *arrays)
 
 
 def halve(halves, arrays, held, rider, index):
@@ -176,47 +219,48 @@
     return lax.optimization_barrier((array,) + others)[0]
 
 
-def slot_blocks(info, planes, nt):
-    for j in range(planes):
-        for c in range(2):
-            d = jnp.bitwise_xor(info[2], 2 * j + c)
-            for s in range(nt):
-                yield j, c, s, d, jnp.bitwise_xor(info[3], s)
-
-
 def aligned(r, w):
     return w % PAIR == 0 and r % 16 == 0
 
 
-def assemble_kernel(info, *refs, planes):
+def assemble_kernel(info, *refs, entries):
     whole = refs[-1]
-    nt, n, r, w = refs[0].shape[-4:]
-    for j, c, s, d, t in slot_blocks(info, planes, nt):
-        rows = pl.ds(pl.multiple_of(d * r, r), r)
-        columns = pl.ds(pl.multiple_of(t * w, w), w)
-        piece = refs[c].at[j] if len(refs) == 3 else refs[c * planes + j]
-        for i in range(n):
-            whole[i, rows, columns] = piece[s, i]
-
-
-def assemble(info, halves):
-    nt, n, r, w = halves[0].shape[-4:]
-    planes = lax.axis_size("dp") // 2
-    nd = 2 * planes
+    for piece, (core, slots, first) in zip(refs, entries):
+        _, nt, n, r, w = piece.shape
+        for k, j in enumerate(slots):
+            d = jnp.bitwise_xor(info[2], 2 * j + core)
+            rows = pl.ds(pl.multiple_of(d * r, r), r)
+            for s in range(nt):
+                t = jnp.bitwise_xor(info[3], s)
+                columns = pl.ds(pl.multiple_of(t * w, w), w)
+                for i in range(n):
+                    whole[first + i, rows, columns] = piece[k, s, i]
+
+
+def assemble(info, arrays, entries):
+    _, nt, _, r, w = arrays[0].shape
+    nd = lax.axis_size("dp")
+    count = max(entry[2] + array.shape[2] for array, entry in zip(arrays, entries))
     if aligned(r, w):
         return pl.pallas_call(
-            functools.partial(assemble_kernel, planes=planes),
-            out_shape=shaped((n, nd * r, nt * w), BF16),
-            in_specs=[SMEM] + [VMEM] * len(halves),
+            functools.partial(assemble_kernel, entries=entries),
+            out_shape=shaped((count, nd * r, nt * w), BF16),
+            in_specs=[SMEM] + [VMEM] * len(arrays),
             out_specs=VMEM,
             compiler_params=limit(18),
-            cost_estimate=cost(0, 8 * nd * nt * n * r * w),
-        )(info, *halves)
-    full = jnp.stack(halves).reshape(2, planes, nt, n, r, w).swapaxes(0, 1)
-    full = full.reshape(nd, nt, n, r, w)
-    full = jnp.take(full, jnp.bitwise_xor(jnp.arange(nd), info[2]), axis=0)
-    full = jnp.take(full, jnp.bitwise_xor(jnp.arange(nt), info[3]), axis=1)
-    return full.transpose(2, 0, 3, 1, 4).reshape(n, nd * r, nt * w)
+            cost_estimate=cost(0, 4 * count * nd * r * nt * w),
+        )(info, *arrays)
+    wholes = []
+    for first in sorted({entry[2] for entry in entries}):
+        found = {}
+        for array, (core, slots, at) in zip(arrays, entries):
+            if at == first:
+                found.update({2 * j + core: array[k] for k, j in enumerate(slots)})
+        full = jnp.stack([found[d] for d in range(nd)])
+        full = jnp.take(full, jnp.bitwise_xor(jnp.arange(nd), info[2]), axis=0)
+        full = jnp.take(full, jnp.bitwise_xor(jnp.arange(nt), info[3]), axis=1)
+        wholes.append(full.transpose(2, 0, 3, 1, 4).reshape(-1, nd * r, nt * w))
+    return jnp.concatenate(wholes)
 
 
 def disperse(info, halves, scratch, i, t, s, keep, send):
@@ -500,7 +544,7 @@
     return pl.pallas_call(
         self_forward_kernel,
         grid=(width // PAIR,),
-        out_shape=(shaped((tokens, width), BF16), shaped((tokens, width), F32)),
+        out_shape=(shaped((tokens, width), BF16), shaped_far((tokens, width), F32)),
         in_specs=[SMEM] + [row] * 5,
         out_specs=(row, row),
         compiler_params=limit(16),
@@ -530,7 +574,7 @@
     return pl.pallas_call(
         cross_forward_kernel,
         grid=(width // PAIR,),
-        out_shape=(shaped((tokens, width), BF16), shaped((tokens, width), F32)),
+        out_shape=(shaped((tokens, width), BF16), shaped_far((tokens, width), F32)),
         in_specs=[lanes_of(tokens), lanes_of(rows), lanes_of(rows)],
         out_specs=(lanes_of(tokens), lanes_of(tokens)),
         compiler_params=limit(16),
@@ -606,8 +650,8 @@
         grid=(1,),
         out_shape=(
             full,
-            full,
-            shaped((tokens, 1), F32),
+            shaped_far(x.shape, F32),
+            shaped_far((tokens, 1), F32),
             shaped(x.shape, BF16),
             shaped((rows, width), BF16),
             shaped((rows, width), BF16),
@@ -842,7 +886,7 @@
         functools.partial(middle_kernel, halves=halves if direct else None),
         grid=(1,),
         out_shape=(
-            shaped(first.shape, F32),
+            shaped_far(first.shape, F32),
             shaped(first.shape, BF16),
             shaped((rows, width), F32),
             shaped((rows, width), BF16),
@@ -1013,20 +1057,42 @@
 
     bits = [1 << i for i in range(nt.bit_length() - 1)]
     swapped = [swap(packed, 0, k) for k in range(1, nt)]
-    line = jnp.stack([packed] + swapped)
-    count = 8 * self_query.shape[0]
-    riders = line[:, count:]
-    line = line[:, :count].reshape((nt, 8) + self_query.shape)
-    line_feed = doubled(after(feed_shard, line)[None], bits)
-    inputs_other = hand_over(after(inputs, line), 0, 1)
+    parts = [packed] + swapped
+    size = 4 * self_query.shape[0]
+    shape = (1, nt, 4) + self_query.shape
+    lines = [
+        jnp.stack([part[g * size : g * size + size] for part in parts]).reshape(shape)
+        for g in range(2)
+    ]
+    riders = jnp.stack([part[2 * size :] for part in parts])
+    rounds = len(plane_bits(0))
+    line_feed = doubled(after(feed_shard, lines[0])[None], bits[:1])
+    held = [([0], line) for line in lines]
+    for index in range(rounds):
+        more = [grown(*held[g], plane_bits(g)[index]) for g in range(2)]
+        if index < rounds - 1:
+            held = [merged([held[g], more[g]]) for g in range(2)]
+    inputs_other = hand_over(after(inputs, line_feed), 0, 1)
+    line_feed = doubled(line_feed, bits[1:])
     head_biases, hidden_bias = spread(info, riders)
-    group = both_cores(over_planes(line), inputs_other, line_feed, head_biases)
-    line_feed = after(line_feed, group[0])
-    memory_other = swap(after(memory, group[0]), 0, 1)
-    planes_feed = over_planes(line_feed)
-
-    weights = assemble(info, group)
+    more[0] = more[0][0], after(more[0][1], inputs_other, line_feed, head_biases)
+    arrays, entries = [], []
+    for g in range(2):
+        for slots, pieces in (held[g], more[g]):
+            arrays += [pieces, swap(pieces, 1, 0)]
+            entries += [(0, tuple(slots), 4 * g), (1, tuple(slots), 4 * g)]
+    weights = assemble(info, arrays, entries)
+
+    line_feed = after(line_feed, more[0][1], more[1][1])
+    memory_other = swap(after(memory, line_feed), 0, 1)
+    held = [([0], line_feed[None, :, g : g + 1]) for g in range(2)]
     q1, k1, v1, k1o, v1o = project_self(info, inputs, inputs_other, weights, head_biases)
+    for index in range(rounds):
+        more = [grown(*held[g], plane_bits(g)[index]) for g in range(2)]
+        if index < rounds - 1:
+            held = [(slots, after(pieces, q1)) for slots, pieces in held]
+            held = [merged([held[g], more[g]]) for g in range(2)]
+    q1 = after(q1, held[0][1], held[1][1])
     ctx1, log1 = self_forward(info, q1, k1, v1, k1o, v1o)
     first, normed1, inverse1, q2, k2, v2 = first_norm(
         ctx1,
@@ -1040,8 +1106,14 @@
         head_biases,
     )
     ctx2, log2 = cross_forward(q2, k2, v2)
-    own = [planes_feed[0]] + [after(piece, ctx2) for piece in planes_feed[1:]]
-    w_feed = assemble(info, planes_feed + [swap(piece, 1, 0) for piece in own])
+    more[0] = more[0][0], after(more[0][1], ctx2)
+    more[1] = more[1][0], after(more[1][1], ctx2)
+    arrays, entries = [], []
+    for g in range(2):
+        for slots, pieces in (held[g], more[g]):
+            arrays += [pieces, swap(pieces, 1, 0)]
+            entries += [(0, tuple(slots), g), (1, tuple(slots), g)]
+    w_feed = assemble(info, arrays, entries)
     feed_halves = Halves((1, 1), width // nd, 0)
     outputs, keep, send, du3, dhidden, normed2, inverse2, sums_feed, sums_hidden = feed(
         info,
@@ -1145,50 +1217,45 @@
     else:
         memory_got = swap(after(memory_back, lines[0]), 0, 1)
     grad_memory = memory_own + memory_got.astype(F32)
+    du1 = after(du1, arrays[0], lines[0], feed_arrays[0])
     grad_inputs = input_grads(du1, grads_early[:3], grads_late[:3], weights, inputs_got)
-    lines[0] = after(lines[0], grad_inputs, grad_feed_in)
+    lines[0] = after(lines[0], grad_inputs, grad_feed_in, grad_memory)
     plans = [
         [(block, [(array, lo + i * block) for array, lo in terms])]
         for count, (_, terms) in zip(middle_halves.groups, segments)
         for i in range(count)
     ]
-    plans.append([rider])
     cuts = [(i * block, block) for i in range(3)] + [(rows, self_halves.rider)]
-    plans += [[(n, [(3 + k, lo) for k in range(nt)])] for lo, n in cuts]
-    sums = add_rows(arrays + lines, plans, F32)
-    grad_middle, early = sums[:5], sums[5]
-    grad_self, late_sums = sums[6:9], sums[9]
-    early = early.reshape(nt, 16, columns).transpose(1, 0, 2).reshape(16, width)
-    late_sums = late_sums[: 2 * nt].reshape(2, width)
-
-    def mine(vector):
-        count = vector.shape[0] // nt
-        return lax.dynamic_slice_in_dim(vector, me_t * count, count)
+    cuts = [[(n, [(3 + k, lo) for k in range(nt)])] for lo, n in cuts]
+    plans = plans + cuts[:3] + [[rider], cuts[3]]
+    sums = finish(info, arrays + lines, plans, nt, width)
+    grad_middle, grad_self = sums[:5], sums[5:8]
+    early, mine, hidden_mine = sums[8:]
 
     return (
         outputs,
         grad_inputs,
         grad_memory,
         grad_self[0],
-        mine(late_sums[0]),
+        mine[2],
         grad_self[1],
         grad_self[2],
-        mine(late_sums[1]),
+        mine[3],
         grad_middle[0].T,
         early[0],
         early[1],
         early[2],
         grad_middle[1],
-        mine(early[9]),
+        mine[0],
         grad_middle[2],
         grad_middle[3],
-        mine(early[10]),
+        mine[1],
         grad_middle[4].T,
         early[3],
         early[4],
         early[5],
         grad_feed_in,
-        mine(early[11:15].reshape(-1)),
+        hidden_mine[0],
         grad_feed_out.T,
         early[6],
         early[7],

time: 179 us -> 173 us (0.966)
  waiting for transfers between devices: 57.2 us -> 45.2 us
  starting transfers between devices: 41.7 us -> 48.5 us
  Pallas kernels: 63.8 us -> 66.2 us
  other arithmetic: 6.86 us -> 4.75 us
    ppermute x38 -> x43, waiting for transfers between devices: 49.9 us -> 34.1 us  [swap(): return lax.ppermute(array, ('dp', 'tensor'), pairs)]
    ppermute x38 -> x43, starting transfers between devices: 36.5 us -> 45.1 us  [swap(): return lax.ppermute(array, ('dp', 'tensor'), pairs)]
    ppermute x2, waiting for transfers between devices: 7.29 us -> 11.1 us  [hand_over(): return lax.ppermute(array, ('dp', 'tensor'), pairs)]
    dynamic_slice x5 -> x0, local copies, waits for them, and re-layouts: 2.99 us -> none  [mine(): return lax.dynamic_slice_in_dim(vector, me_t * count, count)]
    another operation x0 -> x4, local copies, waits for them, and re-layouts: none -> 2.1 us  [on_device(): riders = jnp.stack([part[2 * size:] for part in parts])]
    pallas_call x3 -> x4, Pallas kernels: 3.47 us -> 5.53 us  [the longest x1 2.19 us: first_norm(): pl.pallas_call(first_norm_kernel, grid=(1,), out_shape=(full, shaped_far(...]
    ppermute x2, starting transfers between devices: 5.21 us -> 3.34 us  [hand_over(): return lax.ppermute(array, ('dp', 'tensor'), pairs)]
    pallas_call x12 -> x11, Pallas kernels: 3.81 us -> 2.5 us  [add_rows(): pl.pallas_call(functools.partial(add_rows_kernel, plans=plans, count=len(...]
  transfers between devices with their start and end apart: 40 -> 45, of which waited for: 19 -> 16; matrix products, arithmetic and copies ran while one was open for 2% -> 5% of each run, Pallas kernels for 27% -> 29%
where the time goes in v5:
time: 173 us
  Pallas kernels  66.2 us (38%)
  starting transfers between devices  48.5 us (28%)
  waiting for transfers between devices  45.2 us (26%)
  local copies, waits for them, and re-layouts  5.85 us (3%)
  other arithmetic  4.75 us (3%)
  between operations  2.12 us (1%)
    ppermute x43, starting transfers between devices, swap(): return lax.ppermute(array, ('dp', 'tensor'), pairs)  45.1 us
    ppermute x43, waiting for transfers between devices, swap(): return lax.ppermute(array, ('dp', 'tensor'), pairs)  34.1 us
    pallas_call x2, Pallas kernels, self_backward(): pl.pallas_call(self_backward_kernel, grid=(pairs,), out_shape=(out,) * 5,...  11.7 us
    ppermute x2, waiting for transfers between devices, hand_over(): return lax.ppermute(array, ('dp', 'tensor'), pairs)  11.1 us
    pallas_call x1, Pallas kernels, feed(): pl.pallas_call(functools.partial(feed_kernel, halves=halves), grid=(1,),...  10.8 us
    pallas_call x1, Pallas kernels, middle(): pl.pallas_call(functools.partial(middle_kernel, halves=halves if direct e...  6.6 us
    pallas_call x1, Pallas kernels, cross_backward(): pl.pallas_call(cross_backward_kernel, grid=(width // PAIR,), out_shape=(s...  6.49 us
    pallas_call x1, Pallas kernels, self_forward(): pl.pallas_call(self_forward_kernel, grid=(width // PAIR,), out_shape=(sha...  5.92 us
  transfers between devices with their start and end apart: 45, of which 16 were waited for; matrix products, arithmetic and copies ran while one was open for 5% of the time, Pallas kernels for 29%

profile of v5, /device:TPU:0, one launch (start us, length us, event | category | flops | bytes accessed | tf_op | source)
XLA Modules:
  0.0 172.6 jit_solution(1105809112538561539)
XLA Ops:
  0.7 1.6 shard_map.475
  2.3 5.0 %collective-permute-start.2 = (bf16[528,128]{1,0:T(8,128)(2,1)}, bf16[528,128]{1,0:T(8,128)(2,1)S(1)}, u32[]{:S(2)}, u32[]{:S(2)}) collective-permute-start(bf16[528,128]{1,0:T(8,128)(2,1)} %shard_map.475), channel_id=1, source_target_pairs={{0,3},{1,2},{2,1},{3,0},{4,7},{5,6},{6,5},{7,4},{8,11},{9,10},{10,... | collective-permute-start | bytes 405512 | tf_op jit(solution)/shard_map/ppermute | solution.py:60
  9.5 1.2 dynamic_slice.4
  12.9 6.0 %collective-permute-done.1 = bf16[528,128]{1,0:T(8,128)(2,1)S(1)} collective-permute-done((bf16[528,128]{1,0:T(8,128)(2,1)}, bf16[528,128]{1,0:T(8,128)(2,1)S(1)}, u32[]{:S(2)}, u32[]{:S(2)}) %collective-permute-start.1) | collective-permute-done | bytes 135200 | tf_op jit(solution)/shard_map/ppermute | solution.py:60
  19.1 1.6 collective-permute-start.5
  20.7 1.6 collective-permute-start.10
  22.2 3.3 %collective-permute-done.3 = bf16[1,2,64,512]{3,2,0,1:T(8,128)(2,1)S(1)} collective-permute-done((bf16[1,2,64,512]{3,2,0,1:T(8,128)(2,1)S(1)}, bf16[1,2,64,512]{3,2,0,1:T(8,128)(2,1)S(1)}, u32[]{:S(2)}, u32[]{:S(2)}) %collective-permute-start.3) | collective-permute-done | bytes 131104 | tf_op jit(solution)/shard_map/ppermute | solution.py:60
  26.3 2.1 %collective-permute-start.4 = (bf16[512,512]{1,0:T(8,128)(2,1)S(1)}, bf16[512,512]{1,0:T(8,128)(2,1)S(1)}, u32[]{:S(2)}, u32[]{:S(2)}) collective-permute-start(bf16[512,512]{1,0:T(8,128)(2,1)S(1)} %copy-done.8), channel_id=1, source_target_pairs={{0,1},{2,3},{4,5},{6,7},{8,9},{10,11},{12,13},{14,15},{16,17},{18,... | collective-permute-start | bytes 1572872 | tf_op jit(solution)/shard_map/ppermute | solution.py:66
  28.5 1.6 collective-permute-start.7
  31.4 3.0 %collective-permute-start.8 = (bf16[2,2,64,512]{3,2,0,1:T(8,128)(2,1)}, bf16[2,2,64,512]{3,2,0,1:T(8,128)(2,1)}, u32[]{:S(2)}, u32[]{:S(2)}) collective-permute-start(bf16[2,2,64,512]{3,2,0,1:T(8,128)(2,1)} %pad_maximum_fusion.4), channel_id=1, source_target_pairs={{0,2},{1,3},{2,0},{3,1},{4,6},{5,7},{6,4},{7,5},{8,10},{9,11},{10,... | collective-permute-start | bytes 786440 | tf_op jit(solution)/shard_map/ppermute | solution.py:60
  35.8 1.4 shard_map.476
  37.1 6.6 %collective-permute-done.8 = bf16[2,2,64,512]{3,2,0,1:T(8,128)(2,1)} collective-permute-done((bf16[2,2,64,512]{3,2,0,1:T(8,128)(2,1)}, bf16[2,2,64,512]{3,2,0,1:T(8,128)(2,1)}, u32[]{:S(2)}, u32[]{:S(2)}) %collective-permute-start.8) | collective-permute-done | bytes 262176 | tf_op jit(solution)/shard_map/ppermute | solution.py:60
  43.7 1.0 pad_maximum_fusion.1
  45.4 1.6 collective-permute-start.15
  47.6 1.3 shard_map.477.wq.wk.wv.wo.w
  48.9 1.5 shard_map.478
  50.6 3.6 %collective-permute-done.15 = bf16[1,4,1,64,512]{4,3,2,1,0:T(8,128)(2,1)S(1)} collective-permute-done((bf16[1,4,1,64,512]{4,3,2,1,0:T(8,128)(2,1)S(1)}, bf16[1,4,1,64,512]{4,3,2,1,0:T(8,128)(2,1)S(1)}, u32[]{:S(2)}, u32[]{:S(2)}) %collective-permute-start.15) | collective-permute-done | bytes 262176 | tf_op jit(solution)/shard_map/ppermute | solution.py:60
  55.4 1.0 collective-permute-start.18
  57.1 5.9 %shard_map.479 = (bf16[512,512]{1,0:T(8,128)(2,1)S(1)}, f32[512,512]{1,0:T(8,128)}) custom-call(s32[4]{0:T(128)S(1)} %copy-done.18, bf16[512,512]{1,0:T(8,128)(2,1)S(1)} %get-tuple-element.160.q, bf16[512,512]{1,0:T(8,128)(2,1)S(1)} %get-tuple-element.161.k, bf16[512,512]{1,0:T(8,128)(2,1)S(1)} %get-tuple-element.162.v, ...), custom_call_target="tpu_custom_call" | custom-call | flops 33554432 | bytes 81920 | tf_op jit(solution)/shard_map/pallas_call | solution.py:544
  63.1 2.2 %shard_map.480 = (f32[512,512]{1,0:T(8,128)S(1)}, f32[512,512]{1,0:T(8,128)}, f32[512,1]{1,0:T(8,128)}, bf16[512,512]{1,0:T(8,128)(2,1)S(1)}, bf16[256,512]{1,0:...) custom-call(bf16[512,512]{1,0:T(8,128)(2,1)S(1)} %get-tuple-element.165.ctx.ctx1, bf16[512,512]{1,0:T(8,128)(2,1)S(1)} %copy-done.8, ...), custom_call_target="tpu_custom_call" | custom-call | flops 6291456 | bytes 131072 | tf_op jit(solution)/shard_map/pallas_call | solution.py:648
  65.4 3.6 %shard_map.481 = (bf16[512,512]{1,0:T(8,128)(2,1)S(1)}, f32[512,512]{1,0:T(8,128)}) custom-call(bf16[512,512]{1,0:T(8,128)(2,1)S(1)} %get-tuple-element.167.q, bf16[256,512]{1,0:T(8,128)(2,1)S(1)} %get-tuple-element.168.k, bf16[256,512]{1,0:T(8,128)(2,1)S(1)} %get-tuple-element.169.v), custom_call_target="tpu_custom_call" | custom-call | flops 8388608 | bytes 49152 | tf_op jit(solution)/shard_map/pallas_call | solution.py:574
  69.7 1.3 collective-permute-done.19
  72.8 10.8 %shard_map.483 = (bf16[512,512]{1,0:T(8,128)(2,1)}, bf16[2048,512]{1,0:T(8,128)(2,1)S(1)}, bf16[2048,512]{1,0:T(8,128)(2,1)S(1)}, f32[512,512]{1,0:T(8,128)S(1)}...) custom-call(s32[4]{0:T(128)S(1)} %copy-done.18, ...), custom_call_target="tpu_custom_call" | custom-call | flops 50331648 | bytes 229376 | tf_op jit(solution)/shard_map/pallas_call | solution.py:780
  83.7 1.8 %shard_map.484 = (f32[512,512]{1,0:T(8,128)S(1)}, bf16[512,512]{1,0:T(8,128)(2,1)S(1)}, f32[8,512]{1,0:T(8,128)S(1)}) custom-call(f32[512,512]{1,0:T(8,128)S(1)} %get-tuple-element.176.du3, bf16[512,2048]{1,0:T(8,128)(2,1)S(1)} %get-tuple-element.177.dhid, f32[512,512]{1,0:T(8,128)S(1)} %get-tuple-element.178.normed, ...), custom_call_target="tpu_custom_call" | custom-call | flops 8388608 | bytes 131072 | tf_op jit(solution)/shard_map/pallas_call | solution.py:761
  85.5 2.3 %collective-permute-done.23.refs_1_ = bf16[2048,512]{1,0:T(8,128)(2,1)S(1)} collective-permute-done((bf16[2048,512]{1,0:T(8,128)(2,1)S(1)}, bf16[2048,512]{1,0:T(8,128)(2,1)S(1)}, u32[]{:S(2)}, u32[]{:S(2)}) %collective-permute-start.23) | collective-permute-done | bytes 2097184 | tf_op jit(solution)/shard_map/ppermute | solution.py:60
  88.2 1.5 collective-permute-start.24
  90.4 6.5 %shard_map.486 = (bf16[512,512]{1,0:T(8,128)(2,1)S(1)}, bf16[256,512]{1,0:T(8,128)(2,1)S(1)}, bf16[256,512]{1,0:T(8,128)(2,1)S(1)}) custom-call(bf16[512,512]{1,0:T(8,128)(2,1)} %copy-done.10, bf16[256,512]{1,0:T(8,128)(2,1)} %copy-done.12, bf16[256,512]{1,0:T(8,128)(2,1)} %copy-done.13, bf16[512,512]{1,0:T(8,128)(2,1)} %copy-done.2, ...), custom_call_target="tpu_custom_call" | custom-call | flops 20971520 | bytes 65536 | tf_op jit(solution)/shard_map/pallas_call | solution.py:589
  96.9 6.6 %shard_map.487 = (f32[512,512]{1,0:T(8,128)}, bf16[512,512]{1,0:T(8,128)(2,1)S(1)}, f32[128,512]{1,0:T(8,128)S(1)}, bf16[128,512]{1,0:T(8,128)(2,1)S(1)}, bf16[5...) custom-call(s32[4]{0:T(128)S(1)} %copy-done.18, f32[512,512]{1,0:T(8,128)S(1)} %get-tuple-element.180.du2, ...), custom_call_target="tpu_custom_call" | custom-call | flops 12582912 | bytes 196608 | tf_op jit(solution)/shard_map/pallas_call | solution.py:885
  103.8 1.5 collective-permute-start.26
  105.9 5.8 %shard_map.489 = (bf16[512,256]{1,0:T(8,128)(2,1)S(1)}, bf16[512,256]{1,0:T(8,128)(2,1)S(1)}, bf16[512,256]{1,0:T(8,128)(2,1)S(1)}, bf16[512,256]{1,0:T(8,128)(2,1)S(1)}, bf16[512,256]{1,0:T(8,128)(2,1)S(1)}) custom-call(s32[4]{0:T(128)S(1)} %copy-done.18, bf16[512,512]{1,0:T(8,128)(2,1)} %copy-done.3, bf16[512,512]{1,0:T(8,128)(2,1)} %copy-done.4, ...), custom_call_target="tpu_custom_call" | custom-call | flops 41943040 | bytes 131072 | tf_op jit(solution)/shard_map/pallas_call | solution.py:559
  112.5 1.1 collective-permute-done.27.refs_3_
  114.8 1.1 collective-permute-start.30
  115.8 3.4 %collective-permute-start.33 = (bf16[256,512]{1,0:T(8,128)(2,1)S(1)}, bf16[256,512]{1,0:T(8,128)(2,1)S(1)}, u32[]{:S(2)}, u32[]{:S(2)}) collective-permute-start(bf16[256,512]{1,0:T(8,128)(2,1)S(1)} %get-tuple-element.236.refs_2_), channel_id=1, source_target_pairs={{0,2},{1,3},{2,0},{3,1},{4,6},{5,7},{6,4},{7,5},{8,10},{9,11},{10,... | collective-permute-start | bytes 786440 | tf_op jit(solution)/shard_map/ppermute | solution.py:60
  119.3 5.9 %shard_map.492 = (bf16[512,256]{1,0:T(8,128)(2,1)S(1)}, bf16[512,256]{1,0:T(8,128)(2,1)S(1)}, bf16[512,256]{1,0:T(8,128)(2,1)S(1)}, bf16[512,256]{1,0:T(8,128)(2,1)S(1)}, bf16[512,256]{1,0:T(8,128)(2,1)S(1)}) custom-call(s32[4]{0:T(128)S(1)} %copy-done.18, bf16[512,512]{1,0:T(8,128)(2,1)} %copy-done.3, bf16[512,512]{1,0:T(8,128)(2,1)} %copy-done.4, ...), custom_call_target="tpu_custom_call" | custom-call | flops 41943040 | bytes 131072 | tf_op jit(solution)/shard_map/pallas_call | solution.py:559
  126.3 1.5 collective-permute-start.32
  127.8 3.1 %shard_map.494 = (bf16[512,512]{1,0:T(8,128)(2,1)S(1)}, bf16[3088,128]{1,0:T(8,128)(2,1)S(1)}, bf16[3088,128]{1,0:T(8,128)(2,1)S(1)}) custom-call(s32[4]{0:T(128)S(1)} %copy-done.18, bf16[512,512]{1,0:T(8,128)(2,1)} %x.5, bf16[512,512]{1,0:T(8,128)(2,1)} %copy-done.11, bf16[512,256]{1,0:T(8,128)(2,1)S(1)} %get-tuple-element.206.dqa, ...), custom_call_target="tpu_custom_call" | custom-call | flops 14680064 | bytes 131072 | tf_op jit(solution)/shard_map/pallas_call | solution.py:964
  131.4 1.3 collective-permute-start.36
  133.9 1.6 collective-permute-start.37
  136.1 1.4 collective-permute-start.39
  137.5 2.5 %collective-permute-start.35 = (bf16[704,128]{1,0:T(8,128)(2,1)S(1)}, bf16[704,128]{1,0:T(8,128)(2,1)S(1)}, u32[]{:S(2)}, u32[]{:S(2)}) collective-permute-start(bf16[704,128]{1,0:T(8,128)(2,1)S(1)} %get-tuple-element.243.refs_2_), channel_id=1, source_target_pairs={{0,2},{1,3},{2,0},{3,1},{4,6},{5,7},{6,4},{7,5},{8,10},{9,11},{10,... | collective-permute-start | bytes 540680 | tf_op jit(solution)/shard_map/ppermute | solution.py:60
  140.0 4.2 %collective-permute-done.35.refs_1_ = bf16[704,128]{1,0:T(8,128)(2,1)S(1)} collective-permute-done((bf16[704,128]{1,0:T(8,128)(2,1)S(1)}, bf16[704,128]{1,0:T(8,128)(2,1)S(1)}, u32[]{:S(2)}, u32[]{:S(2)}) %collective-permute-start.35) | collective-permute-done | bytes 180256 | tf_op jit(solution)/shard_map/ppermute | solution.py:60
  144.2 11.1 %collective-permute-done.36.back = bf16[512,512]{1,0:T(8,128)(2,1)S(1)} collective-permute-done((bf16[512,512]{1,0:T(8,128)(2,1)S(1)}, bf16[512,512]{1,0:T(8,128)(2,1)S(1)}, u32[]{:S(2)}, u32[]{:S(2)}) %collective-permute-start.36) | collective-permute-done | bytes 524320 | tf_op jit(solution)/shard_map/ppermute | solution.py:66
  155.5 2.8 %collective-permute-start.40 = (bf16[256,512]{1,0:T(8,128)(2,1)S(1)}, bf16[256,512]{1,0:T(8,128)(2,1)S(1)}, u32[]{:S(2)}, u32[]{:S(2)}) collective-permute-start(bf16[256,512]{1,0:T(8,128)(2,1)S(1)} %get-tuple-element.258), channel_id=1, source_target_pairs={{0,1},{1,0},{2,3},{3,2},{4,5},{5,4},{6,7},{7,6},{8,9},{9,8},{10,11... | collective-permute-start | bytes 786440 | tf_op jit(solution)/shard_map/ppermute | solution.py:60
  158.5 4.3 %collective-permute-start.44 = (bf16[208,128]{1,0:T(8,128)(2,1)S(1)}, bf16[208,128]{1,0:T(8,128)(2,1)S(1)}, u32[]{:S(2)}, u32[]{:S(2)}) collective-permute-start(bf16[208,128]{1,0:T(8,128)(2,1)S(1)} %get-tuple-element.264), channel_id=1, source_target_pairs={{0,3},{1,2},{2,1},{3,0},{4,7},{5,6},{6,5},{7,4},{8,11},{9,10},{10,... | collective-permute-start | bytes 159752 | tf_op jit(solution)/shard_map/ppermute | solution.py:60
  162.8 3.7 %shard_map.500 = f32[512,512]{1,0:T(8,128)} custom-call(f32[512,512]{1,0:T(8,128)} %get-tuple-element.256.du1, bf16[512,256]{1,0:T(8,128)(2,1)S(1)} %get-tuple-element.206.dqa, bf16[512,256]{1,0:T(8,128)(2,1)S(1)} %get-tuple-element.223.dka, bf16[512,256]{1,0:T(8,128)(2,1)S(1)} %get-tuple-element.224.dva, bf16[512,256]{1,0:T(8,128)(2,1)S(1)} %get-tuple-element.227.dqb, ...), custom_call_target="tpu_custom_call" | custom-call | flops 6291456 | bytes 98304 | tf_op jit(solution)/shard_map/pallas_call | solution.py:992
  166.5 1.1 collective-permute-done.40.refs_1_
  169.0 1.2 collective-permute-done.41.refs_1_
  170.2 1.2 shard_map.502
  (167 shorter events, 23.2 us)
Async XLA Ops:
  0.7 25.6 %copy-start.8 = (bf16[512,512]{1,0:T(8,128)(2,1)S(1)}, bf16[512,512]{1,0:T(8,128)(2,1)}, u32[]{:S(2)}) copy-start(bf16[512,512]{1,0:T(8,128)(2,1)} %x.5) | copy-start | bytes 1572868
  2.3 10.6 %collective-permute-start.2 = (bf16[528,128]{1,0:T(8,128)(2,1)}, bf16[528,128]{1,0:T(8,128)(2,1)S(1)}, u32[]{:S(2)}, u32[]{:S(2)}) collective-permute-start(bf16[528,128]{1,0:T(8,128)(2,1)} %shard_map.475), channel_id=1, source_target_pairs={{0,3},{1,2},{2,1},{3,0},{4,7},{5,6},{6,5},{7,4},{8,11},{9,10},{10,... | collective-permute-start | bytes 405512 | tf_op jit(solution)/shard_map/ppermute | solution.py:60
  7.3 11.6 %collective-permute-start.1 = (bf16[528,128]{1,0:T(8,128)(2,1)}, bf16[528,128]{1,0:T(8,128)(2,1)S(1)}, u32[]{:S(2)}, u32[]{:S(2)}) collective-permute-start(bf16[528,128]{1,0:T(8,128)(2,1)} %shard_map.475), channel_id=1, source_target_pairs={{0,2},{1,3},{2,0},{3,1},{4,6},{5,7},{6,4},{7,5},{8,10},{9,11},{10,... | collective-permute-start | bytes 405512 | tf_op jit(solution)/shard_map/ppermute | solution.py:60
  7.3 11.7 %collective-permute-start = (bf16[528,128]{1,0:T(8,128)(2,1)}, bf16[528,128]{1,0:T(8,128)(2,1)S(1)}, u32[]{:S(2)}, u32[]{:S(2)}) collective-permute-start(bf16[528,128]{1,0:T(8,128)(2,1)} %shard_map.475), channel_id=1, source_target_pairs={{0,1},{1,0},{2,3},{3,2},{4,5},{5,4},{6,7},{7,6},{8,9},{9,8},{10,11... | collective-permute-start | bytes 405512 | tf_op jit(solution)/shard_map/ppermute | solution.py:60
  19.1 9.3 %collective-permute-start.5 = (bf16[1,4,4,64,128]{4,3,2,1,0:T(8,128)(2,1)S(1)}, bf16[1,4,4,64,128]{4,3,2,1,0:T(8,128)(2,1)S(1)}, u32[]{:S(2)}, u32[]{:S(2)}) collective-permute-start(bf16[1,4,4,64,128]{4,3,2,1,0:T(8,128)(2,1)S(1)} %pad_maximum_fusion.3), channel_id=1, source_target_pairs={{0,8},{1,9},{2,10},{3,11},{4,12},{5,13},{6,14},{7,15},{8,0},{9,1},... | collective-permute-start | bytes 786440 | tf_op jit(solution)/shard_map/ppermute | solution.py:60
  20.6 5.0 %collective-permute-start.3 = (bf16[1,2,64,512]{3,2,0,1:T(8,128)(2,1)S(1)}, bf16[1,2,64,512]{3,2,0,1:T(8,128)(2,1)S(1)}, u32[]{:S(2)}, u32[]{:S(2)}) collective-permute-start(bf16[1,2,64,512]{3,2,0,1:T(8,128)(2,1)S(1)} %bitcast.66), channel_id=1, source_target_pairs={{0,1},{1,0},{2,3},{3,2},{4,5},{5,4},{6,7},{7,6},{8,9},{9,8},{10,11... | collective-permute-start | bytes 393224 | tf_op jit(solution)/shard_map/ppermute | solution.py:60
  20.7 9.4 %collective-permute-start.10 = (bf16[1,4,4,64,128]{4,3,2,1,0:T(8,128)(2,1)S(1)}, bf16[1,4,4,64,128]{4,3,2,1,0:T(8,128)(2,1)S(1)}, u32[]{:S(2)}, u32[]{:S(2)}) collective-permute-start(bf16[1,4,4,64,128]{4,3,2,1,0:T(8,128)(2,1)S(1)} %pad_maximum_fusion.5), channel_id=1, source_target_pairs={{0,16},{1,17},{2,18},{3,19},{4,20},{5,21},{6,22},{7,23},{8,24},{9,... | collective-permute-start | bytes 786440 | tf_op jit(solution)/shard_map/ppermute | solution.py:60
  26.3 21.3 %copy-start.18 = (s32[4]{0:T(128)S(1)}, s32[4]{0:T(128)}, u32[]{:S(2)}) copy-start(s32[4]{0:T(128)} %pad_add_fusion.info) | copy-start | bytes 52
  26.3 18.4 %collective-permute-start.4 = (bf16[512,512]{1,0:T(8,128)(2,1)S(1)}, bf16[512,512]{1,0:T(8,128)(2,1)S(1)}, u32[]{:S(2)}, u32[]{:S(2)}) collective-permute-start(bf16[512,512]{1,0:T(8,128)(2,1)S(1)} %copy-done.8), channel_id=1, source_target_pairs={{0,1},{2,3},{4,5},{6,7},{8,9},{10,11},{12,13},{14,15},{16,17},{18,... | collective-permute-start | bytes 1572872 | tf_op jit(solution)/shard_map/ppermute | solution.py:66
  28.5 16.3 %collective-permute-start.7 = (bf16[2,4,4,64,128]{4,3,2,1,0:T(8,128)(2,1)S(1)}, bf16[2,4,4,64,128]{4,3,2,1,0:T(8,128)(2,1)S(1)}, u32[]{:S(2)}, u32[]{:S(2)}) collective-permute-start(bf16[2,4,4,64,128]{4,3,2,1,0:T(8,128)(2,1)S(1)} %pad_maximum_fusion.refs_0_), channel_id=1, source_target_pairs={{0,16},{1,17},{2,18},{3,19},{4,20},{5,21},{6,22},{7,23},{8,24},{9,... | collective-permute-start | bytes 1572872 | tf_op jit(solution)/shard_map/ppermute | solution.py:60
  30.1 14.6 %collective-permute-start.12 = (bf16[2,4,4,64,128]{4,3,2,1,0:T(8,128)(2,1)S(1)}, bf16[2,4,4,64,128]{4,3,2,1,0:T(8,128)(2,1)S(1)}, u32[]{:S(2)}, u32[]{:S(2)}) collective-permute-start(bf16[2,4,4,64,128]{4,3,2,1,0:T(8,128)(2,1)S(1)} %pad_maximum_fusion.2.refs_4_), channel_id=1, source_target_pairs={{0,8},{1,9},{2,10},{3,11},{4,12},{5,13},{6,14},{7,15},{8,0},{9,1},... | collective-permute-start | bytes 1572872 | tf_op jit(solution)/shard_map/ppermute | solution.py:60
  31.4 12.3 %collective-permute-start.8 = (bf16[2,2,64,512]{3,2,0,1:T(8,128)(2,1)}, bf16[2,2,64,512]{3,2,0,1:T(8,128)(2,1)}, u32[]{:S(2)}, u32[]{:S(2)}) collective-permute-start(bf16[2,2,64,512]{3,2,0,1:T(8,128)(2,1)} %pad_maximum_fusion.4), channel_id=1, source_target_pairs={{0,2},{1,3},{2,0},{3,1},{4,6},{5,7},{6,4},{7,5},{8,10},{9,11},{10,... | collective-permute-start | bytes 786440 | tf_op jit(solution)/shard_map/ppermute | solution.py:60
  37.1 9.9 %collective-permute-start.6 = (bf16[2,4,4,64,128]{4,3,2,1,0:T(8,128)(2,1)S(1)}, bf16[2,4,4,64,128]{4,3,2,1,0:T(8,128)(2,1)S(1)}, u32[]{:S(2)}, u32[]{:S(2)}) collective-permute-start(bf16[2,4,4,64,128]{4,3,2,1,0:T(8,128)(2,1)S(1)} %pad_maximum_fusion.refs_0_), channel_id=1, source_target_pairs={{0,4},{1,5},{2,6},{3,7},{4,0},{5,1},{6,2},{7,3},{8,12},{9,13},{10,... | collective-permute-start | bytes 1572872 | tf_op jit(solution)/shard_map/ppermute | solution.py:60
  43.7 3.9 %collective-permute-start.11 = (bf16[2,4,4,64,128]{4,3,2,1,0:T(8,128)(2,1)S(1)}, bf16[2,4,4,64,128]{4,3,2,1,0:T(8,128)(2,1)S(1)}, u32[]{:S(2)}, u32[]{:S(2)}) collective-permute-start(bf16[2,4,4,64,128]{4,3,2,1,0:T(8,128)(2,1)S(1)} %pad_maximum_fusion.2.refs_4_), channel_id=1, source_target_pairs={{0,4},{1,5},{2,6},{3,7},{4,0},{5,1},{6,2},{7,3},{8,12},{9,13},{10,... | collective-permute-start | bytes 1572872 | tf_op jit(solution)/shard_map/ppermute | solution.py:60
  44.8 2.8 %collective-permute-start.13 = (bf16[2,4,4,64,128]{4,3,2,1,0:T(8,128)(2,1)S(1)}, bf16[2,4,4,64,128]{4,3,2,1,0:T(8,128)(2,1)S(1)}, u32[]{:S(2)}, u32[]{:S(2)}) collective-permute-start(bf16[2,4,4,64,128]{4,3,2,1,0:T(8,128)(2,1)S(1)} %collective-permute-done.12.refs_6_), channel_id=1, source_target_pairs={{0,4},{1,5},{2,6},{3,7},{4,0},{5,1},{6,2},{7,3},{8,12},{9,13},{10,... | collective-permute-start | bytes 1572872 | tf_op jit(solution)/shard_map/ppermute | solution.py:60
  45.3 2.3 %collective-permute-start.9 = (bf16[2,4,4,64,128]{4,3,2,1,0:T(8,128)(2,1)S(1)}, bf16[2,4,4,64,128]{4,3,2,1,0:T(8,128)(2,1)S(1)}, u32[]{:S(2)}, u32[]{:S(2)}) collective-permute-start(bf16[2,4,4,64,128]{4,3,2,1,0:T(8,128)(2,1)S(1)} %collective-permute-done.7.refs_2_), channel_id=1, source_target_pairs={{0,4},{1,5},{2,6},{3,7},{4,0},{5,1},{6,2},{7,3},{8,12},{9,13},{10,... | collective-permute-start | bytes 1572872 | tf_op jit(solution)/shard_map/ppermute | solution.py:60
  45.4 8.7 %collective-permute-start.15 = (bf16[1,4,1,64,512]{4,3,2,1,0:T(8,128)(2,1)S(1)}, bf16[1,4,1,64,512]{4,3,2,1,0:T(8,128)(2,1)S(1)}, u32[]{:S(2)}, u32[]{:S(2)}) collective-permute-start(bf16[1,4,1,64,512]{4,3,2,1,0:T(8,128)(2,1)S(1)} %get-tuple-element.159), channel_id=1, source_target_pairs={{0,16},{1,17},{2,18},{3,19},{4,20},{5,21},{6,22},{7,23},{8,24},{9,... | collective-permute-start | bytes 786440 | tf_op jit(solution)/shard_map/ppermute | solution.py:60
  47.0 8.4 %collective-permute-start.14 = (bf16[1,4,1,64,512]{4,3,1,2,0:T(8,128)(2,1)S(1)}, bf16[1,4,1,64,512]{4,3,1,2,0:T(8,128)(2,1)S(1)}, u32[]{:S(2)}, u32[]{:S(2)}) collective-permute-start(bf16[1,4,1,64,512]{4,3,1,2,0:T(8,128)(2,1)S(1)} %get-tuple-element.158), channel_id=1, source_target_pairs={{0,8},{1,9},{2,10},{3,11},{4,12},{5,13},{6,14},{7,15},{8,0},{9,1},... | collective-permute-start | bytes 786440 | tf_op jit(solution)/shard_map/ppermute | solution.py:60
  48.9 23.7 %copy-start = (bf16[8,512,512]{2,1,0:T(8,128)(2,1)}, bf16[8,512,512]{2,1,0:T(8,128)(2,1)S(1)}, u32[]{:S(2)}) copy-start(bf16[8,512,512]{2,1,0:T(8,128)(2,1)S(1)} %shard_map.477.wq.wk.wv.wo.w) | copy-start | bytes 12582916
  54.2 14.8 %collective-permute-start.21 = (bf16[2,4,1,64,512]{4,3,2,1,0:T(8,128)(2,1)S(1)}, bf16[2,4,1,64,512]{4,3,2,1,0:T(8,128)(2,1)S(1)}, u32[]{:S(2)}, u32[]{:S(2)}) collective-permute-start(bf16[2,4,1,64,512]{4,3,2,1,0:T(8,128)(2,1)S(1)} %constant_dynamic-update-slice_fusion.2.refs_4_), channel_id=1, source_target_pairs={{0,8},{1,9},{2,10},{3,11},{4,12},{5,13},{6,14},{7,15},{8,0},{9,1},... | collective-permute-start | bytes 1572872 | tf_op jit(solution)/shard_map/ppermute | solution.py:60
  55.4 13.6 %collective-permute-start.18 = (bf16[2,4,1,64,512]{4,3,1,2,0:T(8,128)(2,1)S(1)}, bf16[2,4,1,64,512]{4,3,1,2,0:T(8,128)(2,1)S(1)}, u32[]{:S(2)}, u32[]{:S(2)}) collective-permute-start(bf16[2,4,1,64,512]{4,3,1,2,0:T(8,128)(2,1)S(1)} %constant_dynamic-update-slice_fusion), channel_id=1, source_target_pairs={{0,16},{1,17},{2,18},{3,19},{4,20},{5,21},{6,22},{7,23},{8,24},{9,... | collective-permute-start | bytes 1572872 | tf_op jit(solution)/shard_map/ppermute | solution.py:60
  56.5 6.6 %collective-permute-start.16 = (bf16[128,512]{1,0:T(8,128)(2,1)S(1)}, bf16[128,512]{1,0:T(8,128)(2,1)S(1)}, u32[]{:S(2)}, u32[]{:S(2)}) collective-permute-start(bf16[128,512]{1,0:T(8,128)(2,1)S(1)} %copy-done.14), channel_id=1, source_target_pairs={{0,1},{1,0},{2,3},{3,2},{4,5},{5,4},{6,7},{7,6},{8,9},{9,8},{10,11... | collective-permute-start | bytes 393224 | tf_op jit(solution)/shard_map/ppermute | solution.py:60
  56.5 13.2 %collective-permute-start.20 = (bf16[2,4,1,64,512]{4,3,2,1,0:T(8,128)(2,1)S(1)}, bf16[2,4,1,64,512]{4,3,2,1,0:T(8,128)(2,1)S(1)}, u32[]{:S(2)}, u32[]{:S(2)}) collective-permute-start(bf16[2,4,1,64,512]{4,3,2,1,0:T(8,128)(2,1)S(1)} %constant_dynamic-update-slice_fusion.2.refs_4_), channel_id=1, source_target_pairs={{0,4},{1,5},{2,6},{3,7},{4,0},{5,1},{6,2},{7,3},{8,12},{9,13},{10,... | collective-permute-start | bytes 1572872 | tf_op jit(solution)/shard_map/ppermute | solution.py:60
  56.6 13.1 %collective-permute-start.17 = (bf16[2,4,1,64,512]{4,3,1,2,0:T(8,128)(2,1)S(1)}, bf16[2,4,1,64,512]{4,3,1,2,0:T(8,128)(2,1)S(1)}, u32[]{:S(2)}, u32[]{:S(2)}) collective-permute-start(bf16[2,4,1,64,512]{4,3,1,2,0:T(8,128)(2,1)S(1)} %constant_dynamic-update-slice_fusion), channel_id=1, source_target_pairs={{0,4},{1,5},{2,6},{3,7},{4,0},{5,1},{6,2},{7,3},{8,12},{9,13},{10,... | collective-permute-start | bytes 1572872 | tf_op jit(solution)/shard_map/ppermute | solution.py:60
  69.0 2.0 %collective-permute-start.19 = (bf16[2,4,1,64,512]{4,3,1,2,0:T(8,128)(2,1)S(1)}, bf16[2,4,1,64,512]{4,3,1,2,0:T(8,128)(2,1)S(1)}, u32[]{:S(2)}, u32[]{:S(2)}) collective-permute-start(bf16[2,4,1,64,512]{4,3,1,2,0:T(8,128)(2,1)S(1)} %collective-permute-done.18), channel_id=1, source_target_pairs={{0,4},{1,5},{2,6},{3,7},{4,0},{5,1},{6,2},{7,3},{8,12},{9,13},{10,... | collective-permute-start | bytes 1572872 | tf_op jit(solution)/shard_map/ppermute | solution.py:60
  69.1 2.6 %collective-permute-start.22 = (bf16[2,4,1,64,512]{4,3,2,1,0:T(8,128)(2,1)S(1)}, bf16[2,4,1,64,512]{4,3,2,1,0:T(8,128)(2,1)S(1)}, u32[]{:S(2)}, u32[]{:S(2)}) collective-permute-start(bf16[2,4,1,64,512]{4,3,2,1,0:T(8,128)(2,1)S(1)} %collective-permute-done.21.refs_6_), channel_id=1, source_target_pairs={{0,4},{1,5},{2,6},{3,7},{4,0},{5,1},{6,2},{7,3},{8,12},{9,13},{10,... | collective-permute-start | bytes 1572872 | tf_op jit(solution)/shard_map/ppermute | solution.py:60
  83.6 4.2 %collective-permute-start.23 = (bf16[2048,512]{1,0:T(8,128)(2,1)S(1)}, bf16[2048,512]{1,0:T(8,128)(2,1)S(1)}, u32[]{:S(2)}, u32[]{:S(2)}) collective-permute-start(bf16[2048,512]{1,0:T(8,128)(2,1)S(1)} %get-tuple-element.185), channel_id=1, source_target_pairs={{0,4},{1,5},{2,6},{3,7},{4,0},{5,1},{6,2},{7,3},{8,12},{9,13},{10,... | collective-permute-start | bytes 6291464 | tf_op jit(solution)/shard_map/ppermute | solution.py:60
  88.2 15.2 %collective-permute-start.24 = (bf16[512,512]{1,0:T(8,128)(2,1)S(1)}, bf16[512,512]{1,0:T(8,128)(2,1)S(1)}, u32[]{:S(2)}, u32[]{:S(2)}) collective-permute-start(bf16[512,512]{1,0:T(8,128)(2,1)S(1)} %get-tuple-element.201), channel_id=1, source_target_pairs={{0,8},{1,9},{2,10},{3,11},{4,12},{5,13},{6,14},{7,15},{8,0},{9,1},... | collective-permute-start | bytes 1572872 | tf_op jit(solution)/shard_map/ppermute | solution.py:60
  89.8 13.7 %collective-permute-start.25 = (bf16[512,512]{1,0:T(8,128)(2,1)S(1)}, bf16[512,512]{1,0:T(8,128)(2,1)S(1)}, u32[]{:S(2)}, u32[]{:S(2)}) collective-permute-start(bf16[512,512]{1,0:T(8,128)(2,1)S(1)} %get-tuple-element.202.refs_4_), channel_id=1, source_target_pairs={{0,16},{1,17},{2,18},{3,19},{4,20},{5,21},{6,22},{7,23},{8,24},{9,... | collective-permute-start | bytes 1572872 | tf_op jit(solution)/shard_map/ppermute | solution.py:60
  103.7 10.1 %collective-permute-start.28 = (bf16[5184,128]{1,0:T(8,128)(2,1)S(1)}, bf16[5184,128]{1,0:T(8,128)(2,1)S(1)}, u32[]{:S(2)}, u32[]{:S(2)}) collective-permute-start(bf16[5184,128]{1,0:T(8,128)(2,1)S(1)} %get-tuple-element.214), channel_id=1, source_target_pairs={{0,4},{1,5},{2,6},{3,7},{4,0},{5,1},{6,2},{7,3},{8,12},{9,13},{10,... | collective-permute-start | bytes 3981320 | tf_op jit(solution)/shard_map/ppermute | solution.py:60
  103.8 8.7 %collective-permute-start.26 = (bf16[256,512]{1,0:T(8,128)(2,1)S(1)}, bf16[256,512]{1,0:T(8,128)(2,1)S(1)}, u32[]{:S(2)}, u32[]{:S(2)}) collective-permute-start(bf16[256,512]{1,0:T(8,128)(2,1)S(1)} %get-tuple-element.209), channel_id=1, source_target_pairs={{0,16},{1,17},{2,18},{3,19},{4,20},{5,21},{6,22},{7,23},{8,24},{9,... | collective-permute-start | bytes 786440 | tf_op jit(solution)/shard_map/ppermute | solution.py:60
  105.3 8.4 %collective-permute-start.27 = (bf16[256,512]{1,0:T(8,128)(2,1)S(1)}, bf16[256,512]{1,0:T(8,128)(2,1)S(1)}, u32[]{:S(2)}, u32[]{:S(2)}) collective-permute-start(bf16[256,512]{1,0:T(8,128)(2,1)S(1)} %get-tuple-element.210.refs_4_), channel_id=1, source_target_pairs={{0,8},{1,9},{2,10},{3,11},{4,12},{5,13},{6,14},{7,15},{8,0},{9,1},... | collective-permute-start | bytes 786440 | tf_op jit(solution)/shard_map/ppermute | solution.py:60
  114.1 11.0 %collective-permute-start.29 = (bf16[1536,128]{1,0:T(8,128)(2,1)S(1)}, bf16[1536,128]{1,0:T(8,128)(2,1)S(1)}, u32[]{:S(2)}, u32[]{:S(2)}) collective-permute-start(bf16[1536,128]{1,0:T(8,128)(2,1)S(1)} %get-tuple-element.220), channel_id=1, source_target_pairs={{0,8},{1,9},{2,10},{3,11},{4,12},{5,13},{6,14},{7,15},{8,0},{9,1},... | collective-permute-start | bytes 1179656 | tf_op jit(solution)/shard_map/ppermute | solution.py:60
  114.8 10.4 %collective-permute-start.30 = (bf16[1088,128]{1,0:T(8,128)(2,1)S(1)}, bf16[1088,128]{1,0:T(8,128)(2,1)S(1)}, u32[]{:S(2)}, u32[]{:S(2)}) collective-permute-start(bf16[1088,128]{1,0:T(8,128)(2,1)S(1)} %get-tuple-element.221.refs_4_), channel_id=1, source_target_pairs={{0,16},{1,17},{2,18},{3,19},{4,20},{5,21},{6,22},{7,23},{8,24},{9,... | collective-permute-start | bytes 835592 | tf_op jit(solution)/shard_map/ppermute | solution.py:60
  115.8 15.1 %collective-permute-start.33 = (bf16[256,512]{1,0:T(8,128)(2,1)S(1)}, bf16[256,512]{1,0:T(8,128)(2,1)S(1)}, u32[]{:S(2)}, u32[]{:S(2)}) collective-permute-start(bf16[256,512]{1,0:T(8,128)(2,1)S(1)} %get-tuple-element.236.refs_2_), channel_id=1, source_target_pairs={{0,2},{1,3},{2,0},{3,1},{4,6},{5,7},{6,4},{7,5},{8,10},{9,11},{10,... | collective-permute-start | bytes 786440 | tf_op jit(solution)/shard_map/ppermute | solution.py:60
  125.3 6.1 %collective-permute-start.31 = (bf16[768,128]{1,0:T(8,128)(2,1)S(1)}, bf16[768,128]{1,0:T(8,128)(2,1)S(1)}, u32[]{:S(2)}, u32[]{:S(2)}) collective-permute-start(bf16[768,128]{1,0:T(8,128)(2,1)S(1)} %get-tuple-element.234), channel_id=1, source_target_pairs={{0,16},{1,17},{2,18},{3,19},{4,20},{5,21},{6,22},{7,23},{8,24},{9,... | collective-permute-start | bytes 589832 | tf_op jit(solution)/shard_map/ppermute | solution.py:60
  126.3 5.1 %collective-permute-start.32 = (bf16[576,128]{1,0:T(8,128)(2,1)S(1)}, bf16[576,128]{1,0:T(8,128)(2,1)S(1)}, u32[]{:S(2)}, u32[]{:S(2)}) collective-permute-start(bf16[576,128]{1,0:T(8,128)(2,1)S(1)} %get-tuple-element.235.refs_4_), channel_id=1, source_target_pairs={{0,8},{1,9},{2,10},{3,11},{4,12},{5,13},{6,14},{7,15},{8,0},{9,1},... | collective-permute-start | bytes 442376 | tf_op jit(solution)/shard_map/ppermute | solution.py:60
  131.4 2.3 %collective-permute-start.34 = (bf16[3088,128]{1,0:T(8,128)(2,1)S(1)}, bf16[3088,128]{1,0:T(8,128)(2,1)S(1)}, u32[]{:S(2)}, u32[]{:S(2)}) collective-permute-start(bf16[3088,128]{1,0:T(8,128)(2,1)S(1)} %get-tuple-element.237), channel_id=1, source_target_pairs={{0,4},{1,5},{2,6},{3,7},{4,0},{5,1},{6,2},{7,3},{8,12},{9,13},{10,... | collective-permute-start | bytes 2371592 | tf_op jit(solution)/shard_map/ppermute | solution.py:60
  131.4 23.9 %collective-permute-start.36 = (bf16[512,512]{1,0:T(8,128)(2,1)S(1)}, bf16[512,512]{1,0:T(8,128)(2,1)S(1)}, u32[]{:S(2)}, u32[]{:S(2)}) collective-permute-start(bf16[512,512]{1,0:T(8,128)(2,1)S(1)} %get-tuple-element.245), channel_id=1, source_target_pairs={{1,0},{3,2},{5,4},{7,6},{9,8},{11,10},{13,12},{15,14},{17,16},{19,... | collective-permute-start | bytes 1572872 | tf_op jit(solution)/shard_map/ppermute | solution.py:66
  133.9 21.4 %collective-permute-start.37 = (bf16[784,128]{1,0:T(8,128)(2,1)S(1)}, bf16[784,128]{1,0:T(8,128)(2,1)S(1)}, u32[]{:S(2)}, u32[]{:S(2)}) collective-permute-start(bf16[784,128]{1,0:T(8,128)(2,1)S(1)} %get-tuple-element.247), channel_id=1, source_target_pairs={{0,8},{1,9},{2,10},{3,11},{4,12},{5,13},{6,14},{7,15},{8,0},{9,1},... | collective-permute-start | bytes 602120 | tf_op jit(solution)/shard_map/ppermute | solution.py:60
  135.5 19.9 %collective-permute-start.38 = (bf16[784,128]{1,0:T(8,128)(2,1)S(1)}, bf16[784,128]{1,0:T(8,128)(2,1)S(1)}, u32[]{:S(2)}, u32[]{:S(2)}) collective-permute-start(bf16[784,128]{1,0:T(8,128)(2,1)S(1)} %get-tuple-element.248), channel_id=1, source_target_pairs={{0,16},{1,17},{2,18},{3,19},{4,20},{5,21},{6,22},{7,23},{8,24},{9,... | collective-permute-start | bytes 602120 | tf_op jit(solution)/shard_map/ppermute | solution.py:60
  136.1 19.3 %collective-permute-start.39 = (bf16[784,128]{1,0:T(8,128)(2,1)S(1)}, bf16[784,128]{1,0:T(8,128)(2,1)S(1)}, u32[]{:S(2)}, u32[]{:S(2)}) collective-permute-start(bf16[784,128]{1,0:T(8,128)(2,1)S(1)} %get-tuple-element.249), channel_id=1, source_target_pairs={{0,24},{1,25},{2,26},{3,27},{4,28},{5,29},{6,30},{7,31},{8,16},{9,... | collective-permute-start | bytes 602120 | tf_op jit(solution)/shard_map/ppermute | solution.py:60
  137.5 6.8 %collective-permute-start.35 = (bf16[704,128]{1,0:T(8,128)(2,1)S(1)}, bf16[704,128]{1,0:T(8,128)(2,1)S(1)}, u32[]{:S(2)}, u32[]{:S(2)}) collective-permute-start(bf16[704,128]{1,0:T(8,128)(2,1)S(1)} %get-tuple-element.243.refs_2_), channel_id=1, source_target_pairs={{0,2},{1,3},{2,0},{3,1},{4,6},{5,7},{6,4},{7,5},{8,10},{9,11},{10,... | collective-permute-start | bytes 540680 | tf_op jit(solution)/shard_map/ppermute | solution.py:60
  155.5 12.1 %collective-permute-start.40 = (bf16[256,512]{1,0:T(8,128)(2,1)S(1)}, bf16[256,512]{1,0:T(8,128)(2,1)S(1)}, u32[]{:S(2)}, u32[]{:S(2)}) collective-permute-start(bf16[256,512]{1,0:T(8,128)(2,1)S(1)} %get-tuple-element.258), channel_id=1, source_target_pairs={{0,1},{1,0},{2,3},{3,2},{4,5},{5,4},{6,7},{7,6},{8,9},{9,8},{10,11... | collective-permute-start | bytes 786440 | tf_op jit(solution)/shard_map/ppermute | solution.py:60
  158.4 10.7 %collective-permute-start.42 = (bf16[208,128]{1,0:T(8,128)(2,1)S(1)}, bf16[208,128]{1,0:T(8,128)(2,1)S(1)}, u32[]{:S(2)}, u32[]{:S(2)}) collective-permute-start(bf16[208,128]{1,0:T(8,128)(2,1)S(1)} %get-tuple-element.262), channel_id=1, source_target_pairs={{0,1},{1,0},{2,3},{3,2},{4,5},{5,4},{6,7},{7,6},{8,9},{9,8},{10,11... | collective-permute-start | bytes 159752 | tf_op jit(solution)/shard_map/ppermute | solution.py:60
  158.4 10.6 %collective-permute-start.43 = (bf16[208,128]{1,0:T(8,128)(2,1)S(1)}, bf16[208,128]{1,0:T(8,128)(2,1)S(1)}, u32[]{:S(2)}, u32[]{:S(2)}) collective-permute-start(bf16[208,128]{1,0:T(8,128)(2,1)S(1)} %get-tuple-element.263), channel_id=1, source_target_pairs={{0,2},{1,3},{2,0},{3,1},{4,6},{5,7},{6,4},{7,5},{8,10},{9,11},{10,... | collective-permute-start | bytes 159752 | tf_op jit(solution)/shard_map/ppermute | solution.py:60
  158.5 10.5 %collective-permute-start.44 = (bf16[208,128]{1,0:T(8,128)(2,1)S(1)}, bf16[208,128]{1,0:T(8,128)(2,1)S(1)}, u32[]{:S(2)}, u32[]{:S(2)}) collective-permute-start(bf16[208,128]{1,0:T(8,128)(2,1)S(1)} %get-tuple-element.264), channel_id=1, source_target_pairs={{0,3},{1,2},{2,1},{3,0},{4,7},{5,6},{6,5},{7,4},{8,11},{9,10},{10,... | collective-permute-start | bytes 159752 | tf_op jit(solution)/shard_map/ppermute | solution.py:60
  162.8 7.4 %collective-permute-start.41 = (bf16[384,128]{1,0:T(8,128)(2,1)S(1)}, bf16[384,128]{1,0:T(8,128)(2,1)S(1)}, u32[]{:S(2)}, u32[]{:S(2)}) collective-permute-start(bf16[384,128]{1,0:T(8,128)(2,1)S(1)} %get-tuple-element.259.refs_2_), channel_id=1, source_target_pairs={{0,1},{1,0},{2,3},{3,2},{4,5},{5,4},{6,7},{7,6},{8,9},{9,8},{10,11... | collective-permute-start | bytes 294920 | tf_op jit(solution)/shard_map/ppermute | solution.py:60
  (28 other events, 184.0 us)

commit v6 on v5

--- a/solution.py
+++ b/solution.py
@@ -544,7 +544,7 @@
     return pl.pallas_call(
         self_forward_kernel,
         grid=(width // PAIR,),
-        out_shape=(shaped((tokens, width), BF16), shaped_far((tokens, width), F32)),
+        out_shape=(shaped((tokens, width), BF16), shaped((tokens, width), F32)),
         in_specs=[SMEM] + [row] * 5,
         out_specs=(row, row),
         compiler_params=limit(16),
@@ -1072,7 +1072,7 @@
         more = [grown(*held[g], plane_bits(g)[index]) for g in range(2)]
         if index < rounds - 1:
             held = [merged([held[g], more[g]]) for g in range(2)]
-    inputs_other = hand_over(after(inputs, line_feed), 0, 1)
+    inputs_other = hand_over(after(inputs, lines[0]), 0, 1)
     line_feed = doubled(line_feed, bits[1:])
     head_biases, hidden_bias = spread(info, riders)
     more[0] = more[0][0], after(more[0][1], inputs_other, line_feed, head_biases)
@@ -1195,14 +1195,14 @@
     places = [self_halves.place(0, j)[0] for j in range(nd // 2)]
     parts = add_rows([keep, got], [[(size, [(0, lo), (1, lo)]), end] for lo in places])
     planes = [parts[0]] + [swap(part, 2 * j, 0) for j, part in enumerate(parts) if j]
-    planes[0] = after(planes[0], *arrays, inputs_got)
+    arrays[0] = after(arrays[0], *planes, inputs_got)
+    arrays, segments, rider = line_round(arrays, segments, rider, 1)
+    planes[0] = after(planes[0], arrays[0])
     at = range(len(planes))
     rows = 3 * block
     end = (self_halves.rider, [(p, size) for p in at])
     lines = add_rows(planes, [[(rows, [(p, k * rows) for p in at]), end] for k in range(nt)])
     lines = line_swaps(lines)
-    arrays[0] = after(arrays[0], lines[0])
-    arrays, segments, rider = line_round(arrays, segments, rider, 1)
     riding = memory_back.shape[1] == feed_arrays[0].shape[1]
     feed_arrays[0] = after(feed_arrays[0], lines[0])
     feed_arrays, feed_segments, _ = line_round(

time: 173 us -> 171 us (0.988)
  waiting for transfers between devices: 45.2 us -> 42.2 us
  starting transfers between devices: 48.5 us -> 50.8 us
    ppermute x43, waiting for transfers between devices: 34.1 us -> 26.8 us  [swap(): return lax.ppermute(array, ('dp', 'tensor'), pairs)]
    ppermute x2, waiting for transfers between devices: 11.1 us -> 15.5 us  [hand_over(): return lax.ppermute(array, ('dp', 'tensor'), pairs)]
    ppermute x2, starting transfers between devices: 3.34 us -> 5.23 us  [hand_over(): return lax.ppermute(array, ('dp', 'tensor'), pairs)]
  transfers between devices with their start and end apart: 45 -> 45, of which waited for: 16 -> 14; matrix products, arithmetic and copies ran while one was open for 5% -> 5% of each run, Pallas kernels for 29% -> 29%
where the time goes in v6:
time: 171 us
  Pallas kernels  65.6 us (38%)
  starting transfers between devices  50.8 us (30%)
  waiting for transfers between devices  42.2 us (25%)
  local copies, waits for them, and re-layouts  5.17 us (3%)
  other arithmetic  4.75 us (3%)
  between operations  2.2 us (1%)
    ppermute x43, starting transfers between devices, swap(): return lax.ppermute(array, ('dp', 'tensor'), pairs)  45.6 us
    ppermute x43, waiting for transfers between devices, swap(): return lax.ppermute(array, ('dp', 'tensor'), pairs)  26.8 us
    ppermute x2, waiting for transfers between devices, hand_over(): return lax.ppermute(array, ('dp', 'tensor'), pairs)  15.5 us
    pallas_call x2, Pallas kernels, self_backward(): pl.pallas_call(self_backward_kernel, grid=(pairs,), out_shape=(out,) * 5,...  11.7 us
    pallas_call x1, Pallas kernels, feed(): pl.pallas_call(functools.partial(feed_kernel, halves=halves), grid=(1,),...  10.8 us
    pallas_call x1, Pallas kernels, middle(): pl.pallas_call(functools.partial(middle_kernel, halves=halves if direct e...  6.61 us
    pallas_call x1, Pallas kernels, cross_backward(): pl.pallas_call(cross_backward_kernel, grid=(width // PAIR,), out_shape=(s...  6.49 us
    pallas_call x1, Pallas kernels, self_forward(): pl.pallas_call(self_forward_kernel, grid=(width // PAIR,), out_shape=(sha...  5.28 us
  transfers between devices with their start and end apart: 45, of which 14 were waited for; matrix products, arithmetic and copies ran while one was open for 5% of the time, Pallas kernels for 29%

profile of v6, /device:TPU:0, one launch (start us, length us, event | category | flops | bytes accessed | tf_op | source)
XLA Modules:
  0.0 170.7 jit_solution(12969120305416208571)
XLA Ops:
  0.7 1.6 shard_map.475
  2.3 5.0 %collective-permute-start.2 = (bf16[528,128]{1,0:T(8,128)(2,1)}, bf16[528,128]{1,0:T(8,128)(2,1)S(1)}, u32[]{:S(2)}, u32[]{:S(2)}) collective-permute-start(bf16[528,128]{1,0:T(8,128)(2,1)} %shard_map.475), channel_id=1, source_target_pairs={{0,3},{1,2},{2,1},{3,0},{4,7},{5,6},{6,5},{7,4},{8,11},{9,10},{10,... | collective-permute-start | bytes 405512 | tf_op jit(solution)/shard_map/ppermute | solution.py:60
  9.5 1.2 dynamic_slice.4
  12.9 6.0 %collective-permute-done.1 = bf16[528,128]{1,0:T(8,128)(2,1)S(1)} collective-permute-done((bf16[528,128]{1,0:T(8,128)(2,1)}, bf16[528,128]{1,0:T(8,128)(2,1)S(1)}, u32[]{:S(2)}, u32[]{:S(2)}) %collective-permute-start.1) | collective-permute-done | bytes 135200 | tf_op jit(solution)/shard_map/ppermute | solution.py:60
  19.1 1.6 collective-permute-start.4
  20.7 1.6 collective-permute-start.10
  22.3 3.9 %collective-permute-start.3 = (bf16[512,512]{1,0:T(8,128)(2,1)S(1)}, bf16[512,512]{1,0:T(8,128)(2,1)S(1)}, u32[]{:S(2)}, u32[]{:S(2)}) collective-permute-start(bf16[512,512]{1,0:T(8,128)(2,1)S(1)} %copy-done.8), channel_id=1, source_target_pairs={{0,1},{2,3},{4,5},{6,7},{8,9},{10,11},{12,13},{14,15},{16,17},{18,... | collective-permute-start | bytes 1572872 | tf_op jit(solution)/shard_map/ppermute | solution.py:66
  26.6 1.6 collective-permute-start.6
  28.2 1.6 collective-permute-start.12
  30.5 3.4 %collective-permute-start.8 = (bf16[2,2,64,512]{3,2,0,1:T(8,128)(2,1)}, bf16[2,2,64,512]{3,2,0,1:T(8,128)(2,1)}, u32[]{:S(2)}, u32[]{:S(2)}) collective-permute-start(bf16[2,2,64,512]{3,2,0,1:T(8,128)(2,1)} %pad_maximum_fusion.4), channel_id=1, source_target_pairs={{0,2},{1,3},{2,0},{3,1},{4,6},{5,7},{6,4},{7,5},{8,10},{9,11},{10,... | collective-permute-start | bytes 786440 | tf_op jit(solution)/shard_map/ppermute | solution.py:60
  35.2 1.4 shard_map.476
  36.6 6.2 %collective-permute-done.8 = bf16[2,2,64,512]{3,2,0,1:T(8,128)(2,1)} collective-permute-done((bf16[2,2,64,512]{3,2,0,1:T(8,128)(2,1)}, bf16[2,2,64,512]{3,2,0,1:T(8,128)(2,1)}, u32[]{:S(2)}, u32[]{:S(2)}) %collective-permute-start.8) | collective-permute-done | bytes 262176 | tf_op jit(solution)/shard_map/ppermute | solution.py:60
  42.8 1.0 pad_maximum_fusion.1
  45.5 1.2 collective-permute-start.14
  46.8 1.3 shard_map.477.wq.wk.wv.wo.w
  48.1 1.5 shard_map.478
  49.8 3.5 %collective-permute-done.15 = bf16[1,4,1,64,512]{4,3,2,1,0:T(8,128)(2,1)S(1)} collective-permute-done((bf16[1,4,1,64,512]{4,3,2,1,0:T(8,128)(2,1)S(1)}, bf16[1,4,1,64,512]{4,3,2,1,0:T(8,128)(2,1)S(1)}, u32[]{:S(2)}, u32[]{:S(2)}) %collective-permute-start.15) | collective-permute-done | bytes 262176 | tf_op jit(solution)/shard_map/ppermute | solution.py:60
  53.3 1.0 collective-permute-start.21
  54.4 1.2 collective-permute-start.18
  56.5 5.3 %shard_map.479 = (bf16[512,512]{1,0:T(8,128)(2,1)S(1)}, f32[512,512]{1,0:T(8,128)S(1)}) custom-call(s32[4]{0:T(128)S(1)} %copy-done.19, bf16[512,512]{1,0:T(8,128)(2,1)S(1)} %get-tuple-element.160.q, bf16[512,512]{1,0:T(8,128)(2,1)S(1)} %get-tuple-element.161.k, bf16[512,512]{1,0:T(8,128)(2,1)S(1)} %get-tuple-element.162.v, ...), custom_call_target="tpu_custom_call" | custom-call | flops 33554432 | bytes 81920 | tf_op jit(solution)/shard_map/pallas_call | solution.py:544
  61.9 2.2 %shard_map.480 = (f32[512,512]{1,0:T(8,128)S(1)}, f32[512,512]{1,0:T(8,128)}, f32[512,1]{1,0:T(8,128)}, bf16[512,512]{1,0:T(8,128)(2,1)S(1)}, bf16[256,512]{1,0:...) custom-call(bf16[512,512]{1,0:T(8,128)(2,1)S(1)} %get-tuple-element.165.ctx.ctx1, bf16[512,512]{1,0:T(8,128)(2,1)S(1)} %copy-done.8, ...), custom_call_target="tpu_custom_call" | custom-call | flops 6291456 | bytes 131072 | tf_op jit(solution)/shard_map/pallas_call | solution.py:648
  64.2 3.6 %shard_map.481 = (bf16[512,512]{1,0:T(8,128)(2,1)S(1)}, f32[512,512]{1,0:T(8,128)}) custom-call(bf16[512,512]{1,0:T(8,128)(2,1)S(1)} %get-tuple-element.167.q, bf16[256,512]{1,0:T(8,128)(2,1)S(1)} %get-tuple-element.168.k, bf16[256,512]{1,0:T(8,128)(2,1)S(1)} %get-tuple-element.169.v), custom_call_target="tpu_custom_call" | custom-call | flops 8388608 | bytes 49152 | tf_op jit(solution)/shard_map/pallas_call | solution.py:574
  68.5 1.3 collective-permute-done.19
  71.6 10.8 %shard_map.483 = (bf16[512,512]{1,0:T(8,128)(2,1)}, bf16[2048,512]{1,0:T(8,128)(2,1)S(1)}, bf16[2048,512]{1,0:T(8,128)(2,1)S(1)}, f32[512,512]{1,0:T(8,128)S(1)}...) custom-call(s32[4]{0:T(128)S(1)} %copy-done.19, ...), custom_call_target="tpu_custom_call" | custom-call | flops 50331648 | bytes 229376 | tf_op jit(solution)/shard_map/pallas_call | solution.py:780
  82.5 1.8 %shard_map.484 = (f32[512,512]{1,0:T(8,128)S(1)}, bf16[512,512]{1,0:T(8,128)(2,1)S(1)}, f32[8,512]{1,0:T(8,128)S(1)}) custom-call(f32[512,512]{1,0:T(8,128)S(1)} %get-tuple-element.176.du3, bf16[512,2048]{1,0:T(8,128)(2,1)S(1)} %get-tuple-element.177.dhid, f32[512,512]{1,0:T(8,128)S(1)} %get-tuple-element.178.normed, ...), custom_call_target="tpu_custom_call" | custom-call | flops 8388608 | bytes 131072 | tf_op jit(solution)/shard_map/pallas_call | solution.py:761
  84.3 2.3 %collective-permute-done.23.refs_1_ = bf16[2048,512]{1,0:T(8,128)(2,1)S(1)} collective-permute-done((bf16[2048,512]{1,0:T(8,128)(2,1)S(1)}, bf16[2048,512]{1,0:T(8,128)(2,1)S(1)}, u32[]{:S(2)}, u32[]{:S(2)}) %collective-permute-start.23) | collective-permute-done | bytes 2097184 | tf_op jit(solution)/shard_map/ppermute | solution.py:60
  88.9 6.5 %shard_map.486 = (bf16[512,512]{1,0:T(8,128)(2,1)S(1)}, bf16[256,512]{1,0:T(8,128)(2,1)S(1)}, bf16[256,512]{1,0:T(8,128)(2,1)S(1)}) custom-call(bf16[512,512]{1,0:T(8,128)(2,1)} %copy-done.11, bf16[256,512]{1,0:T(8,128)(2,1)} %copy-done.13, bf16[256,512]{1,0:T(8,128)(2,1)} %copy-done.14, bf16[512,512]{1,0:T(8,128)(2,1)} %copy-done.2, ...), custom_call_target="tpu_custom_call" | custom-call | flops 20971520 | bytes 65536 | tf_op jit(solution)/shard_map/pallas_call | solution.py:589
  95.4 6.6 %shard_map.487 = (f32[512,512]{1,0:T(8,128)}, bf16[512,512]{1,0:T(8,128)(2,1)S(1)}, f32[128,512]{1,0:T(8,128)S(1)}, bf16[128,512]{1,0:T(8,128)(2,1)S(1)}, bf16[5...) custom-call(s32[4]{0:T(128)S(1)} %copy-done.19, f32[512,512]{1,0:T(8,128)S(1)} %get-tuple-element.180.du2, ...), custom_call_target="tpu_custom_call" | custom-call | flops 12582912 | bytes 196608 | tf_op jit(solution)/shard_map/pallas_call | solution.py:885
  102.3 1.2 collective-permute-start.26
  103.5 1.2 collective-permute-start.27
  104.7 5.8 %shard_map.489 = (bf16[512,256]{1,0:T(8,128)(2,1)S(1)}, bf16[512,256]{1,0:T(8,128)(2,1)S(1)}, bf16[512,256]{1,0:T(8,128)(2,1)S(1)}, bf16[512,256]{1,0:T(8,128)(2,1)S(1)}, bf16[512,256]{1,0:T(8,128)(2,1)S(1)}) custom-call(s32[4]{0:T(128)S(1)} %copy-done.19, bf16[512,512]{1,0:T(8,128)(2,1)} %copy-done.3, bf16[512,512]{1,0:T(8,128)(2,1)} %copy-done.4, ...), custom_call_target="tpu_custom_call" | custom-call | flops 41943040 | bytes 131072 | tf_op jit(solution)/shard_map/pallas_call | solution.py:559
  112.3 1.2 collective-permute-start.29
  113.6 1.1 collective-permute-start.30
  114.6 3.3 %collective-permute-start.33 = (bf16[256,512]{1,0:T(8,128)(2,1)S(1)}, bf16[256,512]{1,0:T(8,128)(2,1)S(1)}, u32[]{:S(2)}, u32[]{:S(2)}) collective-permute-start(bf16[256,512]{1,0:T(8,128)(2,1)S(1)} %get-tuple-element.236.refs_2_), channel_id=1, source_target_pairs={{0,2},{1,3},{2,0},{3,1},{4,6},{5,7},{6,4},{7,5},{8,10},{9,11},{10,... | collective-permute-start | bytes 786440 | tf_op jit(solution)/shard_map/ppermute | solution.py:60
  118.0 5.9 %shard_map.492 = (bf16[512,256]{1,0:T(8,128)(2,1)S(1)}, bf16[512,256]{1,0:T(8,128)(2,1)S(1)}, bf16[512,256]{1,0:T(8,128)(2,1)S(1)}, bf16[512,256]{1,0:T(8,128)(2,1)S(1)}, bf16[512,256]{1,0:T(8,128)(2,1)S(1)}) custom-call(s32[4]{0:T(128)S(1)} %copy-done.19, bf16[512,512]{1,0:T(8,128)(2,1)} %copy-done.3, bf16[512,512]{1,0:T(8,128)(2,1)} %copy-done.4, ...), custom_call_target="tpu_custom_call" | custom-call | flops 41943040 | bytes 131072 | tf_op jit(solution)/shard_map/pallas_call | solution.py:559
  124.0 1.1 collective-permute-start.31
  125.8 3.1 %shard_map.494 = (bf16[512,512]{1,0:T(8,128)(2,1)S(1)}, bf16[3088,128]{1,0:T(8,128)(2,1)S(1)}, bf16[3088,128]{1,0:T(8,128)(2,1)S(1)}) custom-call(s32[4]{0:T(128)S(1)} %copy-done.19, bf16[512,512]{1,0:T(8,128)(2,1)} %x.5, bf16[512,512]{1,0:T(8,128)(2,1)} %copy-done.12, bf16[512,256]{1,0:T(8,128)(2,1)S(1)} %get-tuple-element.206.dqa, ...), custom_call_target="tpu_custom_call" | custom-call | flops 14680064 | bytes 131072 | tf_op jit(solution)/shard_map/pallas_call | solution.py:964
  129.0 1.3 collective-permute-done.32.refs_3_
  130.2 1.3 collective-permute-start.38
  133.5 1.3 collective-permute-start.36
  134.8 1.5 collective-permute-start.37
  136.3 2.4 %collective-permute-start.39 = (bf16[704,128]{1,0:T(8,128)(2,1)S(1)}, bf16[704,128]{1,0:T(8,128)(2,1)S(1)}, u32[]{:S(2)}, u32[]{:S(2)}) collective-permute-start(bf16[704,128]{1,0:T(8,128)(2,1)S(1)} %get-tuple-element.249.refs_2_), channel_id=1, source_target_pairs={{0,2},{1,3},{2,0},{3,1},{4,6},{5,7},{6,4},{7,5},{8,10},{9,11},{10,... | collective-permute-start | bytes 540680 | tf_op jit(solution)/shard_map/ppermute | solution.py:60
  138.7 15.5 %collective-permute-done.38.back = bf16[512,512]{1,0:T(8,128)(2,1)S(1)} collective-permute-done((bf16[512,512]{1,0:T(8,128)(2,1)S(1)}, bf16[512,512]{1,0:T(8,128)(2,1)S(1)}, u32[]{:S(2)}, u32[]{:S(2)}) %collective-permute-start.38) | collective-permute-done | bytes 524320 | tf_op jit(solution)/shard_map/ppermute | solution.py:66
  154.4 1.6 collective-permute-start.40
  156.5 3.9 %collective-permute-start.44 = (bf16[208,128]{1,0:T(8,128)(2,1)S(1)}, bf16[208,128]{1,0:T(8,128)(2,1)S(1)}, u32[]{:S(2)}, u32[]{:S(2)}) collective-permute-start(bf16[208,128]{1,0:T(8,128)(2,1)S(1)} %get-tuple-element.264), channel_id=1, source_target_pairs={{0,3},{1,2},{2,1},{3,0},{4,7},{5,6},{6,5},{7,4},{8,11},{9,10},{10,... | collective-permute-start | bytes 159752 | tf_op jit(solution)/shard_map/ppermute | solution.py:60
  160.4 3.7 %shard_map.500 = f32[512,512]{1,0:T(8,128)} custom-call(f32[512,512]{1,0:T(8,128)} %get-tuple-element.256.du1, bf16[512,256]{1,0:T(8,128)(2,1)S(1)} %get-tuple-element.206.dqa, bf16[512,256]{1,0:T(8,128)(2,1)S(1)} %get-tuple-element.223.dka, bf16[512,256]{1,0:T(8,128)(2,1)S(1)} %get-tuple-element.224.dva, bf16[512,256]{1,0:T(8,128)(2,1)S(1)} %get-tuple-element.227.dqb, ...), custom_call_target="tpu_custom_call" | custom-call | flops 6291456 | bytes 98304 | tf_op jit(solution)/shard_map/pallas_call | solution.py:992
  164.0 1.9 %collective-permute-done.40.refs_1_ = bf16[256,512]{1,0:T(8,128)(2,1)S(1)} collective-permute-done((bf16[256,512]{1,0:T(8,128)(2,1)S(1)}, bf16[256,512]{1,0:T(8,128)(2,1)S(1)}, u32[]{:S(2)}, u32[]{:S(2)}) %collective-permute-start.40) | collective-permute-done | bytes 262176 | tf_op jit(solution)/shard_map/ppermute | solution.py:60
  168.3 1.2 shard_map.502
  (167 shorter events, 23.0 us)
Async XLA Ops:
  0.7 21.6 %copy-start.8 = (bf16[512,512]{1,0:T(8,128)(2,1)S(1)}, bf16[512,512]{1,0:T(8,128)(2,1)}, u32[]{:S(2)}) copy-start(bf16[512,512]{1,0:T(8,128)(2,1)} %x.5) | copy-start | bytes 1572868
  2.3 10.6 %collective-permute-start.2 = (bf16[528,128]{1,0:T(8,128)(2,1)}, bf16[528,128]{1,0:T(8,128)(2,1)S(1)}, u32[]{:S(2)}, u32[]{:S(2)}) collective-permute-start(bf16[528,128]{1,0:T(8,128)(2,1)} %shard_map.475), channel_id=1, source_target_pairs={{0,3},{1,2},{2,1},{3,0},{4,7},{5,6},{6,5},{7,4},{8,11},{9,10},{10,... | collective-permute-start | bytes 405512 | tf_op jit(solution)/shard_map/ppermute | solution.py:60
  7.3 11.6 %collective-permute-start.1 = (bf16[528,128]{1,0:T(8,128)(2,1)}, bf16[528,128]{1,0:T(8,128)(2,1)S(1)}, u32[]{:S(2)}, u32[]{:S(2)}) collective-permute-start(bf16[528,128]{1,0:T(8,128)(2,1)} %shard_map.475), channel_id=1, source_target_pairs={{0,2},{1,3},{2,0},{3,1},{4,6},{5,7},{6,4},{7,5},{8,10},{9,11},{10,... | collective-permute-start | bytes 405512 | tf_op jit(solution)/shard_map/ppermute | solution.py:60
  7.3 11.6 %collective-permute-start = (bf16[528,128]{1,0:T(8,128)(2,1)}, bf16[528,128]{1,0:T(8,128)(2,1)S(1)}, u32[]{:S(2)}, u32[]{:S(2)}) collective-permute-start(bf16[528,128]{1,0:T(8,128)(2,1)} %shard_map.475), channel_id=1, source_target_pairs={{0,1},{1,0},{2,3},{3,2},{4,5},{5,4},{6,7},{7,6},{8,9},{9,8},{10,11... | collective-permute-start | bytes 405512 | tf_op jit(solution)/shard_map/ppermute | solution.py:60
  19.1 7.4 %collective-permute-start.4 = (bf16[1,4,4,64,128]{4,3,2,1,0:T(8,128)(2,1)S(1)}, bf16[1,4,4,64,128]{4,3,2,1,0:T(8,128)(2,1)S(1)}, u32[]{:S(2)}, u32[]{:S(2)}) collective-permute-start(bf16[1,4,4,64,128]{4,3,2,1,0:T(8,128)(2,1)S(1)} %pad_maximum_fusion.3), channel_id=1, source_target_pairs={{0,8},{1,9},{2,10},{3,11},{4,12},{5,13},{6,14},{7,15},{8,0},{9,1},... | collective-permute-start | bytes 786440 | tf_op jit(solution)/shard_map/ppermute | solution.py:60
  20.6 9.2 %collective-permute-start.7 = (bf16[1,2,64,512]{3,2,0,1:T(8,128)(2,1)S(1)}, bf16[1,2,64,512]{3,2,0,1:T(8,128)(2,1)S(1)}, u32[]{:S(2)}, u32[]{:S(2)}) collective-permute-start(bf16[1,2,64,512]{3,2,0,1:T(8,128)(2,1)S(1)} %bitcast.66), channel_id=1, source_target_pairs={{0,1},{1,0},{2,3},{3,2},{4,5},{5,4},{6,7},{7,6},{8,9},{9,8},{10,11... | collective-permute-start | bytes 393224 | tf_op jit(solution)/shard_map/ppermute | solution.py:60
  20.7 7.5 %collective-permute-start.10 = (bf16[1,4,4,64,128]{4,3,2,1,0:T(8,128)(2,1)S(1)}, bf16[1,4,4,64,128]{4,3,2,1,0:T(8,128)(2,1)S(1)}, u32[]{:S(2)}, u32[]{:S(2)}) collective-permute-start(bf16[1,4,4,64,128]{4,3,2,1,0:T(8,128)(2,1)S(1)} %pad_maximum_fusion.5), channel_id=1, source_target_pairs={{0,16},{1,17},{2,18},{3,19},{4,20},{5,21},{6,22},{7,23},{8,24},{9,... | collective-permute-start | bytes 786440 | tf_op jit(solution)/shard_map/ppermute | solution.py:60
  22.3 21.6 %collective-permute-start.3 = (bf16[512,512]{1,0:T(8,128)(2,1)S(1)}, bf16[512,512]{1,0:T(8,128)(2,1)S(1)}, u32[]{:S(2)}, u32[]{:S(2)}) collective-permute-start(bf16[512,512]{1,0:T(8,128)(2,1)S(1)} %copy-done.8), channel_id=1, source_target_pairs={{0,1},{2,3},{4,5},{6,7},{8,9},{10,11},{12,13},{14,15},{16,17},{18,... | collective-permute-start | bytes 1572872 | tf_op jit(solution)/shard_map/ppermute | solution.py:66
  26.5 20.2 %copy-start.19 = (s32[4]{0:T(128)S(1)}, s32[4]{0:T(128)}, u32[]{:S(2)}) copy-start(s32[4]{0:T(128)} %pad_add_fusion.info) | copy-start | bytes 52
  26.6 17.3 %collective-permute-start.6 = (bf16[2,4,4,64,128]{4,3,2,1,0:T(8,128)(2,1)S(1)}, bf16[2,4,4,64,128]{4,3,2,1,0:T(8,128)(2,1)S(1)}, u32[]{:S(2)}, u32[]{:S(2)}) collective-permute-start(bf16[2,4,4,64,128]{4,3,2,1,0:T(8,128)(2,1)S(1)} %pad_maximum_fusion.refs_0_), channel_id=1, source_target_pairs={{0,16},{1,17},{2,18},{3,19},{4,20},{5,21},{6,22},{7,23},{8,24},{9,... | collective-permute-start | bytes 1572872 | tf_op jit(solution)/shard_map/ppermute | solution.py:60
  28.2 15.6 %collective-permute-start.12 = (bf16[2,4,4,64,128]{4,3,2,1,0:T(8,128)(2,1)S(1)}, bf16[2,4,4,64,128]{4,3,2,1,0:T(8,128)(2,1)S(1)}, u32[]{:S(2)}, u32[]{:S(2)}) collective-permute-start(bf16[2,4,4,64,128]{4,3,2,1,0:T(8,128)(2,1)S(1)} %pad_maximum_fusion.2.refs_4_), channel_id=1, source_target_pairs={{0,8},{1,9},{2,10},{3,11},{4,12},{5,13},{6,14},{7,15},{8,0},{9,1},... | collective-permute-start | bytes 1572872 | tf_op jit(solution)/shard_map/ppermute | solution.py:60
  30.5 12.3 %collective-permute-start.8 = (bf16[2,2,64,512]{3,2,0,1:T(8,128)(2,1)}, bf16[2,2,64,512]{3,2,0,1:T(8,128)(2,1)}, u32[]{:S(2)}, u32[]{:S(2)}) collective-permute-start(bf16[2,2,64,512]{3,2,0,1:T(8,128)(2,1)} %pad_maximum_fusion.4), channel_id=1, source_target_pairs={{0,2},{1,3},{2,0},{3,1},{4,6},{5,7},{6,4},{7,5},{8,10},{9,11},{10,... | collective-permute-start | bytes 786440 | tf_op jit(solution)/shard_map/ppermute | solution.py:60
  36.6 9.0 %collective-permute-start.5 = (bf16[2,4,4,64,128]{4,3,2,1,0:T(8,128)(2,1)S(1)}, bf16[2,4,4,64,128]{4,3,2,1,0:T(8,128)(2,1)S(1)}, u32[]{:S(2)}, u32[]{:S(2)}) collective-permute-start(bf16[2,4,4,64,128]{4,3,2,1,0:T(8,128)(2,1)S(1)} %pad_maximum_fusion.refs_0_), channel_id=1, source_target_pairs={{0,4},{1,5},{2,6},{3,7},{4,0},{5,1},{6,2},{7,3},{8,12},{9,13},{10,... | collective-permute-start | bytes 1572872 | tf_op jit(solution)/shard_map/ppermute | solution.py:60
  42.8 3.9 %collective-permute-start.11 = (bf16[2,4,4,64,128]{4,3,2,1,0:T(8,128)(2,1)S(1)}, bf16[2,4,4,64,128]{4,3,2,1,0:T(8,128)(2,1)S(1)}, u32[]{:S(2)}, u32[]{:S(2)}) collective-permute-start(bf16[2,4,4,64,128]{4,3,2,1,0:T(8,128)(2,1)S(1)} %pad_maximum_fusion.2.refs_4_), channel_id=1, source_target_pairs={{0,4},{1,5},{2,6},{3,7},{4,0},{5,1},{6,2},{7,3},{8,12},{9,13},{10,... | collective-permute-start | bytes 1572872 | tf_op jit(solution)/shard_map/ppermute | solution.py:60
  43.9 2.9 %collective-permute-start.13 = (bf16[2,4,4,64,128]{4,3,2,1,0:T(8,128)(2,1)S(1)}, bf16[2,4,4,64,128]{4,3,2,1,0:T(8,128)(2,1)S(1)}, u32[]{:S(2)}, u32[]{:S(2)}) collective-permute-start(bf16[2,4,4,64,128]{4,3,2,1,0:T(8,128)(2,1)S(1)} %collective-permute-done.12.refs_6_), channel_id=1, source_target_pairs={{0,4},{1,5},{2,6},{3,7},{4,0},{5,1},{6,2},{7,3},{8,12},{9,13},{10,... | collective-permute-start | bytes 1572872 | tf_op jit(solution)/shard_map/ppermute | solution.py:60
  44.4 2.3 %collective-permute-start.9 = (bf16[2,4,4,64,128]{4,3,2,1,0:T(8,128)(2,1)S(1)}, bf16[2,4,4,64,128]{4,3,2,1,0:T(8,128)(2,1)S(1)}, u32[]{:S(2)}, u32[]{:S(2)}) collective-permute-start(bf16[2,4,4,64,128]{4,3,2,1,0:T(8,128)(2,1)S(1)} %collective-permute-done.6.refs_2_), channel_id=1, source_target_pairs={{0,4},{1,5},{2,6},{3,7},{4,0},{5,1},{6,2},{7,3},{8,12},{9,13},{10,... | collective-permute-start | bytes 1572872 | tf_op jit(solution)/shard_map/ppermute | solution.py:60
  44.6 8.7 %collective-permute-start.15 = (bf16[1,4,1,64,512]{4,3,2,1,0:T(8,128)(2,1)S(1)}, bf16[1,4,1,64,512]{4,3,2,1,0:T(8,128)(2,1)S(1)}, u32[]{:S(2)}, u32[]{:S(2)}) collective-permute-start(bf16[1,4,1,64,512]{4,3,2,1,0:T(8,128)(2,1)S(1)} %get-tuple-element.159), channel_id=1, source_target_pairs={{0,16},{1,17},{2,18},{3,19},{4,20},{5,21},{6,22},{7,23},{8,24},{9,... | collective-permute-start | bytes 786440 | tf_op jit(solution)/shard_map/ppermute | solution.py:60
  45.5 8.8 %collective-permute-start.14 = (bf16[1,4,1,64,512]{4,3,1,2,0:T(8,128)(2,1)S(1)}, bf16[1,4,1,64,512]{4,3,1,2,0:T(8,128)(2,1)S(1)}, u32[]{:S(2)}, u32[]{:S(2)}) collective-permute-start(bf16[1,4,1,64,512]{4,3,1,2,0:T(8,128)(2,1)S(1)} %get-tuple-element.158), channel_id=1, source_target_pairs={{0,8},{1,9},{2,10},{3,11},{4,12},{5,13},{6,14},{7,15},{8,0},{9,1},... | collective-permute-start | bytes 786440 | tf_op jit(solution)/shard_map/ppermute | solution.py:60
  48.1 23.3 %copy-start = (bf16[8,512,512]{2,1,0:T(8,128)(2,1)}, bf16[8,512,512]{2,1,0:T(8,128)(2,1)S(1)}, u32[]{:S(2)}) copy-start(bf16[8,512,512]{2,1,0:T(8,128)(2,1)S(1)} %shard_map.477.wq.wk.wv.wo.w) | copy-start | bytes 12582916
  53.3 14.5 %collective-permute-start.21 = (bf16[2,4,1,64,512]{4,3,2,1,0:T(8,128)(2,1)S(1)}, bf16[2,4,1,64,512]{4,3,2,1,0:T(8,128)(2,1)S(1)}, u32[]{:S(2)}, u32[]{:S(2)}) collective-permute-start(bf16[2,4,1,64,512]{4,3,2,1,0:T(8,128)(2,1)S(1)} %constant_dynamic-update-slice_fusion.2.refs_4_), channel_id=1, source_target_pairs={{0,8},{1,9},{2,10},{3,11},{4,12},{5,13},{6,14},{7,15},{8,0},{9,1},... | collective-permute-start | bytes 1572872 | tf_op jit(solution)/shard_map/ppermute | solution.py:60
  54.4 13.4 %collective-permute-start.18 = (bf16[2,4,1,64,512]{4,3,1,2,0:T(8,128)(2,1)S(1)}, bf16[2,4,1,64,512]{4,3,1,2,0:T(8,128)(2,1)S(1)}, u32[]{:S(2)}, u32[]{:S(2)}) collective-permute-start(bf16[2,4,1,64,512]{4,3,1,2,0:T(8,128)(2,1)S(1)} %constant_dynamic-update-slice_fusion), channel_id=1, source_target_pairs={{0,16},{1,17},{2,18},{3,19},{4,20},{5,21},{6,22},{7,23},{8,24},{9,... | collective-permute-start | bytes 1572872 | tf_op jit(solution)/shard_map/ppermute | solution.py:60
  55.6 6.2 %collective-permute-start.16 = (bf16[128,512]{1,0:T(8,128)(2,1)S(1)}, bf16[128,512]{1,0:T(8,128)(2,1)S(1)}, u32[]{:S(2)}, u32[]{:S(2)}) collective-permute-start(bf16[128,512]{1,0:T(8,128)(2,1)S(1)} %copy-done.15), channel_id=1, source_target_pairs={{0,1},{1,0},{2,3},{3,2},{4,5},{5,4},{6,7},{7,6},{8,9},{9,8},{10,11... | collective-permute-start | bytes 393224 | tf_op jit(solution)/shard_map/ppermute | solution.py:60
  55.9 12.6 %collective-permute-start.20 = (bf16[2,4,1,64,512]{4,3,2,1,0:T(8,128)(2,1)S(1)}, bf16[2,4,1,64,512]{4,3,2,1,0:T(8,128)(2,1)S(1)}, u32[]{:S(2)}, u32[]{:S(2)}) collective-permute-start(bf16[2,4,1,64,512]{4,3,2,1,0:T(8,128)(2,1)S(1)} %constant_dynamic-update-slice_fusion.2.refs_4_), channel_id=1, source_target_pairs={{0,4},{1,5},{2,6},{3,7},{4,0},{5,1},{6,2},{7,3},{8,12},{9,13},{10,... | collective-permute-start | bytes 1572872 | tf_op jit(solution)/shard_map/ppermute | solution.py:60
  56.0 12.5 %collective-permute-start.17 = (bf16[2,4,1,64,512]{4,3,1,2,0:T(8,128)(2,1)S(1)}, bf16[2,4,1,64,512]{4,3,1,2,0:T(8,128)(2,1)S(1)}, u32[]{:S(2)}, u32[]{:S(2)}) collective-permute-start(bf16[2,4,1,64,512]{4,3,1,2,0:T(8,128)(2,1)S(1)} %constant_dynamic-update-slice_fusion), channel_id=1, source_target_pairs={{0,4},{1,5},{2,6},{3,7},{4,0},{5,1},{6,2},{7,3},{8,12},{9,13},{10,... | collective-permute-start | bytes 1572872 | tf_op jit(solution)/shard_map/ppermute | solution.py:60
  67.8 2.0 %collective-permute-start.19 = (bf16[2,4,1,64,512]{4,3,1,2,0:T(8,128)(2,1)S(1)}, bf16[2,4,1,64,512]{4,3,1,2,0:T(8,128)(2,1)S(1)}, u32[]{:S(2)}, u32[]{:S(2)}) collective-permute-start(bf16[2,4,1,64,512]{4,3,1,2,0:T(8,128)(2,1)S(1)} %collective-permute-done.18), channel_id=1, source_target_pairs={{0,4},{1,5},{2,6},{3,7},{4,0},{5,1},{6,2},{7,3},{8,12},{9,13},{10,... | collective-permute-start | bytes 1572872 | tf_op jit(solution)/shard_map/ppermute | solution.py:60
  67.9 2.6 %collective-permute-start.22 = (bf16[2,4,1,64,512]{4,3,2,1,0:T(8,128)(2,1)S(1)}, bf16[2,4,1,64,512]{4,3,2,1,0:T(8,128)(2,1)S(1)}, u32[]{:S(2)}, u32[]{:S(2)}) collective-permute-start(bf16[2,4,1,64,512]{4,3,2,1,0:T(8,128)(2,1)S(1)} %collective-permute-done.21.refs_6_), channel_id=1, source_target_pairs={{0,4},{1,5},{2,6},{3,7},{4,0},{5,1},{6,2},{7,3},{8,12},{9,13},{10,... | collective-permute-start | bytes 1572872 | tf_op jit(solution)/shard_map/ppermute | solution.py:60
  82.4 4.2 %collective-permute-start.23 = (bf16[2048,512]{1,0:T(8,128)(2,1)S(1)}, bf16[2048,512]{1,0:T(8,128)(2,1)S(1)}, u32[]{:S(2)}, u32[]{:S(2)}) collective-permute-start(bf16[2048,512]{1,0:T(8,128)(2,1)S(1)} %get-tuple-element.185), channel_id=1, source_target_pairs={{0,4},{1,5},{2,6},{3,7},{4,0},{5,1},{6,2},{7,3},{8,12},{9,13},{10,... | collective-permute-start | bytes 6291464 | tf_op jit(solution)/shard_map/ppermute | solution.py:60
  87.0 14.9 %collective-permute-start.24 = (bf16[512,512]{1,0:T(8,128)(2,1)S(1)}, bf16[512,512]{1,0:T(8,128)(2,1)S(1)}, u32[]{:S(2)}, u32[]{:S(2)}) collective-permute-start(bf16[512,512]{1,0:T(8,128)(2,1)S(1)} %get-tuple-element.201), channel_id=1, source_target_pairs={{0,8},{1,9},{2,10},{3,11},{4,12},{5,13},{6,14},{7,15},{8,0},{9,1},... | collective-permute-start | bytes 1572872 | tf_op jit(solution)/shard_map/ppermute | solution.py:60
  88.0 14.0 %collective-permute-start.25 = (bf16[512,512]{1,0:T(8,128)(2,1)S(1)}, bf16[512,512]{1,0:T(8,128)(2,1)S(1)}, u32[]{:S(2)}, u32[]{:S(2)}) collective-permute-start(bf16[512,512]{1,0:T(8,128)(2,1)S(1)} %get-tuple-element.202.refs_4_), channel_id=1, source_target_pairs={{0,16},{1,17},{2,18},{3,19},{4,20},{5,21},{6,22},{7,23},{8,24},{9,... | collective-permute-start | bytes 1572872 | tf_op jit(solution)/shard_map/ppermute | solution.py:60
  102.2 9.8 %collective-permute-start.28 = (bf16[5184,128]{1,0:T(8,128)(2,1)S(1)}, bf16[5184,128]{1,0:T(8,128)(2,1)S(1)}, u32[]{:S(2)}, u32[]{:S(2)}) collective-permute-start(bf16[5184,128]{1,0:T(8,128)(2,1)S(1)} %get-tuple-element.214), channel_id=1, source_target_pairs={{0,4},{1,5},{2,6},{3,7},{4,0},{5,1},{6,2},{7,3},{8,12},{9,13},{10,... | collective-permute-start | bytes 3981320 | tf_op jit(solution)/shard_map/ppermute | solution.py:60
  102.3 8.7 %collective-permute-start.26 = (bf16[256,512]{1,0:T(8,128)(2,1)S(1)}, bf16[256,512]{1,0:T(8,128)(2,1)S(1)}, u32[]{:S(2)}, u32[]{:S(2)}) collective-permute-start(bf16[256,512]{1,0:T(8,128)(2,1)S(1)} %get-tuple-element.209), channel_id=1, source_target_pairs={{0,16},{1,17},{2,18},{3,19},{4,20},{5,21},{6,22},{7,23},{8,24},{9,... | collective-permute-start | bytes 786440 | tf_op jit(solution)/shard_map/ppermute | solution.py:60
  103.5 8.4 %collective-permute-start.27 = (bf16[256,512]{1,0:T(8,128)(2,1)S(1)}, bf16[256,512]{1,0:T(8,128)(2,1)S(1)}, u32[]{:S(2)}, u32[]{:S(2)}) collective-permute-start(bf16[256,512]{1,0:T(8,128)(2,1)S(1)} %get-tuple-element.210.refs_4_), channel_id=1, source_target_pairs={{0,8},{1,9},{2,10},{3,11},{4,12},{5,13},{6,14},{7,15},{8,0},{9,1},... | collective-permute-start | bytes 786440 | tf_op jit(solution)/shard_map/ppermute | solution.py:60
  112.3 11.5 %collective-permute-start.29 = (bf16[1536,128]{1,0:T(8,128)(2,1)S(1)}, bf16[1536,128]{1,0:T(8,128)(2,1)S(1)}, u32[]{:S(2)}, u32[]{:S(2)}) collective-permute-start(bf16[1536,128]{1,0:T(8,128)(2,1)S(1)} %get-tuple-element.220), channel_id=1, source_target_pairs={{0,8},{1,9},{2,10},{3,11},{4,12},{5,13},{6,14},{7,15},{8,0},{9,1},... | collective-permute-start | bytes 1179656 | tf_op jit(solution)/shard_map/ppermute | solution.py:60
  113.6 10.2 %collective-permute-start.30 = (bf16[1088,128]{1,0:T(8,128)(2,1)S(1)}, bf16[1088,128]{1,0:T(8,128)(2,1)S(1)}, u32[]{:S(2)}, u32[]{:S(2)}) collective-permute-start(bf16[1088,128]{1,0:T(8,128)(2,1)S(1)} %get-tuple-element.221.refs_4_), channel_id=1, source_target_pairs={{0,16},{1,17},{2,18},{3,19},{4,20},{5,21},{6,22},{7,23},{8,24},{9,... | collective-permute-start | bytes 835592 | tf_op jit(solution)/shard_map/ppermute | solution.py:60
  114.6 14.3 %collective-permute-start.33 = (bf16[256,512]{1,0:T(8,128)(2,1)S(1)}, bf16[256,512]{1,0:T(8,128)(2,1)S(1)}, u32[]{:S(2)}, u32[]{:S(2)}) collective-permute-start(bf16[256,512]{1,0:T(8,128)(2,1)S(1)} %get-tuple-element.236.refs_2_), channel_id=1, source_target_pairs={{0,2},{1,3},{2,0},{3,1},{4,6},{5,7},{6,4},{7,5},{8,10},{9,11},{10,... | collective-permute-start | bytes 786440 | tf_op jit(solution)/shard_map/ppermute | solution.py:60
  124.0 6.2 %collective-permute-start.31 = (bf16[768,128]{1,0:T(8,128)(2,1)S(1)}, bf16[768,128]{1,0:T(8,128)(2,1)S(1)}, u32[]{:S(2)}, u32[]{:S(2)}) collective-permute-start(bf16[768,128]{1,0:T(8,128)(2,1)S(1)} %get-tuple-element.234), channel_id=1, source_target_pairs={{0,16},{1,17},{2,18},{3,19},{4,20},{5,21},{6,22},{7,23},{8,24},{9,... | collective-permute-start | bytes 589832 | tf_op jit(solution)/shard_map/ppermute | solution.py:60
  125.1 5.1 %collective-permute-start.32 = (bf16[576,128]{1,0:T(8,128)(2,1)S(1)}, bf16[576,128]{1,0:T(8,128)(2,1)S(1)}, u32[]{:S(2)}, u32[]{:S(2)}) collective-permute-start(bf16[576,128]{1,0:T(8,128)(2,1)S(1)} %get-tuple-element.235.refs_4_), channel_id=1, source_target_pairs={{0,8},{1,9},{2,10},{3,11},{4,12},{5,13},{6,14},{7,15},{8,0},{9,1},... | collective-permute-start | bytes 442376 | tf_op jit(solution)/shard_map/ppermute | solution.py:60
  130.2 2.3 %collective-permute-start.34 = (bf16[3088,128]{1,0:T(8,128)(2,1)S(1)}, bf16[3088,128]{1,0:T(8,128)(2,1)S(1)}, u32[]{:S(2)}, u32[]{:S(2)}) collective-permute-start(bf16[3088,128]{1,0:T(8,128)(2,1)S(1)} %get-tuple-element.237), channel_id=1, source_target_pairs={{0,4},{1,5},{2,6},{3,7},{4,0},{5,1},{6,2},{7,3},{8,12},{9,13},{10,... | collective-permute-start | bytes 2371592 | tf_op jit(solution)/shard_map/ppermute | solution.py:60
  130.2 23.9 %collective-permute-start.38 = (bf16[512,512]{1,0:T(8,128)(2,1)S(1)}, bf16[512,512]{1,0:T(8,128)(2,1)S(1)}, u32[]{:S(2)}, u32[]{:S(2)}) collective-permute-start(bf16[512,512]{1,0:T(8,128)(2,1)S(1)} %get-tuple-element.247), channel_id=1, source_target_pairs={{1,0},{3,2},{5,4},{7,6},{9,8},{11,10},{13,12},{15,14},{17,16},{19,... | collective-permute-start | bytes 1572872 | tf_op jit(solution)/shard_map/ppermute | solution.py:66
  132.7 21.4 %collective-permute-start.35 = (bf16[784,128]{1,0:T(8,128)(2,1)S(1)}, bf16[784,128]{1,0:T(8,128)(2,1)S(1)}, u32[]{:S(2)}, u32[]{:S(2)}) collective-permute-start(bf16[784,128]{1,0:T(8,128)(2,1)S(1)} %get-tuple-element.243), channel_id=1, source_target_pairs={{0,8},{1,9},{2,10},{3,11},{4,12},{5,13},{6,14},{7,15},{8,0},{9,1},... | collective-permute-start | bytes 602120 | tf_op jit(solution)/shard_map/ppermute | solution.py:60
  133.5 20.6 %collective-permute-start.36 = (bf16[784,128]{1,0:T(8,128)(2,1)S(1)}, bf16[784,128]{1,0:T(8,128)(2,1)S(1)}, u32[]{:S(2)}, u32[]{:S(2)}) collective-permute-start(bf16[784,128]{1,0:T(8,128)(2,1)S(1)} %get-tuple-element.244), channel_id=1, source_target_pairs={{0,16},{1,17},{2,18},{3,19},{4,20},{5,21},{6,22},{7,23},{8,24},{9,... | collective-permute-start | bytes 602120 | tf_op jit(solution)/shard_map/ppermute | solution.py:60
  134.8 19.4 %collective-permute-start.37 = (bf16[784,128]{1,0:T(8,128)(2,1)S(1)}, bf16[784,128]{1,0:T(8,128)(2,1)S(1)}, u32[]{:S(2)}, u32[]{:S(2)}) collective-permute-start(bf16[784,128]{1,0:T(8,128)(2,1)S(1)} %get-tuple-element.245), channel_id=1, source_target_pairs={{0,24},{1,25},{2,26},{3,27},{4,28},{5,29},{6,30},{7,31},{8,16},{9,... | collective-permute-start | bytes 602120 | tf_op jit(solution)/shard_map/ppermute | solution.py:60
  136.3 17.9 %collective-permute-start.39 = (bf16[704,128]{1,0:T(8,128)(2,1)S(1)}, bf16[704,128]{1,0:T(8,128)(2,1)S(1)}, u32[]{:S(2)}, u32[]{:S(2)}) collective-permute-start(bf16[704,128]{1,0:T(8,128)(2,1)S(1)} %get-tuple-element.249.refs_2_), channel_id=1, source_target_pairs={{0,2},{1,3},{2,0},{3,1},{4,6},{5,7},{6,4},{7,5},{8,10},{9,11},{10,... | collective-permute-start | bytes 540680 | tf_op jit(solution)/shard_map/ppermute | solution.py:60
  154.4 11.5 %collective-permute-start.40 = (bf16[256,512]{1,0:T(8,128)(2,1)S(1)}, bf16[256,512]{1,0:T(8,128)(2,1)S(1)}, u32[]{:S(2)}, u32[]{:S(2)}) collective-permute-start(bf16[256,512]{1,0:T(8,128)(2,1)S(1)} %get-tuple-element.258), channel_id=1, source_target_pairs={{0,1},{1,0},{2,3},{3,2},{4,5},{5,4},{6,7},{7,6},{8,9},{9,8},{10,11... | collective-permute-start | bytes 786440 | tf_op jit(solution)/shard_map/ppermute | solution.py:60
  156.0 11.4 %collective-permute-start.42 = (bf16[208,128]{1,0:T(8,128)(2,1)S(1)}, bf16[208,128]{1,0:T(8,128)(2,1)S(1)}, u32[]{:S(2)}, u32[]{:S(2)}) collective-permute-start(bf16[208,128]{1,0:T(8,128)(2,1)S(1)} %get-tuple-element.262), channel_id=1, source_target_pairs={{0,1},{1,0},{2,3},{3,2},{4,5},{5,4},{6,7},{7,6},{8,9},{9,8},{10,11... | collective-permute-start | bytes 159752 | tf_op jit(solution)/shard_map/ppermute | solution.py:60
  156.5 10.9 %collective-permute-start.43 = (bf16[208,128]{1,0:T(8,128)(2,1)S(1)}, bf16[208,128]{1,0:T(8,128)(2,1)S(1)}, u32[]{:S(2)}, u32[]{:S(2)}) collective-permute-start(bf16[208,128]{1,0:T(8,128)(2,1)S(1)} %get-tuple-element.263), channel_id=1, source_target_pairs={{0,2},{1,3},{2,0},{3,1},{4,6},{5,7},{6,4},{7,5},{8,10},{9,11},{10,... | collective-permute-start | bytes 159752 | tf_op jit(solution)/shard_map/ppermute | solution.py:60
  156.5 10.9 %collective-permute-start.44 = (bf16[208,128]{1,0:T(8,128)(2,1)S(1)}, bf16[208,128]{1,0:T(8,128)(2,1)S(1)}, u32[]{:S(2)}, u32[]{:S(2)}) collective-permute-start(bf16[208,128]{1,0:T(8,128)(2,1)S(1)} %get-tuple-element.264), channel_id=1, source_target_pairs={{0,3},{1,2},{2,1},{3,0},{4,7},{5,6},{6,5},{7,4},{8,11},{9,10},{10,... | collective-permute-start | bytes 159752 | tf_op jit(solution)/shard_map/ppermute | solution.py:60
  160.4 8.0 %collective-permute-start.41 = (bf16[384,128]{1,0:T(8,128)(2,1)S(1)}, bf16[384,128]{1,0:T(8,128)(2,1)S(1)}, u32[]{:S(2)}, u32[]{:S(2)}) collective-permute-start(bf16[384,128]{1,0:T(8,128)(2,1)S(1)} %get-tuple-element.259.refs_2_), channel_id=1, source_target_pairs={{0,1},{1,0},{2,3},{3,2},{4,5},{5,4},{6,7},{7,6},{8,9},{9,8},{10,11... | collective-permute-start | bytes 294920 | tf_op jit(solution)/shard_map/ppermute | solution.py:60
  (28 other events, 174.3 us)
